TPU v7x, 256 devices: a whole 4x4x8 slice. The times are simulated.
256 devices in a mesh: tok: 64 (over z_lo, y, x), hid: 4 (over z_hi, core).
Axes of the slice: x: 4, y: 4, z: 8 (z_hi: 2, z_lo: 4; z = z_hi * 4 + z_lo), core: 2. Of those that a mesh axis runs over, the one named last changes fastest.
Arguments:
- train_grads: bfloat16 [32768, 28672], P('tok', 'hid'), may hold values from -6 to 6
- train_acts: bfloat16 [32768, 8192], P('tok', 'hid'), may hold values from -6 to 6
- out_factors: bfloat16 [28672, 1024], P('hid', 'tok'), may hold values from -0.03125 to 0.03125
- in_factors: bfloat16 [8192, 1024], P('hid', 'tok'), may hold values from -0.0625 to 0.0625
Outputs:
- scores: float32 [512, 128], P('tok', 'hid')
All inputs are finite; a program needn't handle non-finite values.
Results may differ from a plain program's by a relative error of at most 0.0003.
Values may be sent and summed in bfloat16 or wider, within the bound.
No kernel may reach another device: no remote copies, remote signals or barrier semaphores. Data moves between devices by JAX's collectives and lax.ppermute only.
A program may use at most 128 MiB of HBM per device.

v0:
```python
import math

import jax
import jax.numpy as jnp
from jax import lax
from jax.sharding import PartitionSpec as P

RANK = 8
SEQ_LEN = 64


def shards(train_grads, train_acts, out_factors, in_factors):
    tok_rows = train_grads.shape[0]
    columns = out_factors.shape[1] * lax.axis_size("tok")
    grad_piece = jnp.dot(
        train_grads,
        lax.all_gather(out_factors, "tok", axis=1, tiled=True),
        preferred_element_type=jnp.float32,
    )
    act_piece = jnp.dot(
        train_acts,
        lax.all_gather(in_factors, "tok", axis=1, tiled=True),
        preferred_element_type=jnp.float32,
    )
    block = columns // lax.axis_size("hid")
    grad_full, act_full = lax.psum((grad_piece, act_piece), "hid")
    offset = lax.axis_index("hid") * block
    grad_sum = lax.dynamic_slice_in_dim(grad_full, offset, block, 1)
    act_sum = lax.dynamic_slice_in_dim(act_full, offset, block, 1)
    joined = (grad_sum * act_sum).reshape(tok_rows // SEQ_LEN, SEQ_LEN, block // RANK, RANK)
    scale = 1.0 / math.sqrt(SEQ_LEN * RANK)
    return jnp.sum(joined, axis=(1, 3)) * scale


def solution(mesh):
    return jax.shard_map(
        shards,
        mesh=mesh,
        in_specs=(P("tok", "hid"), P("tok", "hid"), P("hid", "tok"), P("hid", "tok")),
        out_specs=P("tok", "hid"),
        check_vma=False,
    )
```

profile of v0, /device:TPU:33, one launch (start us, length us, event | category | flops | bytes accessed | tf_op | source)
XLA Modules:
  0.0 933.3 jit_solution(12771596410618873492)
XLA Ops:
  6.5 0.0 copy-start
  6.5 0.0 all-gather.5.cloned.1.call-start
  6.5 0.7 all-gather.5.cloned.1.call-update
  7.3 0.0 all-gather.3.cloned.1.call-start
  7.3 0.7 all-gather.3.cloned.1.call-update
  8.0 0.0 all-reduce.3.cloned.1.call-start
  8.1 280.4 %all-gather.5.cloned.1.call-done = bf16[2048,1024]{0,1:T(8,128)(2,1)} async-done(((bf16[2048,16]{0,1:T(8,128)(2,1)}), bf16[2048,1024]{0,1:T(8,128)(2,1)}) %all-gather.5.cloned.1.call-update) | async-done | bytes 4194320 | tf_op jit(solution)/shard_map/all_gather | solution.py:22
  288.4 0.0 copy-done
  288.4 5.9 fusion.1
  294.3 373.2 %all-gather.3.cloned.1.call-done = bf16[7168,1024]{0,1:T(8,128)(2,1)} async-done(((bf16[7168,16]{0,1:T(8,128)(2,1)}), bf16[7168,1024]{0,1:T(8,128)(2,1)}) %all-gather.3.cloned.1.call-update) | async-done | bytes 14680080 | tf_op jit(solution)/shard_map/all_gather | solution.py:17
  667.5 14.2 %fusion = f32[512,1024]{1,0:T(8,128)} fusion(bf16[512,7168]{1,0:T(8,128)(2,1)} %param.4, bf16[7168,1024]{0,1:T(8,128)(2,1)} %all-gather.3.cloned.1.call-done), kind=kOutput, calls=%fused_computation.2 | convolution fusion | flops 7516192768 | bytes 24117248 | tf_op jit(solution)/shard_map/dot_general | solution.py:15
  681.6 0.0 all-reduce.3.cloned.1.call-update
  681.7 240.7 %all-reduce.3.cloned.1.call-done = (f32[512,1024]{1,0:T(8,128)}, f32[512,1024]{1,0:T(8,128)}) async-done(((f32[512,1024]{1,0:T(8,128)}, f32[512,1024]{1,0:T(8,128)}), (f32[512,1024]{1,0:T(8,128)}, f32[512,1024]{1,0:T(8,128)})) %all-reduce.3.cloned.1.call-update) | async-done | bytes 4194320 | tf_op jit(solution)/shard_map/psum | solution.py:26
  922.4 1.3 dynamic-slice_multiply_fusion
  923.7 1.0 copy.8
  924.7 1.2 reshape.3
  925.9 0.1 reduce_sum.9
  926.1 0.1 copy.9
  926.1 0.6 broadcast_multiply_fusion
Async XLA Ops:
  6.5 281.9 %copy-start = (bf16[512,2048]{1,0:T(8,128)(2,1)S(1)}, bf16[512,2048]{1,0:T(8,128)(2,1)}, u32[]{:S(2)}) copy-start(bf16[512,2048]{1,0:T(8,128)(2,1)} %param.5) | copy-start | bytes 6291460
  6.5 281.9 %all-gather.5.cloned.1.call-start = ((), (), s32[]{:S(2)}) async-start(), calls=%async_computation.1 | async-start | bytes 4259840 | tf_op jit(solution)/shard_map/all_gather | solution.py:22
  7.3 660.2 %all-gather.3.cloned.1.call-start = ((), (), s32[]{:S(2)}) async-start(), calls=%async_computation | async-start | bytes 14909440 | tf_op jit(solution)/shard_map/all_gather | solution.py:17
  8.0 914.4 %all-reduce.3.cloned.1.call-start = ((), (), s32[]{:S(2)}) async-start(), calls=%async_computation.2 | async-start | bytes 8388608 | tf_op jit(solution)/shard_map/psum | solution.py:26
Sparse Core Ops, SparseCore 0:
  9.1 279.2 all-gather.4
  290.2 377.2 all-gather.2
  681.8 240.5 all-reduce.2
where the time goes:
time: 936 us; the launch traced here: 933 us
  waiting for transfers between devices  896 us (96%)
  matrix products  20 us (2%)
  between operations  13.1 us (1%)
    all_gather x1, waiting for transfers between devices, shards(): lax.all_gather(out_factors, 'tok', axis=1, tiled=True)  373 us
    all_gather x1, waiting for transfers between devices, shards(): lax.all_gather(in_factors, 'tok', axis=1, tiled=True)  280 us
    psum x1, waiting for transfers between devices, shards(): grad_full, act_full = lax.psum((grad_piece, act_piece), 'hid')  241 us
  transfers between devices with their start and end apart: 3, of which 3 were waited for; matrix products, arithmetic and copies ran while one was open for 1% of the time, Pallas kernels for 0%

commit v1 on v0

v1 whole, which is shorter than its diff:
```python
import functools
import math

import jax
import jax.numpy as jnp
from jax import lax
from jax.experimental import pallas as pl
from jax.experimental.pallas import tpu as pltpu
from jax.sharding import Mesh, PartitionSpec as P

RANK = 8
SEQ_LEN = 64
AXES = ("zl", "y", "x", "zh", "core")
SIZES = (4, 4, 4, 2, 2)
DEPTH = 1024
VMEM_LIMIT = 20 << 20
SLOTS = 3


def ring(x, axis, step):
    n = SIZES[AXES.index(axis)]
    return lax.ppermute(x, axis, [(i, (i + step) % n) for i in range(n)])


def flip(x, axis, mask):
    n = SIZES[AXES.index(axis)]
    return lax.ppermute(x, axis, [(i, i ^ mask) for i in range(n)])


def flip_hid(x, mask):
    return lax.ppermute(x, ("zh", "core"), [(i, i ^ mask) for i in range(4)])


def project_kernel(blocks, grad_steps, place_ref, *refs):
    rows_refs = refs[:blocks]
    grads_ref, acts_ref, keep_ref, send_ref, total_ref, held_ref, sems = refs[blocks:]
    step, steps = pl.program_id(0), pl.num_programs(0)

    def copy(source, at):
        depth = held_ref.shape[2]
        start = at * depth
        if not isinstance(start, int):
            start = pl.multiple_of(start, depth)
        return source.at[:, pl.ds(start, depth)]

    def fetch(at):
        slot = lax.rem(at, SLOTS)

        @pl.when(at < grad_steps)
        def _():
            pltpu.make_async_copy(copy(grads_ref, at), held_ref.at[slot], sems.at[slot]).start()

        @pl.when(at >= grad_steps)
        def _():
            pltpu.make_async_copy(
                copy(acts_ref, at - grad_steps), held_ref.at[slot], sems.at[slot]
            ).start()

    @pl.when(step == 0)
    def _():
        total_ref[...] = jnp.zeros_like(total_ref)
        for at in range(SLOTS - 1):
            fetch(jnp.int32(at))

    @pl.when(step + SLOTS - 1 < steps)
    def _():
        fetch(step + SLOTS - 1)

    slot = lax.rem(step, SLOTS)
    pltpu.make_async_copy(copy(acts_ref, 0), held_ref.at[slot], sems.at[slot]).wait()
    rows = jnp.concatenate([r[...] for r in rows_refs], axis=0)
    part = jnp.where(step < grad_steps, 0, 1)
    total_ref[part] += lax.dot_general(
        rows, held_ref[slot], (((1,), (1,)), ((), ())), preferred_element_type=jnp.float32
    )

    @pl.when(step == steps - 1)
    def _():
        quarter = total_ref.shape[2] // 4
        zh, core = place_ref[0], place_ref[1]
        for to, ref in ((core, keep_ref), (1 - core, send_ref)):
            for other in range(2):
                at = (2 * to + (zh ^ other)) * quarter
                ref[other] = total_ref[:, :, pl.ds(pl.multiple_of(at, quarter), quarter)]


def project(blocks, grads, acts, place):
    tokens = grads.shape[0]
    grad_steps, act_steps = grads.shape[1] // DEPTH, acts.shape[1] // DEPTH
    rows = sum(b.shape[0] for b in blocks)
    half = jax.ShapeDtypeStruct((2, 2, rows, tokens // 4), jnp.float32)
    return pl.pallas_call(
        functools.partial(project_kernel, len(blocks), grad_steps),
        out_shape=(half, half),
        grid_spec=pltpu.PrefetchScalarGridSpec(
            num_scalar_prefetch=1,
            grid=(grad_steps + act_steps,),
            in_specs=[pl.BlockSpec((b.shape[0], DEPTH), lambda k, p: (0, k)) for b in blocks]
            + [pl.BlockSpec(memory_space=pltpu.HBM)] * 2,
            out_specs=(pl.BlockSpec(half.shape, lambda k, p: (0, 0, 0, 0)),) * 2,
            scratch_shapes=[
                pltpu.VMEM((2, rows, tokens), jnp.float32),
                pltpu.VMEM((SLOTS, tokens, DEPTH), jnp.bfloat16),
                pltpu.SemaphoreType.DMA((SLOTS,)),
            ],
        ),
        compiler_params=pltpu.CompilerParams(vmem_limit_bytes=VMEM_LIMIT),
        cost_estimate=pl.CostEstimate(flops=1 << 20, bytes_accessed=1 << 16, transcendentals=0),
    )(place, *blocks, grads, acts)


def pick_kernel(place_ref, sums1_ref, sums2_ref, kept_ref, got_ref, back_ref, out_ref):
    zh, core, zl, y, x = (place_ref[i] for i in range(5))
    total = kept_ref[0] + got_ref[0] + back_ref[...]
    product = total[0] * total[1]
    sums3 = product.reshape(-1, RANK, product.shape[-1]).sum(axis=1)
    sums = jnp.concatenate([sums1_ref[...], sums2_ref[...], sums3], axis=0)
    row = lax.broadcasted_iota(jnp.int32, (128, 128), 0)
    column = lax.broadcasted_iota(jnp.int32, (128, 128), 1)
    mask, query = row // 32, row % 32
    group = zl ^ (2 * zh + core) ^ mask
    colour = query % 2
    off_y, off_x = (query // 8 - y) & 3, ((query // 2) % 4 - x) & 3

    def place(off):
        return jnp.where(off == 3, 1, jnp.where(off == 0, 0, off + 1))

    first = place(jnp.where(colour == 0, off_y, off_x))
    second = place(jnp.where(colour == 0, off_x, off_y))
    inner = first * 3 + group - 1
    source = jnp.where(
        second == 0,
        32 + colour * 12,
        jnp.where(second == 3, 104 + colour * 12, 56 + colour * 24 + (second - 1) * 12),
    )
    source = jnp.where(group == 0, query, source + inner)
    out = jnp.dot(
        (source == column).astype(jnp.float32),
        sums,
        precision=lax.Precision.HIGHEST,
        preferred_element_type=jnp.float32,
    )
    for m in range(4):
        out_ref[m] = out[32 * m : 32 * m + 32]


def pick(place, sums1, sums2, kept, got, back):
    return pl.pallas_call(
        pick_kernel,
        out_shape=jax.ShapeDtypeStruct((4, 32, 128), jnp.float32),
        in_specs=[pl.BlockSpec(memory_space=pltpu.SMEM)] + [pl.BlockSpec(memory_space=pltpu.VMEM)] * 5,
        out_specs=pl.BlockSpec(memory_space=pltpu.VMEM),
        compiler_params=pltpu.CompilerParams(vmem_limit_bytes=4 << 20),
    )(place, sums1, sums2, kept, got, back)


def finish_kernel(place_ref, *refs):
    parts, out_ref = refs[:4], refs[4]
    zh, core = place_ref[0], place_ref[1]
    row = lax.broadcasted_iota(jnp.int32, (8, 128), 0)
    token = lax.broadcasted_iota(jnp.int32, (8, 128), 1)
    total = jnp.zeros(out_ref.shape, jnp.float32)
    for m, part in enumerate(parts):
        quarter = 2 * (core ^ (m & 1)) + (zh ^ (m >> 1))
        ones = (row == 2 * quarter + token // SEQ_LEN).astype(jnp.float32)
        total += lax.dot_general(
            ones,
            part[...],
            (((1,), (1,)), ((), ())),
            precision=lax.Precision.HIGHEST,
            preferred_element_type=jnp.float32,
        )
    out_ref[...] = total * (1.0 / math.sqrt(SEQ_LEN * RANK))


def finish(place, parts):
    return pl.pallas_call(
        finish_kernel,
        out_shape=jax.ShapeDtypeStruct((8, 32), jnp.float32),
        in_specs=[pl.BlockSpec(memory_space=pltpu.SMEM)] + [pl.BlockSpec(memory_space=pltpu.VMEM)] * 4,
        out_specs=pl.BlockSpec(memory_space=pltpu.VMEM),
        compiler_params=pltpu.CompilerParams(vmem_limit_bytes=4 << 20),
    )(place, *parts)


def shards(train_grads, train_acts, out_factors, in_factors):
    place = jnp.stack([lax.axis_index(a) for a in ("zh", "core", "zl", "y", "x")])
    own = jnp.concatenate([out_factors.T, in_factors.T], axis=1)
    features = own.shape[1]
    wide = 3 * RANK

    with jax.named_scope("own_columns"):
        near = lax.all_gather(own, ("y", "x"), axis=0, tiled=True)

    with jax.named_scope("z_shifts"):
        shifted = jnp.stack([flip(own, "zl", k) for k in (1, 2, 3)])

    def first(rows, axis):
        block = rows.reshape(wide, features)
        return jnp.concatenate([block] + [ring(block, axis, s) for s in (1, -1, 2)])

    def halves(before, after):
        half = before.shape[0] // 2
        return before[:half], after[half:]

    def exchange(sent):
        return lax.ppermute(sent, "zh", [(0, 1), (1, 0)])

    def over(send):
        return lax.ppermute(send, "core", [(0, 1), (1, 0)])

    def sums(keep, got, back):
        total = keep[0] + got[0] + back
        return (total[0] * total[1]).reshape(-1, RANK, total.shape[-1]).sum(axis=1)

    with jax.named_scope("first_axis"):
        col_a = first(shifted[:, :RANK], "y")
        col_b = first(shifted[:, RANK:], "x")
        col_a, col_b = lax.optimization_barrier((col_a, col_b))
    with jax.named_scope("second_axis"):
        next_a = ring(col_a, "x", 1), ring(col_a, "x", -1)
        next_b = ring(col_b, "y", 1), ring(col_b, "y", -1)
    with jax.named_scope("reduce"):
        keep1, send1 = project((near, col_a, col_b), train_grads, train_acts, place)
        got1 = over(send1)
        next_a, next_b, keep1 = lax.optimization_barrier((next_a, next_b, keep1))
    with jax.named_scope("second_axis"):
        half_a, half_b = lax.optimization_barrier((halves(*next_a), halves(*next_b)))
        far_a = ring(half_a[0], "x", 1), ring(half_a[1], "x", -1)
        far_b = ring(half_b[0], "y", 1), ring(half_b[1], "y", -1)
    with jax.named_scope("reduce"):
        sums1 = sums(keep1, got1, exchange(keep1[1] + got1[1]))
        keep2, send2 = project(next_a + next_b, train_grads, train_acts, place)
        got2 = over(send2)
        sent2 = keep2[1] + got2[1]
        back2 = exchange(sent2)
        far_a, far_b, sums1 = lax.optimization_barrier((far_a, far_b, sums1))
        keep3, send3 = project(far_a + far_b, train_grads, train_acts, place)
        got3 = over(send3)
        sums2 = sums(keep2, got2, back2)
        back3 = exchange(keep3[1] + got3[1])
    with jax.named_scope("order"):
        parts = pick(place, sums1, sums2, keep3, got3, back3)
        parts = [parts[0]] + [flip_hid(parts[m], m) for m in (1, 2, 3)]
        return finish(place, parts)


def solution(mesh):
    fine = Mesh(mesh.devices.reshape(SIZES), AXES)
    tok, hid = ("zl", "y", "x"), ("zh", "core")
    return jax.shard_map(
        shards,
        mesh=fine,
        in_specs=(P(tok, hid), P(tok, hid), P(hid, tok), P(hid, tok)),
        out_specs=P(tok, hid),
        check_vma=False,
    )
```

time: 936 us -> 212 us (0.23)
  waiting for transfers between devices: 896 us -> 99 us
  starting transfers between devices: 0.08 us -> 51.7 us
  Pallas kernels: 0 us -> 31.2 us
  matrix products: 20 us -> 0 us
    all_gather x2 -> x1, waiting for transfers between devices: 654 us -> 6.44 us  [shards(): near = lax.all_gather(own, ('y', 'x'), axis=0, tiled=True)]
    psum x1 -> x0, waiting for transfers between devices: 241 us -> none  [shards(): grad_full, act_full = lax.psum((grad_piece, act_piece), 'hid')]
    ppermute x0 -> x26, waiting for transfers between devices: none -> 92.5 us  [the longest x14 41.5 us: ring(): return lax.ppermute(x, axis, [(i, (i + step) % n) for i in range(n)])]
    ppermute x0 -> x26, starting transfers between devices: none -> 51.7 us  [the longest x14 21.2 us: ring(): return lax.ppermute(x, axis, [(i, (i + step) % n) for i in range(n)])]
    pallas_call x0 -> x5, Pallas kernels: none -> 31.2 us  [the longest x3 28.9 us: project(): pl.pallas_call(functools.partial(project_kernel, len(blocks), grad_steps)...]
    dot_general x2 -> x0, matrix products: 20 us -> none  [the longest x1 14.2 us: shards(): jnp.dot(train_grads, lax.all_gather(out_factors, 'tok', axis=1, tiled=Tru...]
  transfers between devices with their start and end apart: 3 -> 27, of which waited for: 3 -> 13; matrix products, arithmetic and copies ran while one was open for 1% -> 4% of each run, Pallas kernels for 0% -> 14%
where the time goes in v1:
time: 212 us; the launch traced here: 211 us
  waiting for transfers between devices  99 us (47%)
  starting transfers between devices  51.7 us (24%)
  Pallas kernels  31.2 us (15%)
  between operations  13.6 us (6%)
  local copies, waits for them, and re-layouts  10.5 us (5%)
  other arithmetic  4.91 us (2%)
    ppermute x14, waiting for transfers between devices, ring(): return lax.ppermute(x, axis, [(i, (i + step) % n) for i in range(n)])  41.5 us
    pallas_call x3, Pallas kernels, project(): pl.pallas_call(functools.partial(project_kernel, len(blocks), grad_steps)...  28.9 us
    ppermute x3, waiting for transfers between devices, exchange(): return lax.ppermute(sent, 'zh', [(0, 1), (1, 0)])  25.8 us
    ppermute x3, waiting for transfers between devices, flip(): return lax.ppermute(x, axis, [(i, i ^ mask) for i in range(n)])  22.4 us
    ppermute x14, starting transfers between devices, ring(): return lax.ppermute(x, axis, [(i, (i + step) % n) for i in range(n)])  21.2 us
    ppermute x3, starting transfers between devices, exchange(): return lax.ppermute(sent, 'zh', [(0, 1), (1, 0)])  10.1 us
    ppermute x3, starting transfers between devices, over(): return lax.ppermute(send, 'core', [(0, 1), (1, 0)])  9.99 us
    all_gather x1, waiting for transfers between devices, shards(): near = lax.all_gather(own, ('y', 'x'), axis=0, tiled=True)  6.44 us
  transfers between devices with their start and end apart: 27, of which 13 were waited for; matrix products, arithmetic and copies ran while one was open for 4% of the time, Pallas kernels for 14%

profile of v1, /device:TPU:33, one launch (start us, length us, event | category | flops | bytes accessed | tf_op | source)
XLA Modules:
  0.0 210.9 jit_solution(14979628245796386970)
XLA Ops:
  6.5 1.7 pad_maximum_fusion.3
  8.3 0.0 all-gather.2.cloned.1.call-update
  8.3 1.7 collective-permute-start.2
  10.0 1.5 collective-permute-start.1
  11.5 1.1 collective-permute-start
  12.5 17.0 %collective-permute-done.2 = bf16[16,9216]{1,0:T(8,128)(2,1)S(1)} collective-permute-done((bf16[16,9216]{1,0:T(8,128)(2,1)}, bf16[16,9216]{1,0:T(8,128)(2,1)S(1)}, u32[]{:S(2)}, u32[]{:S(2)}) %collective-permute-start.2) | collective-permute-done | bytes 294944 | tf_op jit(solution)/shard_map/z_shifts/ppermute | solution.py:27
  29.6 5.4 %collective-permute-done.1 = bf16[16,9216]{1,0:T(8,128)(2,1)S(1)} collective-permute-done((bf16[16,9216]{1,0:T(8,128)(2,1)}, bf16[16,9216]{1,0:T(8,128)(2,1)S(1)}, u32[]{:S(2)}, u32[]{:S(2)}) %collective-permute-start.1) | collective-permute-done | bytes 294944 | tf_op jit(solution)/shard_map/z_shifts/ppermute | solution.py:27
  35.0 0.1 pad_maximum_fusion.2
  35.1 0.1 slice_bitcast_fusion
  35.1 2.8 %collective-permute-start.8 = (bf16[24,9216]{1,0:T(8,128)(2,1)S(1)}, bf16[24,9216]{1,0:T(8,128)(2,1)S(1)}, u32[]{:S(2)}, u32[]{:S(2)}) collective-permute-start(bf16[24,9216]{1,0:T(8,128)(2,1)S(1)} %get-tuple-element.49), channel_id=1, source_target_pairs={{0,8},{4,12},{8,0},{12,4},{1,9},{5,13},{9,1},{13,5},{2,10},{6,14},... | collective-permute-start | bytes 1327112 | tf_op jit(solution)/shard_map/first_axis/ppermute | solution.py:22
  38.0 0.9 collective-permute-start.7
  38.8 0.6 collective-permute-start.6
  39.4 2.9 %collective-permute-start.5 = (bf16[24,9216]{1,0:T(8,128)(2,1)S(1)}, bf16[24,9216]{1,0:T(8,128)(2,1)S(1)}, u32[]{:S(2)}, u32[]{:S(2)}) collective-permute-start(bf16[24,9216]{1,0:T(8,128)(2,1)S(1)} %get-tuple-element.50), channel_id=1, source_target_pairs={{0,32},{16,48},{32,0},{48,16},{1,33},{17,49},{33,1},{49,17},{2,34}... | collective-permute-start | bytes 1327112 | tf_op jit(solution)/shard_map/first_axis/ppermute | solution.py:22
  42.3 0.8 collective-permute-start.4
  43.1 3.8 %collective-permute-done.8 = bf16[24,9216]{1,0:T(8,128)(2,1)S(1)} collective-permute-done((bf16[24,9216]{1,0:T(8,128)(2,1)S(1)}, bf16[24,9216]{1,0:T(8,128)(2,1)S(1)}, u32[]{:S(2)}, u32[]{:S(2)}) %collective-permute-start.8) | collective-permute-done | bytes 442400 | tf_op jit(solution)/shard_map/first_axis/ppermute | solution.py:22
  46.9 1.3 collective-permute-start.3
  48.2 16.8 %collective-permute-done.7 = bf16[24,9216]{1,0:T(8,128)(2,1)S(1)} collective-permute-done((bf16[24,9216]{1,0:T(8,128)(2,1)S(1)}, bf16[24,9216]{1,0:T(8,128)(2,1)S(1)}, u32[]{:S(2)}, u32[]{:S(2)}) %collective-permute-start.7) | collective-permute-done | bytes 442400 | tf_op jit(solution)/shard_map/first_axis/ppermute | solution.py:22
  65.0 0.0 collective-permute-done.6
  65.0 1.4 pad_maximum_fusion.1.refs_2_
  66.4 0.0 collective-permute-done.5
  66.4 4.7 %collective-permute-done.4 = bf16[24,9216]{1,0:T(8,128)(2,1)S(1)} collective-permute-done((bf16[24,9216]{1,0:T(8,128)(2,1)S(1)}, bf16[24,9216]{1,0:T(8,128)(2,1)S(1)}, u32[]{:S(2)}, u32[]{:S(2)}) %collective-permute-start.4) | collective-permute-done | bytes 442400 | tf_op jit(solution)/shard_map/first_axis/ppermute | solution.py:22
  71.1 1.3 pad_maximum_fusion.refs_1_
  72.4 2.1 collective-permute-start.10
  74.5 0.0 collective-permute-start.9
  74.5 3.5 %collective-permute-start.12 = (bf16[96,9216]{1,0:T(8,128)(2,1)}, bf16[96,9216]{1,0:T(8,128)(2,1)}, u32[]{:S(2)}, u32[]{:S(2)}) collective-permute-start(bf16[96,9216]{1,0:T(8,128)(2,1)} %pad_maximum_fusion.1.refs_2_), channel_id=1, source_target_pairs={{0,48},{16,0},{32,16},{48,32},{1,49},{17,1},{33,17},{49,33},{2,50}... | collective-permute-start | bytes 5308424 | tf_op jit(solution)/shard_map/second_axis/ppermute | solution.py:22
  78.0 0.0 collective-permute-start.11
  78.0 0.1 stack.35.place_ref
  78.1 6.4 %all-gather.2.cloned.1.call-done.refs_0_ = bf16[256,9216]{1,0:T(8,128)(2,1)} async-done(((bf16[16,9216]{1,0:T(8,128)(2,1)}), bf16[256,9216]{1,0:T(8,128)(2,1)}) %all-gather.2.cloned.1.call-update) | async-done | bytes 4718608 | tf_op jit(solution)/shard_map/own_columns/all_gather | solution.py:193
  84.6 3.1 %copy-done = bf16[512,7168]{1,0:T(8,128)(2,1)S(1)} copy-done((bf16[512,7168]{1,0:T(8,128)(2,1)S(1)}, bf16[512,7168]{1,0:T(8,128)(2,1)}, u32[]{:S(2)}) %copy-start) | copy-done | bytes 7340056
  87.7 2.3 %copy-done.3 = bf16[256,9216]{1,0:T(8,128)(2,1)S(1)} copy-done((bf16[256,9216]{1,0:T(8,128)(2,1)S(1)}, bf16[256,9216]{1,0:T(8,128)(2,1)}, u32[]{:S(2)}) %copy-start.3) | copy-done | bytes 4718616
  90.0 10.6 %reduce.3 = (f32[2,2,448,128]{3,2,1,0:T(8,128)S(1)}, f32[2,2,448,128]{3,2,1,0:T(8,128)S(1)}) custom-call(s32[5]{0:T(128)S(1)} %stack.35.place_ref, bf16[256,9216]{1,0:T(8,128)(2,1)S(1)} %copy-done.3, bf16[96,9216]{1,0:T(8,128)(2,1)} %pad_maximum_fusion.refs_1_, bf16[96,9216]{1,0:T(8,128)(2,1)} %pad_maximum_fusion.1.refs_2_, bf16[512,7168]{1,0:T(8,128)(2,1)S(1)} %copy-done, ...), custom_call_target="tpu_custom_call" | custom-call | flops 1048576 | bytes 65536 | tf_op jit(solution)/shard_map/reduce/pallas_call | solution.py:92
  100.6 0.5 collective-permute-start.17
  101.2 10.8 %collective-permute-done.10.refs_1_ = bf16[96,9216]{1,0:T(8,128)(2,1)} collective-permute-done((bf16[96,9216]{1,0:T(8,128)(2,1)}, bf16[96,9216]{1,0:T(8,128)(2,1)}, u32[]{:S(2)}, u32[]{:S(2)}) %collective-permute-start.10) | collective-permute-done | bytes 1769504 | tf_op jit(solution)/shard_map/second_axis/ppermute | solution.py:22
  112.0 0.6 collective-permute-done.9.refs_0_
  112.6 4.7 %collective-permute-done.12.refs_3_ = bf16[96,9216]{1,0:T(8,128)(2,1)} collective-permute-done((bf16[96,9216]{1,0:T(8,128)(2,1)}, bf16[96,9216]{1,0:T(8,128)(2,1)}, u32[]{:S(2)}, u32[]{:S(2)}) %collective-permute-start.12) | collective-permute-done | bytes 1769504 | tf_op jit(solution)/shard_map/second_axis/ppermute | solution.py:22
  117.3 0.0 collective-permute-done.17
  117.4 4.6 %collective-permute-start.18 = (f32[2,448,128]{2,1,0:T(8,128)S(1)}, f32[2,448,128]{2,1,0:T(8,128)S(1)}, u32[]{:S(2)}, u32[]{:S(2)}) collective-permute-start(f32[2,448,128]{2,1,0:T(8,128)S(1)} %fusion), channel_id=1, source_target_pairs={{0,2},{2,0},{1,3},{3,1},{4,6},{6,4},{5,7},{7,5},{8,10},{10,8},{9,1... | collective-permute-start | bytes 1376264 | tf_op jit(solution)/shard_map/reduce/ppermute | solution.py:207
  122.0 1.2 slice.74
  123.2 1.2 slice.77
  124.4 1.2 slice.76
  125.6 1.2 slice.75
  126.9 1.2 collective-permute-start.13
  128.0 1.8 collective-permute-start.14
  129.8 0.0 collective-permute-start.15
  129.8 3.4 %collective-permute-start.16 = (bf16[48,9216]{1,0:T(8,128)(2,1)S(1)}, bf16[48,9216]{1,0:T(8,128)(2,1)S(1)}, u32[]{:S(2)}, u32[]{:S(2)}) collective-permute-start(bf16[48,9216]{1,0:T(8,128)(2,1)S(1)} %slice.77), channel_id=1, source_target_pairs={{0,48},{16,0},{32,16},{48,32},{1,49},{17,1},{33,17},{49,33},{2,50}... | collective-permute-start | bytes 2654216 | tf_op jit(solution)/shard_map/second_axis/ppermute | solution.py:22
  133.2 11.0 %reduce.4 = (f32[2,2,384,128]{3,2,1,0:T(8,128)S(1)}, f32[2,2,384,128]{3,2,1,0:T(8,128)S(1)}) custom-call(s32[5]{0:T(128)S(1)} %stack.35.place_ref, bf16[96,9216]{1,0:T(8,128)(2,1)} %collective-permute-done.9.refs_0_, bf16[96,9216]{1,0:T(8,128)(2,1)} %collective-permute-done.10.refs_1_, bf16[96,9216]{1,0:T(8,128)(2,1)} %collective-permute-done.11.refs_2_, ...), custom_call_target="tpu_custom_call" | custom-call | flops 1048576 | bytes 65536 | tf_op jit(solution)/shard_map/reduce/pallas_call | solution.py:92
  144.3 4.5 %collective-permute-start.19 = (f32[2,2,384,128]{3,2,1,0:T(8,128)S(1)}, f32[2,2,384,128]{3,2,1,0:T(8,128)S(1)}, u32[]{:S(2)}, u32[]{:S(2)}) collective-permute-start(f32[2,2,384,128]{3,2,1,0:T(8,128)S(1)} %get-tuple-element.42), channel_id=1, source_target_pairs={{0,1},{1,0},{2,3},{3,2},{4,5},{5,4},{6,7},{7,6},{8,9},{9,8},{10,11... | collective-permute-start | bytes 2359304 | tf_op jit(solution)/shard_map/reduce/ppermute | solution.py:210
  148.8 0.1 fusion.2
  148.9 0.1 fusion.7.sums1_ref
  149.0 7.3 %reduce.5 = (f32[2,2,192,128]{3,2,1,0:T(8,128)S(1)}, f32[2,2,192,128]{3,2,1,0:T(8,128)S(1)}) custom-call(s32[5]{0:T(128)S(1)} %stack.35.place_ref, bf16[48,9216]{1,0:T(8,128)(2,1)S(1)} %collective-permute-done.13.refs_0_, bf16[48,9216]{1,0:T(8,128)(2,1)S(1)} %collective-permute-done.14.refs_1_, bf16[48,9216]{1,0:T(8,128)(2,1)S(1)} %collective-permute-done.15.refs_2_, ...), custom_call_target="tpu_custom_call" | custom-call | flops 1048576 | bytes 65536 | tf_op jit(solution)/shard_map/reduce/pallas_call | solution.py:92
  156.3 4.9 %collective-permute-start.21 = (f32[2,2,192,128]{3,2,1,0:T(8,128)S(1)}, f32[2,2,192,128]{3,2,1,0:T(8,128)S(1)}, u32[]{:S(2)}, u32[]{:S(2)}) collective-permute-start(f32[2,2,192,128]{3,2,1,0:T(8,128)S(1)} %get-tuple-element.48), channel_id=1, source_target_pairs={{0,1},{1,0},{2,3},{3,2},{4,5},{5,4},{6,7},{7,6},{8,9},{9,8},{10,11... | collective-permute-start | bytes 1179656 | tf_op jit(solution)/shard_map/reduce/ppermute | solution.py:210
  161.3 1.4 collective-permute-start.20
  162.7 4.1 %collective-permute-start.22 = (f32[2,192,128]{2,1,0:T(8,128)S(1)}, f32[2,192,128]{2,1,0:T(8,128)S(1)}, u32[]{:S(2)}, u32[]{:S(2)}) collective-permute-start(f32[2,192,128]{2,1,0:T(8,128)S(1)} %fusion.8), channel_id=1, source_target_pairs={{0,2},{2,0},{1,3},{3,1},{4,6},{6,4},{5,7},{7,5},{8,10},{10,8},{9,1... | collective-permute-start | bytes 589832 | tf_op jit(solution)/shard_map/reduce/ppermute | solution.py:207
  166.8 21.7 %collective-permute-done.20 = f32[2,384,128]{2,1,0:T(8,128)S(1)} collective-permute-done((f32[2,384,128]{2,1,0:T(8,128)S(1)}, f32[2,384,128]{2,1,0:T(8,128)S(1)}, u32[]{:S(2)}, u32[]{:S(2)}) %collective-permute-start.20) | collective-permute-done | bytes 393248 | tf_op jit(solution)/shard_map/reduce/ppermute | solution.py:207
  188.6 0.1 fusion.5
  188.6 0.1 fusion.10.sums2_ref
  188.7 4.1 %collective-permute-done.22.back_ref = f32[2,192,128]{2,1,0:T(8,128)S(1)} collective-permute-done((f32[2,192,128]{2,1,0:T(8,128)S(1)}, f32[2,192,128]{2,1,0:T(8,128)S(1)}, u32[]{:S(2)}, u32[]{:S(2)}) %collective-permute-start.22) | collective-permute-done | bytes 196640 | tf_op jit(solution)/shard_map/reduce/ppermute | solution.py:207
  192.8 0.9 order.2
  193.7 2.2 %collective-permute-start.25 = (f32[32,128]{1,0:T(8,128)S(1)}, f32[32,128]{1,0:T(8,128)S(1)}, u32[]{:S(2)}, u32[]{:S(2)}) collective-permute-start(f32[32,128]{1,0:T(8,128)S(1)} %get-tuple-element.51), channel_id=1, source_target_pairs={{0,3},{1,2},{2,1},{3,0},{4,7},{5,6},{6,5},{7,4},{8,11},{9,10},{10,... | collective-permute-start | bytes 49160 | tf_op jit(solution)/shard_map/order/ppermute | solution.py:31
  195.9 3.7 %collective-permute-start.24 = (f32[32,128]{1,0:T(8,128)S(1)}, f32[32,128]{1,0:T(8,128)S(1)}, u32[]{:S(2)}, u32[]{:S(2)}) collective-permute-start(f32[32,128]{1,0:T(8,128)S(1)} %get-tuple-element.52), channel_id=1, source_target_pairs={{0,2},{1,3},{2,0},{3,1},{4,6},{5,7},{6,4},{7,5},{8,10},{9,11},{10,... | collective-permute-start | bytes 49160 | tf_op jit(solution)/shard_map/order/ppermute | solution.py:31
  199.6 0.3 collective-permute-start.23
  199.8 1.2 collective-permute-done.25.refs_3_
  201.0 1.7 collective-permute-done.24.refs_2_
  202.7 1.4 order.3
  (22 shorter events, 0.2 us)
Async XLA Ops:
  6.5 78.0 %all-gather.2.cloned.1.call-start = ((), (), s32[]{:S(2)}) async-start(), calls=%async_computation | async-start | bytes 5013504 | tf_op jit(solution)/shard_map/own_columns/all_gather | solution.py:193
  8.3 21.3 %collective-permute-start.2 = (bf16[16,9216]{1,0:T(8,128)(2,1)}, bf16[16,9216]{1,0:T(8,128)(2,1)S(1)}, u32[]{:S(2)}, u32[]{:S(2)}) collective-permute-start(bf16[16,9216]{1,0:T(8,128)(2,1)} %pad_maximum_fusion.3), channel_id=1, source_target_pairs={{0,192},{64,128},{128,64},{192,0},{1,193},{65,129},{129,65},{193,1... | collective-permute-start | bytes 884744 | tf_op jit(solution)/shard_map/z_shifts/ppermute | solution.py:27
  10.0 25.0 %collective-permute-start.1 = (bf16[16,9216]{1,0:T(8,128)(2,1)}, bf16[16,9216]{1,0:T(8,128)(2,1)S(1)}, u32[]{:S(2)}, u32[]{:S(2)}) collective-permute-start(bf16[16,9216]{1,0:T(8,128)(2,1)} %pad_maximum_fusion.3), channel_id=1, source_target_pairs={{0,128},{64,192},{128,0},{192,64},{1,129},{65,193},{129,1},{193,65... | collective-permute-start | bytes 884744 | tf_op jit(solution)/shard_map/z_shifts/ppermute | solution.py:27
  11.5 23.5 %collective-permute-start = (bf16[16,9216]{1,0:T(8,128)(2,1)}, bf16[16,9216]{1,0:T(8,128)(2,1)S(1)}, u32[]{:S(2)}, u32[]{:S(2)}) collective-permute-start(bf16[16,9216]{1,0:T(8,128)(2,1)} %pad_maximum_fusion.3), channel_id=1, source_target_pairs={{0,64},{64,0},{128,192},{192,128},{1,65},{65,1},{129,193},{193,129... | collective-permute-start | bytes 884744 | tf_op jit(solution)/shard_map/z_shifts/ppermute | solution.py:27
  35.1 11.7 %collective-permute-start.8 = (bf16[24,9216]{1,0:T(8,128)(2,1)S(1)}, bf16[24,9216]{1,0:T(8,128)(2,1)S(1)}, u32[]{:S(2)}, u32[]{:S(2)}) collective-permute-start(bf16[24,9216]{1,0:T(8,128)(2,1)S(1)} %get-tuple-element.49), channel_id=1, source_target_pairs={{0,8},{4,12},{8,0},{12,4},{1,9},{5,13},{9,1},{13,5},{2,10},{6,14},... | collective-permute-start | bytes 1327112 | tf_op jit(solution)/shard_map/first_axis/ppermute | solution.py:22
  38.0 27.0 %collective-permute-start.7 = (bf16[24,9216]{1,0:T(8,128)(2,1)S(1)}, bf16[24,9216]{1,0:T(8,128)(2,1)S(1)}, u32[]{:S(2)}, u32[]{:S(2)}) collective-permute-start(bf16[24,9216]{1,0:T(8,128)(2,1)S(1)} %get-tuple-element.49), channel_id=1, source_target_pairs={{0,12},{4,0},{8,4},{12,8},{1,13},{5,1},{9,5},{13,9},{2,14},{6,2},{... | collective-permute-start | bytes 1327112 | tf_op jit(solution)/shard_map/first_axis/ppermute | solution.py:22
  38.8 26.2 %collective-permute-start.6 = (bf16[24,9216]{1,0:T(8,128)(2,1)S(1)}, bf16[24,9216]{1,0:T(8,128)(2,1)S(1)}, u32[]{:S(2)}, u32[]{:S(2)}) collective-permute-start(bf16[24,9216]{1,0:T(8,128)(2,1)S(1)} %get-tuple-element.49), channel_id=1, source_target_pairs={{0,4},{4,8},{8,12},{12,0},{1,5},{5,9},{9,13},{13,1},{2,6},{6,10},{... | collective-permute-start | bytes 1327112 | tf_op jit(solution)/shard_map/first_axis/ppermute | solution.py:22
  39.4 27.0 %collective-permute-start.5 = (bf16[24,9216]{1,0:T(8,128)(2,1)S(1)}, bf16[24,9216]{1,0:T(8,128)(2,1)S(1)}, u32[]{:S(2)}, u32[]{:S(2)}) collective-permute-start(bf16[24,9216]{1,0:T(8,128)(2,1)S(1)} %get-tuple-element.50), channel_id=1, source_target_pairs={{0,32},{16,48},{32,0},{48,16},{1,33},{17,49},{33,1},{49,17},{2,34}... | collective-permute-start | bytes 1327112 | tf_op jit(solution)/shard_map/first_axis/ppermute | solution.py:22
  42.3 28.8 %collective-permute-start.4 = (bf16[24,9216]{1,0:T(8,128)(2,1)S(1)}, bf16[24,9216]{1,0:T(8,128)(2,1)S(1)}, u32[]{:S(2)}, u32[]{:S(2)}) collective-permute-start(bf16[24,9216]{1,0:T(8,128)(2,1)S(1)} %get-tuple-element.50), channel_id=1, source_target_pairs={{0,48},{16,0},{32,16},{48,32},{1,49},{17,1},{33,17},{49,33},{2,50}... | collective-permute-start | bytes 1327112 | tf_op jit(solution)/shard_map/first_axis/ppermute | solution.py:22
  46.9 24.2 %collective-permute-start.3 = (bf16[24,9216]{1,0:T(8,128)(2,1)S(1)}, bf16[24,9216]{1,0:T(8,128)(2,1)S(1)}, u32[]{:S(2)}, u32[]{:S(2)}) collective-permute-start(bf16[24,9216]{1,0:T(8,128)(2,1)S(1)} %get-tuple-element.50), channel_id=1, source_target_pairs={{0,16},{16,32},{32,48},{48,0},{1,17},{17,33},{33,49},{49,1},{2,18}... | collective-permute-start | bytes 1327112 | tf_op jit(solution)/shard_map/first_axis/ppermute | solution.py:22
  66.4 18.2 %copy-start.2 = (bf16[512,2048]{1,0:T(8,128)(2,1)S(1)}, bf16[512,2048]{1,0:T(8,128)(2,1)}, u32[]{:S(2)}) copy-start(bf16[512,2048]{1,0:T(8,128)(2,1)} %refs_5_.3) | copy-start | bytes 6291460
  72.4 39.6 %collective-permute-start.10 = (bf16[96,9216]{1,0:T(8,128)(2,1)}, bf16[96,9216]{1,0:T(8,128)(2,1)}, u32[]{:S(2)}, u32[]{:S(2)}) collective-permute-start(bf16[96,9216]{1,0:T(8,128)(2,1)} %pad_maximum_fusion.refs_1_), channel_id=1, source_target_pairs={{0,12},{4,0},{8,4},{12,8},{1,13},{5,1},{9,5},{13,9},{2,14},{6,2},{... | collective-permute-start | bytes 5308424 | tf_op jit(solution)/shard_map/second_axis/ppermute | solution.py:22
  74.5 38.1 %collective-permute-start.9 = (bf16[96,9216]{1,0:T(8,128)(2,1)}, bf16[96,9216]{1,0:T(8,128)(2,1)}, u32[]{:S(2)}, u32[]{:S(2)}) collective-permute-start(bf16[96,9216]{1,0:T(8,128)(2,1)} %pad_maximum_fusion.refs_1_), channel_id=1, source_target_pairs={{0,4},{4,8},{8,12},{12,0},{1,5},{5,9},{9,13},{13,1},{2,6},{6,10},{... | collective-permute-start | bytes 5308424 | tf_op jit(solution)/shard_map/second_axis/ppermute | solution.py:22
  74.5 42.8 %collective-permute-start.12 = (bf16[96,9216]{1,0:T(8,128)(2,1)}, bf16[96,9216]{1,0:T(8,128)(2,1)}, u32[]{:S(2)}, u32[]{:S(2)}) collective-permute-start(bf16[96,9216]{1,0:T(8,128)(2,1)} %pad_maximum_fusion.1.refs_2_), channel_id=1, source_target_pairs={{0,48},{16,0},{32,16},{48,32},{1,49},{17,1},{33,17},{49,33},{2,50}... | collective-permute-start | bytes 5308424 | tf_op jit(solution)/shard_map/second_axis/ppermute | solution.py:22
  78.0 39.3 %collective-permute-start.11 = (bf16[96,9216]{1,0:T(8,128)(2,1)}, bf16[96,9216]{1,0:T(8,128)(2,1)}, u32[]{:S(2)}, u32[]{:S(2)}) collective-permute-start(bf16[96,9216]{1,0:T(8,128)(2,1)} %pad_maximum_fusion.1.refs_2_), channel_id=1, source_target_pairs={{0,16},{16,32},{32,48},{48,0},{1,17},{17,33},{33,49},{49,1},{2,18}... | collective-permute-start | bytes 5308424 | tf_op jit(solution)/shard_map/second_axis/ppermute | solution.py:22
  84.6 3.1 %copy-start = (bf16[512,7168]{1,0:T(8,128)(2,1)S(1)}, bf16[512,7168]{1,0:T(8,128)(2,1)}, u32[]{:S(2)}) copy-start(bf16[512,7168]{1,0:T(8,128)(2,1)} %refs_4_.5) | copy-start | bytes 22020100
  87.7 2.3 %copy-start.3 = (bf16[256,9216]{1,0:T(8,128)(2,1)S(1)}, bf16[256,9216]{1,0:T(8,128)(2,1)}, u32[]{:S(2)}) copy-start(bf16[256,9216]{1,0:T(8,128)(2,1)} %all-gather.2.cloned.1.call-done.refs_0_) | copy-start | bytes 14155780
  100.6 16.7 %collective-permute-start.17 = (f32[2,2,448,128]{3,2,1,0:T(8,128)S(1)}, f32[2,2,448,128]{3,2,1,0:T(8,128)S(1)}, u32[]{:S(2)}, u32[]{:S(2)}) collective-permute-start(f32[2,2,448,128]{3,2,1,0:T(8,128)S(1)} %get-tuple-element.39), channel_id=1, source_target_pairs={{0,1},{1,0},{2,3},{3,2},{4,5},{5,4},{6,7},{7,6},{8,9},{9,8},{10,11... | collective-permute-start | bytes 2752520 | tf_op jit(solution)/shard_map/reduce/ppermute | solution.py:210
  117.3 15.9 %copy-start.1 = (bf16[512,7168]{1,0:T(8,128)(2,1)S(1)}, bf16[512,7168]{1,0:T(8,128)(2,1)}, u32[]{:S(2)}) copy-start(bf16[512,7168]{1,0:T(8,128)(2,1)} %refs_4_.5) | copy-start | bytes 22020100
  117.4 26.9 %collective-permute-start.18 = (f32[2,448,128]{2,1,0:T(8,128)S(1)}, f32[2,448,128]{2,1,0:T(8,128)S(1)}, u32[]{:S(2)}, u32[]{:S(2)}) collective-permute-start(f32[2,448,128]{2,1,0:T(8,128)S(1)} %fusion), channel_id=1, source_target_pairs={{0,2},{2,0},{1,3},{3,1},{4,6},{6,4},{5,7},{7,5},{8,10},{10,8},{9,1... | collective-permute-start | bytes 1376264 | tf_op jit(solution)/shard_map/reduce/ppermute | solution.py:207
  126.9 22.1 %collective-permute-start.13 = (bf16[48,9216]{1,0:T(8,128)(2,1)S(1)}, bf16[48,9216]{1,0:T(8,128)(2,1)S(1)}, u32[]{:S(2)}, u32[]{:S(2)}) collective-permute-start(bf16[48,9216]{1,0:T(8,128)(2,1)S(1)} %slice.74), channel_id=1, source_target_pairs={{0,4},{4,8},{8,12},{12,0},{1,5},{5,9},{9,13},{13,1},{2,6},{6,10},{... | collective-permute-start | bytes 2654216 | tf_op jit(solution)/shard_map/second_axis/ppermute | solution.py:22
  128.0 20.9 %collective-permute-start.14 = (bf16[48,9216]{1,0:T(8,128)(2,1)S(1)}, bf16[48,9216]{1,0:T(8,128)(2,1)S(1)}, u32[]{:S(2)}, u32[]{:S(2)}) collective-permute-start(bf16[48,9216]{1,0:T(8,128)(2,1)S(1)} %slice.75), channel_id=1, source_target_pairs={{0,12},{4,0},{8,4},{12,8},{1,13},{5,1},{9,5},{13,9},{2,14},{6,2},{... | collective-permute-start | bytes 2654216 | tf_op jit(solution)/shard_map/second_axis/ppermute | solution.py:22
  129.8 19.2 %collective-permute-start.15 = (bf16[48,9216]{1,0:T(8,128)(2,1)S(1)}, bf16[48,9216]{1,0:T(8,128)(2,1)S(1)}, u32[]{:S(2)}, u32[]{:S(2)}) collective-permute-start(bf16[48,9216]{1,0:T(8,128)(2,1)S(1)} %slice.76), channel_id=1, source_target_pairs={{0,16},{16,32},{32,48},{48,0},{1,17},{17,33},{33,49},{49,1},{2,18}... | collective-permute-start | bytes 2654216 | tf_op jit(solution)/shard_map/second_axis/ppermute | solution.py:22
  129.8 19.2 %collective-permute-start.16 = (bf16[48,9216]{1,0:T(8,128)(2,1)S(1)}, bf16[48,9216]{1,0:T(8,128)(2,1)S(1)}, u32[]{:S(2)}, u32[]{:S(2)}) collective-permute-start(bf16[48,9216]{1,0:T(8,128)(2,1)S(1)} %slice.77), channel_id=1, source_target_pairs={{0,48},{16,0},{32,16},{48,32},{1,49},{17,1},{33,17},{49,33},{2,50}... | collective-permute-start | bytes 2654216 | tf_op jit(solution)/shard_map/second_axis/ppermute | solution.py:22
  144.3 16.9 %collective-permute-start.19 = (f32[2,2,384,128]{3,2,1,0:T(8,128)S(1)}, f32[2,2,384,128]{3,2,1,0:T(8,128)S(1)}, u32[]{:S(2)}, u32[]{:S(2)}) collective-permute-start(f32[2,2,384,128]{3,2,1,0:T(8,128)S(1)} %get-tuple-element.42), channel_id=1, source_target_pairs={{0,1},{1,0},{2,3},{3,2},{4,5},{5,4},{6,7},{7,6},{8,9},{9,8},{10,11... | collective-permute-start | bytes 2359304 | tf_op jit(solution)/shard_map/reduce/ppermute | solution.py:210
  156.3 6.4 %collective-permute-start.21 = (f32[2,2,192,128]{3,2,1,0:T(8,128)S(1)}, f32[2,2,192,128]{3,2,1,0:T(8,128)S(1)}, u32[]{:S(2)}, u32[]{:S(2)}) collective-permute-start(f32[2,2,192,128]{3,2,1,0:T(8,128)S(1)} %get-tuple-element.48), channel_id=1, source_target_pairs={{0,1},{1,0},{2,3},{3,2},{4,5},{5,4},{6,7},{7,6},{8,9},{9,8},{10,11... | collective-permute-start | bytes 1179656 | tf_op jit(solution)/shard_map/reduce/ppermute | solution.py:210
  161.3 27.3 %collective-permute-start.20 = (f32[2,384,128]{2,1,0:T(8,128)S(1)}, f32[2,384,128]{2,1,0:T(8,128)S(1)}, u32[]{:S(2)}, u32[]{:S(2)}) collective-permute-start(f32[2,384,128]{2,1,0:T(8,128)S(1)} %fusion.3), channel_id=1, source_target_pairs={{0,2},{2,0},{1,3},{3,1},{4,6},{6,4},{5,7},{7,5},{8,10},{10,8},{9,1... | collective-permute-start | bytes 1179656 | tf_op jit(solution)/shard_map/reduce/ppermute | solution.py:207
  162.7 30.1 %collective-permute-start.22 = (f32[2,192,128]{2,1,0:T(8,128)S(1)}, f32[2,192,128]{2,1,0:T(8,128)S(1)}, u32[]{:S(2)}, u32[]{:S(2)}) collective-permute-start(f32[2,192,128]{2,1,0:T(8,128)S(1)} %fusion.8), channel_id=1, source_target_pairs={{0,2},{2,0},{1,3},{3,1},{4,6},{6,4},{5,7},{7,5},{8,10},{10,8},{9,1... | collective-permute-start | bytes 589832 | tf_op jit(solution)/shard_map/reduce/ppermute | solution.py:207
  193.7 7.3 %collective-permute-start.25 = (f32[32,128]{1,0:T(8,128)S(1)}, f32[32,128]{1,0:T(8,128)S(1)}, u32[]{:S(2)}, u32[]{:S(2)}) collective-permute-start(f32[32,128]{1,0:T(8,128)S(1)} %get-tuple-element.51), channel_id=1, source_target_pairs={{0,3},{1,2},{2,1},{3,0},{4,7},{5,6},{6,5},{7,4},{8,11},{9,10},{10,... | collective-permute-start | bytes 49160 | tf_op jit(solution)/shard_map/order/ppermute | solution.py:31
  195.9 6.8 %collective-permute-start.24 = (f32[32,128]{1,0:T(8,128)S(1)}, f32[32,128]{1,0:T(8,128)S(1)}, u32[]{:S(2)}, u32[]{:S(2)}) collective-permute-start(f32[32,128]{1,0:T(8,128)S(1)} %get-tuple-element.52), channel_id=1, source_target_pairs={{0,2},{1,3},{2,0},{3,1},{4,6},{5,7},{6,4},{7,5},{8,10},{9,11},{10,... | collective-permute-start | bytes 49160 | tf_op jit(solution)/shard_map/order/ppermute | solution.py:31
  199.6 3.1 %collective-permute-start.23 = (f32[32,128]{1,0:T(8,128)S(1)}, f32[32,128]{1,0:T(8,128)S(1)}, u32[]{:S(2)}, u32[]{:S(2)}) collective-permute-start(f32[32,128]{1,0:T(8,128)S(1)} %get-tuple-element.53), channel_id=1, source_target_pairs={{0,1},{1,0},{2,3},{3,2},{4,5},{5,4},{6,7},{7,6},{8,9},{9,8},{10,11... | collective-permute-start | bytes 49160 | tf_op jit(solution)/shard_map/order/ppermute | solution.py:31
Sparse Core Ops, SparseCore 0:
  9.8 74.7 all-gather.1

commit v2 on v0

v2 whole, which is shorter than its diff:
```python
import functools
import math

import jax
import jax.numpy as jnp
from jax import lax
from jax.experimental import pallas as pl
from jax.experimental.pallas import tpu as pltpu
from jax.sharding import Mesh, PartitionSpec as P

RANK = 8
SEQ_LEN = 64
AXES = ("zl", "y", "x", "zh", "core")
SIZES = (4, 4, 4, 2, 2)
DEPTH = 1024
GROUPS = 4


def ring(x, axis, step):
    n = SIZES[AXES.index(axis)]
    return lax.ppermute(x, axis, [(i, (i + step) % n) for i in range(n)])


def flip(x, axis, mask):
    n = SIZES[AXES.index(axis)]
    return lax.ppermute(x, axis, [(i, i ^ mask) for i in range(n)])


def project_kernel(count, place_ref, *refs):
    rows_refs = refs[:count]
    grads_ref, acts_ref, keep_ref, send_ref, total_ref = refs[count:]
    tokens = grads_ref.shape[0]
    shape = (-1, GROUPS, RANK, tokens)
    start = 0
    for part, source in enumerate((grads_ref, acts_ref)):
        for at in range(0, source.shape[1], DEPTH):
            rows = jnp.concatenate([r[:, start : start + DEPTH] for r in rows_refs], axis=0)
            product = lax.dot_general(
                rows,
                source[:, at : at + DEPTH],
                (((1,), (1,)), ((), ())),
                preferred_element_type=jnp.float32,
            ).reshape(shape)
            total_ref[part] = product if at == 0 else total_ref[part] + product
            start += DEPTH
    base = place_ref[0]
    for other in range(2):
        mine = base ^ (2 * other)
        keep_ref[other] = total_ref[:, :, mine]
        send_ref[other] = total_ref[:, :, mine ^ 1]


def project(blocks, grads, acts, place):
    tokens, features = grads.shape[0], grads.shape[1] + acts.shape[1]
    rows = sum(b.shape[0] for b in blocks)
    parts = rows // (GROUPS * RANK)
    half = jax.ShapeDtypeStruct((2, 2, parts, RANK, tokens), jnp.float32)
    vmem = pl.BlockSpec(memory_space=pltpu.VMEM)
    return pl.pallas_call(
        functools.partial(project_kernel, len(blocks)),
        out_shape=(half, half),
        in_specs=[pl.BlockSpec(memory_space=pltpu.SMEM)] + [vmem] * (len(blocks) + 2),
        out_specs=(vmem, vmem),
        scratch_shapes=[pltpu.VMEM((2, parts, GROUPS, RANK, tokens), jnp.float32)],
        compiler_params=pltpu.CompilerParams(vmem_limit_bytes=VMEM_LIMIT),
        cost_estimate=pl.CostEstimate(flops=1 << 20, bytes_accessed=1 << 16, transcendentals=0),
    )(place, *blocks, grads, acts)


VMEM_LIMIT = 12 << 20


def finish_kernel(place_ref, sums1_ref, sums2_ref, kept_ref, got_ref, back_ref, out_ref):
    y, x = place_ref[1], place_ref[2]
    total = kept_ref[0] + got_ref[0] + back_ref[...]
    sums3 = (total[0] * total[1]).sum(axis=1)
    sums = jnp.concatenate([sums1_ref[...], sums2_ref[...], sums3], axis=0)
    seqs, tokens = out_ref.shape[0], sums.shape[1]
    row = lax.broadcasted_iota(jnp.int32, (seqs, tokens), 0)
    token = lax.broadcasted_iota(jnp.int32, (seqs, tokens), 1)
    ones = (row == token // SEQ_LEN).astype(jnp.float32)
    scores = lax.dot_general(
        ones,
        sums,
        (((1,), (1,)), ((), ())),
        precision=lax.Precision.HIGHEST,
        preferred_element_type=jnp.float32,
    )
    source = lax.broadcasted_iota(jnp.int32, (32, 32), 0)
    query = lax.broadcasted_iota(jnp.int32, (32, 32), 1)
    colour = query % 2
    off_y, off_x = (query // 8 - y) & 3, ((query // 2) % 4 - x) & 3

    def stands(off):
        return jnp.where(off == 3, 1, jnp.where(off == 0, 0, off + 1))

    first = stands(jnp.where(colour == 0, off_y, off_x))
    second = stands(jnp.where(colour == 0, off_x, off_y))
    wanted = first + jnp.where(
        second == 0,
        colour * 4,
        jnp.where(second == 3, 24 + colour * 4, 8 + colour * 8 + (second - 1) * 4),
    )
    out = jnp.dot(
        scores,
        (source == wanted).astype(jnp.float32),
        precision=lax.Precision.HIGHEST,
        preferred_element_type=jnp.float32,
    )
    out_ref[...] = out * (1.0 / math.sqrt(SEQ_LEN * RANK))


def finish(place, sums1, sums2, kept, got, back):
    vmem = pl.BlockSpec(memory_space=pltpu.VMEM)
    return pl.pallas_call(
        finish_kernel,
        out_shape=jax.ShapeDtypeStruct((8, 32), jnp.float32),
        in_specs=[pl.BlockSpec(memory_space=pltpu.SMEM)] + [vmem] * 5,
        out_specs=vmem,
        compiler_params=pltpu.CompilerParams(vmem_limit_bytes=4 << 20),
    )(place, sums1, sums2, kept, got, back)


def shards(train_grads, train_acts, out_factors, in_factors):
    zl, y, x, zh, core = (lax.axis_index(a) for a in AXES)
    place = jnp.stack([zl ^ (2 * zh + core), y, x])
    own = jnp.concatenate([out_factors.T, in_factors.T], axis=1)
    features = own.shape[1]

    with jax.named_scope("z_shifts"):
        stacked = jnp.stack([own] + [flip(own, "zl", k) for k in (1, 2, 3)])

    def first(rows, axis):
        block = rows.reshape(GROUPS * RANK, features)
        half = block.shape[0] // 2
        before, after = ring(block, axis, 1), ring(block, axis, -1)
        far = ring(before[:half], axis, 1), ring(after[half:], axis, -1)
        return jnp.concatenate([block, before, after, *far])

    def halves(before, after):
        half = before.shape[0] // 2
        return before[:half], after[half:]

    def exchange(sent):
        return lax.ppermute(sent, "zh", [(0, 1), (1, 0)])

    def over(send):
        return lax.ppermute(send, "core", [(0, 1), (1, 0)])

    def sums(keep, got, back):
        total = keep[0] + got[0] + back
        return (total[0] * total[1]).sum(axis=1)

    with jax.named_scope("first_axis"):
        col_a = first(stacked[:, :RANK], "y")
        col_b = first(stacked[:, RANK:], "x")
        col_a, col_b = lax.optimization_barrier((col_a, col_b))
    with jax.named_scope("second_axis"):
        next_a = ring(col_a, "x", 1), ring(col_a, "x", -1)
        next_b = ring(col_b, "y", 1), ring(col_b, "y", -1)
    with jax.named_scope("reduce"):
        keep1, send1 = project((col_a, col_b), train_grads, train_acts, place)
        got1 = over(send1)
        next_a, next_b, keep1 = lax.optimization_barrier((next_a, next_b, keep1))
    with jax.named_scope("second_axis"):
        half_a, half_b = lax.optimization_barrier((halves(*next_a), halves(*next_b)))
        far_a = ring(half_a[0], "x", 1), ring(half_a[1], "x", -1)
        far_b = ring(half_b[0], "y", 1), ring(half_b[1], "y", -1)
    with jax.named_scope("reduce"):
        sums1 = sums(keep1, got1, exchange(keep1[1] + got1[1]))
        keep2, send2 = project(next_a + next_b, train_grads, train_acts, place)
        got2 = over(send2)
        back2 = exchange(keep2[1] + got2[1])
        far_a, far_b, sums1 = lax.optimization_barrier((far_a, far_b, sums1))
        keep3, send3 = project(far_a + far_b, train_grads, train_acts, place)
        got3 = over(send3)
        sums2 = sums(keep2, got2, back2)
        back3 = exchange(keep3[1] + got3[1])
        return finish(place, sums1, sums2, keep3, got3, back3)


def solution(mesh):
    fine = Mesh(mesh.devices.reshape(SIZES), AXES)
    tok, hid = ("zl", "y", "x"), ("zh", "core")
    return jax.shard_map(
        shards,
        mesh=fine,
        in_specs=(P(tok, hid), P(tok, hid), P(hid, tok), P(hid, tok)),
        out_specs=P(tok, hid),
        check_vma=False,
    )
```

time: 936 us -> 196 us (0.21)
  waiting for transfers between devices: 896 us -> 106 us
  starting transfers between devices: 0.08 us -> 51.1 us
  matrix products: 20 us -> 0 us
  Pallas kernels: 0 us -> 19 us
  local copies, waits for them, and re-layouts: 2.31 us -> 17.9 us
  between operations: 13.1 us -> 0.18 us
    all_gather x2 -> x0, waiting for transfers between devices: 654 us -> none  [the longest x1 373 us: shards(): lax.all_gather(out_factors, 'tok', axis=1, tiled=True)]
    psum x1 -> x0, waiting for transfers between devices: 241 us -> none  [shards(): grad_full, act_full = lax.psum((grad_piece, act_piece), 'hid')]
    ppermute x0 -> x25, waiting for transfers between devices: none -> 106 us  [the longest x16 52.2 us: ring(): return lax.ppermute(x, axis, [(i, (i + step) % n) for i in range(n)])]
    ppermute x0 -> x25, starting transfers between devices: none -> 51.1 us  [the longest x16 21.1 us: ring(): return lax.ppermute(x, axis, [(i, (i + step) % n) for i in range(n)])]
    dot_general x2 -> x0, matrix products: 20 us -> none  [the longest x1 14.2 us: shards(): jnp.dot(train_grads, lax.all_gather(out_factors, 'tok', axis=1, tiled=Tru...]
    pallas_call x0 -> x4, Pallas kernels: none -> 19 us  [the longest x3 17.4 us: project(): pl.pallas_call(functools.partial(project_kernel, len(blocks)), out_shape=...]
    unnamed x2 -> x17, local copies, waits for them, and re-layouts: 0.01 us -> 10.7 us
  transfers between devices with their start and end apart: 3 -> 25, of which waited for: 3 -> 13; matrix products, arithmetic and copies ran while one was open for 1% -> 7% of each run, Pallas kernels for 0% -> 9%
where the time goes in v2:
time: 196 us
  waiting for transfers between devices  106 us (54%)
  starting transfers between devices  51.1 us (26%)
  Pallas kernels  19 us (10%)
  local copies, waits for them, and re-layouts  17.9 us (9%)
    ppermute x16, waiting for transfers between devices, ring(): return lax.ppermute(x, axis, [(i, (i + step) % n) for i in range(n)])  52.2 us
    ppermute x3, waiting for transfers between devices, exchange(): return lax.ppermute(sent, 'zh', [(0, 1), (1, 0)])  28.5 us
    ppermute x3, waiting for transfers between devices, flip(): return lax.ppermute(x, axis, [(i, i ^ mask) for i in range(n)])  24.8 us
    ppermute x16, starting transfers between devices, ring(): return lax.ppermute(x, axis, [(i, (i + step) % n) for i in range(n)])  21.1 us
    pallas_call x3, Pallas kernels, project(): pl.pallas_call(functools.partial(project_kernel, len(blocks)), out_shape=...  17.4 us
    ppermute x3, starting transfers between devices, over(): return lax.ppermute(send, 'core', [(0, 1), (1, 0)])  16.9 us
    unnamed x17, local copies, waits for them, and re-layouts  10.7 us
    ppermute x3, starting transfers between devices, exchange(): return lax.ppermute(sent, 'zh', [(0, 1), (1, 0)])  9.53 us
  transfers between devices with their start and end apart: 25, of which 13 were waited for; matrix products, arithmetic and copies ran while one was open for 7% of the time, Pallas kernels for 9%

profile of v2, /device:TPU:33, one launch (start us, length us, event | category | flops | bytes accessed | tf_op | source)
XLA Modules:
  0.0 195.7 jit_solution(2211474982608524334)
XLA Ops:
  0.0 1.0 fusion.9
  1.0 3.1 %collective-permute-start.1 = (bf16[16,9216]{1,0:T(8,128)(2,1)S(1)}, bf16[16,9216]{1,0:T(8,128)(2,1)S(1)}, u32[]{:S(2)}, u32[]{:S(2)}) collective-permute-start(bf16[16,9216]{1,0:T(8,128)(2,1)S(1)} %get-tuple-element.54), channel_id=1, source_target_pairs={{0,128},{64,192},{128,0},{192,64},{1,129},{65,193},{129,1},{193,65... | collective-permute-start | bytes 884744 | tf_op jit(solution)/shard_map/z_shifts/ppermute | solution.py:26
  4.1 0.4 collective-permute-start.2
  4.5 12.7 %collective-permute-done.1 = bf16[16,9216]{1,0:T(8,128)(2,1)S(1)} collective-permute-done((bf16[16,9216]{1,0:T(8,128)(2,1)S(1)}, bf16[16,9216]{1,0:T(8,128)(2,1)S(1)}, u32[]{:S(2)}, u32[]{:S(2)}) %collective-permute-start.1) | collective-permute-done | bytes 294944 | tf_op jit(solution)/shard_map/z_shifts/ppermute | solution.py:26
  17.2 0.0 collective-permute-done
  17.2 12.1 %collective-permute-done.2 = bf16[16,9216]{1,0:T(8,128)(2,1)S(1)} collective-permute-done((bf16[16,9216]{1,0:T(8,128)(2,1)S(1)}, bf16[16,9216]{1,0:T(8,128)(2,1)S(1)}, u32[]{:S(2)}, u32[]{:S(2)}) %collective-permute-start.2) | collective-permute-done | bytes 294944 | tf_op jit(solution)/shard_map/z_shifts/ppermute | solution.py:26
  29.3 0.1 pad_maximum_fusion
  29.5 0.1 slice_bitcast_fusion
  29.6 2.6 %collective-permute-start.8 = (bf16[32,9216]{1,0:T(8,128)(2,1)S(1)}, bf16[32,9216]{1,0:T(8,128)(2,1)S(1)}, u32[]{:S(2)}, u32[]{:S(2)}) collective-permute-start(bf16[32,9216]{1,0:T(8,128)(2,1)S(1)} %get-tuple-element.49), channel_id=1, source_target_pairs={{0,12},{4,0},{8,4},{12,8},{1,13},{5,1},{9,5},{13,9},{2,14},{6,2},{... | collective-permute-start | bytes 1769480 | tf_op jit(solution)/shard_map/first_axis/ppermute | solution.py:21
  32.1 0.0 collective-permute-start.7
  32.1 2.7 %collective-permute-start.4 = (bf16[32,9216]{1,0:T(8,128)(2,1)S(1)}, bf16[32,9216]{1,0:T(8,128)(2,1)S(1)}, u32[]{:S(2)}, u32[]{:S(2)}) collective-permute-start(bf16[32,9216]{1,0:T(8,128)(2,1)S(1)} %get-tuple-element.50), channel_id=1, source_target_pairs={{0,48},{16,0},{32,16},{48,32},{1,49},{17,1},{33,17},{49,33},{2,50}... | collective-permute-start | bytes 1769480 | tf_op jit(solution)/shard_map/first_axis/ppermute | solution.py:21
  34.9 1.1 constant_dynamic-update-slice_fusion.9
  35.9 8.4 %collective-permute-done.8 = bf16[32,9216]{1,0:T(8,128)(2,1)S(1)} collective-permute-done((bf16[32,9216]{1,0:T(8,128)(2,1)S(1)}, bf16[32,9216]{1,0:T(8,128)(2,1)S(1)}, u32[]{:S(2)}, u32[]{:S(2)}) %collective-permute-start.8) | collective-permute-done | bytes 589856 | tf_op jit(solution)/shard_map/first_axis/ppermute | solution.py:21
  44.4 3.5 %collective-permute-start.10 = (bf16[16,9216]{1,0:T(8,128)(2,1)S(1)}, bf16[16,9216]{1,0:T(8,128)(2,1)S(1)}, u32[]{:S(2)}, u32[]{:S(2)}) collective-permute-start(bf16[16,9216]{1,0:T(8,128)(2,1)S(1)} %slice.101), channel_id=1, source_target_pairs={{0,12},{4,0},{8,4},{12,8},{1,13},{5,1},{9,5},{13,9},{2,14},{6,2},{... | collective-permute-start | bytes 884744 | tf_op jit(solution)/shard_map/first_axis/ppermute | solution.py:21
  47.8 0.0 collective-permute-done.7
  47.9 0.1 collective-permute-start.9
  48.0 2.8 %collective-permute-start.6 = (bf16[16,9216]{1,0:T(8,128)(2,1)S(1)}, bf16[16,9216]{1,0:T(8,128)(2,1)S(1)}, u32[]{:S(2)}, u32[]{:S(2)}) collective-permute-start(bf16[16,9216]{1,0:T(8,128)(2,1)S(1)} %slice.98), channel_id=1, source_target_pairs={{0,48},{16,0},{32,16},{48,32},{1,49},{17,1},{33,17},{49,33},{2,50}... | collective-permute-start | bytes 884744 | tf_op jit(solution)/shard_map/first_axis/ppermute | solution.py:21
  50.8 0.1 collective-permute-start.5
  50.9 0.9 constant_dynamic-update-slice_fusion.8
  51.8 0.9 constant_dynamic-update-slice_fusion.7
  52.7 0.9 constant_dynamic-update-slice_fusion.3
  53.6 0.9 constant_dynamic-update-slice_fusion.2
  54.4 1.6 collective-permute-done.9
  56.0 0.7 constant_dynamic-update-slice_fusion.6
  56.8 0.7 constant_dynamic-update-slice_fusion.5.refs_1_
  57.5 1.2 collective-permute-done.5
  58.7 0.7 constant_dynamic-update-slice_fusion.1
  59.5 0.7 constant_dynamic-update-slice_fusion.refs_0_
  60.2 2.4 %collective-permute-start.12 = (bf16[128,9216]{1,0:T(8,128)(2,1)}, bf16[128,9216]{1,0:T(8,128)(2,1)}, u32[]{:S(2)}, u32[]{:S(2)}) collective-permute-start(bf16[128,9216]{1,0:T(8,128)(2,1)} %constant_dynamic-update-slice_fusion.refs_0_), channel_id=1, source_target_pairs={{0,12},{4,0},{8,4},{12,8},{1,13},{5,1},{9,5},{13,9},{2,14},{6,2},{... | collective-permute-start | bytes 7077896 | tf_op jit(solution)/shard_map/second_axis/ppermute | solution.py:21
  62.6 0.6 collective-permute-start.14
  63.2 0.9 collective-permute-start.13
  64.0 0.1 pad_add_fusion.place_ref
  64.1 3.1 %copy-done = bf16[512,7168]{1,0:T(8,128)(2,1)S(1)} copy-done((bf16[512,7168]{1,0:T(8,128)(2,1)S(1)}, bf16[512,7168]{1,0:T(8,128)(2,1)}, u32[]{:S(2)}) %copy-start) | copy-done | bytes 7340056
  67.2 1.6 copy-done.1
  68.8 5.2 %reduce.6 = (f32[2,2,8,8,512]{4,3,2,1,0:T(8,128)S(1)}, f32[2,2,8,8,512]{4,3,2,1,0:T(8,128)S(1)}) custom-call(s32[3]{0:T(128)S(1)} %pad_add_fusion.place_ref, bf16[128,9216]{1,0:T(8,128)(2,1)} %constant_dynamic-update-slice_fusion.refs_0_, bf16[128,9216]{1,0:T(8,128)(2,1)} %constant_dynamic-update-slice_fusion.5.refs_1_, bf16[512,7168]{1,0:T(8,128)(2,1)S(1)} %copy-done, ...), custom_call_target="tpu_custom_call" | custom-call | flops 1048576 | bytes 65536 | tf_op jit(solution)/shard_map/reduce/pallas_call | solution.py:59
  74.1 4.0 %collective-permute-start.19 = (f32[2,2,8,8,512]{4,3,2,1,0:T(8,128)S(1)}, f32[2,2,8,8,512]{4,3,2,1,0:T(8,128)S(1)}, u32[]{:S(2)}, u32[]{:S(2)}) collective-permute-start(f32[2,2,8,8,512]{4,3,2,1,0:T(8,128)S(1)} %get-tuple-element.39), channel_id=1, source_target_pairs={{0,1},{1,0},{2,3},{3,2},{4,5},{5,4},{6,7},{7,6},{8,9},{9,8},{10,11... | collective-permute-start | bytes 1572872 | tf_op jit(solution)/shard_map/reduce/ppermute | solution.py:148
  78.1 32.4 %collective-permute-done.12.refs_1_ = bf16[128,9216]{1,0:T(8,128)(2,1)} collective-permute-done((bf16[128,9216]{1,0:T(8,128)(2,1)}, bf16[128,9216]{1,0:T(8,128)(2,1)}, u32[]{:S(2)}, u32[]{:S(2)}) %collective-permute-start.12) | collective-permute-done | bytes 2359328 | tf_op jit(solution)/shard_map/second_axis/ppermute | solution.py:21
  110.4 3.0 %collective-permute-done.11.refs_0_ = bf16[128,9216]{1,0:T(8,128)(2,1)} collective-permute-done((bf16[128,9216]{1,0:T(8,128)(2,1)}, bf16[128,9216]{1,0:T(8,128)(2,1)}, u32[]{:S(2)}, u32[]{:S(2)}) %collective-permute-start.11) | collective-permute-done | bytes 2359328 | tf_op jit(solution)/shard_map/second_axis/ppermute | solution.py:21
  113.5 0.6 collective-permute-done.13.refs_2_
  114.1 4.2 %collective-permute-start.20 = (f32[2,8,8,512]{3,2,1,0:T(8,128)S(1)}, f32[2,8,8,512]{3,2,1,0:T(8,128)S(1)}, u32[]{:S(2)}, u32[]{:S(2)}) collective-permute-start(f32[2,8,8,512]{3,2,1,0:T(8,128)S(1)} %fusion.5), channel_id=1, source_target_pairs={{0,2},{2,0},{1,3},{3,1},{4,6},{6,4},{5,7},{7,5},{8,10},{10,8},{9,1... | collective-permute-start | bytes 786440 | tf_op jit(solution)/shard_map/reduce/ppermute | solution.py:145
  118.4 1.3 slice.78
  119.7 1.3 slice.81
  121.1 0.0 copy-start.2
  121.1 1.5 slice.80
  122.6 1.3 slice.79
  123.9 0.3 collective-permute-start.15
  124.2 2.6 %collective-permute-start.16 = (bf16[64,9216]{1,0:T(8,128)(2,1)S(1)}, bf16[64,9216]{1,0:T(8,128)(2,1)S(1)}, u32[]{:S(2)}, u32[]{:S(2)}) collective-permute-start(bf16[64,9216]{1,0:T(8,128)(2,1)S(1)} %slice.79), channel_id=1, source_target_pairs={{0,12},{4,0},{8,4},{12,8},{1,13},{5,1},{9,5},{13,9},{2,14},{6,2},{... | collective-permute-start | bytes 3538952 | tf_op jit(solution)/shard_map/second_axis/ppermute | solution.py:21
  126.8 2.7 %collective-permute-start.18 = (bf16[64,9216]{1,0:T(8,128)(2,1)S(1)}, bf16[64,9216]{1,0:T(8,128)(2,1)S(1)}, u32[]{:S(2)}, u32[]{:S(2)}) collective-permute-start(bf16[64,9216]{1,0:T(8,128)(2,1)S(1)} %slice.81), channel_id=1, source_target_pairs={{0,48},{16,0},{32,16},{48,32},{1,49},{17,1},{33,17},{49,33},{2,50}... | collective-permute-start | bytes 3538952 | tf_op jit(solution)/shard_map/second_axis/ppermute | solution.py:21
  129.5 9.0 %reduce.7 = (f32[2,2,16,8,512]{4,3,2,1,0:T(8,128)S(1)}, f32[2,2,16,8,512]{4,3,2,1,0:T(8,128)S(1)}) custom-call(s32[3]{0:T(128)S(1)} %pad_add_fusion.place_ref, bf16[128,9216]{1,0:T(8,128)(2,1)} %collective-permute-done.11.refs_0_, bf16[128,9216]{1,0:T(8,128)(2,1)} %collective-permute-done.12.refs_1_, bf16[128,9216]{1,0:T(8,128)(2,1)} %collective-permute-done.13.refs_2_, ...), custom_call_target="tpu_custom_call" | custom-call | flops 1048576 | bytes 65536 | tf_op jit(solution)/shard_map/reduce/pallas_call | solution.py:59
  138.5 6.4 %collective-permute-start.21 = (f32[2,2,16,8,512]{4,3,2,1,0:T(8,128)S(1)}, f32[2,2,16,8,512]{4,3,2,1,0:T(8,128)S(1)}, u32[]{:S(2)}, u32[]{:S(2)}) collective-permute-start(f32[2,2,16,8,512]{4,3,2,1,0:T(8,128)S(1)} %get-tuple-element.42), channel_id=1, source_target_pairs={{0,1},{1,0},{2,3},{3,2},{4,5},{5,4},{6,7},{7,6},{8,9},{9,8},{10,11... | collective-permute-start | bytes 3145736 | tf_op jit(solution)/shard_map/reduce/ppermute | solution.py:148
  144.9 0.1 fusion.7
  145.0 2.7 %collective-permute-done.15.refs_0_ = bf16[64,9216]{1,0:T(8,128)(2,1)S(1)} collective-permute-done((bf16[64,9216]{1,0:T(8,128)(2,1)S(1)}, bf16[64,9216]{1,0:T(8,128)(2,1)S(1)}, u32[]{:S(2)}, u32[]{:S(2)}) %collective-permute-start.15) | collective-permute-done | bytes 1179680 | tf_op jit(solution)/shard_map/second_axis/ppermute | solution.py:21
  147.7 2.3 %collective-permute-done.17.refs_2_ = bf16[64,9216]{1,0:T(8,128)(2,1)S(1)} collective-permute-done((bf16[64,9216]{1,0:T(8,128)(2,1)S(1)}, bf16[64,9216]{1,0:T(8,128)(2,1)S(1)}, u32[]{:S(2)}, u32[]{:S(2)}) %collective-permute-start.17) | collective-permute-done | bytes 1179680 | tf_op jit(solution)/shard_map/second_axis/ppermute | solution.py:21
  150.0 3.2 %reduce.8 = (f32[2,2,8,8,512]{4,3,2,1,0:T(8,128)S(1)}, f32[2,2,8,8,512]{4,3,2,1,0:T(8,128)S(1)}) custom-call(s32[3]{0:T(128)S(1)} %pad_add_fusion.place_ref, bf16[64,9216]{1,0:T(8,128)(2,1)S(1)} %collective-permute-done.15.refs_0_, bf16[64,9216]{1,0:T(8,128)(2,1)S(1)} %collective-permute-done.16.refs_1_, ...), custom_call_target="tpu_custom_call" | custom-call | flops 1048576 | bytes 65536 | tf_op jit(solution)/shard_map/reduce/pallas_call | solution.py:59
  153.2 6.5 %collective-permute-start.23 = (f32[2,2,8,8,512]{4,3,2,1,0:T(8,128)S(1)}, f32[2,2,8,8,512]{4,3,2,1,0:T(8,128)S(1)}, u32[]{:S(2)}, u32[]{:S(2)}) collective-permute-start(f32[2,2,8,8,512]{4,3,2,1,0:T(8,128)S(1)} %get-tuple-element.48), channel_id=1, source_target_pairs={{0,1},{1,0},{2,3},{3,2},{4,5},{5,4},{6,7},{7,6},{8,9},{9,8},{10,11... | collective-permute-start | bytes 1572872 | tf_op jit(solution)/shard_map/reduce/ppermute | solution.py:148
  159.7 0.1 fusion
  159.8 1.2 collective-permute-start.22
  161.0 0.2 collective-permute-done.23.got_ref
  161.3 4.1 %collective-permute-start.24 = (f32[2,8,8,512]{3,2,1,0:T(8,128)S(1)}, f32[2,8,8,512]{3,2,1,0:T(8,128)S(1)}, u32[]{:S(2)}, u32[]{:S(2)}) collective-permute-start(f32[2,8,8,512]{3,2,1,0:T(8,128)S(1)} %fusion.3), channel_id=1, source_target_pairs={{0,2},{2,0},{1,3},{3,1},{4,6},{6,4},{5,7},{7,5},{8,10},{10,8},{9,1... | collective-permute-start | bytes 786440 | tf_op jit(solution)/shard_map/reduce/ppermute | solution.py:145
  165.4 23.1 %collective-permute-done.22 = f32[2,16,8,512]{3,2,1,0:T(8,128)S(1)} collective-permute-done((f32[2,16,8,512]{3,2,1,0:T(8,128)S(1)}, f32[2,16,8,512]{3,2,1,0:T(8,128)S(1)}, u32[]{:S(2)}, u32[]{:S(2)}) %collective-permute-start.22) | collective-permute-done | bytes 524320 | tf_op jit(solution)/shard_map/reduce/ppermute | solution.py:145
  188.5 0.1 fusion.2
  188.7 0.1 fusion.4.sums2_ref
  188.8 5.4 %collective-permute-done.24.back_ref = f32[2,8,8,512]{3,2,1,0:T(8,128)S(1)} collective-permute-done((f32[2,8,8,512]{3,2,1,0:T(8,128)S(1)}, f32[2,8,8,512]{3,2,1,0:T(8,128)S(1)}, u32[]{:S(2)}, u32[]{:S(2)}) %collective-permute-start.24) | collective-permute-done | bytes 262176 | tf_op jit(solution)/shard_map/reduce/ppermute | solution.py:145
  194.1 1.6 reduce.9
  (29 shorter events, 0.3 us)
Async XLA Ops:
  1.0 16.2 %collective-permute-start.1 = (bf16[16,9216]{1,0:T(8,128)(2,1)S(1)}, bf16[16,9216]{1,0:T(8,128)(2,1)S(1)}, u32[]{:S(2)}, u32[]{:S(2)}) collective-permute-start(bf16[16,9216]{1,0:T(8,128)(2,1)S(1)} %get-tuple-element.54), channel_id=1, source_target_pairs={{0,128},{64,192},{128,0},{192,64},{1,129},{65,193},{129,1},{193,65... | collective-permute-start | bytes 884744 | tf_op jit(solution)/shard_map/z_shifts/ppermute | solution.py:26
  4.1 13.1 %collective-permute-start = (bf16[16,9216]{1,0:T(8,128)(2,1)S(1)}, bf16[16,9216]{1,0:T(8,128)(2,1)S(1)}, u32[]{:S(2)}, u32[]{:S(2)}) collective-permute-start(bf16[16,9216]{1,0:T(8,128)(2,1)S(1)} %get-tuple-element.54), channel_id=1, source_target_pairs={{0,64},{64,0},{128,192},{192,128},{1,65},{65,1},{129,193},{193,129... | collective-permute-start | bytes 884744 | tf_op jit(solution)/shard_map/z_shifts/ppermute | solution.py:26
  4.1 25.2 %collective-permute-start.2 = (bf16[16,9216]{1,0:T(8,128)(2,1)S(1)}, bf16[16,9216]{1,0:T(8,128)(2,1)S(1)}, u32[]{:S(2)}, u32[]{:S(2)}) collective-permute-start(bf16[16,9216]{1,0:T(8,128)(2,1)S(1)} %get-tuple-element.54), channel_id=1, source_target_pairs={{0,192},{64,128},{128,64},{192,0},{1,193},{65,129},{129,65},{193,1... | collective-permute-start | bytes 884744 | tf_op jit(solution)/shard_map/z_shifts/ppermute | solution.py:26
  29.6 14.8 %collective-permute-start.8 = (bf16[32,9216]{1,0:T(8,128)(2,1)S(1)}, bf16[32,9216]{1,0:T(8,128)(2,1)S(1)}, u32[]{:S(2)}, u32[]{:S(2)}) collective-permute-start(bf16[32,9216]{1,0:T(8,128)(2,1)S(1)} %get-tuple-element.49), channel_id=1, source_target_pairs={{0,12},{4,0},{8,4},{12,8},{1,13},{5,1},{9,5},{13,9},{2,14},{6,2},{... | collective-permute-start | bytes 1769480 | tf_op jit(solution)/shard_map/first_axis/ppermute | solution.py:21
  32.1 15.7 %collective-permute-start.7 = (bf16[32,9216]{1,0:T(8,128)(2,1)S(1)}, bf16[32,9216]{1,0:T(8,128)(2,1)S(1)}, u32[]{:S(2)}, u32[]{:S(2)}) collective-permute-start(bf16[32,9216]{1,0:T(8,128)(2,1)S(1)} %get-tuple-element.49), channel_id=1, source_target_pairs={{0,4},{4,8},{8,12},{12,0},{1,5},{5,9},{9,13},{13,1},{2,6},{6,10},{... | collective-permute-start | bytes 1769480 | tf_op jit(solution)/shard_map/first_axis/ppermute | solution.py:21
  32.1 15.8 %collective-permute-start.4 = (bf16[32,9216]{1,0:T(8,128)(2,1)S(1)}, bf16[32,9216]{1,0:T(8,128)(2,1)S(1)}, u32[]{:S(2)}, u32[]{:S(2)}) collective-permute-start(bf16[32,9216]{1,0:T(8,128)(2,1)S(1)} %get-tuple-element.50), channel_id=1, source_target_pairs={{0,48},{16,0},{32,16},{48,32},{1,49},{17,1},{33,17},{49,33},{2,50}... | collective-permute-start | bytes 1769480 | tf_op jit(solution)/shard_map/first_axis/ppermute | solution.py:21
  34.9 15.9 %collective-permute-start.3 = (bf16[32,9216]{1,0:T(8,128)(2,1)S(1)}, bf16[32,9216]{1,0:T(8,128)(2,1)S(1)}, u32[]{:S(2)}, u32[]{:S(2)}) collective-permute-start(bf16[32,9216]{1,0:T(8,128)(2,1)S(1)} %get-tuple-element.50), channel_id=1, source_target_pairs={{0,16},{16,32},{32,48},{48,0},{1,17},{17,33},{33,49},{49,1},{2,18}... | collective-permute-start | bytes 1769480 | tf_op jit(solution)/shard_map/first_axis/ppermute | solution.py:21
  44.4 12.4 %collective-permute-start.10 = (bf16[16,9216]{1,0:T(8,128)(2,1)S(1)}, bf16[16,9216]{1,0:T(8,128)(2,1)S(1)}, u32[]{:S(2)}, u32[]{:S(2)}) collective-permute-start(bf16[16,9216]{1,0:T(8,128)(2,1)S(1)} %slice.101), channel_id=1, source_target_pairs={{0,12},{4,0},{8,4},{12,8},{1,13},{5,1},{9,5},{13,9},{2,14},{6,2},{... | collective-permute-start | bytes 884744 | tf_op jit(solution)/shard_map/first_axis/ppermute | solution.py:21
  47.9 8.2 %collective-permute-start.9 = (bf16[16,9216]{1,0:T(8,128)(2,1)S(1)}, bf16[16,9216]{1,0:T(8,128)(2,1)S(1)}, u32[]{:S(2)}, u32[]{:S(2)}) collective-permute-start(bf16[16,9216]{1,0:T(8,128)(2,1)S(1)} %slice.100), channel_id=1, source_target_pairs={{0,4},{4,8},{8,12},{12,0},{1,5},{5,9},{9,13},{13,1},{2,6},{6,10},{... | collective-permute-start | bytes 884744 | tf_op jit(solution)/shard_map/first_axis/ppermute | solution.py:21
  48.0 11.5 %collective-permute-start.6 = (bf16[16,9216]{1,0:T(8,128)(2,1)S(1)}, bf16[16,9216]{1,0:T(8,128)(2,1)S(1)}, u32[]{:S(2)}, u32[]{:S(2)}) collective-permute-start(bf16[16,9216]{1,0:T(8,128)(2,1)S(1)} %slice.98), channel_id=1, source_target_pairs={{0,48},{16,0},{32,16},{48,32},{1,49},{17,1},{33,17},{49,33},{2,50}... | collective-permute-start | bytes 884744 | tf_op jit(solution)/shard_map/first_axis/ppermute | solution.py:21
  50.8 7.9 %collective-permute-start.5 = (bf16[16,9216]{1,0:T(8,128)(2,1)S(1)}, bf16[16,9216]{1,0:T(8,128)(2,1)S(1)}, u32[]{:S(2)}, u32[]{:S(2)}) collective-permute-start(bf16[16,9216]{1,0:T(8,128)(2,1)S(1)} %slice.97), channel_id=1, source_target_pairs={{0,16},{16,32},{32,48},{48,0},{1,17},{17,33},{33,49},{49,1},{2,18}... | collective-permute-start | bytes 884744 | tf_op jit(solution)/shard_map/first_axis/ppermute | solution.py:21
  51.8 77.6 %slice-start = ((s8[7340032]{0:T(1024)(128)(4,1)}), s8[3145728]{0:T(1024)(128)(4,1)S(1)}, s32[]{:S(2)}) async-start(s8[7340032]{0:T(1024)(128)(4,1)} %bitcast.32), calls=%async_computation | async-start | bytes 6291456
  60.2 50.2 %collective-permute-start.12 = (bf16[128,9216]{1,0:T(8,128)(2,1)}, bf16[128,9216]{1,0:T(8,128)(2,1)}, u32[]{:S(2)}, u32[]{:S(2)}) collective-permute-start(bf16[128,9216]{1,0:T(8,128)(2,1)} %constant_dynamic-update-slice_fusion.refs_0_), channel_id=1, source_target_pairs={{0,12},{4,0},{8,4},{12,8},{1,13},{5,1},{9,5},{13,9},{2,14},{6,2},{... | collective-permute-start | bytes 7077896 | tf_op jit(solution)/shard_map/second_axis/ppermute | solution.py:21
  62.6 50.9 %collective-permute-start.11 = (bf16[128,9216]{1,0:T(8,128)(2,1)}, bf16[128,9216]{1,0:T(8,128)(2,1)}, u32[]{:S(2)}, u32[]{:S(2)}) collective-permute-start(bf16[128,9216]{1,0:T(8,128)(2,1)} %constant_dynamic-update-slice_fusion.refs_0_), channel_id=1, source_target_pairs={{0,4},{4,8},{8,12},{12,0},{1,5},{5,9},{9,13},{13,1},{2,6},{6,10},{... | collective-permute-start | bytes 7077896 | tf_op jit(solution)/shard_map/second_axis/ppermute | solution.py:21
  62.6 50.9 %collective-permute-start.14 = (bf16[128,9216]{1,0:T(8,128)(2,1)}, bf16[128,9216]{1,0:T(8,128)(2,1)}, u32[]{:S(2)}, u32[]{:S(2)}) collective-permute-start(bf16[128,9216]{1,0:T(8,128)(2,1)} %constant_dynamic-update-slice_fusion.5.refs_1_), channel_id=1, source_target_pairs={{0,48},{16,0},{32,16},{48,32},{1,49},{17,1},{33,17},{49,33},{2,50}... | collective-permute-start | bytes 7077896 | tf_op jit(solution)/shard_map/second_axis/ppermute | solution.py:21
  63.2 50.9 %collective-permute-start.13 = (bf16[128,9216]{1,0:T(8,128)(2,1)}, bf16[128,9216]{1,0:T(8,128)(2,1)}, u32[]{:S(2)}, u32[]{:S(2)}) collective-permute-start(bf16[128,9216]{1,0:T(8,128)(2,1)} %constant_dynamic-update-slice_fusion.5.refs_1_), channel_id=1, source_target_pairs={{0,16},{16,32},{32,48},{48,0},{1,17},{17,33},{33,49},{49,1},{2,18}... | collective-permute-start | bytes 7077896 | tf_op jit(solution)/shard_map/second_axis/ppermute | solution.py:21
  64.1 3.1 %copy-start = (bf16[512,7168]{1,0:T(8,128)(2,1)S(1)}, bf16[512,7168]{1,0:T(8,128)(2,1)}, u32[]{:S(2)}) copy-start(bf16[512,7168]{1,0:T(8,128)(2,1)} %refs_4_.3) | copy-start | bytes 22020100
  67.2 1.6 copy-start.1
  68.8 60.7 %slice-start.1 = ((s8[7340032]{0:T(1024)(128)(4,1)}), s8[4194304]{0:T(1024)(128)(4,1)S(1)}, s32[]{:S(2)}) async-start(s8[7340032]{0:T(1024)(128)(4,1)} %bitcast.32), calls=%async_computation.1 | async-start | bytes 8388608
  74.1 40.0 %collective-permute-start.19 = (f32[2,2,8,8,512]{4,3,2,1,0:T(8,128)S(1)}, f32[2,2,8,8,512]{4,3,2,1,0:T(8,128)S(1)}, u32[]{:S(2)}, u32[]{:S(2)}) collective-permute-start(f32[2,2,8,8,512]{4,3,2,1,0:T(8,128)S(1)} %get-tuple-element.39), channel_id=1, source_target_pairs={{0,1},{1,0},{2,3},{3,2},{4,5},{5,4},{6,7},{7,6},{8,9},{9,8},{10,11... | collective-permute-start | bytes 1572872 | tf_op jit(solution)/shard_map/reduce/ppermute | solution.py:148
  114.1 24.3 %collective-permute-start.20 = (f32[2,8,8,512]{3,2,1,0:T(8,128)S(1)}, f32[2,8,8,512]{3,2,1,0:T(8,128)S(1)}, u32[]{:S(2)}, u32[]{:S(2)}) collective-permute-start(f32[2,8,8,512]{3,2,1,0:T(8,128)S(1)} %fusion.5), channel_id=1, source_target_pairs={{0,2},{2,0},{1,3},{3,1},{4,6},{6,4},{5,7},{7,5},{8,10},{10,8},{9,1... | collective-permute-start | bytes 786440 | tf_op jit(solution)/shard_map/reduce/ppermute | solution.py:145
  121.1 8.4 %copy-start.2 = (bf16[512,2048]{1,0:T(8,128)(2,1)S(1)}, bf16[512,2048]{1,0:T(8,128)(2,1)}, u32[]{:S(2)}) copy-start(bf16[512,2048]{1,0:T(8,128)(2,1)} %refs_5_.3) | copy-start | bytes 6291460
  123.9 23.7 %collective-permute-start.15 = (bf16[64,9216]{1,0:T(8,128)(2,1)S(1)}, bf16[64,9216]{1,0:T(8,128)(2,1)S(1)}, u32[]{:S(2)}, u32[]{:S(2)}) collective-permute-start(bf16[64,9216]{1,0:T(8,128)(2,1)S(1)} %slice.78), channel_id=1, source_target_pairs={{0,4},{4,8},{8,12},{12,0},{1,5},{5,9},{9,13},{13,1},{2,6},{6,10},{... | collective-permute-start | bytes 3538952 | tf_op jit(solution)/shard_map/second_axis/ppermute | solution.py:21
  124.2 23.5 %collective-permute-start.16 = (bf16[64,9216]{1,0:T(8,128)(2,1)S(1)}, bf16[64,9216]{1,0:T(8,128)(2,1)S(1)}, u32[]{:S(2)}, u32[]{:S(2)}) collective-permute-start(bf16[64,9216]{1,0:T(8,128)(2,1)S(1)} %slice.79), channel_id=1, source_target_pairs={{0,12},{4,0},{8,4},{12,8},{1,13},{5,1},{9,5},{13,9},{2,14},{6,2},{... | collective-permute-start | bytes 3538952 | tf_op jit(solution)/shard_map/second_axis/ppermute | solution.py:21
  126.8 23.2 %collective-permute-start.17 = (bf16[64,9216]{1,0:T(8,128)(2,1)S(1)}, bf16[64,9216]{1,0:T(8,128)(2,1)S(1)}, u32[]{:S(2)}, u32[]{:S(2)}) collective-permute-start(bf16[64,9216]{1,0:T(8,128)(2,1)S(1)} %slice.80), channel_id=1, source_target_pairs={{0,16},{16,32},{32,48},{48,0},{1,17},{17,33},{33,49},{49,1},{2,18}... | collective-permute-start | bytes 3538952 | tf_op jit(solution)/shard_map/second_axis/ppermute | solution.py:21
  126.8 23.2 %collective-permute-start.18 = (bf16[64,9216]{1,0:T(8,128)(2,1)S(1)}, bf16[64,9216]{1,0:T(8,128)(2,1)S(1)}, u32[]{:S(2)}, u32[]{:S(2)}) collective-permute-start(bf16[64,9216]{1,0:T(8,128)(2,1)S(1)} %slice.81), channel_id=1, source_target_pairs={{0,48},{16,0},{32,16},{48,32},{1,49},{17,1},{33,17},{49,33},{2,50}... | collective-permute-start | bytes 3538952 | tf_op jit(solution)/shard_map/second_axis/ppermute | solution.py:21
  138.5 21.3 %collective-permute-start.21 = (f32[2,2,16,8,512]{4,3,2,1,0:T(8,128)S(1)}, f32[2,2,16,8,512]{4,3,2,1,0:T(8,128)S(1)}, u32[]{:S(2)}, u32[]{:S(2)}) collective-permute-start(f32[2,2,16,8,512]{4,3,2,1,0:T(8,128)S(1)} %get-tuple-element.42), channel_id=1, source_target_pairs={{0,1},{1,0},{2,3},{3,2},{4,5},{5,4},{6,7},{7,6},{8,9},{9,8},{10,11... | collective-permute-start | bytes 3145736 | tf_op jit(solution)/shard_map/reduce/ppermute | solution.py:148
  153.2 8.1 %collective-permute-start.23 = (f32[2,2,8,8,512]{4,3,2,1,0:T(8,128)S(1)}, f32[2,2,8,8,512]{4,3,2,1,0:T(8,128)S(1)}, u32[]{:S(2)}, u32[]{:S(2)}) collective-permute-start(f32[2,2,8,8,512]{4,3,2,1,0:T(8,128)S(1)} %get-tuple-element.48), channel_id=1, source_target_pairs={{0,1},{1,0},{2,3},{3,2},{4,5},{5,4},{6,7},{7,6},{8,9},{9,8},{10,11... | collective-permute-start | bytes 1572872 | tf_op jit(solution)/shard_map/reduce/ppermute | solution.py:148
  159.8 28.7 %collective-permute-start.22 = (f32[2,16,8,512]{3,2,1,0:T(8,128)S(1)}, f32[2,16,8,512]{3,2,1,0:T(8,128)S(1)}, u32[]{:S(2)}, u32[]{:S(2)}) collective-permute-start(f32[2,16,8,512]{3,2,1,0:T(8,128)S(1)} %fusion), channel_id=1, source_target_pairs={{0,2},{2,0},{1,3},{3,1},{4,6},{6,4},{5,7},{7,5},{8,10},{10,8},{9,1... | collective-permute-start | bytes 1572872 | tf_op jit(solution)/shard_map/reduce/ppermute | solution.py:145
  161.3 32.8 %collective-permute-start.24 = (f32[2,8,8,512]{3,2,1,0:T(8,128)S(1)}, f32[2,8,8,512]{3,2,1,0:T(8,128)S(1)}, u32[]{:S(2)}, u32[]{:S(2)}) collective-permute-start(f32[2,8,8,512]{3,2,1,0:T(8,128)S(1)} %fusion.3), channel_id=1, source_target_pairs={{0,2},{2,0},{1,3},{3,1},{4,6},{6,4},{5,7},{7,5},{8,10},{10,8},{9,1... | collective-permute-start | bytes 786440 | tf_op jit(solution)/shard_map/reduce/ppermute | solution.py:145

commit v3 on v2

--- a/solution.py
+++ b/solution.py
@@ -70,11 +70,11 @@
 VMEM_LIMIT = 12 << 20
 
 
-def finish_kernel(place_ref, sums1_ref, sums2_ref, kept_ref, got_ref, back_ref, out_ref):
+def finish_kernel(place_ref, sums1_ref, sums2_ref, sums3_ref, kept_ref, got_ref, back_ref, out_ref):
     y, x = place_ref[1], place_ref[2]
     total = kept_ref[0] + got_ref[0] + back_ref[...]
-    sums3 = (total[0] * total[1]).sum(axis=1)
-    sums = jnp.concatenate([sums1_ref[...], sums2_ref[...], sums3], axis=0)
+    sums4 = (total[0] * total[1]).sum(axis=1)
+    sums = jnp.concatenate([sums1_ref[...], sums2_ref[...], sums3_ref[...], sums4], axis=0)
     seqs, tokens = out_ref.shape[0], sums.shape[1]
     row = lax.broadcasted_iota(jnp.int32, (seqs, tokens), 0)
     token = lax.broadcasted_iota(jnp.int32, (seqs, tokens), 1)
@@ -96,10 +96,10 @@
 
     first = stands(jnp.where(colour == 0, off_y, off_x))
     second = stands(jnp.where(colour == 0, off_x, off_y))
-    wanted = first + jnp.where(
+    wanted = colour * 4 + jnp.where(
         second == 0,
-        colour * 4,
-        jnp.where(second == 3, 24 + colour * 4, 8 + colour * 8 + (second - 1) * 4),
+        first,
+        jnp.where(second == 3, 24 + first, 8 + 8 * (first // 2) + 2 * (second - 1) + first % 2),
     )
     out = jnp.dot(
         scores,
@@ -110,15 +110,15 @@
     out_ref[...] = out * (1.0 / math.sqrt(SEQ_LEN * RANK))
 
 
-def finish(place, sums1, sums2, kept, got, back):
+def finish(place, sums, kept, got, back):
     vmem = pl.BlockSpec(memory_space=pltpu.VMEM)
     return pl.pallas_call(
         finish_kernel,
         out_shape=jax.ShapeDtypeStruct((8, 32), jnp.float32),
-        in_specs=[pl.BlockSpec(memory_space=pltpu.SMEM)] + [vmem] * 5,
+        in_specs=[pl.BlockSpec(memory_space=pltpu.SMEM)] + [vmem] * 6,
         out_specs=vmem,
         compiler_params=pltpu.CompilerParams(vmem_limit_bytes=4 << 20),
-    )(place, sums1, sums2, kept, got, back)
+    )(place, *sums, kept, got, back)
 
 
 def shards(train_grads, train_acts, out_factors, in_factors):
@@ -135,11 +135,10 @@
         half = block.shape[0] // 2
         before, after = ring(block, axis, 1), ring(block, axis, -1)
         far = ring(before[:half], axis, 1), ring(after[half:], axis, -1)
-        return jnp.concatenate([block, before, after, *far])
+        return jnp.concatenate([block, before]), jnp.concatenate([after, *far])
 
-    def halves(before, after):
-        half = before.shape[0] // 2
-        return before[:half], after[half:]
+    def both(block, axis):
+        return ring(block, axis, 1), ring(block, axis, -1)
 
     def exchange(sent):
         return lax.ppermute(sent, "zh", [(0, 1), (1, 0)])
@@ -151,32 +150,41 @@
         total = keep[0] + got[0] + back
         return (total[0] * total[1]).sum(axis=1)
 
+    def work(blocks):
+        keep, send = project(blocks, train_grads, train_acts, place)
+        return keep, over(send)
+
     with jax.named_scope("first_axis"):
-        col_a = first(stacked[:, :RANK], "y")
-        col_b = first(stacked[:, RANK:], "x")
-        col_a, col_b = lax.optimization_barrier((col_a, col_b))
+        lo_a, hi_a = first(stacked[:, :RANK], "y")
+        lo_b, hi_b = first(stacked[:, RANK:], "x")
+        lo_a, lo_b = lax.optimization_barrier((lo_a, lo_b))
+        hi_a, hi_b = lax.optimization_barrier((hi_a, hi_b))
     with jax.named_scope("second_axis"):
-        next_a = ring(col_a, "x", 1), ring(col_a, "x", -1)
-        next_b = ring(col_b, "y", 1), ring(col_b, "y", -1)
+        lo = both(lo_a, "x") + both(lo_b, "y")
+        hi = both(hi_a, "x") + both(hi_b, "y")
     with jax.named_scope("reduce"):
-        keep1, send1 = project((col_a, col_b), train_grads, train_acts, place)
-        got1 = over(send1)
-        next_a, next_b, keep1 = lax.optimization_barrier((next_a, next_b, keep1))
+        keep1, got1 = work((lo_a, hi_a, lo_b, hi_b))
+        lo, keep1 = lax.optimization_barrier((lo, keep1))
+        sums1 = sums(keep1, got1, exchange(keep1[1] + got1[1]))
+        keep2, got2 = work(lo)
+        hi, keep2 = lax.optimization_barrier((hi, keep2))
+        sums2 = sums(keep2, got2, exchange(keep2[1] + got2[1]))
     with jax.named_scope("second_axis"):
-        half_a, half_b = lax.optimization_barrier((halves(*next_a), halves(*next_b)))
-        far_a = ring(half_a[0], "x", 1), ring(half_a[1], "x", -1)
-        far_b = ring(half_b[0], "y", 1), ring(half_b[1], "y", -1)
+        from_lo, from_hi = lax.optimization_barrier(((lo[0], lo[2]), (hi[1], hi[3])))
+        far = (
+            ring(from_lo[0], "x", 1),
+            ring(from_hi[0], "x", -1),
+            ring(from_lo[1], "y", 1),
+            ring(from_hi[1], "y", -1),
+        )
     with jax.named_scope("reduce"):
-        sums1 = sums(keep1, got1, exchange(keep1[1] + got1[1]))
-        keep2, send2 = project(next_a + next_b, train_grads, train_acts, place)
-        got2 = over(send2)
-        back2 = exchange(keep2[1] + got2[1])
-        far_a, far_b, sums1 = lax.optimization_barrier((far_a, far_b, sums1))
-        keep3, send3 = project(far_a + far_b, train_grads, train_acts, place)
-        got3 = over(send3)
-        sums2 = sums(keep2, got2, back2)
+        keep3, got3 = work(hi)
         back3 = exchange(keep3[1] + got3[1])
-        return finish(place, sums1, sums2, keep3, got3, back3)
+        far, sums1, sums2 = lax.optimization_barrier((far, sums1, sums2))
+        keep4, got4 = work(far)
+        sums3 = sums(keep3, got3, back3)
+        back4 = exchange(keep4[1] + got4[1])
+        return finish(place, (sums1, sums2, sums3), keep4, got4, back4)
 
 
 def solution(mesh):

time: 196 us -> 175 us (0.89)
  waiting for transfers between devices: 106 us -> 90.4 us
  local copies, waits for them, and re-layouts: 17.9 us -> 9.27 us
  other arithmetic: 1.74 us -> 5.04 us
    ppermute x16 -> x20, waiting for transfers between devices: 52.2 us -> 33 us  [ring(): return lax.ppermute(x, axis, [(i, (i + step) % n) for i in range(n)])]
    ppermute x3 -> x4, starting transfers between devices: 16.9 us -> 9.28 us  [over(): return lax.ppermute(send, 'core', [(0, 1), (1, 0)])]
    slice x4 -> x0, local copies, waits for them, and re-layouts: 5.54 us -> none  [halves(): return (before[:half], after[half:])]
    ppermute x3 -> x4, starting transfers between devices: 9.53 us -> 14.9 us  [exchange(): return lax.ppermute(sent, 'zh', [(0, 1), (1, 0)])]
    ppermute x3 -> x4, waiting for transfers between devices: 28.5 us -> 31.9 us  [exchange(): return lax.ppermute(sent, 'zh', [(0, 1), (1, 0)])]
    concatenate x0 -> x4, other arithmetic: none -> 3.36 us  [first(): return (jnp.concatenate([block, before]), jnp.concatenate([after, *far]))]
    ppermute x16 -> x20, starting transfers between devices: 21.1 us -> 24.1 us  [ring(): return lax.ppermute(x, axis, [(i, (i + step) % n) for i in range(n)])]
    unnamed x17 -> x26, local copies, waits for them, and re-layouts: 10.7 us -> 9.11 us
  transfers between devices with their start and end apart: 25 -> 31, of which waited for: 13 -> 13; matrix products, arithmetic and copies ran while one was open for 7% -> 2% of each run, Pallas kernels for 9% -> 10%
where the time goes in v3:
time: 175 us
  waiting for transfers between devices  90.4 us (52%)
  starting transfers between devices  51.6 us (29%)
  Pallas kernels  18.7 us (11%)
  local copies, waits for them, and re-layouts  9.27 us (5%)
  other arithmetic  5.04 us (3%)
    ppermute x20, waiting for transfers between devices, ring(): return lax.ppermute(x, axis, [(i, (i + step) % n) for i in range(n)])  33 us
    ppermute x4, waiting for transfers between devices, exchange(): return lax.ppermute(sent, 'zh', [(0, 1), (1, 0)])  31.9 us
    ppermute x3, waiting for transfers between devices, flip(): return lax.ppermute(x, axis, [(i, i ^ mask) for i in range(n)])  25.5 us
    ppermute x20, starting transfers between devices, ring(): return lax.ppermute(x, axis, [(i, (i + step) % n) for i in range(n)])  24.1 us
    pallas_call x4, Pallas kernels, project(): pl.pallas_call(functools.partial(project_kernel, len(blocks)), out_shape=...  17.1 us
    ppermute x4, starting transfers between devices, exchange(): return lax.ppermute(sent, 'zh', [(0, 1), (1, 0)])  14.9 us
    ppermute x4, starting transfers between devices, over(): return lax.ppermute(send, 'core', [(0, 1), (1, 0)])  9.28 us
    unnamed x26, local copies, waits for them, and re-layouts  9.11 us
  transfers between devices with their start and end apart: 31, of which 13 were waited for; matrix products, arithmetic and copies ran while one was open for 2% of the time, Pallas kernels for 10%

profile of v3, /device:TPU:33, one launch (start us, length us, event | category | flops | bytes accessed | tf_op | source)
XLA Modules:
  0.0 175.2 jit_solution(6076682398326222937)
XLA Ops:
  0.0 1.0 fusion.13
  1.0 0.1 collective-permute-start
  1.1 3.1 %collective-permute-start.1 = (bf16[16,9216]{1,0:T(8,128)(2,1)S(1)}, bf16[16,9216]{1,0:T(8,128)(2,1)S(1)}, u32[]{:S(2)}, u32[]{:S(2)}) collective-permute-start(bf16[16,9216]{1,0:T(8,128)(2,1)S(1)} %get-tuple-element.72), channel_id=1, source_target_pairs={{0,128},{64,192},{128,0},{192,64},{1,129},{65,193},{129,1},{193,65... | collective-permute-start | bytes 884744 | tf_op jit(solution)/shard_map/z_shifts/ppermute | solution.py:26
  4.2 0.2 collective-permute-start.2
  4.4 5.9 %collective-permute-done = bf16[16,9216]{1,0:T(8,128)(2,1)S(1)} collective-permute-done((bf16[16,9216]{1,0:T(8,128)(2,1)S(1)}, bf16[16,9216]{1,0:T(8,128)(2,1)S(1)}, u32[]{:S(2)}, u32[]{:S(2)}) %collective-permute-start) | collective-permute-done | bytes 294944 | tf_op jit(solution)/shard_map/z_shifts/ppermute | solution.py:26
  10.2 12.2 %collective-permute-done.1 = bf16[16,9216]{1,0:T(8,128)(2,1)S(1)} collective-permute-done((bf16[16,9216]{1,0:T(8,128)(2,1)S(1)}, bf16[16,9216]{1,0:T(8,128)(2,1)S(1)}, u32[]{:S(2)}, u32[]{:S(2)}) %collective-permute-start.1) | collective-permute-done | bytes 294944 | tf_op jit(solution)/shard_map/z_shifts/ppermute | solution.py:26
  22.5 7.4 %collective-permute-done.2 = bf16[16,9216]{1,0:T(8,128)(2,1)S(1)} collective-permute-done((bf16[16,9216]{1,0:T(8,128)(2,1)S(1)}, bf16[16,9216]{1,0:T(8,128)(2,1)S(1)}, u32[]{:S(2)}, u32[]{:S(2)}) %collective-permute-start.2) | collective-permute-done | bytes 294944 | tf_op jit(solution)/shard_map/z_shifts/ppermute | solution.py:26
  29.8 0.1 pad_maximum_fusion
  30.0 0.1 slice_bitcast_fusion
  30.1 1.3 collective-permute-start.4
  31.4 1.5 collective-permute-start.12
  32.8 1.3 collective-permute-start.3
  34.1 1.4 collective-permute-start.9
  35.6 9.1 %collective-permute-done.4 = bf16[32,9216]{1,0:T(8,128)(2,1)S(1)} collective-permute-done((bf16[32,9216]{1,0:T(8,128)(2,1)S(1)}, bf16[32,9216]{1,0:T(8,128)(2,1)S(1)}, u32[]{:S(2)}, u32[]{:S(2)}) %collective-permute-start.4) | collective-permute-done | bytes 589856 | tf_op jit(solution)/shard_map/first_axis/ppermute | solution.py:21
  44.7 0.1 collective-permute-start.13
  44.8 2.7 %collective-permute-start.14 = (bf16[16,9216]{1,0:T(8,128)(2,1)S(1)}, bf16[16,9216]{1,0:T(8,128)(2,1)S(1)}, u32[]{:S(2)}, u32[]{:S(2)}) collective-permute-start(bf16[16,9216]{1,0:T(8,128)(2,1)S(1)} %slice.109), channel_id=1, source_target_pairs={{0,12},{4,0},{8,4},{12,8},{1,13},{5,1},{9,5},{13,9},{2,14},{6,2},{... | collective-permute-start | bytes 884744 | tf_op jit(solution)/shard_map/first_axis/ppermute | solution.py:21
  47.6 1.1 pad_maximum_fusion.2.refs_2_
  48.7 0.1 pad_maximum_fusion.1.refs_0_
  48.8 0.1 collective-permute-start.5
  48.8 2.7 %collective-permute-start.6 = (bf16[64,9216]{1,0:T(8,128)(2,1)S(1)}, bf16[64,9216]{1,0:T(8,128)(2,1)S(1)}, u32[]{:S(2)}, u32[]{:S(2)}) collective-permute-start(bf16[64,9216]{1,0:T(8,128)(2,1)S(1)} %pad_maximum_fusion.1.refs_0_), channel_id=1, source_target_pairs={{0,12},{4,0},{8,4},{12,8},{1,13},{5,1},{9,5},{13,9},{2,14},{6,2},{... | collective-permute-start | bytes 3538952 | tf_op jit(solution)/shard_map/second_axis/ppermute | solution.py:21
  51.5 0.0 collective-permute-done.9
  51.5 1.4 collective-permute-start.10
  53.0 1.9 %collective-permute-start.11 = (bf16[16,9216]{1,0:T(8,128)(2,1)S(1)}, bf16[16,9216]{1,0:T(8,128)(2,1)S(1)}, u32[]{:S(2)}, u32[]{:S(2)}) collective-permute-start(bf16[16,9216]{1,0:T(8,128)(2,1)S(1)} %slice.107), channel_id=1, source_target_pairs={{0,48},{16,0},{32,16},{48,32},{1,49},{17,1},{33,17},{49,33},{2,50}... | collective-permute-start | bytes 884744 | tf_op jit(solution)/shard_map/first_axis/ppermute | solution.py:21
  54.8 1.1 pad_maximum_fusion.4.refs_3_
  55.9 2.8 %collective-permute-done.10 = bf16[16,9216]{1,0:T(8,128)(2,1)S(1)} collective-permute-done((bf16[16,9216]{1,0:T(8,128)(2,1)S(1)}, bf16[16,9216]{1,0:T(8,128)(2,1)S(1)}, u32[]{:S(2)}, u32[]{:S(2)}) %collective-permute-start.10) | collective-permute-done | bytes 294944 | tf_op jit(solution)/shard_map/first_axis/ppermute | solution.py:21
  58.8 1.5 collective-permute-start.8
  60.2 1.1 pad_maximum_fusion.3.refs_1_
  61.3 0.0 collective-permute-start.15
  61.3 16.7 %collective-permute-done.5.refs_0_ = bf16[64,9216]{1,0:T(8,128)(2,1)S(1)} collective-permute-done((bf16[64,9216]{1,0:T(8,128)(2,1)S(1)}, bf16[64,9216]{1,0:T(8,128)(2,1)S(1)}, u32[]{:S(2)}, u32[]{:S(2)}) %collective-permute-start.5) | collective-permute-done | bytes 1179680 | tf_op jit(solution)/shard_map/second_axis/ppermute | solution.py:21
  78.1 1.0 copy-done.5
  79.1 1.1 copy-done.9
  80.2 1.3 collective-permute-start.17
  81.5 2.3 %collective-permute-done.7.refs_2_ = bf16[64,9216]{1,0:T(8,128)(2,1)S(1)} collective-permute-done((bf16[64,9216]{1,0:T(8,128)(2,1)}, bf16[64,9216]{1,0:T(8,128)(2,1)S(1)}, u32[]{:S(2)}, u32[]{:S(2)}) %collective-permute-start.7) | collective-permute-done | bytes 1179680 | tf_op jit(solution)/shard_map/second_axis/ppermute | solution.py:21
  83.8 1.0 copy-done.7
  84.8 0.9 collective-permute-start.18
  85.7 0.1 pad_add_fusion.place_ref
  85.8 3.1 %copy-done = bf16[512,7168]{1,0:T(8,128)(2,1)S(1)} copy-done((bf16[512,7168]{1,0:T(8,128)(2,1)S(1)}, bf16[512,7168]{1,0:T(8,128)(2,1)}, u32[]{:S(2)}) %copy-start) | copy-done | bytes 7340056
  88.9 1.6 copy-done.1
  90.5 1.3 copy-done.4
  91.8 4.8 %reduce.8 = (f32[2,2,8,8,512]{4,3,2,1,0:T(8,128)S(1)}, f32[2,2,8,8,512]{4,3,2,1,0:T(8,128)S(1)}) custom-call(s32[3]{0:T(128)S(1)} %pad_add_fusion.place_ref, bf16[64,9216]{1,0:T(8,128)(2,1)S(1)} %copy-done.4, bf16[64,9216]{1,0:T(8,128)(2,1)} %pad_maximum_fusion.3.refs_1_, bf16[64,9216]{1,0:T(8,128)(2,1)} %pad_maximum_fusion.2.refs_2_, ...), custom_call_target="tpu_custom_call" | custom-call | flops 1048576 | bytes 65536 | tf_op jit(solution)/shard_map/reduce/pallas_call | solution.py:59
  96.6 7.4 %collective-permute-start.23 = (f32[2,2,8,8,512]{4,3,2,1,0:T(8,128)S(1)}, f32[2,2,8,8,512]{4,3,2,1,0:T(8,128)S(1)}, u32[]{:S(2)}, u32[]{:S(2)}) collective-permute-start(f32[2,2,8,8,512]{4,3,2,1,0:T(8,128)S(1)} %get-tuple-element.54), channel_id=1, source_target_pairs={{0,1},{1,0},{2,3},{3,2},{4,5},{5,4},{6,7},{7,6},{8,9},{9,8},{10,11... | collective-permute-start | bytes 1572872 | tf_op jit(solution)/shard_map/reduce/ppermute | solution.py:147
  104.1 4.0 %reduce.9 = (f32[2,2,8,8,512]{4,3,2,1,0:T(8,128)S(1)}, f32[2,2,8,8,512]{4,3,2,1,0:T(8,128)S(1)}) custom-call(s32[3]{0:T(128)S(1)} %pad_add_fusion.place_ref, bf16[64,9216]{1,0:T(8,128)(2,1)S(1)} %copy-done.6, bf16[64,9216]{1,0:T(8,128)(2,1)S(1)} %copy-done.10, bf16[64,9216]{1,0:T(8,128)(2,1)S(1)} %copy-done.8, ...), custom_call_target="tpu_custom_call" | custom-call | flops 1048576 | bytes 65536 | tf_op jit(solution)/shard_map/reduce/pallas_call | solution.py:59
  108.1 0.1 collective-permute-start.25
  108.2 1.2 collective-permute-done.17.refs_2_
  109.4 0.8 collective-permute-done.18.refs_3_
  110.2 2.7 %collective-permute-start.20 = (bf16[64,9216]{1,0:T(8,128)(2,1)}, bf16[64,9216]{1,0:T(8,128)(2,1)S(1)}, u32[]{:S(2)}, u32[]{:S(2)}) collective-permute-start(bf16[64,9216]{1,0:T(8,128)(2,1)} %collective-permute-done.16.refs_1_), channel_id=1, source_target_pairs={{0,12},{4,0},{8,4},{12,8},{1,13},{5,1},{9,5},{13,9},{2,14},{6,2},{... | collective-permute-start | bytes 3538952 | tf_op jit(solution)/shard_map/second_axis/ppermute | solution.py:21
  112.8 0.7 collective-permute-start.21
  113.5 2.8 %collective-permute-start.22 = (bf16[64,9216]{1,0:T(8,128)(2,1)}, bf16[64,9216]{1,0:T(8,128)(2,1)S(1)}, u32[]{:S(2)}, u32[]{:S(2)}) collective-permute-start(bf16[64,9216]{1,0:T(8,128)(2,1)} %collective-permute-done.18.refs_3_), channel_id=1, source_target_pairs={{0,48},{16,0},{32,16},{48,32},{1,49},{17,1},{33,17},{49,33},{2,50}... | collective-permute-start | bytes 3538952 | tf_op jit(solution)/shard_map/second_axis/ppermute | solution.py:21
  116.3 4.8 %collective-permute-start.24 = (f32[2,8,8,512]{3,2,1,0:T(8,128)S(1)}, f32[2,8,8,512]{3,2,1,0:T(8,128)S(1)}, u32[]{:S(2)}, u32[]{:S(2)}) collective-permute-start(f32[2,8,8,512]{3,2,1,0:T(8,128)S(1)} %fusion.7), channel_id=1, source_target_pairs={{0,2},{2,0},{1,3},{3,1},{4,6},{6,4},{5,7},{7,5},{8,10},{10,8},{9,1... | collective-permute-start | bytes 786440 | tf_op jit(solution)/shard_map/reduce/ppermute | solution.py:144
  121.1 10.7 %collective-permute-done.24 = f32[2,8,8,512]{3,2,1,0:T(8,128)S(1)} collective-permute-done((f32[2,8,8,512]{3,2,1,0:T(8,128)S(1)}, f32[2,8,8,512]{3,2,1,0:T(8,128)S(1)}, u32[]{:S(2)}, u32[]{:S(2)}) %collective-permute-start.24) | collective-permute-done | bytes 262176 | tf_op jit(solution)/shard_map/reduce/ppermute | solution.py:144
  131.8 4.5 %collective-permute-start.26 = (f32[2,8,8,512]{3,2,1,0:T(8,128)S(1)}, f32[2,8,8,512]{3,2,1,0:T(8,128)S(1)}, u32[]{:S(2)}, u32[]{:S(2)}) collective-permute-start(f32[2,8,8,512]{3,2,1,0:T(8,128)S(1)} %fusion.4), channel_id=1, source_target_pairs={{0,2},{2,0},{1,3},{3,1},{4,6},{6,4},{5,7},{7,5},{8,10},{10,8},{9,1... | collective-permute-start | bytes 786440 | tf_op jit(solution)/shard_map/reduce/ppermute | solution.py:144
  136.4 0.1 fusion.9
  136.5 5.0 %reduce.10 = (f32[2,2,8,8,512]{4,3,2,1,0:T(8,128)S(1)}, f32[2,2,8,8,512]{4,3,2,1,0:T(8,128)S(1)}) custom-call(s32[3]{0:T(128)S(1)} %pad_add_fusion.place_ref, bf16[64,9216]{1,0:T(8,128)(2,1)} %collective-permute-done.15.refs_0_, bf16[64,9216]{1,0:T(8,128)(2,1)} %collective-permute-done.16.refs_1_, bf16[64,9216]{1,0:T(8,128)(2,1)} %collective-permute-done.17.refs_2_, ...), custom_call_target="tpu_custom_call" | custom-call | flops 1048576 | bytes 65536 | tf_op jit(solution)/shard_map/reduce/pallas_call | solution.py:59
  141.5 3.3 %collective-permute-done.26 = f32[2,8,8,512]{3,2,1,0:T(8,128)S(1)} collective-permute-done((f32[2,8,8,512]{3,2,1,0:T(8,128)S(1)}, f32[2,8,8,512]{3,2,1,0:T(8,128)S(1)}, u32[]{:S(2)}, u32[]{:S(2)}) %collective-permute-start.26) | collective-permute-done | bytes 262176 | tf_op jit(solution)/shard_map/reduce/ppermute | solution.py:144
  144.9 1.7 collective-permute-start.27
  146.5 0.1 fusion.6
  146.7 3.2 %reduce.11 = (f32[2,2,8,8,512]{4,3,2,1,0:T(8,128)S(1)}, f32[2,2,8,8,512]{4,3,2,1,0:T(8,128)S(1)}) custom-call(s32[3]{0:T(128)S(1)} %pad_add_fusion.place_ref, bf16[64,9216]{1,0:T(8,128)(2,1)S(1)} %collective-permute-done.19.refs_0_, bf16[64,9216]{1,0:T(8,128)(2,1)S(1)} %collective-permute-done.20.refs_1_, ...), custom_call_target="tpu_custom_call" | custom-call | flops 1048576 | bytes 65536 | tf_op jit(solution)/shard_map/reduce/pallas_call | solution.py:59
  149.9 0.1 collective-permute-start.29
  150.1 2.7 %collective-permute-start.28 = (f32[2,8,8,512]{3,2,1,0:T(8,128)S(1)}, f32[2,8,8,512]{3,2,1,0:T(8,128)S(1)}, u32[]{:S(2)}, u32[]{:S(2)}) collective-permute-start(f32[2,8,8,512]{3,2,1,0:T(8,128)S(1)} %fusion.1), channel_id=1, source_target_pairs={{0,2},{2,0},{1,3},{3,1},{4,6},{6,4},{5,7},{7,5},{8,10},{10,8},{9,1... | collective-permute-start | bytes 786440 | tf_op jit(solution)/shard_map/reduce/ppermute | solution.py:144
  152.8 2.8 %collective-permute-start.30 = (f32[2,8,8,512]{3,2,1,0:T(8,128)S(1)}, f32[2,8,8,512]{3,2,1,0:T(8,128)S(1)}, u32[]{:S(2)}, u32[]{:S(2)}) collective-permute-start(f32[2,8,8,512]{3,2,1,0:T(8,128)S(1)} %fusion), channel_id=1, source_target_pairs={{0,2},{2,0},{1,3},{3,1},{4,6},{6,4},{5,7},{7,5},{8,10},{10,8},{9,1... | collective-permute-start | bytes 786440 | tf_op jit(solution)/shard_map/reduce/ppermute | solution.py:144
  155.7 12.4 %collective-permute-done.28 = f32[2,8,8,512]{3,2,1,0:T(8,128)S(1)} collective-permute-done((f32[2,8,8,512]{3,2,1,0:T(8,128)S(1)}, f32[2,8,8,512]{3,2,1,0:T(8,128)S(1)}, u32[]{:S(2)}, u32[]{:S(2)}) %collective-permute-start.28) | collective-permute-done | bytes 262176 | tf_op jit(solution)/shard_map/reduce/ppermute | solution.py:144
  168.0 0.1 fusion.3
  168.1 5.5 %collective-permute-done.30.back_ref = f32[2,8,8,512]{3,2,1,0:T(8,128)S(1)} collective-permute-done((f32[2,8,8,512]{3,2,1,0:T(8,128)S(1)}, f32[2,8,8,512]{3,2,1,0:T(8,128)S(1)}, u32[]{:S(2)}, u32[]{:S(2)}) %collective-permute-start.30) | collective-permute-done | bytes 262176 | tf_op jit(solution)/shard_map/reduce/ppermute | solution.py:144
  173.6 1.6 reduce.12
  (52 shorter events, 0.4 us)
Async XLA Ops:
  1.0 9.2 %collective-permute-start = (bf16[16,9216]{1,0:T(8,128)(2,1)S(1)}, bf16[16,9216]{1,0:T(8,128)(2,1)S(1)}, u32[]{:S(2)}, u32[]{:S(2)}) collective-permute-start(bf16[16,9216]{1,0:T(8,128)(2,1)S(1)} %get-tuple-element.72), channel_id=1, source_target_pairs={{0,64},{64,0},{128,192},{192,128},{1,65},{65,1},{129,193},{193,129... | collective-permute-start | bytes 884744 | tf_op jit(solution)/shard_map/z_shifts/ppermute | solution.py:26
  1.1 21.3 %collective-permute-start.1 = (bf16[16,9216]{1,0:T(8,128)(2,1)S(1)}, bf16[16,9216]{1,0:T(8,128)(2,1)S(1)}, u32[]{:S(2)}, u32[]{:S(2)}) collective-permute-start(bf16[16,9216]{1,0:T(8,128)(2,1)S(1)} %get-tuple-element.72), channel_id=1, source_target_pairs={{0,128},{64,192},{128,0},{192,64},{1,129},{65,193},{129,1},{193,65... | collective-permute-start | bytes 884744 | tf_op jit(solution)/shard_map/z_shifts/ppermute | solution.py:26
  4.2 25.6 %collective-permute-start.2 = (bf16[16,9216]{1,0:T(8,128)(2,1)S(1)}, bf16[16,9216]{1,0:T(8,128)(2,1)S(1)}, u32[]{:S(2)}, u32[]{:S(2)}) collective-permute-start(bf16[16,9216]{1,0:T(8,128)(2,1)S(1)} %get-tuple-element.72), channel_id=1, source_target_pairs={{0,192},{64,128},{128,64},{192,0},{1,193},{65,129},{129,65},{193,1... | collective-permute-start | bytes 884744 | tf_op jit(solution)/shard_map/z_shifts/ppermute | solution.py:26
  30.1 14.6 %collective-permute-start.4 = (bf16[32,9216]{1,0:T(8,128)(2,1)S(1)}, bf16[32,9216]{1,0:T(8,128)(2,1)S(1)}, u32[]{:S(2)}, u32[]{:S(2)}) collective-permute-start(bf16[32,9216]{1,0:T(8,128)(2,1)S(1)} %get-tuple-element.69), channel_id=1, source_target_pairs={{0,4},{4,8},{8,12},{12,0},{1,5},{5,9},{9,13},{13,1},{2,6},{6,10},{... | collective-permute-start | bytes 1769480 | tf_op jit(solution)/shard_map/first_axis/ppermute | solution.py:21
  31.4 13.4 %collective-permute-start.12 = (bf16[32,9216]{1,0:T(8,128)(2,1)S(1)}, bf16[32,9216]{1,0:T(8,128)(2,1)S(1)}, u32[]{:S(2)}, u32[]{:S(2)}) collective-permute-start(bf16[32,9216]{1,0:T(8,128)(2,1)S(1)} %get-tuple-element.69), channel_id=1, source_target_pairs={{0,12},{4,0},{8,4},{12,8},{1,13},{5,1},{9,5},{13,9},{2,14},{6,2},{... | collective-permute-start | bytes 1769480 | tf_op jit(solution)/shard_map/first_axis/ppermute | solution.py:21
  32.8 15.8 %collective-permute-start.3 = (bf16[32,9216]{1,0:T(8,128)(2,1)S(1)}, bf16[32,9216]{1,0:T(8,128)(2,1)S(1)}, u32[]{:S(2)}, u32[]{:S(2)}) collective-permute-start(bf16[32,9216]{1,0:T(8,128)(2,1)S(1)} %get-tuple-element.70), channel_id=1, source_target_pairs={{0,16},{16,32},{32,48},{48,0},{1,17},{17,33},{33,49},{49,1},{2,18}... | collective-permute-start | bytes 1769480 | tf_op jit(solution)/shard_map/first_axis/ppermute | solution.py:21
  34.1 17.4 %collective-permute-start.9 = (bf16[32,9216]{1,0:T(8,128)(2,1)S(1)}, bf16[32,9216]{1,0:T(8,128)(2,1)S(1)}, u32[]{:S(2)}, u32[]{:S(2)}) collective-permute-start(bf16[32,9216]{1,0:T(8,128)(2,1)S(1)} %get-tuple-element.70), channel_id=1, source_target_pairs={{0,48},{16,0},{32,16},{48,32},{1,49},{17,1},{33,17},{49,33},{2,50}... | collective-permute-start | bytes 1769480 | tf_op jit(solution)/shard_map/first_axis/ppermute | solution.py:21
  44.7 8.2 %collective-permute-start.13 = (bf16[16,9216]{1,0:T(8,128)(2,1)S(1)}, bf16[16,9216]{1,0:T(8,128)(2,1)S(1)}, u32[]{:S(2)}, u32[]{:S(2)}) collective-permute-start(bf16[16,9216]{1,0:T(8,128)(2,1)S(1)} %slice.108), channel_id=1, source_target_pairs={{0,4},{4,8},{8,12},{12,0},{1,5},{5,9},{9,13},{13,1},{2,6},{6,10},{... | collective-permute-start | bytes 884744 | tf_op jit(solution)/shard_map/first_axis/ppermute | solution.py:21
  44.8 10.0 %collective-permute-start.14 = (bf16[16,9216]{1,0:T(8,128)(2,1)S(1)}, bf16[16,9216]{1,0:T(8,128)(2,1)S(1)}, u32[]{:S(2)}, u32[]{:S(2)}) collective-permute-start(bf16[16,9216]{1,0:T(8,128)(2,1)S(1)} %slice.109), channel_id=1, source_target_pairs={{0,12},{4,0},{8,4},{12,8},{1,13},{5,1},{9,5},{13,9},{2,14},{6,2},{... | collective-permute-start | bytes 884744 | tf_op jit(solution)/shard_map/first_axis/ppermute | solution.py:21
  48.7 7.2 %copy-start.3 = (bf16[64,9216]{1,0:T(8,128)(2,1)}, bf16[64,9216]{1,0:T(8,128)(2,1)S(1)}, u32[]{:S(2)}) copy-start(bf16[64,9216]{1,0:T(8,128)(2,1)S(1)} %pad_maximum_fusion.1.refs_0_) | copy-start | bytes 3538948
  48.8 29.3 %collective-permute-start.5 = (bf16[64,9216]{1,0:T(8,128)(2,1)S(1)}, bf16[64,9216]{1,0:T(8,128)(2,1)S(1)}, u32[]{:S(2)}, u32[]{:S(2)}) collective-permute-start(bf16[64,9216]{1,0:T(8,128)(2,1)S(1)} %pad_maximum_fusion.1.refs_0_), channel_id=1, source_target_pairs={{0,4},{4,8},{8,12},{12,0},{1,5},{5,9},{9,13},{13,1},{2,6},{6,10},{... | collective-permute-start | bytes 3538952 | tf_op jit(solution)/shard_map/second_axis/ppermute | solution.py:21
  48.8 30.2 %collective-permute-start.6 = (bf16[64,9216]{1,0:T(8,128)(2,1)S(1)}, bf16[64,9216]{1,0:T(8,128)(2,1)S(1)}, u32[]{:S(2)}, u32[]{:S(2)}) collective-permute-start(bf16[64,9216]{1,0:T(8,128)(2,1)S(1)} %pad_maximum_fusion.1.refs_0_), channel_id=1, source_target_pairs={{0,12},{4,0},{8,4},{12,8},{1,13},{5,1},{9,5},{13,9},{2,14},{6,2},{... | collective-permute-start | bytes 3538952 | tf_op jit(solution)/shard_map/second_axis/ppermute | solution.py:21
  51.5 52.5 %slice-start = ((s8[7340032]{0:T(1024)(128)(4,1)}), s8[3145728]{0:T(1024)(128)(4,1)S(1)}, s32[]{:S(2)}) async-start(s8[7340032]{0:T(1024)(128)(4,1)} %bitcast.34), calls=%async_computation | async-start | bytes 6291456
  51.5 7.2 %collective-permute-start.10 = (bf16[16,9216]{1,0:T(8,128)(2,1)S(1)}, bf16[16,9216]{1,0:T(8,128)(2,1)S(1)}, u32[]{:S(2)}, u32[]{:S(2)}) collective-permute-start(bf16[16,9216]{1,0:T(8,128)(2,1)S(1)} %slice.106), channel_id=1, source_target_pairs={{0,16},{16,32},{32,48},{48,0},{1,17},{17,33},{33,49},{49,1},{2,18}... | collective-permute-start | bytes 884744 | tf_op jit(solution)/shard_map/first_axis/ppermute | solution.py:21
  53.0 7.3 %collective-permute-start.11 = (bf16[16,9216]{1,0:T(8,128)(2,1)S(1)}, bf16[16,9216]{1,0:T(8,128)(2,1)S(1)}, u32[]{:S(2)}, u32[]{:S(2)}) collective-permute-start(bf16[16,9216]{1,0:T(8,128)(2,1)S(1)} %slice.107), channel_id=1, source_target_pairs={{0,48},{16,0},{32,16},{48,32},{1,49},{17,1},{33,17},{49,33},{2,50}... | collective-permute-start | bytes 884744 | tf_op jit(solution)/shard_map/first_axis/ppermute | solution.py:21
  54.8 29.0 %collective-permute-start.7 = (bf16[64,9216]{1,0:T(8,128)(2,1)}, bf16[64,9216]{1,0:T(8,128)(2,1)S(1)}, u32[]{:S(2)}, u32[]{:S(2)}) collective-permute-start(bf16[64,9216]{1,0:T(8,128)(2,1)} %pad_maximum_fusion.2.refs_2_), channel_id=1, source_target_pairs={{0,16},{16,32},{32,48},{48,0},{1,17},{17,33},{33,49},{49,1},{2,18}... | collective-permute-start | bytes 3538952 | tf_op jit(solution)/shard_map/second_axis/ppermute | solution.py:21
  58.8 37.9 %collective-permute-start.8 = (bf16[64,9216]{1,0:T(8,128)(2,1)}, bf16[64,9216]{1,0:T(8,128)(2,1)}, u32[]{:S(2)}, u32[]{:S(2)}) collective-permute-start(bf16[64,9216]{1,0:T(8,128)(2,1)} %pad_maximum_fusion.2.refs_2_), channel_id=1, source_target_pairs={{0,48},{16,0},{32,16},{48,32},{1,49},{17,1},{33,17},{49,33},{2,50}... | collective-permute-start | bytes 3538952 | tf_op jit(solution)/shard_map/second_axis/ppermute | solution.py:21
  61.3 46.8 %collective-permute-start.15 = (bf16[64,9216]{1,0:T(8,128)(2,1)}, bf16[64,9216]{1,0:T(8,128)(2,1)}, u32[]{:S(2)}, u32[]{:S(2)}) collective-permute-start(bf16[64,9216]{1,0:T(8,128)(2,1)} %pad_maximum_fusion.3.refs_1_), channel_id=1, source_target_pairs={{0,4},{4,8},{8,12},{12,0},{1,5},{5,9},{9,13},{13,1},{2,6},{6,10},{... | collective-permute-start | bytes 3538952 | tf_op jit(solution)/shard_map/second_axis/ppermute | solution.py:21
  78.1 1.0 copy-start.5
  79.1 29.1 %collective-permute-start.16 = (bf16[64,9216]{1,0:T(8,128)(2,1)}, bf16[64,9216]{1,0:T(8,128)(2,1)}, u32[]{:S(2)}, u32[]{:S(2)}) collective-permute-start(bf16[64,9216]{1,0:T(8,128)(2,1)} %pad_maximum_fusion.3.refs_1_), channel_id=1, source_target_pairs={{0,12},{4,0},{8,4},{12,8},{1,13},{5,1},{9,5},{13,9},{2,14},{6,2},{... | collective-permute-start | bytes 3538952 | tf_op jit(solution)/shard_map/second_axis/ppermute | solution.py:21
  79.1 1.1 copy-start.9
  80.2 29.2 %collective-permute-start.17 = (bf16[64,9216]{1,0:T(8,128)(2,1)}, bf16[64,9216]{1,0:T(8,128)(2,1)}, u32[]{:S(2)}, u32[]{:S(2)}) collective-permute-start(bf16[64,9216]{1,0:T(8,128)(2,1)} %pad_maximum_fusion.4.refs_3_), channel_id=1, source_target_pairs={{0,16},{16,32},{32,48},{48,0},{1,17},{17,33},{33,49},{49,1},{2,18}... | collective-permute-start | bytes 3538952 | tf_op jit(solution)/shard_map/second_axis/ppermute | solution.py:21
  83.8 1.0 copy-start.7
  84.8 25.4 %collective-permute-start.18 = (bf16[64,9216]{1,0:T(8,128)(2,1)}, bf16[64,9216]{1,0:T(8,128)(2,1)}, u32[]{:S(2)}, u32[]{:S(2)}) collective-permute-start(bf16[64,9216]{1,0:T(8,128)(2,1)} %pad_maximum_fusion.4.refs_3_), channel_id=1, source_target_pairs={{0,48},{16,0},{32,16},{48,32},{1,49},{17,1},{33,17},{49,33},{2,50}... | collective-permute-start | bytes 3538952 | tf_op jit(solution)/shard_map/second_axis/ppermute | solution.py:21
  85.8 3.1 %copy-start = (bf16[512,7168]{1,0:T(8,128)(2,1)S(1)}, bf16[512,7168]{1,0:T(8,128)(2,1)}, u32[]{:S(2)}) copy-start(bf16[512,7168]{1,0:T(8,128)(2,1)} %refs_4_.7) | copy-start | bytes 22020100
  88.9 1.6 copy-start.1
  90.5 1.3 copy-start.4
  91.8 12.3 %slice-start.1 = ((s8[7340032]{0:T(1024)(128)(4,1)}), s8[4194304]{0:T(1024)(128)(4,1)S(1)}, s32[]{:S(2)}) async-start(s8[7340032]{0:T(1024)(128)(4,1)} %bitcast.34), calls=%async_computation.1 | async-start | bytes 8388608
  91.8 12.3 %copy-start.2 = (bf16[512,2048]{1,0:T(8,128)(2,1)S(1)}, bf16[512,2048]{1,0:T(8,128)(2,1)}, u32[]{:S(2)}) copy-start(bf16[512,2048]{1,0:T(8,128)(2,1)} %refs_5_.7) | copy-start | bytes 6291460
  91.8 12.3 %copy-start.6 = (bf16[64,9216]{1,0:T(8,128)(2,1)S(1)}, bf16[64,9216]{1,0:T(8,128)(2,1)}, u32[]{:S(2)}) copy-start(bf16[64,9216]{1,0:T(8,128)(2,1)} %copy-done.5) | copy-start | bytes 3538948
  91.8 12.3 %copy-start.8 = (bf16[64,9216]{1,0:T(8,128)(2,1)S(1)}, bf16[64,9216]{1,0:T(8,128)(2,1)}, u32[]{:S(2)}) copy-start(bf16[64,9216]{1,0:T(8,128)(2,1)} %copy-done.7) | copy-start | bytes 3538948
  91.8 12.3 %copy-start.10 = (bf16[64,9216]{1,0:T(8,128)(2,1)S(1)}, bf16[64,9216]{1,0:T(8,128)(2,1)}, u32[]{:S(2)}) copy-start(bf16[64,9216]{1,0:T(8,128)(2,1)} %copy-done.9) | copy-start | bytes 3538948
  96.6 16.9 %collective-permute-start.23 = (f32[2,2,8,8,512]{4,3,2,1,0:T(8,128)S(1)}, f32[2,2,8,8,512]{4,3,2,1,0:T(8,128)S(1)}, u32[]{:S(2)}, u32[]{:S(2)}) collective-permute-start(f32[2,2,8,8,512]{4,3,2,1,0:T(8,128)S(1)} %get-tuple-element.54), channel_id=1, source_target_pairs={{0,1},{1,0},{2,3},{3,2},{4,5},{5,4},{6,7},{7,6},{8,9},{9,8},{10,11... | collective-permute-start | bytes 1572872 | tf_op jit(solution)/shard_map/reduce/ppermute | solution.py:147
  108.1 8.2 %collective-permute-start.25 = (f32[2,2,8,8,512]{4,3,2,1,0:T(8,128)S(1)}, f32[2,2,8,8,512]{4,3,2,1,0:T(8,128)S(1)}, u32[]{:S(2)}, u32[]{:S(2)}) collective-permute-start(f32[2,2,8,8,512]{4,3,2,1,0:T(8,128)S(1)} %get-tuple-element.56), channel_id=1, source_target_pairs={{0,1},{1,0},{2,3},{3,2},{4,5},{5,4},{6,7},{7,6},{8,9},{9,8},{10,11... | collective-permute-start | bytes 1572872 | tf_op jit(solution)/shard_map/reduce/ppermute | solution.py:147
  110.2 36.5 %collective-permute-start.19 = (bf16[64,9216]{1,0:T(8,128)(2,1)S(1)}, bf16[64,9216]{1,0:T(8,128)(2,1)S(1)}, u32[]{:S(2)}, u32[]{:S(2)}) collective-permute-start(bf16[64,9216]{1,0:T(8,128)(2,1)S(1)} %copy-done.6), channel_id=1, source_target_pairs={{0,4},{4,8},{8,12},{12,0},{1,5},{5,9},{9,13},{13,1},{2,6},{6,10},{... | collective-permute-start | bytes 3538952 | tf_op jit(solution)/shard_map/second_axis/ppermute | solution.py:21
  110.2 36.5 %collective-permute-start.20 = (bf16[64,9216]{1,0:T(8,128)(2,1)}, bf16[64,9216]{1,0:T(8,128)(2,1)S(1)}, u32[]{:S(2)}, u32[]{:S(2)}) collective-permute-start(bf16[64,9216]{1,0:T(8,128)(2,1)} %collective-permute-done.16.refs_1_), channel_id=1, source_target_pairs={{0,12},{4,0},{8,4},{12,8},{1,13},{5,1},{9,5},{13,9},{2,14},{6,2},{... | collective-permute-start | bytes 3538952 | tf_op jit(solution)/shard_map/second_axis/ppermute | solution.py:21
  112.8 33.8 %collective-permute-start.21 = (bf16[64,9216]{1,0:T(8,128)(2,1)S(1)}, bf16[64,9216]{1,0:T(8,128)(2,1)S(1)}, u32[]{:S(2)}, u32[]{:S(2)}) collective-permute-start(bf16[64,9216]{1,0:T(8,128)(2,1)S(1)} %copy-done.8), channel_id=1, source_target_pairs={{0,16},{16,32},{32,48},{48,0},{1,17},{17,33},{33,49},{49,1},{2,18}... | collective-permute-start | bytes 3538952 | tf_op jit(solution)/shard_map/second_axis/ppermute | solution.py:21
  113.5 33.2 %collective-permute-start.22 = (bf16[64,9216]{1,0:T(8,128)(2,1)}, bf16[64,9216]{1,0:T(8,128)(2,1)S(1)}, u32[]{:S(2)}, u32[]{:S(2)}) collective-permute-start(bf16[64,9216]{1,0:T(8,128)(2,1)} %collective-permute-done.18.refs_3_), channel_id=1, source_target_pairs={{0,48},{16,0},{32,16},{48,32},{1,49},{17,1},{33,17},{49,33},{2,50}... | collective-permute-start | bytes 3538952 | tf_op jit(solution)/shard_map/second_axis/ppermute | solution.py:21
  116.3 15.5 %collective-permute-start.24 = (f32[2,8,8,512]{3,2,1,0:T(8,128)S(1)}, f32[2,8,8,512]{3,2,1,0:T(8,128)S(1)}, u32[]{:S(2)}, u32[]{:S(2)}) collective-permute-start(f32[2,8,8,512]{3,2,1,0:T(8,128)S(1)} %fusion.7), channel_id=1, source_target_pairs={{0,2},{2,0},{1,3},{3,1},{4,6},{6,4},{5,7},{7,5},{8,10},{10,8},{9,1... | collective-permute-start | bytes 786440 | tf_op jit(solution)/shard_map/reduce/ppermute | solution.py:144
  131.8 13.0 %collective-permute-start.26 = (f32[2,8,8,512]{3,2,1,0:T(8,128)S(1)}, f32[2,8,8,512]{3,2,1,0:T(8,128)S(1)}, u32[]{:S(2)}, u32[]{:S(2)}) collective-permute-start(f32[2,8,8,512]{3,2,1,0:T(8,128)S(1)} %fusion.4), channel_id=1, source_target_pairs={{0,2},{2,0},{1,3},{3,1},{4,6},{6,4},{5,7},{7,5},{8,10},{10,8},{9,1... | collective-permute-start | bytes 786440 | tf_op jit(solution)/shard_map/reduce/ppermute | solution.py:144
  144.9 5.2 %collective-permute-start.27 = (f32[2,2,8,8,512]{4,3,2,1,0:T(8,128)S(1)}, f32[2,2,8,8,512]{4,3,2,1,0:T(8,128)S(1)}, u32[]{:S(2)}, u32[]{:S(2)}) collective-permute-start(f32[2,2,8,8,512]{4,3,2,1,0:T(8,128)S(1)} %get-tuple-element.62), channel_id=1, source_target_pairs={{0,1},{1,0},{2,3},{3,2},{4,5},{5,4},{6,7},{7,6},{8,9},{9,8},{10,11... | collective-permute-start | bytes 1572872 | tf_op jit(solution)/shard_map/reduce/ppermute | solution.py:147
  149.9 2.9 %collective-permute-start.29 = (f32[2,2,8,8,512]{4,3,2,1,0:T(8,128)S(1)}, f32[2,2,8,8,512]{4,3,2,1,0:T(8,128)S(1)}, u32[]{:S(2)}, u32[]{:S(2)}) collective-permute-start(f32[2,2,8,8,512]{4,3,2,1,0:T(8,128)S(1)} %get-tuple-element.68), channel_id=1, source_target_pairs={{0,1},{1,0},{2,3},{3,2},{4,5},{5,4},{6,7},{7,6},{8,9},{9,8},{10,11... | collective-permute-start | bytes 1572872 | tf_op jit(solution)/shard_map/reduce/ppermute | solution.py:147
  150.1 17.9 %collective-permute-start.28 = (f32[2,8,8,512]{3,2,1,0:T(8,128)S(1)}, f32[2,8,8,512]{3,2,1,0:T(8,128)S(1)}, u32[]{:S(2)}, u32[]{:S(2)}) collective-permute-start(f32[2,8,8,512]{3,2,1,0:T(8,128)S(1)} %fusion.1), channel_id=1, source_target_pairs={{0,2},{2,0},{1,3},{3,1},{4,6},{6,4},{5,7},{7,5},{8,10},{10,8},{9,1... | collective-permute-start | bytes 786440 | tf_op jit(solution)/shard_map/reduce/ppermute | solution.py:144
  152.8 20.8 %collective-permute-start.30 = (f32[2,8,8,512]{3,2,1,0:T(8,128)S(1)}, f32[2,8,8,512]{3,2,1,0:T(8,128)S(1)}, u32[]{:S(2)}, u32[]{:S(2)}) collective-permute-start(f32[2,8,8,512]{3,2,1,0:T(8,128)S(1)} %fusion), channel_id=1, source_target_pairs={{0,2},{2,0},{1,3},{3,1},{4,6},{6,4},{5,7},{7,5},{8,10},{10,8},{9,1... | collective-permute-start | bytes 786440 | tf_op jit(solution)/shard_map/reduce/ppermute | solution.py:144

commit v4 on v3

--- a/solution.py
+++ b/solution.py
@@ -126,7 +126,6 @@
     place = jnp.stack([zl ^ (2 * zh + core), y, x])
     own = jnp.concatenate([out_factors.T, in_factors.T], axis=1)
     features = own.shape[1]
-
     with jax.named_scope("z_shifts"):
         stacked = jnp.stack([own] + [flip(own, "zl", k) for k in (1, 2, 3)])
 
@@ -153,7 +152,6 @@
     def work(blocks):
         keep, send = project(blocks, train_grads, train_acts, place)
         return keep, over(send)
-
     with jax.named_scope("first_axis"):
         lo_a, hi_a = first(stacked[:, :RANK], "y")
         lo_b, hi_b = first(stacked[:, RANK:], "x")
@@ -161,13 +159,16 @@
         hi_a, hi_b = lax.optimization_barrier((hi_a, hi_b))
     with jax.named_scope("second_axis"):
         lo = both(lo_a, "x") + both(lo_b, "y")
+    with jax.named_scope("reduce"):
+        keep1, got1 = work((lo_a, hi_a, lo_b, hi_b))
+        hi_a, hi_b, keep1 = lax.optimization_barrier((hi_a, hi_b, keep1))
+        sums1 = sums(keep1, got1, exchange(keep1[1] + got1[1]))
+        lo, keep1 = lax.optimization_barrier((lo, keep1))
+    with jax.named_scope("second_axis"):
         hi = both(hi_a, "x") + both(hi_b, "y")
     with jax.named_scope("reduce"):
-        keep1, got1 = work((lo_a, hi_a, lo_b, hi_b))
-        lo, keep1 = lax.optimization_barrier((lo, keep1))
-        sums1 = sums(keep1, got1, exchange(keep1[1] + got1[1]))
         keep2, got2 = work(lo)
-        hi, keep2 = lax.optimization_barrier((hi, keep2))
+        hi, (keep2, sums1) = lax.optimization_barrier((hi, (keep2, sums1)))
         sums2 = sums(keep2, got2, exchange(keep2[1] + got2[1]))
     with jax.named_scope("second_axis"):
         from_lo, from_hi = lax.optimization_barrier(((lo[0], lo[2]), (hi[1], hi[3])))
@@ -179,8 +180,9 @@
         )
     with jax.named_scope("reduce"):
         keep3, got3 = work(hi)
-        back3 = exchange(keep3[1] + got3[1])
-        far, sums1, sums2 = lax.optimization_barrier((far, sums1, sums2))
+        sent3 = keep3[1] + got3[1]
+        back3 = exchange(sent3)
+        far, sums2, sent3 = lax.optimization_barrier((far, sums2, sent3))
         keep4, got4 = work(far)
         sums3 = sums(keep3, got3, back3)
         back4 = exchange(keep4[1] + got4[1])

time: 175 us -> 174 us (level)
  starting transfers between devices: 51.6 us -> 74 us
  waiting for transfers between devices: 90.4 us -> 77 us
  local copies, waits for them, and re-layouts: 9.27 us -> 3.14 us
  Pallas kernels: 18.7 us -> 14.5 us
    ppermute x4, starting transfers between devices: 9.28 us -> 30.1 us  [over(): return lax.ppermute(send, 'core', [(0, 1), (1, 0)])]
    ppermute x4, waiting for transfers between devices: 31.9 us -> 22.3 us  [exchange(): return lax.ppermute(sent, 'zh', [(0, 1), (1, 0)])]
    unnamed x26 -> x8, local copies, waits for them, and re-layouts: 9.11 us -> 0.03 us
    ppermute x20, waiting for transfers between devices: 33 us -> 26.3 us  [ring(): return lax.ppermute(x, axis, [(i, (i + step) % n) for i in range(n)])]
    pallas_call x4, Pallas kernels: 17.1 us -> 12.9 us  [project(): pl.pallas_call(functools.partial(project_kernel, len(blocks)), out_shape=...]
    ppermute x4, waiting for transfers between devices: 0.01 us -> 2.96 us  [over(): return lax.ppermute(send, 'core', [(0, 1), (1, 0)])]
    slice x4, local copies, waits for them, and re-layouts: 0.08 us -> 2 us  [first(): far = (ring(before[:half], axis, 1), ring(after[half:], axis, -1))]
  transfers between devices with their start and end apart: 31 -> 31, of which waited for: 13 -> 16; matrix products, arithmetic and copies ran while one was open for 2% -> 3% of each run, Pallas kernels for 10% -> 6%
where the time goes in v4:
time: 174 us; the launch traced here: 173 us
  waiting for transfers between devices  77 us (44%)
  starting transfers between devices  74 us (43%)
  Pallas kernels  14.5 us (8%)
  other arithmetic  4.38 us (3%)
  local copies, waits for them, and re-layouts  3.14 us (2%)
    ppermute x4, starting transfers between devices, over(): return lax.ppermute(send, 'core', [(0, 1), (1, 0)])  30.1 us
    ppermute x20, waiting for transfers between devices, ring(): return lax.ppermute(x, axis, [(i, (i + step) % n) for i in range(n)])  26.3 us
    ppermute x3, waiting for transfers between devices, flip(): return lax.ppermute(x, axis, [(i, i ^ mask) for i in range(n)])  25.5 us
    ppermute x20, starting transfers between devices, ring(): return lax.ppermute(x, axis, [(i, (i + step) % n) for i in range(n)])  24.9 us
    ppermute x4, waiting for transfers between devices, exchange(): return lax.ppermute(sent, 'zh', [(0, 1), (1, 0)])  22.3 us
    ppermute x4, starting transfers between devices, exchange(): return lax.ppermute(sent, 'zh', [(0, 1), (1, 0)])  15.7 us
    pallas_call x4, Pallas kernels, project(): pl.pallas_call(functools.partial(project_kernel, len(blocks)), out_shape=...  12.9 us
  transfers between devices with their start and end apart: 31, of which 16 were waited for; matrix products, arithmetic and copies ran while one was open for 3% of the time, Pallas kernels for 6%

profile of v4, /device:TPU:33, one launch (start us, length us, event | category | flops | bytes accessed | tf_op | source)
XLA Modules:
  0.0 173.3 jit_solution(11273583847794151365)
XLA Ops:
  0.0 1.0 fusion.13
  1.0 0.1 collective-permute-start
  1.1 3.1 %collective-permute-start.1 = (bf16[16,9216]{1,0:T(8,128)(2,1)S(1)}, bf16[16,9216]{1,0:T(8,128)(2,1)S(1)}, u32[]{:S(2)}, u32[]{:S(2)}) collective-permute-start(bf16[16,9216]{1,0:T(8,128)(2,1)S(1)} %get-tuple-element.76), channel_id=1, source_target_pairs={{0,128},{64,192},{128,0},{192,64},{1,129},{65,193},{129,1},{193,65... | collective-permute-start | bytes 884744 | tf_op jit(solution)/shard_map/z_shifts/ppermute | solution.py:26
  4.2 0.2 collective-permute-start.2
  4.4 5.9 %collective-permute-done = bf16[16,9216]{1,0:T(8,128)(2,1)S(1)} collective-permute-done((bf16[16,9216]{1,0:T(8,128)(2,1)S(1)}, bf16[16,9216]{1,0:T(8,128)(2,1)S(1)}, u32[]{:S(2)}, u32[]{:S(2)}) %collective-permute-start) | collective-permute-done | bytes 294944 | tf_op jit(solution)/shard_map/z_shifts/ppermute | solution.py:26
  10.2 12.2 %collective-permute-done.1 = bf16[16,9216]{1,0:T(8,128)(2,1)S(1)} collective-permute-done((bf16[16,9216]{1,0:T(8,128)(2,1)S(1)}, bf16[16,9216]{1,0:T(8,128)(2,1)S(1)}, u32[]{:S(2)}, u32[]{:S(2)}) %collective-permute-start.1) | collective-permute-done | bytes 294944 | tf_op jit(solution)/shard_map/z_shifts/ppermute | solution.py:26
  22.5 7.4 %collective-permute-done.2 = bf16[16,9216]{1,0:T(8,128)(2,1)S(1)} collective-permute-done((bf16[16,9216]{1,0:T(8,128)(2,1)S(1)}, bf16[16,9216]{1,0:T(8,128)(2,1)S(1)}, u32[]{:S(2)}, u32[]{:S(2)}) %collective-permute-start.2) | collective-permute-done | bytes 294944 | tf_op jit(solution)/shard_map/z_shifts/ppermute | solution.py:26
  29.8 0.1 pad_maximum_fusion
  30.0 0.0 slice-start
  30.0 1.1 slice_bitcast_fusion
  31.1 2.5 %collective-permute-start.7 = (bf16[32,9216]{1,0:T(8,128)(2,1)}, bf16[32,9216]{1,0:T(8,128)(2,1)}, u32[]{:S(2)}, u32[]{:S(2)}) collective-permute-start(bf16[32,9216]{1,0:T(8,128)(2,1)} %get-tuple-element.73), channel_id=1, source_target_pairs={{0,12},{4,0},{8,4},{12,8},{1,13},{5,1},{9,5},{13,9},{2,14},{6,2},{... | collective-permute-start | bytes 1769480 | tf_op jit(solution)/shard_map/first_axis/ppermute | solution.py:21
  33.6 0.1 pad_add_fusion.place_ref
  33.7 1.3 collective-permute-start.4
  35.0 1.5 collective-permute-start.3
  36.5 8.5 %collective-permute-done.7 = bf16[32,9216]{1,0:T(8,128)(2,1)} collective-permute-done((bf16[32,9216]{1,0:T(8,128)(2,1)}, bf16[32,9216]{1,0:T(8,128)(2,1)}, u32[]{:S(2)}, u32[]{:S(2)}) %collective-permute-start.7) | collective-permute-done | bytes 589856 | tf_op jit(solution)/shard_map/first_axis/ppermute | solution.py:21
  45.0 1.0 slice.109
  46.0 3.5 %collective-permute-start.10 = (bf16[16,9216]{1,0:T(8,128)(2,1)S(1)}, bf16[16,9216]{1,0:T(8,128)(2,1)S(1)}, u32[]{:S(2)}, u32[]{:S(2)}) collective-permute-start(bf16[16,9216]{1,0:T(8,128)(2,1)S(1)} %slice.109), channel_id=1, source_target_pairs={{0,12},{4,0},{8,4},{12,8},{1,13},{5,1},{9,5},{13,9},{2,14},{6,2},{... | collective-permute-start | bytes 884744 | tf_op jit(solution)/shard_map/first_axis/ppermute | solution.py:21
  49.5 1.0 slice.108
  50.5 0.1 collective-permute-start.9
  50.6 1.4 pad_maximum_fusion.4.refs_2_
  52.0 0.0 slice-start.1
  52.0 0.1 pad_maximum_fusion.3.refs_0_
  52.1 0.1 collective-permute-start.15
  52.2 2.7 %collective-permute-start.16 = (bf16[64,9216]{1,0:T(8,128)(2,1)S(1)}, bf16[64,9216]{1,0:T(8,128)(2,1)S(1)}, u32[]{:S(2)}, u32[]{:S(2)}) collective-permute-start(bf16[64,9216]{1,0:T(8,128)(2,1)S(1)} %pad_maximum_fusion.3.refs_0_), channel_id=1, source_target_pairs={{0,12},{4,0},{8,4},{12,8},{1,13},{5,1},{9,5},{13,9},{2,14},{6,2},{... | collective-permute-start | bytes 3538952 | tf_op jit(solution)/shard_map/second_axis/ppermute | solution.py:21
  54.9 1.4 collective-permute-start.5
  56.3 1.5 collective-permute-start.6
  57.9 0.8 collective-permute-start.17
  58.7 1.1 pad_maximum_fusion.2.refs_3_
  59.8 0.0 copy-start
  59.8 2.3 %collective-permute-done.5 = bf16[16,9216]{1,0:T(8,128)(2,1)S(1)} collective-permute-done((bf16[16,9216]{1,0:T(8,128)(2,1)S(1)}, bf16[16,9216]{1,0:T(8,128)(2,1)S(1)}, u32[]{:S(2)}, u32[]{:S(2)}) %collective-permute-start.5) | collective-permute-done | bytes 294944 | tf_op jit(solution)/shard_map/first_axis/ppermute | solution.py:21
  62.1 1.5 collective-permute-start.18
  63.6 0.1 pad_maximum_fusion.1.refs_1_
  63.7 3.2 %reduce.8 = (f32[2,2,8,8,512]{4,3,2,1,0:T(8,128)S(1)}, f32[2,2,8,8,512]{4,3,2,1,0:T(8,128)S(1)}) custom-call(s32[3]{0:T(128)S(1)} %pad_add_fusion.place_ref, bf16[64,9216]{1,0:T(8,128)(2,1)S(1)} %pad_maximum_fusion.3.refs_0_, bf16[64,9216]{1,0:T(8,128)(2,1)S(1)} %pad_maximum_fusion.1.refs_1_, bf16[64,9216]{1,0:T(8,128)(2,1)S(1)} %pad_maximum_fusion.4.refs_2_, ...), custom_call_target="tpu_custom_call" | custom-call | flops 1048576 | bytes 65536 | tf_op jit(solution)/shard_map/reduce/pallas_call | solution.py:59
  67.0 7.7 %collective-permute-start.19 = (f32[2,2,8,8,512]{4,3,2,1,0:T(8,128)S(1)}, f32[2,2,8,8,512]{4,3,2,1,0:T(8,128)S(1)}, u32[]{:S(2)}, u32[]{:S(2)}) collective-permute-start(f32[2,2,8,8,512]{4,3,2,1,0:T(8,128)S(1)} %get-tuple-element.52), channel_id=1, source_target_pairs={{0,1},{1,0},{2,3},{3,2},{4,5},{5,4},{6,7},{7,6},{8,9},{9,8},{10,11... | collective-permute-start | bytes 1572872 | tf_op jit(solution)/shard_map/reduce/ppermute | solution.py:146
  74.7 1.5 collective-permute-done.19
  76.2 6.7 %collective-permute-done.15.refs_0_ = bf16[64,9216]{1,0:T(8,128)(2,1)S(1)} collective-permute-done((bf16[64,9216]{1,0:T(8,128)(2,1)S(1)}, bf16[64,9216]{1,0:T(8,128)(2,1)S(1)}, u32[]{:S(2)}, u32[]{:S(2)}) %collective-permute-start.15) | collective-permute-done | bytes 1179680 | tf_op jit(solution)/shard_map/second_axis/ppermute | solution.py:21
  82.9 1.3 collective-permute-start.13
  84.2 2.7 %collective-permute-done.17.refs_2_ = bf16[64,9216]{1,0:T(8,128)(2,1)S(1)} collective-permute-done((bf16[64,9216]{1,0:T(8,128)(2,1)S(1)}, bf16[64,9216]{1,0:T(8,128)(2,1)S(1)}, u32[]{:S(2)}, u32[]{:S(2)}) %collective-permute-start.17) | collective-permute-done | bytes 1179680 | tf_op jit(solution)/shard_map/second_axis/ppermute | solution.py:21
  86.8 1.4 collective-permute-start.14
  88.3 4.5 %collective-permute-start.20 = (f32[2,8,8,512]{3,2,1,0:T(8,128)S(1)}, f32[2,8,8,512]{3,2,1,0:T(8,128)S(1)}, u32[]{:S(2)}, u32[]{:S(2)}) collective-permute-start(f32[2,8,8,512]{3,2,1,0:T(8,128)S(1)} %fusion.7), channel_id=1, source_target_pairs={{0,2},{2,0},{1,3},{3,1},{4,6},{6,4},{5,7},{7,5},{8,10},{10,8},{9,1... | collective-permute-start | bytes 786440 | tf_op jit(solution)/shard_map/reduce/ppermute | solution.py:143
  92.8 3.2 %reduce.9 = (f32[2,2,8,8,512]{4,3,2,1,0:T(8,128)S(1)}, f32[2,2,8,8,512]{4,3,2,1,0:T(8,128)S(1)}) custom-call(s32[3]{0:T(128)S(1)} %pad_add_fusion.place_ref, bf16[64,9216]{1,0:T(8,128)(2,1)S(1)} %collective-permute-done.15.refs_0_, bf16[64,9216]{1,0:T(8,128)(2,1)S(1)} %collective-permute-done.16.refs_1_, ...), custom_call_target="tpu_custom_call" | custom-call | flops 1048576 | bytes 65536 | tf_op jit(solution)/shard_map/reduce/pallas_call | solution.py:59
  96.0 1.5 collective-permute-done.20
  97.5 10.1 %collective-permute-start.25 = (f32[2,2,8,8,512]{4,3,2,1,0:T(8,128)S(1)}, f32[2,2,8,8,512]{4,3,2,1,0:T(8,128)S(1)}, u32[]{:S(2)}, u32[]{:S(2)}) collective-permute-start(f32[2,2,8,8,512]{4,3,2,1,0:T(8,128)S(1)} %get-tuple-element.61), channel_id=1, source_target_pairs={{0,1},{1,0},{2,3},{3,2},{4,5},{5,4},{6,7},{7,6},{8,9},{9,8},{10,11... | collective-permute-start | bytes 1572872 | tf_op jit(solution)/shard_map/reduce/ppermute | solution.py:146
  107.6 0.1 fusion.9
  107.7 0.5 collective-permute-done.11.refs_0_
  108.2 4.0 %collective-permute-done.13.refs_2_ = bf16[64,9216]{1,0:T(8,128)(2,1)S(1)} collective-permute-done((bf16[64,9216]{1,0:T(8,128)(2,1)S(1)}, bf16[64,9216]{1,0:T(8,128)(2,1)S(1)}, u32[]{:S(2)}, u32[]{:S(2)}) %collective-permute-start.13) | collective-permute-done | bytes 1179680 | tf_op jit(solution)/shard_map/second_axis/ppermute | solution.py:21
  112.2 2.7 %collective-permute-start.22 = (bf16[64,9216]{1,0:T(8,128)(2,1)S(1)}, bf16[64,9216]{1,0:T(8,128)(2,1)S(1)}, u32[]{:S(2)}, u32[]{:S(2)}) collective-permute-start(bf16[64,9216]{1,0:T(8,128)(2,1)S(1)} %collective-permute-done.12.refs_1_), channel_id=1, source_target_pairs={{0,12},{4,0},{8,4},{12,8},{1,13},{5,1},{9,5},{13,9},{2,14},{6,2},{... | collective-permute-start | bytes 3538952 | tf_op jit(solution)/shard_map/second_axis/ppermute | solution.py:21
  114.9 0.9 collective-permute-start.23
  115.8 1.8 %collective-permute-start.24 = (bf16[64,9216]{1,0:T(8,128)(2,1)S(1)}, bf16[64,9216]{1,0:T(8,128)(2,1)S(1)}, u32[]{:S(2)}, u32[]{:S(2)}) collective-permute-start(bf16[64,9216]{1,0:T(8,128)(2,1)S(1)} %collective-permute-done.14.refs_3_), channel_id=1, source_target_pairs={{0,48},{16,0},{32,16},{48,32},{1,49},{17,1},{33,17},{49,33},{2,50}... | collective-permute-start | bytes 3538952 | tf_op jit(solution)/shard_map/second_axis/ppermute | solution.py:21
  117.6 4.6 %collective-permute-start.26 = (f32[2,8,8,512]{3,2,1,0:T(8,128)S(1)}, f32[2,8,8,512]{3,2,1,0:T(8,128)S(1)}, u32[]{:S(2)}, u32[]{:S(2)}) collective-permute-start(f32[2,8,8,512]{3,2,1,0:T(8,128)S(1)} %fusion.4), channel_id=1, source_target_pairs={{0,2},{2,0},{1,3},{3,1},{4,6},{6,4},{5,7},{7,5},{8,10},{10,8},{9,1... | collective-permute-start | bytes 786440 | tf_op jit(solution)/shard_map/reduce/ppermute | solution.py:143
  122.2 3.2 %reduce.10 = (f32[2,2,8,8,512]{4,3,2,1,0:T(8,128)S(1)}, f32[2,2,8,8,512]{4,3,2,1,0:T(8,128)S(1)}) custom-call(s32[3]{0:T(128)S(1)} %pad_add_fusion.place_ref, bf16[64,9216]{1,0:T(8,128)(2,1)S(1)} %collective-permute-done.11.refs_0_, bf16[64,9216]{1,0:T(8,128)(2,1)S(1)} %collective-permute-done.12.refs_1_, ...), custom_call_target="tpu_custom_call" | custom-call | flops 1048576 | bytes 65536 | tf_op jit(solution)/shard_map/reduce/pallas_call | solution.py:59
  125.4 3.6 %collective-permute-done.26 = f32[2,8,8,512]{3,2,1,0:T(8,128)S(1)} collective-permute-done((f32[2,8,8,512]{3,2,1,0:T(8,128)S(1)}, f32[2,8,8,512]{3,2,1,0:T(8,128)S(1)}, u32[]{:S(2)}, u32[]{:S(2)}) %collective-permute-start.26) | collective-permute-done | bytes 262176 | tf_op jit(solution)/shard_map/reduce/ppermute | solution.py:143
  129.0 5.8 %collective-permute-start.27 = (f32[2,2,8,8,512]{4,3,2,1,0:T(8,128)S(1)}, f32[2,2,8,8,512]{4,3,2,1,0:T(8,128)S(1)}, u32[]{:S(2)}, u32[]{:S(2)}) collective-permute-start(f32[2,2,8,8,512]{4,3,2,1,0:T(8,128)S(1)} %get-tuple-element.65), channel_id=1, source_target_pairs={{0,1},{1,0},{2,3},{3,2},{4,5},{5,4},{6,7},{7,6},{8,9},{9,8},{10,11... | collective-permute-start | bytes 1572872 | tf_op jit(solution)/shard_map/reduce/ppermute | solution.py:146
  134.8 0.1 fusion.6
  134.9 1.4 collective-permute-done.27
  136.4 1.6 collective-permute-done.23.refs_2_
  138.0 3.2 %reduce.11 = (f32[2,2,8,8,512]{4,3,2,1,0:T(8,128)S(1)}, f32[2,2,8,8,512]{4,3,2,1,0:T(8,128)S(1)}) custom-call(s32[3]{0:T(128)S(1)} %pad_add_fusion.place_ref, bf16[64,9216]{1,0:T(8,128)(2,1)S(1)} %collective-permute-done.21.refs_0_, bf16[64,9216]{1,0:T(8,128)(2,1)S(1)} %collective-permute-done.22.refs_1_, ...), custom_call_target="tpu_custom_call" | custom-call | flops 1048576 | bytes 65536 | tf_op jit(solution)/shard_map/reduce/pallas_call | solution.py:59
  141.2 6.6 %collective-permute-start.29 = (f32[2,2,8,8,512]{4,3,2,1,0:T(8,128)S(1)}, f32[2,2,8,8,512]{4,3,2,1,0:T(8,128)S(1)}, u32[]{:S(2)}, u32[]{:S(2)}) collective-permute-start(f32[2,2,8,8,512]{4,3,2,1,0:T(8,128)S(1)} %get-tuple-element.72), channel_id=1, source_target_pairs={{0,1},{1,0},{2,3},{3,2},{4,5},{5,4},{6,7},{7,6},{8,9},{9,8},{10,11... | collective-permute-start | bytes 1572872 | tf_op jit(solution)/shard_map/reduce/ppermute | solution.py:146
  147.8 5.0 %collective-permute-start.28 = (f32[2,8,8,512]{3,2,1,0:T(8,128)S(1)}, f32[2,8,8,512]{3,2,1,0:T(8,128)S(1)}, u32[]{:S(2)}, u32[]{:S(2)}) collective-permute-start(f32[2,8,8,512]{3,2,1,0:T(8,128)S(1)} %fusion.3), channel_id=1, source_target_pairs={{0,2},{2,0},{1,3},{3,1},{4,6},{6,4},{5,7},{7,5},{8,10},{10,8},{9,1... | collective-permute-start | bytes 786440 | tf_op jit(solution)/shard_map/reduce/ppermute | solution.py:143
  152.8 1.6 collective-permute-start.30
  154.4 11.7 %collective-permute-done.28 = f32[2,8,8,512]{3,2,1,0:T(8,128)S(1)} collective-permute-done((f32[2,8,8,512]{3,2,1,0:T(8,128)S(1)}, f32[2,8,8,512]{3,2,1,0:T(8,128)S(1)}, u32[]{:S(2)}, u32[]{:S(2)}) %collective-permute-start.28) | collective-permute-done | bytes 262176 | tf_op jit(solution)/shard_map/reduce/ppermute | solution.py:143
  166.2 0.1 fusion.2
  166.3 5.5 %collective-permute-done.30.back_ref = f32[2,8,8,512]{3,2,1,0:T(8,128)S(1)} collective-permute-done((f32[2,8,8,512]{3,2,1,0:T(8,128)S(1)}, f32[2,8,8,512]{3,2,1,0:T(8,128)S(1)}, u32[]{:S(2)}, u32[]{:S(2)}) %collective-permute-start.30) | collective-permute-done | bytes 262176 | tf_op jit(solution)/shard_map/reduce/ppermute | solution.py:143
  171.8 1.6 reduce.12
  (34 shorter events, 0.4 us)
Async XLA Ops:
  1.0 9.2 %collective-permute-start = (bf16[16,9216]{1,0:T(8,128)(2,1)S(1)}, bf16[16,9216]{1,0:T(8,128)(2,1)S(1)}, u32[]{:S(2)}, u32[]{:S(2)}) collective-permute-start(bf16[16,9216]{1,0:T(8,128)(2,1)S(1)} %get-tuple-element.76), channel_id=1, source_target_pairs={{0,64},{64,0},{128,192},{192,128},{1,65},{65,1},{129,193},{193,129... | collective-permute-start | bytes 884744 | tf_op jit(solution)/shard_map/z_shifts/ppermute | solution.py:26
  1.1 21.3 %collective-permute-start.1 = (bf16[16,9216]{1,0:T(8,128)(2,1)S(1)}, bf16[16,9216]{1,0:T(8,128)(2,1)S(1)}, u32[]{:S(2)}, u32[]{:S(2)}) collective-permute-start(bf16[16,9216]{1,0:T(8,128)(2,1)S(1)} %get-tuple-element.76), channel_id=1, source_target_pairs={{0,128},{64,192},{128,0},{192,64},{1,129},{65,193},{129,1},{193,65... | collective-permute-start | bytes 884744 | tf_op jit(solution)/shard_map/z_shifts/ppermute | solution.py:26
  4.2 25.6 %collective-permute-start.2 = (bf16[16,9216]{1,0:T(8,128)(2,1)S(1)}, bf16[16,9216]{1,0:T(8,128)(2,1)S(1)}, u32[]{:S(2)}, u32[]{:S(2)}) collective-permute-start(bf16[16,9216]{1,0:T(8,128)(2,1)S(1)} %get-tuple-element.76), channel_id=1, source_target_pairs={{0,192},{64,128},{128,64},{192,0},{1,193},{65,129},{129,65},{193,1... | collective-permute-start | bytes 884744 | tf_op jit(solution)/shard_map/z_shifts/ppermute | solution.py:26
  30.0 33.7 %slice-start = ((s8[7340032]{0:T(1024)(128)(4,1)}), s8[3145728]{0:T(1024)(128)(4,1)S(1)}, s32[]{:S(2)}) async-start(s8[7340032]{0:T(1024)(128)(4,1)} %bitcast.34), calls=%async_computation | async-start | bytes 6291456
  31.1 13.9 %collective-permute-start.7 = (bf16[32,9216]{1,0:T(8,128)(2,1)}, bf16[32,9216]{1,0:T(8,128)(2,1)}, u32[]{:S(2)}, u32[]{:S(2)}) collective-permute-start(bf16[32,9216]{1,0:T(8,128)(2,1)} %get-tuple-element.73), channel_id=1, source_target_pairs={{0,12},{4,0},{8,4},{12,8},{1,13},{5,1},{9,5},{13,9},{2,14},{6,2},{... | collective-permute-start | bytes 1769480 | tf_op jit(solution)/shard_map/first_axis/ppermute | solution.py:21
  33.6 15.9 %collective-permute-start.8 = (bf16[32,9216]{1,0:T(8,128)(2,1)}, bf16[32,9216]{1,0:T(8,128)(2,1)}, u32[]{:S(2)}, u32[]{:S(2)}) collective-permute-start(bf16[32,9216]{1,0:T(8,128)(2,1)} %get-tuple-element.73), channel_id=1, source_target_pairs={{0,4},{4,8},{8,12},{12,0},{1,5},{5,9},{9,13},{13,1},{2,6},{6,10},{... | collective-permute-start | bytes 1769480 | tf_op jit(solution)/shard_map/first_axis/ppermute | solution.py:21
  33.7 18.3 %collective-permute-start.4 = (bf16[32,9216]{1,0:T(8,128)(2,1)}, bf16[32,9216]{1,0:T(8,128)(2,1)S(1)}, u32[]{:S(2)}, u32[]{:S(2)}) collective-permute-start(bf16[32,9216]{1,0:T(8,128)(2,1)} %get-tuple-element.74), channel_id=1, source_target_pairs={{0,16},{16,32},{32,48},{48,0},{1,17},{17,33},{33,49},{49,1},{2,18}... | collective-permute-start | bytes 1769480 | tf_op jit(solution)/shard_map/first_axis/ppermute | solution.py:21
  35.0 19.9 %collective-permute-start.3 = (bf16[32,9216]{1,0:T(8,128)(2,1)}, bf16[32,9216]{1,0:T(8,128)(2,1)S(1)}, u32[]{:S(2)}, u32[]{:S(2)}) collective-permute-start(bf16[32,9216]{1,0:T(8,128)(2,1)} %get-tuple-element.74), channel_id=1, source_target_pairs={{0,48},{16,0},{32,16},{48,32},{1,49},{17,1},{33,17},{49,33},{2,50}... | collective-permute-start | bytes 1769480 | tf_op jit(solution)/shard_map/first_axis/ppermute | solution.py:21
  46.0 10.3 %collective-permute-start.10 = (bf16[16,9216]{1,0:T(8,128)(2,1)S(1)}, bf16[16,9216]{1,0:T(8,128)(2,1)S(1)}, u32[]{:S(2)}, u32[]{:S(2)}) collective-permute-start(bf16[16,9216]{1,0:T(8,128)(2,1)S(1)} %slice.109), channel_id=1, source_target_pairs={{0,12},{4,0},{8,4},{12,8},{1,13},{5,1},{9,5},{13,9},{2,14},{6,2},{... | collective-permute-start | bytes 884744 | tf_op jit(solution)/shard_map/first_axis/ppermute | solution.py:21
  50.5 1.5 copy-start.1
  50.5 7.4 %collective-permute-start.9 = (bf16[16,9216]{1,0:T(8,128)(2,1)S(1)}, bf16[16,9216]{1,0:T(8,128)(2,1)S(1)}, u32[]{:S(2)}, u32[]{:S(2)}) collective-permute-start(bf16[16,9216]{1,0:T(8,128)(2,1)S(1)} %slice.108), channel_id=1, source_target_pairs={{0,4},{4,8},{8,12},{12,0},{1,5},{5,9},{9,13},{13,1},{2,6},{6,10},{... | collective-permute-start | bytes 884744 | tf_op jit(solution)/shard_map/first_axis/ppermute | solution.py:21
  52.0 11.7 %slice-start.1 = ((s8[7340032]{0:T(1024)(128)(4,1)}), s8[4194304]{0:T(1024)(128)(4,1)S(1)}, s32[]{:S(2)}) async-start(s8[7340032]{0:T(1024)(128)(4,1)} %bitcast.34), calls=%async_computation.1 | async-start | bytes 8388608
  52.1 30.8 %collective-permute-start.15 = (bf16[64,9216]{1,0:T(8,128)(2,1)S(1)}, bf16[64,9216]{1,0:T(8,128)(2,1)S(1)}, u32[]{:S(2)}, u32[]{:S(2)}) collective-permute-start(bf16[64,9216]{1,0:T(8,128)(2,1)S(1)} %pad_maximum_fusion.3.refs_0_), channel_id=1, source_target_pairs={{0,4},{4,8},{8,12},{12,0},{1,5},{5,9},{9,13},{13,1},{2,6},{6,10},{... | collective-permute-start | bytes 3538952 | tf_op jit(solution)/shard_map/second_axis/ppermute | solution.py:21
  52.2 30.7 %collective-permute-start.16 = (bf16[64,9216]{1,0:T(8,128)(2,1)S(1)}, bf16[64,9216]{1,0:T(8,128)(2,1)S(1)}, u32[]{:S(2)}, u32[]{:S(2)}) collective-permute-start(bf16[64,9216]{1,0:T(8,128)(2,1)S(1)} %pad_maximum_fusion.3.refs_0_), channel_id=1, source_target_pairs={{0,12},{4,0},{8,4},{12,8},{1,13},{5,1},{9,5},{13,9},{2,14},{6,2},{... | collective-permute-start | bytes 3538952 | tf_op jit(solution)/shard_map/second_axis/ppermute | solution.py:21
  54.9 7.2 %collective-permute-start.5 = (bf16[16,9216]{1,0:T(8,128)(2,1)S(1)}, bf16[16,9216]{1,0:T(8,128)(2,1)S(1)}, u32[]{:S(2)}, u32[]{:S(2)}) collective-permute-start(bf16[16,9216]{1,0:T(8,128)(2,1)S(1)} %slice.105), channel_id=1, source_target_pairs={{0,16},{16,32},{32,48},{48,0},{1,17},{17,33},{33,49},{49,1},{2,18}... | collective-permute-start | bytes 884744 | tf_op jit(solution)/shard_map/first_axis/ppermute | solution.py:21
  56.3 7.3 %collective-permute-start.6 = (bf16[16,9216]{1,0:T(8,128)(2,1)S(1)}, bf16[16,9216]{1,0:T(8,128)(2,1)S(1)}, u32[]{:S(2)}, u32[]{:S(2)}) collective-permute-start(bf16[16,9216]{1,0:T(8,128)(2,1)S(1)} %slice.106), channel_id=1, source_target_pairs={{0,48},{16,0},{32,16},{48,32},{1,49},{17,1},{33,17},{49,33},{2,50}... | collective-permute-start | bytes 884744 | tf_op jit(solution)/shard_map/first_axis/ppermute | solution.py:21
  57.9 29.0 %collective-permute-start.17 = (bf16[64,9216]{1,0:T(8,128)(2,1)S(1)}, bf16[64,9216]{1,0:T(8,128)(2,1)S(1)}, u32[]{:S(2)}, u32[]{:S(2)}) collective-permute-start(bf16[64,9216]{1,0:T(8,128)(2,1)S(1)} %pad_maximum_fusion.4.refs_2_), channel_id=1, source_target_pairs={{0,16},{16,32},{32,48},{48,0},{1,17},{17,33},{33,49},{49,1},{2,18}... | collective-permute-start | bytes 3538952 | tf_op jit(solution)/shard_map/second_axis/ppermute | solution.py:21
  59.8 3.9 %copy-start = (bf16[512,2048]{1,0:T(8,128)(2,1)S(1)}, bf16[512,2048]{1,0:T(8,128)(2,1)}, u32[]{:S(2)}) copy-start(bf16[512,2048]{1,0:T(8,128)(2,1)} %refs_5_.7) | copy-start | bytes 6291460
  62.1 26.2 %collective-permute-start.18 = (bf16[64,9216]{1,0:T(8,128)(2,1)S(1)}, bf16[64,9216]{1,0:T(8,128)(2,1)S(1)}, u32[]{:S(2)}, u32[]{:S(2)}) collective-permute-start(bf16[64,9216]{1,0:T(8,128)(2,1)S(1)} %pad_maximum_fusion.4.refs_2_), channel_id=1, source_target_pairs={{0,48},{16,0},{32,16},{48,32},{1,49},{17,1},{33,17},{49,33},{2,50}... | collective-permute-start | bytes 3538952 | tf_op jit(solution)/shard_map/second_axis/ppermute | solution.py:21
  67.0 9.2 %collective-permute-start.19 = (f32[2,2,8,8,512]{4,3,2,1,0:T(8,128)S(1)}, f32[2,2,8,8,512]{4,3,2,1,0:T(8,128)S(1)}, u32[]{:S(2)}, u32[]{:S(2)}) collective-permute-start(f32[2,2,8,8,512]{4,3,2,1,0:T(8,128)S(1)} %get-tuple-element.52), channel_id=1, source_target_pairs={{0,1},{1,0},{2,3},{3,2},{4,5},{5,4},{6,7},{7,6},{8,9},{9,8},{10,11... | collective-permute-start | bytes 1572872 | tf_op jit(solution)/shard_map/reduce/ppermute | solution.py:146
  76.2 31.9 %collective-permute-start.11 = (bf16[64,9216]{1,0:T(8,128)(2,1)S(1)}, bf16[64,9216]{1,0:T(8,128)(2,1)S(1)}, u32[]{:S(2)}, u32[]{:S(2)}) collective-permute-start(bf16[64,9216]{1,0:T(8,128)(2,1)S(1)} %pad_maximum_fusion.1.refs_1_), channel_id=1, source_target_pairs={{0,4},{4,8},{8,12},{12,0},{1,5},{5,9},{9,13},{13,1},{2,6},{6,10},{... | collective-permute-start | bytes 3538952 | tf_op jit(solution)/shard_map/second_axis/ppermute | solution.py:21
  82.9 25.3 %collective-permute-start.12 = (bf16[64,9216]{1,0:T(8,128)(2,1)S(1)}, bf16[64,9216]{1,0:T(8,128)(2,1)S(1)}, u32[]{:S(2)}, u32[]{:S(2)}) collective-permute-start(bf16[64,9216]{1,0:T(8,128)(2,1)S(1)} %pad_maximum_fusion.1.refs_1_), channel_id=1, source_target_pairs={{0,12},{4,0},{8,4},{12,8},{1,13},{5,1},{9,5},{13,9},{2,14},{6,2},{... | collective-permute-start | bytes 3538952 | tf_op jit(solution)/shard_map/second_axis/ppermute | solution.py:21
  82.9 29.3 %collective-permute-start.13 = (bf16[64,9216]{1,0:T(8,128)(2,1)S(1)}, bf16[64,9216]{1,0:T(8,128)(2,1)S(1)}, u32[]{:S(2)}, u32[]{:S(2)}) collective-permute-start(bf16[64,9216]{1,0:T(8,128)(2,1)S(1)} %pad_maximum_fusion.2.refs_3_), channel_id=1, source_target_pairs={{0,16},{16,32},{32,48},{48,0},{1,17},{17,33},{33,49},{49,1},{2,18}... | collective-permute-start | bytes 3538952 | tf_op jit(solution)/shard_map/second_axis/ppermute | solution.py:21
  86.8 25.4 %collective-permute-start.14 = (bf16[64,9216]{1,0:T(8,128)(2,1)S(1)}, bf16[64,9216]{1,0:T(8,128)(2,1)S(1)}, u32[]{:S(2)}, u32[]{:S(2)}) collective-permute-start(bf16[64,9216]{1,0:T(8,128)(2,1)S(1)} %pad_maximum_fusion.2.refs_3_), channel_id=1, source_target_pairs={{0,48},{16,0},{32,16},{48,32},{1,49},{17,1},{33,17},{49,33},{2,50}... | collective-permute-start | bytes 3538952 | tf_op jit(solution)/shard_map/second_axis/ppermute | solution.py:21
  88.3 9.2 %collective-permute-start.20 = (f32[2,8,8,512]{3,2,1,0:T(8,128)S(1)}, f32[2,8,8,512]{3,2,1,0:T(8,128)S(1)}, u32[]{:S(2)}, u32[]{:S(2)}) collective-permute-start(f32[2,8,8,512]{3,2,1,0:T(8,128)S(1)} %fusion.7), channel_id=1, source_target_pairs={{0,2},{2,0},{1,3},{3,1},{4,6},{6,4},{5,7},{7,5},{8,10},{10,8},{9,1... | collective-permute-start | bytes 786440 | tf_op jit(solution)/shard_map/reduce/ppermute | solution.py:143
  97.5 20.1 %collective-permute-start.25 = (f32[2,2,8,8,512]{4,3,2,1,0:T(8,128)S(1)}, f32[2,2,8,8,512]{4,3,2,1,0:T(8,128)S(1)}, u32[]{:S(2)}, u32[]{:S(2)}) collective-permute-start(f32[2,2,8,8,512]{4,3,2,1,0:T(8,128)S(1)} %get-tuple-element.61), channel_id=1, source_target_pairs={{0,1},{1,0},{2,3},{3,2},{4,5},{5,4},{6,7},{7,6},{8,9},{9,8},{10,11... | collective-permute-start | bytes 1572872 | tf_op jit(solution)/shard_map/reduce/ppermute | solution.py:146
  112.2 24.2 %collective-permute-start.21 = (bf16[64,9216]{1,0:T(8,128)(2,1)S(1)}, bf16[64,9216]{1,0:T(8,128)(2,1)S(1)}, u32[]{:S(2)}, u32[]{:S(2)}) collective-permute-start(bf16[64,9216]{1,0:T(8,128)(2,1)S(1)} %collective-permute-done.15.refs_0_), channel_id=1, source_target_pairs={{0,4},{4,8},{8,12},{12,0},{1,5},{5,9},{9,13},{13,1},{2,6},{6,10},{... | collective-permute-start | bytes 3538952 | tf_op jit(solution)/shard_map/second_axis/ppermute | solution.py:21
  112.2 24.2 %collective-permute-start.22 = (bf16[64,9216]{1,0:T(8,128)(2,1)S(1)}, bf16[64,9216]{1,0:T(8,128)(2,1)S(1)}, u32[]{:S(2)}, u32[]{:S(2)}) collective-permute-start(bf16[64,9216]{1,0:T(8,128)(2,1)S(1)} %collective-permute-done.12.refs_1_), channel_id=1, source_target_pairs={{0,12},{4,0},{8,4},{12,8},{1,13},{5,1},{9,5},{13,9},{2,14},{6,2},{... | collective-permute-start | bytes 3538952 | tf_op jit(solution)/shard_map/second_axis/ppermute | solution.py:21
  114.9 23.1 %collective-permute-start.23 = (bf16[64,9216]{1,0:T(8,128)(2,1)S(1)}, bf16[64,9216]{1,0:T(8,128)(2,1)S(1)}, u32[]{:S(2)}, u32[]{:S(2)}) collective-permute-start(bf16[64,9216]{1,0:T(8,128)(2,1)S(1)} %collective-permute-done.17.refs_2_), channel_id=1, source_target_pairs={{0,16},{16,32},{32,48},{48,0},{1,17},{17,33},{33,49},{49,1},{2,18}... | collective-permute-start | bytes 3538952 | tf_op jit(solution)/shard_map/second_axis/ppermute | solution.py:21
  115.8 22.2 %collective-permute-start.24 = (bf16[64,9216]{1,0:T(8,128)(2,1)S(1)}, bf16[64,9216]{1,0:T(8,128)(2,1)S(1)}, u32[]{:S(2)}, u32[]{:S(2)}) collective-permute-start(bf16[64,9216]{1,0:T(8,128)(2,1)S(1)} %collective-permute-done.14.refs_3_), channel_id=1, source_target_pairs={{0,48},{16,0},{32,16},{48,32},{1,49},{17,1},{33,17},{49,33},{2,50}... | collective-permute-start | bytes 3538952 | tf_op jit(solution)/shard_map/second_axis/ppermute | solution.py:21
  117.6 11.4 %collective-permute-start.26 = (f32[2,8,8,512]{3,2,1,0:T(8,128)S(1)}, f32[2,8,8,512]{3,2,1,0:T(8,128)S(1)}, u32[]{:S(2)}, u32[]{:S(2)}) collective-permute-start(f32[2,8,8,512]{3,2,1,0:T(8,128)S(1)} %fusion.4), channel_id=1, source_target_pairs={{0,2},{2,0},{1,3},{3,1},{4,6},{6,4},{5,7},{7,5},{8,10},{10,8},{9,1... | collective-permute-start | bytes 786440 | tf_op jit(solution)/shard_map/reduce/ppermute | solution.py:143
  129.0 7.3 %collective-permute-start.27 = (f32[2,2,8,8,512]{4,3,2,1,0:T(8,128)S(1)}, f32[2,2,8,8,512]{4,3,2,1,0:T(8,128)S(1)}, u32[]{:S(2)}, u32[]{:S(2)}) collective-permute-start(f32[2,2,8,8,512]{4,3,2,1,0:T(8,128)S(1)} %get-tuple-element.65), channel_id=1, source_target_pairs={{0,1},{1,0},{2,3},{3,2},{4,5},{5,4},{6,7},{7,6},{8,9},{9,8},{10,11... | collective-permute-start | bytes 1572872 | tf_op jit(solution)/shard_map/reduce/ppermute | solution.py:146
  141.2 11.6 %collective-permute-start.29 = (f32[2,2,8,8,512]{4,3,2,1,0:T(8,128)S(1)}, f32[2,2,8,8,512]{4,3,2,1,0:T(8,128)S(1)}, u32[]{:S(2)}, u32[]{:S(2)}) collective-permute-start(f32[2,2,8,8,512]{4,3,2,1,0:T(8,128)S(1)} %get-tuple-element.72), channel_id=1, source_target_pairs={{0,1},{1,0},{2,3},{3,2},{4,5},{5,4},{6,7},{7,6},{8,9},{9,8},{10,11... | collective-permute-start | bytes 1572872 | tf_op jit(solution)/shard_map/reduce/ppermute | solution.py:146
  147.8 18.4 %collective-permute-start.28 = (f32[2,8,8,512]{3,2,1,0:T(8,128)S(1)}, f32[2,8,8,512]{3,2,1,0:T(8,128)S(1)}, u32[]{:S(2)}, u32[]{:S(2)}) collective-permute-start(f32[2,8,8,512]{3,2,1,0:T(8,128)S(1)} %fusion.3), channel_id=1, source_target_pairs={{0,2},{2,0},{1,3},{3,1},{4,6},{6,4},{5,7},{7,5},{8,10},{10,8},{9,1... | collective-permute-start | bytes 786440 | tf_op jit(solution)/shard_map/reduce/ppermute | solution.py:143
  152.8 19.0 %collective-permute-start.30 = (f32[2,8,8,512]{3,2,1,0:T(8,128)S(1)}, f32[2,8,8,512]{3,2,1,0:T(8,128)S(1)}, u32[]{:S(2)}, u32[]{:S(2)}) collective-permute-start(f32[2,8,8,512]{3,2,1,0:T(8,128)S(1)} %fusion), channel_id=1, source_target_pairs={{0,2},{2,0},{1,3},{3,1},{4,6},{6,4},{5,7},{7,5},{8,10},{10,8},{9,1... | collective-permute-start | bytes 786440 | tf_op jit(solution)/shard_map/reduce/ppermute | solution.py:143

commit v5 on v4

--- a/solution.py
+++ b/solution.py
@@ -127,14 +127,11 @@
     own = jnp.concatenate([out_factors.T, in_factors.T], axis=1)
     features = own.shape[1]
     with jax.named_scope("z_shifts"):
-        stacked = jnp.stack([own] + [flip(own, "zl", k) for k in (1, 2, 3)])
-
-    def first(rows, axis):
-        block = rows.reshape(GROUPS * RANK, features)
-        half = block.shape[0] // 2
-        before, after = ring(block, axis, 1), ring(block, axis, -1)
-        far = ring(before[:half], axis, 1), ring(after[half:], axis, -1)
-        return jnp.concatenate([block, before]), jnp.concatenate([after, *far])
+        shifts = [own] + [flip(own, "zl", k) for k in (1, 2, 3)]
+        pairs = [jnp.stack(shifts[k : k + 2]) for k in (0, 2)]
+        pieces = [
+            [p[:, at : at + RANK].reshape(2 * RANK, features) for p in pairs] for at in (0, RANK)
+        ]
 
     def both(block, axis):
         return ring(block, axis, 1), ring(block, axis, -1)
@@ -153,9 +150,18 @@
         keep, send = project(blocks, train_grads, train_acts, place)
         return keep, over(send)
     with jax.named_scope("first_axis"):
-        lo_a, hi_a = first(stacked[:, :RANK], "y")
-        lo_b, hi_b = first(stacked[:, RANK:], "x")
-        lo_a, lo_b = lax.optimization_barrier((lo_a, lo_b))
+        (near_a, rest_a), (near_b, rest_b) = pieces
+        around_a, around_b = both(near_a, "y"), both(near_b, "x")
+        around_a, around_b, rest_a, rest_b = lax.optimization_barrier(
+            (around_a, around_b, rest_a, rest_b)
+        )
+        beyond_a, beyond_b = both(rest_a, "y"), both(rest_b, "x")
+        far_a = ring(around_a[0], "y", 1), ring(beyond_a[1], "y", -1)
+        far_b = ring(around_b[0], "x", 1), ring(beyond_b[1], "x", -1)
+        lo_a = jnp.concatenate([near_a, rest_a, around_a[0], beyond_a[0]])
+        lo_b = jnp.concatenate([near_b, rest_b, around_b[0], beyond_b[0]])
+        hi_a = jnp.concatenate([around_a[1], beyond_a[1], *far_a])
+        hi_b = jnp.concatenate([around_b[1], beyond_b[1], *far_b])
         hi_a, hi_b = lax.optimization_barrier((hi_a, hi_b))
     with jax.named_scope("second_axis"):
         lo = both(lo_a, "x") + both(lo_b, "y")

time: 174 us -> 183 us (1.052)
  waiting for transfers between devices: 77 us -> 90.6 us
  local copies, waits for them, and re-layouts: 3.14 us -> 0.76 us
    ppermute x20 -> x24, waiting for transfers between devices: 26.3 us -> 37.4 us  [ring(): return lax.ppermute(x, axis, [(i, (i + step) % n) for i in range(n)])]
    ppermute x4, waiting for transfers between devices: 22.3 us -> 32.8 us  [exchange(): return lax.ppermute(sent, 'zh', [(0, 1), (1, 0)])]
    ppermute x4, starting transfers between devices: 30.1 us -> 20.3 us  [over(): return lax.ppermute(send, 'core', [(0, 1), (1, 0)])]
    ppermute x3, waiting for transfers between devices: 25.5 us -> 17.4 us  [flip(): return lax.ppermute(x, axis, [(i, i ^ mask) for i in range(n)])]
    ppermute x20 -> x24, starting transfers between devices: 24.9 us -> 32.9 us  [ring(): return lax.ppermute(x, axis, [(i, (i + step) % n) for i in range(n)])]
    slice x4 -> x0, local copies, waits for them, and re-layouts: 2 us -> none  [first(): far = (ring(before[:half], axis, 1), ring(after[half:], axis, -1))]
  transfers between devices with their start and end apart: 31 -> 35, of which waited for: 16 -> 18; matrix products, arithmetic and copies ran while one was open for 3% -> 2% of each run, Pallas kernels for 6% -> 5%
where the time goes in v5:
time: 183 us
  waiting for transfers between devices  90.6 us (50%)
  starting transfers between devices  72.6 us (40%)
  Pallas kernels  14.5 us (8%)
  other arithmetic  4.18 us (2%)
    ppermute x24, waiting for transfers between devices, ring(): return lax.ppermute(x, axis, [(i, (i + step) % n) for i in range(n)])  37.4 us
    ppermute x24, starting transfers between devices, ring(): return lax.ppermute(x, axis, [(i, (i + step) % n) for i in range(n)])  32.9 us
    ppermute x4, waiting for transfers between devices, exchange(): return lax.ppermute(sent, 'zh', [(0, 1), (1, 0)])  32.8 us
    ppermute x4, starting transfers between devices, over(): return lax.ppermute(send, 'core', [(0, 1), (1, 0)])  20.3 us
    ppermute x3, waiting for transfers between devices, flip(): return lax.ppermute(x, axis, [(i, i ^ mask) for i in range(n)])  17.4 us
    ppermute x4, starting transfers between devices, exchange(): return lax.ppermute(sent, 'zh', [(0, 1), (1, 0)])  15.8 us
    pallas_call x4, Pallas kernels, project(): pl.pallas_call(functools.partial(project_kernel, len(blocks)), out_shape=...  12.9 us
  transfers between devices with their start and end apart: 35, of which 18 were waited for; matrix products, arithmetic and copies ran while one was open for 2% of the time, Pallas kernels for 5%

profile of v5, /device:TPU:33, one launch (start us, length us, event | category | flops | bytes accessed | tf_op | source)
XLA Modules:
  0.0 182.9 jit_solution(5077741917377776395)
XLA Ops:
  0.0 1.0 pad_maximum_fusion.6
  1.0 0.1 collective-permute-start
  1.1 3.3 %collective-permute-start.6 = (bf16[16,9216]{1,0:T(8,128)(2,1)S(1)}, bf16[16,9216]{1,0:T(8,128)(2,1)S(1)}, u32[]{:S(2)}, u32[]{:S(2)}) collective-permute-start(bf16[16,9216]{1,0:T(8,128)(2,1)S(1)} %get-tuple-element.85), channel_id=1, source_target_pairs={{0,192},{64,128},{128,64},{192,0},{1,193},{65,129},{129,65},{193,1... | collective-permute-start | bytes 884744 | tf_op jit(solution)/shard_map/z_shifts/ppermute | solution.py:26
  4.4 0.3 collective-permute-start.5
  4.7 4.3 %collective-permute-done = bf16[16,9216]{1,0:T(8,128)(2,1)S(1)} collective-permute-done((bf16[16,9216]{1,0:T(8,128)(2,1)S(1)}, bf16[16,9216]{1,0:T(8,128)(2,1)S(1)}, u32[]{:S(2)}, u32[]{:S(2)}) %collective-permute-start) | collective-permute-done | bytes 294944 | tf_op jit(solution)/shard_map/z_shifts/ppermute | solution.py:26
  9.0 1.4 collective-permute-start.1
  10.4 1.5 collective-permute-start.2
  11.9 1.2 collective-permute-start.3
  13.1 9.1 %collective-permute-done.6 = bf16[16,9216]{1,0:T(8,128)(2,1)S(1)} collective-permute-done((bf16[16,9216]{1,0:T(8,128)(2,1)S(1)}, bf16[16,9216]{1,0:T(8,128)(2,1)S(1)}, u32[]{:S(2)}, u32[]{:S(2)}) %collective-permute-start.6) | collective-permute-done | bytes 294944 | tf_op jit(solution)/shard_map/z_shifts/ppermute | solution.py:26
  22.2 2.5 %collective-permute-start.4 = (bf16[16,9216]{1,0:T(8,128)(2,1)S(1)}, bf16[16,9216]{1,0:T(8,128)(2,1)S(1)}, u32[]{:S(2)}, u32[]{:S(2)}) collective-permute-start(bf16[16,9216]{1,0:T(8,128)(2,1)S(1)} %get-tuple-element.83), channel_id=1, source_target_pairs={{0,12},{4,0},{8,4},{12,8},{1,13},{5,1},{9,5},{13,9},{2,14},{6,2},{... | collective-permute-start | bytes 884744 | tf_op jit(solution)/shard_map/first_axis/ppermute | solution.py:21
  24.7 4.0 %collective-permute-done.5 = bf16[16,9216]{1,0:T(8,128)(2,1)S(1)} collective-permute-done((bf16[16,9216]{1,0:T(8,128)(2,1)S(1)}, bf16[16,9216]{1,0:T(8,128)(2,1)S(1)}, u32[]{:S(2)}, u32[]{:S(2)}) %collective-permute-start.5) | collective-permute-done | bytes 294944 | tf_op jit(solution)/shard_map/z_shifts/ppermute | solution.py:26
  28.8 0.7 copy-done.2
  29.5 0.1 copy-done.3
  29.6 1.2 collective-permute-start.14
  30.8 0.1 pad_add_fusion.place_ref
  30.9 1.5 collective-permute-start.10
  32.3 2.7 %collective-permute-start.7 = (bf16[16,9216]{1,0:T(8,128)(2,1)S(1)}, bf16[16,9216]{1,0:T(8,128)(2,1)S(1)}, u32[]{:S(2)}, u32[]{:S(2)}) collective-permute-start(bf16[16,9216]{1,0:T(8,128)(2,1)S(1)} %get-tuple-element.44), channel_id=1, source_target_pairs={{0,48},{16,0},{32,16},{48,32},{1,49},{17,1},{33,17},{49,33},{2,50}... | collective-permute-start | bytes 884744 | tf_op jit(solution)/shard_map/first_axis/ppermute | solution.py:21
  35.1 1.4 collective-permute-done.14
  36.5 1.3 collective-permute-start.8
  37.8 1.4 pad_maximum_fusion.3.refs_2_
  39.1 1.4 collective-permute-start.21
  40.5 1.8 collective-permute-done.13
  42.3 1.2 collective-permute-start.12
  43.4 0.1 pad_maximum_fusion.2.refs_0_
  43.5 0.6 collective-permute-done.11
  44.1 3.0 %collective-permute-start.22 = (bf16[64,9216]{1,0:T(8,128)(2,1)S(1)}, bf16[64,9216]{1,0:T(8,128)(2,1)S(1)}, u32[]{:S(2)}, u32[]{:S(2)}) collective-permute-start(bf16[64,9216]{1,0:T(8,128)(2,1)S(1)} %pad_maximum_fusion.3.refs_2_), channel_id=1, source_target_pairs={{0,48},{16,0},{32,16},{48,32},{1,49},{17,1},{33,17},{49,33},{2,50}... | collective-permute-start | bytes 3538952 | tf_op jit(solution)/shard_map/second_axis/ppermute | solution.py:21
  47.1 0.0 collective-permute-start.19
  47.1 1.0 collective-permute-done.12
  48.1 0.1 pad_maximum_fusion.1.refs_3_
  48.2 2.5 %collective-permute-start.20 = (bf16[64,9216]{1,0:T(8,128)(2,1)S(1)}, bf16[64,9216]{1,0:T(8,128)(2,1)S(1)}, u32[]{:S(2)}, u32[]{:S(2)}) collective-permute-start(bf16[64,9216]{1,0:T(8,128)(2,1)S(1)} %pad_maximum_fusion.2.refs_0_), channel_id=1, source_target_pairs={{0,12},{4,0},{8,4},{12,8},{1,13},{5,1},{9,5},{13,9},{2,14},{6,2},{... | collective-permute-start | bytes 3538952 | tf_op jit(solution)/shard_map/second_axis/ppermute | solution.py:21
  50.7 22.0 %collective-permute-done.9 = bf16[16,9216]{1,0:T(8,128)(2,1)S(1)} collective-permute-done((bf16[16,9216]{1,0:T(8,128)(2,1)S(1)}, bf16[16,9216]{1,0:T(8,128)(2,1)S(1)}, u32[]{:S(2)}, u32[]{:S(2)}) %collective-permute-start.9) | collective-permute-done | bytes 294944 | tf_op jit(solution)/shard_map/first_axis/ppermute | solution.py:21
  72.7 1.0 pad_maximum_fusion.refs_1_
  73.8 3.2 %reduce.8 = (f32[2,2,8,8,512]{4,3,2,1,0:T(8,128)S(1)}, f32[2,2,8,8,512]{4,3,2,1,0:T(8,128)S(1)}) custom-call(s32[3]{0:T(128)S(1)} %pad_add_fusion.place_ref, bf16[64,9216]{1,0:T(8,128)(2,1)S(1)} %pad_maximum_fusion.2.refs_0_, bf16[64,9216]{1,0:T(8,128)(2,1)S(1)} %pad_maximum_fusion.refs_1_, bf16[64,9216]{1,0:T(8,128)(2,1)S(1)} %pad_maximum_fusion.3.refs_2_, ...), custom_call_target="tpu_custom_call" | custom-call | flops 1048576 | bytes 65536 | tf_op jit(solution)/shard_map/reduce/pallas_call | solution.py:59
  77.0 7.0 %collective-permute-start.23 = (f32[2,2,8,8,512]{4,3,2,1,0:T(8,128)S(1)}, f32[2,2,8,8,512]{4,3,2,1,0:T(8,128)S(1)}, u32[]{:S(2)}, u32[]{:S(2)}) collective-permute-start(f32[2,2,8,8,512]{4,3,2,1,0:T(8,128)S(1)} %get-tuple-element.60), channel_id=1, source_target_pairs={{0,1},{1,0},{2,3},{3,2},{4,5},{5,4},{6,7},{7,6},{8,9},{9,8},{10,11... | collective-permute-start | bytes 1572872 | tf_op jit(solution)/shard_map/reduce/ppermute | solution.py:143
  84.0 1.5 collective-permute-done.23
  85.5 2.7 %collective-permute-start.16 = (bf16[64,9216]{1,0:T(8,128)(2,1)S(1)}, bf16[64,9216]{1,0:T(8,128)(2,1)S(1)}, u32[]{:S(2)}, u32[]{:S(2)}) collective-permute-start(bf16[64,9216]{1,0:T(8,128)(2,1)S(1)} %pad_maximum_fusion.refs_1_), channel_id=1, source_target_pairs={{0,12},{4,0},{8,4},{12,8},{1,13},{5,1},{9,5},{13,9},{2,14},{6,2},{... | collective-permute-start | bytes 3538952 | tf_op jit(solution)/shard_map/second_axis/ppermute | solution.py:21
  88.2 0.7 collective-permute-start.17
  88.9 2.8 %collective-permute-start.18 = (bf16[64,9216]{1,0:T(8,128)(2,1)S(1)}, bf16[64,9216]{1,0:T(8,128)(2,1)S(1)}, u32[]{:S(2)}, u32[]{:S(2)}) collective-permute-start(bf16[64,9216]{1,0:T(8,128)(2,1)S(1)} %pad_maximum_fusion.1.refs_3_), channel_id=1, source_target_pairs={{0,48},{16,0},{32,16},{48,32},{1,49},{17,1},{33,17},{49,33},{2,50}... | collective-permute-start | bytes 3538952 | tf_op jit(solution)/shard_map/second_axis/ppermute | solution.py:21
  91.8 4.8 %collective-permute-start.24 = (f32[2,8,8,512]{3,2,1,0:T(8,128)S(1)}, f32[2,8,8,512]{3,2,1,0:T(8,128)S(1)}, u32[]{:S(2)}, u32[]{:S(2)}) collective-permute-start(f32[2,8,8,512]{3,2,1,0:T(8,128)S(1)} %fusion.13), channel_id=1, source_target_pairs={{0,2},{2,0},{1,3},{3,1},{4,6},{6,4},{5,7},{7,5},{8,10},{10,8},{9,1... | collective-permute-start | bytes 786440 | tf_op jit(solution)/shard_map/reduce/ppermute | solution.py:140
  96.5 3.2 %reduce.9 = (f32[2,2,8,8,512]{4,3,2,1,0:T(8,128)S(1)}, f32[2,2,8,8,512]{4,3,2,1,0:T(8,128)S(1)}) custom-call(s32[3]{0:T(128)S(1)} %pad_add_fusion.place_ref, bf16[64,9216]{1,0:T(8,128)(2,1)S(1)} %collective-permute-done.19.refs_0_, bf16[64,9216]{1,0:T(8,128)(2,1)S(1)} %collective-permute-done.20.refs_1_, ...), custom_call_target="tpu_custom_call" | custom-call | flops 1048576 | bytes 65536 | tf_op jit(solution)/shard_map/reduce/pallas_call | solution.py:59
  99.8 5.4 %collective-permute-done.24 = f32[2,8,8,512]{3,2,1,0:T(8,128)S(1)} collective-permute-done((f32[2,8,8,512]{3,2,1,0:T(8,128)S(1)}, f32[2,8,8,512]{3,2,1,0:T(8,128)S(1)}, u32[]{:S(2)}, u32[]{:S(2)}) %collective-permute-start.24) | collective-permute-done | bytes 262176 | tf_op jit(solution)/shard_map/reduce/ppermute | solution.py:140
  105.1 5.1 %collective-permute-start.29 = (f32[2,2,8,8,512]{4,3,2,1,0:T(8,128)S(1)}, f32[2,2,8,8,512]{4,3,2,1,0:T(8,128)S(1)}, u32[]{:S(2)}, u32[]{:S(2)}) collective-permute-start(f32[2,2,8,8,512]{4,3,2,1,0:T(8,128)S(1)} %get-tuple-element.69), channel_id=1, source_target_pairs={{0,1},{1,0},{2,3},{3,2},{4,5},{5,4},{6,7},{7,6},{8,9},{9,8},{10,11... | collective-permute-start | bytes 1572872 | tf_op jit(solution)/shard_map/reduce/ppermute | solution.py:143
  110.2 0.1 fusion.15
  110.3 3.6 %collective-permute-done.15.refs_0_ = bf16[64,9216]{1,0:T(8,128)(2,1)S(1)} collective-permute-done((bf16[64,9216]{1,0:T(8,128)(2,1)S(1)}, bf16[64,9216]{1,0:T(8,128)(2,1)S(1)}, u32[]{:S(2)}, u32[]{:S(2)}) %collective-permute-start.15) | collective-permute-done | bytes 1179680 | tf_op jit(solution)/shard_map/second_axis/ppermute | solution.py:21
  113.9 3.1 %collective-permute-done.17.refs_2_ = bf16[64,9216]{1,0:T(8,128)(2,1)S(1)} collective-permute-done((bf16[64,9216]{1,0:T(8,128)(2,1)S(1)}, bf16[64,9216]{1,0:T(8,128)(2,1)S(1)}, u32[]{:S(2)}, u32[]{:S(2)}) %collective-permute-start.17) | collective-permute-done | bytes 1179680 | tf_op jit(solution)/shard_map/second_axis/ppermute | solution.py:21
  117.0 2.7 %collective-permute-start.26 = (bf16[64,9216]{1,0:T(8,128)(2,1)S(1)}, bf16[64,9216]{1,0:T(8,128)(2,1)S(1)}, u32[]{:S(2)}, u32[]{:S(2)}) collective-permute-start(bf16[64,9216]{1,0:T(8,128)(2,1)S(1)} %collective-permute-done.16.refs_1_), channel_id=1, source_target_pairs={{0,12},{4,0},{8,4},{12,8},{1,13},{5,1},{9,5},{13,9},{2,14},{6,2},{... | collective-permute-start | bytes 3538952 | tf_op jit(solution)/shard_map/second_axis/ppermute | solution.py:21
  119.7 0.5 collective-permute-start.27
  120.3 2.1 %collective-permute-start.28 = (bf16[64,9216]{1,0:T(8,128)(2,1)S(1)}, bf16[64,9216]{1,0:T(8,128)(2,1)S(1)}, u32[]{:S(2)}, u32[]{:S(2)}) collective-permute-start(bf16[64,9216]{1,0:T(8,128)(2,1)S(1)} %collective-permute-done.18.refs_3_), channel_id=1, source_target_pairs={{0,48},{16,0},{32,16},{48,32},{1,49},{17,1},{33,17},{49,33},{2,50}... | collective-permute-start | bytes 3538952 | tf_op jit(solution)/shard_map/second_axis/ppermute | solution.py:21
  122.4 4.8 %collective-permute-start.30 = (f32[2,8,8,512]{3,2,1,0:T(8,128)S(1)}, f32[2,8,8,512]{3,2,1,0:T(8,128)S(1)}, u32[]{:S(2)}, u32[]{:S(2)}) collective-permute-start(f32[2,8,8,512]{3,2,1,0:T(8,128)S(1)} %fusion.10), channel_id=1, source_target_pairs={{0,2},{2,0},{1,3},{3,1},{4,6},{6,4},{5,7},{7,5},{8,10},{10,8},{9,1... | collective-permute-start | bytes 786440 | tf_op jit(solution)/shard_map/reduce/ppermute | solution.py:140
  127.2 3.2 %reduce.10 = (f32[2,2,8,8,512]{4,3,2,1,0:T(8,128)S(1)}, f32[2,2,8,8,512]{4,3,2,1,0:T(8,128)S(1)}) custom-call(s32[3]{0:T(128)S(1)} %pad_add_fusion.place_ref, bf16[64,9216]{1,0:T(8,128)(2,1)S(1)} %collective-permute-done.15.refs_0_, bf16[64,9216]{1,0:T(8,128)(2,1)S(1)} %collective-permute-done.16.refs_1_, ...), custom_call_target="tpu_custom_call" | custom-call | flops 1048576 | bytes 65536 | tf_op jit(solution)/shard_map/reduce/pallas_call | solution.py:59
  130.4 5.2 %collective-permute-done.30 = f32[2,8,8,512]{3,2,1,0:T(8,128)S(1)} collective-permute-done((f32[2,8,8,512]{3,2,1,0:T(8,128)S(1)}, f32[2,8,8,512]{3,2,1,0:T(8,128)S(1)}, u32[]{:S(2)}, u32[]{:S(2)}) %collective-permute-start.30) | collective-permute-done | bytes 262176 | tf_op jit(solution)/shard_map/reduce/ppermute | solution.py:140
  135.7 5.2 %collective-permute-start.31 = (f32[2,2,8,8,512]{4,3,2,1,0:T(8,128)S(1)}, f32[2,2,8,8,512]{4,3,2,1,0:T(8,128)S(1)}, u32[]{:S(2)}, u32[]{:S(2)}) collective-permute-start(f32[2,2,8,8,512]{4,3,2,1,0:T(8,128)S(1)} %get-tuple-element.73), channel_id=1, source_target_pairs={{0,1},{1,0},{2,3},{3,2},{4,5},{5,4},{6,7},{7,6},{8,9},{9,8},{10,11... | collective-permute-start | bytes 1572872 | tf_op jit(solution)/shard_map/reduce/ppermute | solution.py:143
  140.9 0.1 fusion.12
  141.0 1.4 collective-permute-done.31
  142.4 1.7 collective-permute-done.25.refs_0_
  144.2 2.1 %collective-permute-done.27.refs_2_ = bf16[64,9216]{1,0:T(8,128)(2,1)S(1)} collective-permute-done((bf16[64,9216]{1,0:T(8,128)(2,1)S(1)}, bf16[64,9216]{1,0:T(8,128)(2,1)S(1)}, u32[]{:S(2)}, u32[]{:S(2)}) %collective-permute-start.27) | collective-permute-done | bytes 1179680 | tf_op jit(solution)/shard_map/second_axis/ppermute | solution.py:21
  146.3 3.2 %reduce.11 = (f32[2,2,8,8,512]{4,3,2,1,0:T(8,128)S(1)}, f32[2,2,8,8,512]{4,3,2,1,0:T(8,128)S(1)}) custom-call(s32[3]{0:T(128)S(1)} %pad_add_fusion.place_ref, bf16[64,9216]{1,0:T(8,128)(2,1)S(1)} %collective-permute-done.25.refs_0_, bf16[64,9216]{1,0:T(8,128)(2,1)S(1)} %collective-permute-done.26.refs_1_, ...), custom_call_target="tpu_custom_call" | custom-call | flops 1048576 | bytes 65536 | tf_op jit(solution)/shard_map/reduce/pallas_call | solution.py:59
  149.6 3.1 %collective-permute-start.33 = (f32[2,2,8,8,512]{4,3,2,1,0:T(8,128)S(1)}, f32[2,2,8,8,512]{4,3,2,1,0:T(8,128)S(1)}, u32[]{:S(2)}, u32[]{:S(2)}) collective-permute-start(f32[2,2,8,8,512]{4,3,2,1,0:T(8,128)S(1)} %get-tuple-element.80), channel_id=1, source_target_pairs={{0,1},{1,0},{2,3},{3,2},{4,5},{5,4},{6,7},{7,6},{8,9},{9,8},{10,11... | collective-permute-start | bytes 1572872 | tf_op jit(solution)/shard_map/reduce/ppermute | solution.py:143
  152.6 4.7 %collective-permute-start.32 = (f32[2,8,8,512]{3,2,1,0:T(8,128)S(1)}, f32[2,8,8,512]{3,2,1,0:T(8,128)S(1)}, u32[]{:S(2)}, u32[]{:S(2)}) collective-permute-start(f32[2,8,8,512]{3,2,1,0:T(8,128)S(1)} %fusion.9), channel_id=1, source_target_pairs={{0,2},{2,0},{1,3},{3,1},{4,6},{6,4},{5,7},{7,5},{8,10},{10,8},{9,1... | collective-permute-start | bytes 786440 | tf_op jit(solution)/shard_map/reduce/ppermute | solution.py:140
  157.4 1.6 collective-permute-start.34
  159.0 11.1 %collective-permute-done.32 = f32[2,8,8,512]{3,2,1,0:T(8,128)S(1)} collective-permute-done((f32[2,8,8,512]{3,2,1,0:T(8,128)S(1)}, f32[2,8,8,512]{3,2,1,0:T(8,128)S(1)}, u32[]{:S(2)}, u32[]{:S(2)}) %collective-permute-start.32) | collective-permute-done | bytes 262176 | tf_op jit(solution)/shard_map/reduce/ppermute | solution.py:140
  170.1 0.1 fusion.8
  170.2 11.1 %collective-permute-done.34.back_ref = f32[2,8,8,512]{3,2,1,0:T(8,128)S(1)} collective-permute-done((f32[2,8,8,512]{3,2,1,0:T(8,128)S(1)}, f32[2,8,8,512]{3,2,1,0:T(8,128)S(1)}, u32[]{:S(2)}, u32[]{:S(2)}) %collective-permute-start.34) | collective-permute-done | bytes 262176 | tf_op jit(solution)/shard_map/reduce/ppermute | solution.py:140
  181.3 1.6 reduce.12
  (45 shorter events, 0.4 us)
Async XLA Ops:
  1.0 8.0 %collective-permute-start = (bf16[16,9216]{1,0:T(8,128)(2,1)S(1)}, bf16[16,9216]{1,0:T(8,128)(2,1)S(1)}, u32[]{:S(2)}, u32[]{:S(2)}) collective-permute-start(bf16[16,9216]{1,0:T(8,128)(2,1)S(1)} %get-tuple-element.85), channel_id=1, source_target_pairs={{0,64},{64,0},{128,192},{192,128},{1,65},{65,1},{129,193},{193,129... | collective-permute-start | bytes 884744 | tf_op jit(solution)/shard_map/z_shifts/ppermute | solution.py:26
  1.1 21.1 %collective-permute-start.6 = (bf16[16,9216]{1,0:T(8,128)(2,1)S(1)}, bf16[16,9216]{1,0:T(8,128)(2,1)S(1)}, u32[]{:S(2)}, u32[]{:S(2)}) collective-permute-start(bf16[16,9216]{1,0:T(8,128)(2,1)S(1)} %get-tuple-element.85), channel_id=1, source_target_pairs={{0,192},{64,128},{128,64},{192,0},{1,193},{65,129},{129,65},{193,1... | collective-permute-start | bytes 884744 | tf_op jit(solution)/shard_map/z_shifts/ppermute | solution.py:26
  4.4 24.3 %collective-permute-start.5 = (bf16[16,9216]{1,0:T(8,128)(2,1)S(1)}, bf16[16,9216]{1,0:T(8,128)(2,1)S(1)}, u32[]{:S(2)}, u32[]{:S(2)}) collective-permute-start(bf16[16,9216]{1,0:T(8,128)(2,1)S(1)} %get-tuple-element.85), channel_id=1, source_target_pairs={{0,128},{64,192},{128,0},{192,64},{1,129},{65,193},{129,1},{193,65... | collective-permute-start | bytes 884744 | tf_op jit(solution)/shard_map/z_shifts/ppermute | solution.py:26
  9.0 19.7 %collective-permute-start.1 = (bf16[16,9216]{1,0:T(8,128)(2,1)S(1)}, bf16[16,9216]{1,0:T(8,128)(2,1)S(1)}, u32[]{:S(2)}, u32[]{:S(2)}) collective-permute-start(bf16[16,9216]{1,0:T(8,128)(2,1)S(1)} %get-tuple-element.84), channel_id=1, source_target_pairs={{0,16},{16,32},{32,48},{48,0},{1,17},{17,33},{33,49},{49,1},{2,18}... | collective-permute-start | bytes 884744 | tf_op jit(solution)/shard_map/first_axis/ppermute | solution.py:21
  10.4 18.4 %collective-permute-start.2 = (bf16[16,9216]{1,0:T(8,128)(2,1)S(1)}, bf16[16,9216]{1,0:T(8,128)(2,1)S(1)}, u32[]{:S(2)}, u32[]{:S(2)}) collective-permute-start(bf16[16,9216]{1,0:T(8,128)(2,1)S(1)} %get-tuple-element.84), channel_id=1, source_target_pairs={{0,48},{16,0},{32,16},{48,32},{1,49},{17,1},{33,17},{49,33},{2,50}... | collective-permute-start | bytes 884744 | tf_op jit(solution)/shard_map/first_axis/ppermute | solution.py:21
  11.9 16.9 %collective-permute-start.3 = (bf16[16,9216]{1,0:T(8,128)(2,1)S(1)}, bf16[16,9216]{1,0:T(8,128)(2,1)S(1)}, u32[]{:S(2)}, u32[]{:S(2)}) collective-permute-start(bf16[16,9216]{1,0:T(8,128)(2,1)S(1)} %get-tuple-element.83), channel_id=1, source_target_pairs={{0,4},{4,8},{8,12},{12,0},{1,5},{5,9},{9,13},{13,1},{2,6},{6,10},{... | collective-permute-start | bytes 884744 | tf_op jit(solution)/shard_map/first_axis/ppermute | solution.py:21
  22.2 6.6 %collective-permute-start.4 = (bf16[16,9216]{1,0:T(8,128)(2,1)S(1)}, bf16[16,9216]{1,0:T(8,128)(2,1)S(1)}, u32[]{:S(2)}, u32[]{:S(2)}) collective-permute-start(bf16[16,9216]{1,0:T(8,128)(2,1)S(1)} %get-tuple-element.83), channel_id=1, source_target_pairs={{0,12},{4,0},{8,4},{12,8},{1,13},{5,1},{9,5},{13,9},{2,14},{6,2},{... | collective-permute-start | bytes 884744 | tf_op jit(solution)/shard_map/first_axis/ppermute | solution.py:21
  28.7 45.0 %copy-start.1 = (bf16[512,2048]{1,0:T(8,128)(2,1)S(1)}, bf16[512,2048]{1,0:T(8,128)(2,1)}, u32[]{:S(2)}) copy-start(bf16[512,2048]{1,0:T(8,128)(2,1)} %refs_5_.7) | copy-start | bytes 6291460
  28.8 0.8 copy-start.3
  28.8 0.7 copy-start.2
  28.8 2.0 %copy-start.7 = (bf16[16,9216]{1,0:T(8,128)(2,1)}, bf16[16,9216]{1,0:T(8,128)(2,1)S(1)}, u32[]{:S(2)}) copy-start(bf16[16,9216]{1,0:T(8,128)(2,1)S(1)} %collective-permute-done.3) | copy-start | bytes 884740
  28.8 2.0 %copy-start.5 = (bf16[16,9216]{1,0:T(8,128)(2,1)}, bf16[16,9216]{1,0:T(8,128)(2,1)S(1)}, u32[]{:S(2)}) copy-start(bf16[16,9216]{1,0:T(8,128)(2,1)S(1)} %collective-permute-done.4) | copy-start | bytes 884740
  29.6 6.9 %collective-permute-start.14 = (bf16[16,9216]{1,0:T(8,128)(2,1)S(1)}, bf16[16,9216]{1,0:T(8,128)(2,1)}, u32[]{:S(2)}, u32[]{:S(2)}) collective-permute-start(bf16[16,9216]{1,0:T(8,128)(2,1)S(1)} %get-tuple-element.47), channel_id=1, source_target_pairs={{0,4},{4,8},{8,12},{12,0},{1,5},{5,9},{9,13},{13,1},{2,6},{6,10},{... | collective-permute-start | bytes 884744 | tf_op jit(solution)/shard_map/first_axis/ppermute | solution.py:21
  30.9 12.6 %copy-start.4 = (bf16[16,9216]{1,0:T(8,128)(2,1)S(1)}, bf16[16,9216]{1,0:T(8,128)(2,1)}, u32[]{:S(2)}) copy-start(bf16[16,9216]{1,0:T(8,128)(2,1)} %copy-done.3) | copy-start | bytes 884740
  30.9 8.3 %collective-permute-start.10 = (bf16[16,9216]{1,0:T(8,128)(2,1)S(1)}, bf16[16,9216]{1,0:T(8,128)(2,1)S(1)}, u32[]{:S(2)}, u32[]{:S(2)}) collective-permute-start(bf16[16,9216]{1,0:T(8,128)(2,1)S(1)} %get-tuple-element.47), channel_id=1, source_target_pairs={{0,12},{4,0},{8,4},{12,8},{1,13},{5,1},{9,5},{13,9},{2,14},{6,2},{... | collective-permute-start | bytes 884744 | tf_op jit(solution)/shard_map/first_axis/ppermute | solution.py:21
  32.3 14.8 %collective-permute-start.7 = (bf16[16,9216]{1,0:T(8,128)(2,1)S(1)}, bf16[16,9216]{1,0:T(8,128)(2,1)S(1)}, u32[]{:S(2)}, u32[]{:S(2)}) collective-permute-start(bf16[16,9216]{1,0:T(8,128)(2,1)S(1)} %get-tuple-element.44), channel_id=1, source_target_pairs={{0,48},{16,0},{32,16},{48,32},{1,49},{17,1},{33,17},{49,33},{2,50}... | collective-permute-start | bytes 884744 | tf_op jit(solution)/shard_map/first_axis/ppermute | solution.py:21
  35.1 7.2 %collective-permute-start.13 = (bf16[16,9216]{1,0:T(8,128)(2,1)S(1)}, bf16[16,9216]{1,0:T(8,128)(2,1)S(1)}, u32[]{:S(2)}, u32[]{:S(2)}) collective-permute-start(bf16[16,9216]{1,0:T(8,128)(2,1)S(1)} %get-tuple-element.44), channel_id=1, source_target_pairs={{0,16},{16,32},{32,48},{48,0},{1,17},{17,33},{33,49},{49,1},{2,18}... | collective-permute-start | bytes 884744 | tf_op jit(solution)/shard_map/first_axis/ppermute | solution.py:21
  35.1 9.0 %collective-permute-start.11 = (bf16[16,9216]{1,0:T(8,128)(2,1)}, bf16[16,9216]{1,0:T(8,128)(2,1)S(1)}, u32[]{:S(2)}, u32[]{:S(2)}) collective-permute-start(bf16[16,9216]{1,0:T(8,128)(2,1)} %copy-done.7), channel_id=1, source_target_pairs={{0,4},{4,8},{8,12},{12,0},{1,5},{5,9},{9,13},{13,1},{2,6},{6,10},{... | collective-permute-start | bytes 884744 | tf_op jit(solution)/shard_map/first_axis/ppermute | solution.py:21
  36.5 11.7 %copy-start.6 = (bf16[16,9216]{1,0:T(8,128)(2,1)S(1)}, bf16[16,9216]{1,0:T(8,128)(2,1)}, u32[]{:S(2)}) copy-start(bf16[16,9216]{1,0:T(8,128)(2,1)} %copy-done.5) | copy-start | bytes 884740
  36.5 11.8 %collective-permute-start.8 = (bf16[16,9216]{1,0:T(8,128)(2,1)}, bf16[16,9216]{1,0:T(8,128)(2,1)S(1)}, u32[]{:S(2)}, u32[]{:S(2)}) collective-permute-start(bf16[16,9216]{1,0:T(8,128)(2,1)} %copy-done.3), channel_id=1, source_target_pairs={{0,16},{16,32},{32,48},{48,0},{1,17},{17,33},{33,49},{49,1},{2,18}... | collective-permute-start | bytes 884744 | tf_op jit(solution)/shard_map/first_axis/ppermute | solution.py:21
  37.7 36.0 %copy-start = (bf16[512,7168]{1,0:T(8,128)(2,1)S(1)}, bf16[512,7168]{1,0:T(8,128)(2,1)}, u32[]{:S(2)}) copy-start(bf16[512,7168]{1,0:T(8,128)(2,1)} %refs_4_.7) | copy-start | bytes 22020100
  39.1 46.4 %collective-permute-start.21 = (bf16[64,9216]{1,0:T(8,128)(2,1)S(1)}, bf16[64,9216]{1,0:T(8,128)(2,1)S(1)}, u32[]{:S(2)}, u32[]{:S(2)}) collective-permute-start(bf16[64,9216]{1,0:T(8,128)(2,1)S(1)} %pad_maximum_fusion.3.refs_2_), channel_id=1, source_target_pairs={{0,16},{16,32},{32,48},{48,0},{1,17},{17,33},{33,49},{49,1},{2,18}... | collective-permute-start | bytes 3538952 | tf_op jit(solution)/shard_map/second_axis/ppermute | solution.py:21
  42.3 5.9 %collective-permute-start.12 = (bf16[16,9216]{1,0:T(8,128)(2,1)S(1)}, bf16[16,9216]{1,0:T(8,128)(2,1)S(1)}, u32[]{:S(2)}, u32[]{:S(2)}) collective-permute-start(bf16[16,9216]{1,0:T(8,128)(2,1)S(1)} %collective-permute-done.10), channel_id=1, source_target_pairs={{0,12},{4,0},{8,4},{12,8},{1,13},{5,1},{9,5},{13,9},{2,14},{6,2},{... | collective-permute-start | bytes 884744 | tf_op jit(solution)/shard_map/first_axis/ppermute | solution.py:21
  44.1 44.1 %collective-permute-start.22 = (bf16[64,9216]{1,0:T(8,128)(2,1)S(1)}, bf16[64,9216]{1,0:T(8,128)(2,1)S(1)}, u32[]{:S(2)}, u32[]{:S(2)}) collective-permute-start(bf16[64,9216]{1,0:T(8,128)(2,1)S(1)} %pad_maximum_fusion.3.refs_2_), channel_id=1, source_target_pairs={{0,48},{16,0},{32,16},{48,32},{1,49},{17,1},{33,17},{49,33},{2,50}... | collective-permute-start | bytes 3538952 | tf_op jit(solution)/shard_map/second_axis/ppermute | solution.py:21
  47.1 41.8 %collective-permute-start.19 = (bf16[64,9216]{1,0:T(8,128)(2,1)S(1)}, bf16[64,9216]{1,0:T(8,128)(2,1)S(1)}, u32[]{:S(2)}, u32[]{:S(2)}) collective-permute-start(bf16[64,9216]{1,0:T(8,128)(2,1)S(1)} %pad_maximum_fusion.2.refs_0_), channel_id=1, source_target_pairs={{0,4},{4,8},{8,12},{12,0},{1,5},{5,9},{9,13},{13,1},{2,6},{6,10},{... | collective-permute-start | bytes 3538952 | tf_op jit(solution)/shard_map/second_axis/ppermute | solution.py:21
  48.1 24.6 %collective-permute-start.9 = (bf16[16,9216]{1,0:T(8,128)(2,1)S(1)}, bf16[16,9216]{1,0:T(8,128)(2,1)S(1)}, u32[]{:S(2)}, u32[]{:S(2)}) collective-permute-start(bf16[16,9216]{1,0:T(8,128)(2,1)S(1)} %collective-permute-done.7), channel_id=1, source_target_pairs={{0,48},{16,0},{32,16},{48,32},{1,49},{17,1},{33,17},{49,33},{2,50}... | collective-permute-start | bytes 884744 | tf_op jit(solution)/shard_map/first_axis/ppermute | solution.py:21
  48.2 43.5 %collective-permute-start.20 = (bf16[64,9216]{1,0:T(8,128)(2,1)S(1)}, bf16[64,9216]{1,0:T(8,128)(2,1)S(1)}, u32[]{:S(2)}, u32[]{:S(2)}) collective-permute-start(bf16[64,9216]{1,0:T(8,128)(2,1)S(1)} %pad_maximum_fusion.2.refs_0_), channel_id=1, source_target_pairs={{0,12},{4,0},{8,4},{12,8},{1,13},{5,1},{9,5},{13,9},{2,14},{6,2},{... | collective-permute-start | bytes 3538952 | tf_op jit(solution)/shard_map/second_axis/ppermute | solution.py:21
  77.0 8.5 %collective-permute-start.23 = (f32[2,2,8,8,512]{4,3,2,1,0:T(8,128)S(1)}, f32[2,2,8,8,512]{4,3,2,1,0:T(8,128)S(1)}, u32[]{:S(2)}, u32[]{:S(2)}) collective-permute-start(f32[2,2,8,8,512]{4,3,2,1,0:T(8,128)S(1)} %get-tuple-element.60), channel_id=1, source_target_pairs={{0,1},{1,0},{2,3},{3,2},{4,5},{5,4},{6,7},{7,6},{8,9},{9,8},{10,11... | collective-permute-start | bytes 1572872 | tf_op jit(solution)/shard_map/reduce/ppermute | solution.py:143
  85.5 28.4 %collective-permute-start.15 = (bf16[64,9216]{1,0:T(8,128)(2,1)S(1)}, bf16[64,9216]{1,0:T(8,128)(2,1)S(1)}, u32[]{:S(2)}, u32[]{:S(2)}) collective-permute-start(bf16[64,9216]{1,0:T(8,128)(2,1)S(1)} %pad_maximum_fusion.refs_1_), channel_id=1, source_target_pairs={{0,4},{4,8},{8,12},{12,0},{1,5},{5,9},{9,13},{13,1},{2,6},{6,10},{... | collective-permute-start | bytes 3538952 | tf_op jit(solution)/shard_map/second_axis/ppermute | solution.py:21
  85.5 28.4 %collective-permute-start.16 = (bf16[64,9216]{1,0:T(8,128)(2,1)S(1)}, bf16[64,9216]{1,0:T(8,128)(2,1)S(1)}, u32[]{:S(2)}, u32[]{:S(2)}) collective-permute-start(bf16[64,9216]{1,0:T(8,128)(2,1)S(1)} %pad_maximum_fusion.refs_1_), channel_id=1, source_target_pairs={{0,12},{4,0},{8,4},{12,8},{1,13},{5,1},{9,5},{13,9},{2,14},{6,2},{... | collective-permute-start | bytes 3538952 | tf_op jit(solution)/shard_map/second_axis/ppermute | solution.py:21
  88.2 28.8 %collective-permute-start.17 = (bf16[64,9216]{1,0:T(8,128)(2,1)S(1)}, bf16[64,9216]{1,0:T(8,128)(2,1)S(1)}, u32[]{:S(2)}, u32[]{:S(2)}) collective-permute-start(bf16[64,9216]{1,0:T(8,128)(2,1)S(1)} %pad_maximum_fusion.1.refs_3_), channel_id=1, source_target_pairs={{0,16},{16,32},{32,48},{48,0},{1,17},{17,33},{33,49},{49,1},{2,18}... | collective-permute-start | bytes 3538952 | tf_op jit(solution)/shard_map/second_axis/ppermute | solution.py:21
  88.9 28.2 %collective-permute-start.18 = (bf16[64,9216]{1,0:T(8,128)(2,1)S(1)}, bf16[64,9216]{1,0:T(8,128)(2,1)S(1)}, u32[]{:S(2)}, u32[]{:S(2)}) collective-permute-start(bf16[64,9216]{1,0:T(8,128)(2,1)S(1)} %pad_maximum_fusion.1.refs_3_), channel_id=1, source_target_pairs={{0,48},{16,0},{32,16},{48,32},{1,49},{17,1},{33,17},{49,33},{2,50}... | collective-permute-start | bytes 3538952 | tf_op jit(solution)/shard_map/second_axis/ppermute | solution.py:21
  91.8 13.4 %collective-permute-start.24 = (f32[2,8,8,512]{3,2,1,0:T(8,128)S(1)}, f32[2,8,8,512]{3,2,1,0:T(8,128)S(1)}, u32[]{:S(2)}, u32[]{:S(2)}) collective-permute-start(f32[2,8,8,512]{3,2,1,0:T(8,128)S(1)} %fusion.13), channel_id=1, source_target_pairs={{0,2},{2,0},{1,3},{3,1},{4,6},{6,4},{5,7},{7,5},{8,10},{10,8},{9,1... | collective-permute-start | bytes 786440 | tf_op jit(solution)/shard_map/reduce/ppermute | solution.py:140
  105.1 17.3 %collective-permute-start.29 = (f32[2,2,8,8,512]{4,3,2,1,0:T(8,128)S(1)}, f32[2,2,8,8,512]{4,3,2,1,0:T(8,128)S(1)}, u32[]{:S(2)}, u32[]{:S(2)}) collective-permute-start(f32[2,2,8,8,512]{4,3,2,1,0:T(8,128)S(1)} %get-tuple-element.69), channel_id=1, source_target_pairs={{0,1},{1,0},{2,3},{3,2},{4,5},{5,4},{6,7},{7,6},{8,9},{9,8},{10,11... | collective-permute-start | bytes 1572872 | tf_op jit(solution)/shard_map/reduce/ppermute | solution.py:143
  117.0 27.2 %collective-permute-start.25 = (bf16[64,9216]{1,0:T(8,128)(2,1)S(1)}, bf16[64,9216]{1,0:T(8,128)(2,1)S(1)}, u32[]{:S(2)}, u32[]{:S(2)}) collective-permute-start(bf16[64,9216]{1,0:T(8,128)(2,1)S(1)} %collective-permute-done.19.refs_0_), channel_id=1, source_target_pairs={{0,4},{4,8},{8,12},{12,0},{1,5},{5,9},{9,13},{13,1},{2,6},{6,10},{... | collective-permute-start | bytes 3538952 | tf_op jit(solution)/shard_map/second_axis/ppermute | solution.py:21
  117.0 27.2 %collective-permute-start.26 = (bf16[64,9216]{1,0:T(8,128)(2,1)S(1)}, bf16[64,9216]{1,0:T(8,128)(2,1)S(1)}, u32[]{:S(2)}, u32[]{:S(2)}) collective-permute-start(bf16[64,9216]{1,0:T(8,128)(2,1)S(1)} %collective-permute-done.16.refs_1_), channel_id=1, source_target_pairs={{0,12},{4,0},{8,4},{12,8},{1,13},{5,1},{9,5},{13,9},{2,14},{6,2},{... | collective-permute-start | bytes 3538952 | tf_op jit(solution)/shard_map/second_axis/ppermute | solution.py:21
  119.7 26.6 %collective-permute-start.27 = (bf16[64,9216]{1,0:T(8,128)(2,1)S(1)}, bf16[64,9216]{1,0:T(8,128)(2,1)S(1)}, u32[]{:S(2)}, u32[]{:S(2)}) collective-permute-start(bf16[64,9216]{1,0:T(8,128)(2,1)S(1)} %collective-permute-done.21.refs_2_), channel_id=1, source_target_pairs={{0,16},{16,32},{32,48},{48,0},{1,17},{17,33},{33,49},{49,1},{2,18}... | collective-permute-start | bytes 3538952 | tf_op jit(solution)/shard_map/second_axis/ppermute | solution.py:21
  120.3 26.1 %collective-permute-start.28 = (bf16[64,9216]{1,0:T(8,128)(2,1)S(1)}, bf16[64,9216]{1,0:T(8,128)(2,1)S(1)}, u32[]{:S(2)}, u32[]{:S(2)}) collective-permute-start(bf16[64,9216]{1,0:T(8,128)(2,1)S(1)} %collective-permute-done.18.refs_3_), channel_id=1, source_target_pairs={{0,48},{16,0},{32,16},{48,32},{1,49},{17,1},{33,17},{49,33},{2,50}... | collective-permute-start | bytes 3538952 | tf_op jit(solution)/shard_map/second_axis/ppermute | solution.py:21
  122.4 13.2 %collective-permute-start.30 = (f32[2,8,8,512]{3,2,1,0:T(8,128)S(1)}, f32[2,8,8,512]{3,2,1,0:T(8,128)S(1)}, u32[]{:S(2)}, u32[]{:S(2)}) collective-permute-start(f32[2,8,8,512]{3,2,1,0:T(8,128)S(1)} %fusion.10), channel_id=1, source_target_pairs={{0,2},{2,0},{1,3},{3,1},{4,6},{6,4},{5,7},{7,5},{8,10},{10,8},{9,1... | collective-permute-start | bytes 786440 | tf_op jit(solution)/shard_map/reduce/ppermute | solution.py:140
  135.7 6.7 %collective-permute-start.31 = (f32[2,2,8,8,512]{4,3,2,1,0:T(8,128)S(1)}, f32[2,2,8,8,512]{4,3,2,1,0:T(8,128)S(1)}, u32[]{:S(2)}, u32[]{:S(2)}) collective-permute-start(f32[2,2,8,8,512]{4,3,2,1,0:T(8,128)S(1)} %get-tuple-element.73), channel_id=1, source_target_pairs={{0,1},{1,0},{2,3},{3,2},{4,5},{5,4},{6,7},{7,6},{8,9},{9,8},{10,11... | collective-permute-start | bytes 1572872 | tf_op jit(solution)/shard_map/reduce/ppermute | solution.py:143
  149.6 7.8 %collective-permute-start.33 = (f32[2,2,8,8,512]{4,3,2,1,0:T(8,128)S(1)}, f32[2,2,8,8,512]{4,3,2,1,0:T(8,128)S(1)}, u32[]{:S(2)}, u32[]{:S(2)}) collective-permute-start(f32[2,2,8,8,512]{4,3,2,1,0:T(8,128)S(1)} %get-tuple-element.80), channel_id=1, source_target_pairs={{0,1},{1,0},{2,3},{3,2},{4,5},{5,4},{6,7},{7,6},{8,9},{9,8},{10,11... | collective-permute-start | bytes 1572872 | tf_op jit(solution)/shard_map/reduce/ppermute | solution.py:143
  152.6 17.4 %collective-permute-start.32 = (f32[2,8,8,512]{3,2,1,0:T(8,128)S(1)}, f32[2,8,8,512]{3,2,1,0:T(8,128)S(1)}, u32[]{:S(2)}, u32[]{:S(2)}) collective-permute-start(f32[2,8,8,512]{3,2,1,0:T(8,128)S(1)} %fusion.9), channel_id=1, source_target_pairs={{0,2},{2,0},{1,3},{3,1},{4,6},{6,4},{5,7},{7,5},{8,10},{10,8},{9,1... | collective-permute-start | bytes 786440 | tf_op jit(solution)/shard_map/reduce/ppermute | solution.py:140
  157.4 24.0 %collective-permute-start.34 = (f32[2,8,8,512]{3,2,1,0:T(8,128)S(1)}, f32[2,8,8,512]{3,2,1,0:T(8,128)S(1)}, u32[]{:S(2)}, u32[]{:S(2)}) collective-permute-start(f32[2,8,8,512]{3,2,1,0:T(8,128)S(1)} %fusion.6), channel_id=1, source_target_pairs={{0,2},{2,0},{1,3},{3,1},{4,6},{6,4},{5,7},{7,5},{8,10},{10,8},{9,1... | collective-permute-start | bytes 786440 | tf_op jit(solution)/shard_map/reduce/ppermute | solution.py:140

commit v6 on v4

--- a/solution.py
+++ b/solution.py
@@ -131,10 +131,8 @@
 
     def first(rows, axis):
         block = rows.reshape(GROUPS * RANK, features)
-        half = block.shape[0] // 2
-        before, after = ring(block, axis, 1), ring(block, axis, -1)
-        far = ring(before[:half], axis, 1), ring(after[half:], axis, -1)
-        return jnp.concatenate([block, before]), jnp.concatenate([after, *far])
+        before, after, far = (ring(block, axis, step) for step in (1, -1, 2))
+        return jnp.concatenate([block, before]), jnp.concatenate([after, far])
 
     def both(block, axis):
         return ring(block, axis, 1), ring(block, axis, -1)

time: 174 us -> 176 us (1.011)
  waiting for transfers between devices: 77 us -> 99.9 us
  starting transfers between devices: 74 us -> 56.5 us
  local copies, waits for them, and re-layouts: 3.14 us -> 1.11 us
    ppermute x20 -> x18, waiting for transfers between devices: 26.3 us -> 45.2 us  [ring(): return lax.ppermute(x, axis, [(i, (i + step) % n) for i in range(n)])]
    ppermute x4, starting transfers between devices: 30.1 us -> 13.3 us  [over(): return lax.ppermute(send, 'core', [(0, 1), (1, 0)])]
    ppermute x4, waiting for transfers between devices: 22.3 us -> 26.1 us  [exchange(): return lax.ppermute(sent, 'zh', [(0, 1), (1, 0)])]
    slice x4 -> x0, local copies, waits for them, and re-layouts: 2 us -> none  [first(): far = (ring(before[:half], axis, 1), ring(after[half:], axis, -1))]
    ppermute x20 -> x18, starting transfers between devices: 24.9 us -> 23.8 us  [ring(): return lax.ppermute(x, axis, [(i, (i + step) % n) for i in range(n)])]
  transfers between devices with their start and end apart: 31 -> 29, of which waited for: 16 -> 17; matrix products, arithmetic and copies ran while one was open for 3% -> 1% of each run, Pallas kernels for 6% -> 6%
where the time goes in v6:
time: 176 us; the launch traced here: 175 us
  waiting for transfers between devices  99.9 us (57%)
  starting transfers between devices  56.5 us (32%)
  Pallas kernels  14.5 us (8%)
  other arithmetic  3.26 us (2%)
    ppermute x18, waiting for transfers between devices, ring(): return lax.ppermute(x, axis, [(i, (i + step) % n) for i in range(n)])  45.2 us
    ppermute x4, waiting for transfers between devices, exchange(): return lax.ppermute(sent, 'zh', [(0, 1), (1, 0)])  26.1 us
    ppermute x3, waiting for transfers between devices, flip(): return lax.ppermute(x, axis, [(i, i ^ mask) for i in range(n)])  25.5 us
    ppermute x18, starting transfers between devices, ring(): return lax.ppermute(x, axis, [(i, (i + step) % n) for i in range(n)])  23.8 us
    ppermute x4, starting transfers between devices, exchange(): return lax.ppermute(sent, 'zh', [(0, 1), (1, 0)])  16 us
    ppermute x4, starting transfers between devices, over(): return lax.ppermute(send, 'core', [(0, 1), (1, 0)])  13.3 us
    pallas_call x4, Pallas kernels, project(): pl.pallas_call(functools.partial(project_kernel, len(blocks)), out_shape=...  12.9 us
  transfers between devices with their start and end apart: 29, of which 17 were waited for; matrix products, arithmetic and copies ran while one was open for 1% of the time, Pallas kernels for 6%

profile of v6, /device:TPU:33, one launch (start us, length us, event | category | flops | bytes accessed | tf_op | source)
XLA Modules:
  0.0 175.4 jit_solution(3443877856774091016)
XLA Ops:
  0.0 1.0 fusion.13
  1.0 0.1 collective-permute-start
  1.1 3.1 %collective-permute-start.1 = (bf16[16,9216]{1,0:T(8,128)(2,1)S(1)}, bf16[16,9216]{1,0:T(8,128)(2,1)S(1)}, u32[]{:S(2)}, u32[]{:S(2)}) collective-permute-start(bf16[16,9216]{1,0:T(8,128)(2,1)S(1)} %get-tuple-element.76), channel_id=1, source_target_pairs={{0,128},{64,192},{128,0},{192,64},{1,129},{65,193},{129,1},{193,65... | collective-permute-start | bytes 884744 | tf_op jit(solution)/shard_map/z_shifts/ppermute | solution.py:26
  4.2 0.2 collective-permute-start.2
  4.4 5.9 %collective-permute-done = bf16[16,9216]{1,0:T(8,128)(2,1)S(1)} collective-permute-done((bf16[16,9216]{1,0:T(8,128)(2,1)S(1)}, bf16[16,9216]{1,0:T(8,128)(2,1)S(1)}, u32[]{:S(2)}, u32[]{:S(2)}) %collective-permute-start) | collective-permute-done | bytes 294944 | tf_op jit(solution)/shard_map/z_shifts/ppermute | solution.py:26
  10.2 12.2 %collective-permute-done.1 = bf16[16,9216]{1,0:T(8,128)(2,1)S(1)} collective-permute-done((bf16[16,9216]{1,0:T(8,128)(2,1)S(1)}, bf16[16,9216]{1,0:T(8,128)(2,1)S(1)}, u32[]{:S(2)}, u32[]{:S(2)}) %collective-permute-start.1) | collective-permute-done | bytes 294944 | tf_op jit(solution)/shard_map/z_shifts/ppermute | solution.py:26
  22.5 7.4 %collective-permute-done.2 = bf16[16,9216]{1,0:T(8,128)(2,1)S(1)} collective-permute-done((bf16[16,9216]{1,0:T(8,128)(2,1)S(1)}, bf16[16,9216]{1,0:T(8,128)(2,1)S(1)}, u32[]{:S(2)}, u32[]{:S(2)}) %collective-permute-start.2) | collective-permute-done | bytes 294944 | tf_op jit(solution)/shard_map/z_shifts/ppermute | solution.py:26
  29.8 0.1 pad_maximum_fusion
  30.0 1.1 slice_bitcast_fusion
  31.1 1.3 collective-permute-start.7
  32.4 0.1 pad_add_fusion.place_ref
  32.5 1.2 collective-permute-start.8
  33.7 1.5 collective-permute-start.5
  35.2 1.5 collective-permute-start.6
  36.7 1.4 collective-permute-start.3
  38.2 7.9 %collective-permute-done.7 = bf16[32,9216]{1,0:T(8,128)(2,1)} collective-permute-done((bf16[32,9216]{1,0:T(8,128)(2,1)}, bf16[32,9216]{1,0:T(8,128)(2,1)}, u32[]{:S(2)}, u32[]{:S(2)}) %collective-permute-start.7) | collective-permute-done | bytes 589856 | tf_op jit(solution)/shard_map/first_axis/ppermute | solution.py:21
  46.1 1.6 collective-permute-start.4
  47.6 1.3 pad_maximum_fusion.3.refs_0_
  49.0 0.0 collective-permute-done.8
  49.0 0.1 pad_maximum_fusion.4.refs_2_
  49.1 1.3 collective-permute-start.13
  50.4 1.5 collective-permute-start.14
  51.8 8.8 %collective-permute-done.6 = bf16[32,9216]{1,0:T(8,128)(2,1)S(1)} collective-permute-done((bf16[32,9216]{1,0:T(8,128)(2,1)}, bf16[32,9216]{1,0:T(8,128)(2,1)S(1)}, u32[]{:S(2)}, u32[]{:S(2)}) %collective-permute-start.6) | collective-permute-done | bytes 589856 | tf_op jit(solution)/shard_map/first_axis/ppermute | solution.py:21
  60.6 1.3 collective-permute-start.15
  61.9 0.1 pad_maximum_fusion.2.refs_3_
  62.0 0.0 copy-start
  62.0 1.5 collective-permute-start.16
  63.5 0.1 pad_maximum_fusion.1.refs_1_
  63.6 3.2 %reduce.8 = (f32[2,2,8,8,512]{4,3,2,1,0:T(8,128)S(1)}, f32[2,2,8,8,512]{4,3,2,1,0:T(8,128)S(1)}) custom-call(s32[3]{0:T(128)S(1)} %pad_add_fusion.place_ref, bf16[64,9216]{1,0:T(8,128)(2,1)S(1)} %pad_maximum_fusion.3.refs_0_, bf16[64,9216]{1,0:T(8,128)(2,1)S(1)} %pad_maximum_fusion.1.refs_1_, bf16[64,9216]{1,0:T(8,128)(2,1)S(1)} %pad_maximum_fusion.4.refs_2_, ...), custom_call_target="tpu_custom_call" | custom-call | flops 1048576 | bytes 65536 | tf_op jit(solution)/shard_map/reduce/pallas_call | solution.py:59
  66.9 5.8 %collective-permute-start.17 = (f32[2,2,8,8,512]{4,3,2,1,0:T(8,128)S(1)}, f32[2,2,8,8,512]{4,3,2,1,0:T(8,128)S(1)}, u32[]{:S(2)}, u32[]{:S(2)}) collective-permute-start(f32[2,2,8,8,512]{4,3,2,1,0:T(8,128)S(1)} %get-tuple-element.52), channel_id=1, source_target_pairs={{0,1},{1,0},{2,3},{3,2},{4,5},{5,4},{6,7},{7,6},{8,9},{9,8},{10,11... | collective-permute-start | bytes 1572872 | tf_op jit(solution)/shard_map/reduce/ppermute | solution.py:144
  72.7 1.5 collective-permute-done.17
  74.2 1.7 collective-permute-start.10
  75.9 12.1 %collective-permute-done.13.refs_0_ = bf16[64,9216]{1,0:T(8,128)(2,1)S(1)} collective-permute-done((bf16[64,9216]{1,0:T(8,128)(2,1)S(1)}, bf16[64,9216]{1,0:T(8,128)(2,1)S(1)}, u32[]{:S(2)}, u32[]{:S(2)}) %collective-permute-start.13) | collective-permute-done | bytes 1179680 | tf_op jit(solution)/shard_map/second_axis/ppermute | solution.py:21
  88.1 0.9 collective-permute-start.11
  89.0 0.0 collective-permute-done.14.refs_1_
  89.0 1.8 %collective-permute-start.12 = (bf16[64,9216]{1,0:T(8,128)(2,1)S(1)}, bf16[64,9216]{1,0:T(8,128)(2,1)S(1)}, u32[]{:S(2)}, u32[]{:S(2)}) collective-permute-start(bf16[64,9216]{1,0:T(8,128)(2,1)S(1)} %pad_maximum_fusion.2.refs_3_), channel_id=1, source_target_pairs={{0,48},{16,0},{32,16},{48,32},{1,49},{17,1},{33,17},{49,33},{2,50}... | collective-permute-start | bytes 3538952 | tf_op jit(solution)/shard_map/second_axis/ppermute | solution.py:21
  90.8 0.0 collective-permute-start.9
  90.8 0.0 collective-permute-done.16.refs_3_
  90.8 5.0 %collective-permute-start.18 = (f32[2,8,8,512]{3,2,1,0:T(8,128)S(1)}, f32[2,8,8,512]{3,2,1,0:T(8,128)S(1)}, u32[]{:S(2)}, u32[]{:S(2)}) collective-permute-start(f32[2,8,8,512]{3,2,1,0:T(8,128)S(1)} %fusion.7), channel_id=1, source_target_pairs={{0,2},{2,0},{1,3},{3,1},{4,6},{6,4},{5,7},{7,5},{8,10},{10,8},{9,1... | collective-permute-start | bytes 786440 | tf_op jit(solution)/shard_map/reduce/ppermute | solution.py:141
  95.8 3.2 %reduce.9 = (f32[2,2,8,8,512]{4,3,2,1,0:T(8,128)S(1)}, f32[2,2,8,8,512]{4,3,2,1,0:T(8,128)S(1)}) custom-call(s32[3]{0:T(128)S(1)} %pad_add_fusion.place_ref, bf16[64,9216]{1,0:T(8,128)(2,1)S(1)} %collective-permute-done.13.refs_0_, bf16[64,9216]{1,0:T(8,128)(2,1)S(1)} %collective-permute-done.14.refs_1_, ...), custom_call_target="tpu_custom_call" | custom-call | flops 1048576 | bytes 65536 | tf_op jit(solution)/shard_map/reduce/pallas_call | solution.py:59
  99.1 6.0 %collective-permute-done.18 = f32[2,8,8,512]{3,2,1,0:T(8,128)S(1)} collective-permute-done((f32[2,8,8,512]{3,2,1,0:T(8,128)S(1)}, f32[2,8,8,512]{3,2,1,0:T(8,128)S(1)}, u32[]{:S(2)}, u32[]{:S(2)}) %collective-permute-start.18) | collective-permute-done | bytes 262176 | tf_op jit(solution)/shard_map/reduce/ppermute | solution.py:141
  105.1 0.6 collective-permute-start.23
  105.6 0.1 fusion.9
  105.7 4.2 %collective-permute-done.10.refs_1_ = bf16[64,9216]{1,0:T(8,128)(2,1)S(1)} collective-permute-done((bf16[64,9216]{1,0:T(8,128)(2,1)S(1)}, bf16[64,9216]{1,0:T(8,128)(2,1)S(1)}, u32[]{:S(2)}, u32[]{:S(2)}) %collective-permute-start.10) | collective-permute-done | bytes 1179680 | tf_op jit(solution)/shard_map/second_axis/ppermute | solution.py:21
  109.9 6.4 %collective-permute-done.11.refs_2_ = bf16[64,9216]{1,0:T(8,128)(2,1)S(1)} collective-permute-done((bf16[64,9216]{1,0:T(8,128)(2,1)S(1)}, bf16[64,9216]{1,0:T(8,128)(2,1)S(1)}, u32[]{:S(2)}, u32[]{:S(2)}) %collective-permute-start.11) | collective-permute-done | bytes 1179680 | tf_op jit(solution)/shard_map/second_axis/ppermute | solution.py:21
  116.3 2.0 %collective-permute-done.9.refs_0_ = bf16[64,9216]{1,0:T(8,128)(2,1)S(1)} collective-permute-done((bf16[64,9216]{1,0:T(8,128)(2,1)S(1)}, bf16[64,9216]{1,0:T(8,128)(2,1)S(1)}, u32[]{:S(2)}, u32[]{:S(2)}) %collective-permute-start.9) | collective-permute-done | bytes 1179680 | tf_op jit(solution)/shard_map/second_axis/ppermute | solution.py:21
  118.3 2.7 %collective-permute-start.20 = (bf16[64,9216]{1,0:T(8,128)(2,1)S(1)}, bf16[64,9216]{1,0:T(8,128)(2,1)S(1)}, u32[]{:S(2)}, u32[]{:S(2)}) collective-permute-start(bf16[64,9216]{1,0:T(8,128)(2,1)S(1)} %collective-permute-done.10.refs_1_), channel_id=1, source_target_pairs={{0,12},{4,0},{8,4},{12,8},{1,13},{5,1},{9,5},{13,9},{2,14},{6,2},{... | collective-permute-start | bytes 3538952 | tf_op jit(solution)/shard_map/second_axis/ppermute | solution.py:21
  121.0 2.7 %collective-permute-start.22 = (bf16[64,9216]{1,0:T(8,128)(2,1)S(1)}, bf16[64,9216]{1,0:T(8,128)(2,1)S(1)}, u32[]{:S(2)}, u32[]{:S(2)}) collective-permute-start(bf16[64,9216]{1,0:T(8,128)(2,1)S(1)} %collective-permute-done.12.refs_3_), channel_id=1, source_target_pairs={{0,48},{16,0},{32,16},{48,32},{1,49},{17,1},{33,17},{49,33},{2,50}... | collective-permute-start | bytes 3538952 | tf_op jit(solution)/shard_map/second_axis/ppermute | solution.py:21
  123.7 3.2 %reduce.10 = (f32[2,2,8,8,512]{4,3,2,1,0:T(8,128)S(1)}, f32[2,2,8,8,512]{4,3,2,1,0:T(8,128)S(1)}) custom-call(s32[3]{0:T(128)S(1)} %pad_add_fusion.place_ref, bf16[64,9216]{1,0:T(8,128)(2,1)S(1)} %collective-permute-done.9.refs_0_, bf16[64,9216]{1,0:T(8,128)(2,1)S(1)} %collective-permute-done.10.refs_1_, ...), custom_call_target="tpu_custom_call" | custom-call | flops 1048576 | bytes 65536 | tf_op jit(solution)/shard_map/reduce/pallas_call | solution.py:59
  126.9 3.3 %collective-permute-start.25 = (f32[2,2,8,8,512]{4,3,2,1,0:T(8,128)S(1)}, f32[2,2,8,8,512]{4,3,2,1,0:T(8,128)S(1)}, u32[]{:S(2)}, u32[]{:S(2)}) collective-permute-start(f32[2,2,8,8,512]{4,3,2,1,0:T(8,128)S(1)} %get-tuple-element.65), channel_id=1, source_target_pairs={{0,1},{1,0},{2,3},{3,2},{4,5},{5,4},{6,7},{7,6},{8,9},{9,8},{10,11... | collective-permute-start | bytes 1572872 | tf_op jit(solution)/shard_map/reduce/ppermute | solution.py:144
  130.2 1.5 collective-permute-done.25
  131.7 4.9 %collective-permute-start.24 = (f32[2,8,8,512]{3,2,1,0:T(8,128)S(1)}, f32[2,8,8,512]{3,2,1,0:T(8,128)S(1)}, u32[]{:S(2)}, u32[]{:S(2)}) collective-permute-start(f32[2,8,8,512]{3,2,1,0:T(8,128)S(1)} %fusion.4), channel_id=1, source_target_pairs={{0,2},{2,0},{1,3},{3,1},{4,6},{6,4},{5,7},{7,5},{8,10},{10,8},{9,1... | collective-permute-start | bytes 786440 | tf_op jit(solution)/shard_map/reduce/ppermute | solution.py:141
  136.7 6.5 %collective-permute-done.24 = f32[2,8,8,512]{3,2,1,0:T(8,128)S(1)} collective-permute-done((f32[2,8,8,512]{3,2,1,0:T(8,128)S(1)}, f32[2,8,8,512]{3,2,1,0:T(8,128)S(1)}, u32[]{:S(2)}, u32[]{:S(2)}) %collective-permute-start.24) | collective-permute-done | bytes 262176 | tf_op jit(solution)/shard_map/reduce/ppermute | solution.py:141
  143.1 0.1 fusion.6
  143.2 1.7 collective-permute-done.19.refs_0_
  144.9 2.1 %collective-permute-done.21.refs_2_ = bf16[64,9216]{1,0:T(8,128)(2,1)S(1)} collective-permute-done((bf16[64,9216]{1,0:T(8,128)(2,1)S(1)}, bf16[64,9216]{1,0:T(8,128)(2,1)S(1)}, u32[]{:S(2)}, u32[]{:S(2)}) %collective-permute-start.21) | collective-permute-done | bytes 1179680 | tf_op jit(solution)/shard_map/second_axis/ppermute | solution.py:21
  147.1 3.2 %reduce.11 = (f32[2,2,8,8,512]{4,3,2,1,0:T(8,128)S(1)}, f32[2,2,8,8,512]{4,3,2,1,0:T(8,128)S(1)}) custom-call(s32[3]{0:T(128)S(1)} %pad_add_fusion.place_ref, bf16[64,9216]{1,0:T(8,128)(2,1)S(1)} %collective-permute-done.19.refs_0_, bf16[64,9216]{1,0:T(8,128)(2,1)S(1)} %collective-permute-done.20.refs_1_, ...), custom_call_target="tpu_custom_call" | custom-call | flops 1048576 | bytes 65536 | tf_op jit(solution)/shard_map/reduce/pallas_call | solution.py:59
  150.3 3.6 %collective-permute-start.27 = (f32[2,2,8,8,512]{4,3,2,1,0:T(8,128)S(1)}, f32[2,2,8,8,512]{4,3,2,1,0:T(8,128)S(1)}, u32[]{:S(2)}, u32[]{:S(2)}) collective-permute-start(f32[2,2,8,8,512]{4,3,2,1,0:T(8,128)S(1)} %get-tuple-element.72), channel_id=1, source_target_pairs={{0,1},{1,0},{2,3},{3,2},{4,5},{5,4},{6,7},{7,6},{8,9},{9,8},{10,11... | collective-permute-start | bytes 1572872 | tf_op jit(solution)/shard_map/reduce/ppermute | solution.py:144
  153.9 4.5 %collective-permute-start.26 = (f32[2,8,8,512]{3,2,1,0:T(8,128)S(1)}, f32[2,8,8,512]{3,2,1,0:T(8,128)S(1)}, u32[]{:S(2)}, u32[]{:S(2)}) collective-permute-start(f32[2,8,8,512]{3,2,1,0:T(8,128)S(1)} %fusion.3), channel_id=1, source_target_pairs={{0,2},{2,0},{1,3},{3,1},{4,6},{6,4},{5,7},{7,5},{8,10},{10,8},{9,1... | collective-permute-start | bytes 786440 | tf_op jit(solution)/shard_map/reduce/ppermute | solution.py:141
  158.5 1.6 collective-permute-start.28
  160.1 8.2 %collective-permute-done.26 = f32[2,8,8,512]{3,2,1,0:T(8,128)S(1)} collective-permute-done((f32[2,8,8,512]{3,2,1,0:T(8,128)S(1)}, f32[2,8,8,512]{3,2,1,0:T(8,128)S(1)}, u32[]{:S(2)}, u32[]{:S(2)}) %collective-permute-start.26) | collective-permute-done | bytes 262176 | tf_op jit(solution)/shard_map/reduce/ppermute | solution.py:141
  168.2 0.1 fusion.2
  168.3 5.5 %collective-permute-done.28.back_ref = f32[2,8,8,512]{3,2,1,0:T(8,128)S(1)} collective-permute-done((f32[2,8,8,512]{3,2,1,0:T(8,128)S(1)}, f32[2,8,8,512]{3,2,1,0:T(8,128)S(1)}, u32[]{:S(2)}, u32[]{:S(2)}) %collective-permute-start.28) | collective-permute-done | bytes 262176 | tf_op jit(solution)/shard_map/reduce/ppermute | solution.py:141
  173.9 1.6 reduce.12
  (26 shorter events, 0.3 us)
Async XLA Ops:
  1.0 9.2 %collective-permute-start = (bf16[16,9216]{1,0:T(8,128)(2,1)S(1)}, bf16[16,9216]{1,0:T(8,128)(2,1)S(1)}, u32[]{:S(2)}, u32[]{:S(2)}) collective-permute-start(bf16[16,9216]{1,0:T(8,128)(2,1)S(1)} %get-tuple-element.76), channel_id=1, source_target_pairs={{0,64},{64,0},{128,192},{192,128},{1,65},{65,1},{129,193},{193,129... | collective-permute-start | bytes 884744 | tf_op jit(solution)/shard_map/z_shifts/ppermute | solution.py:26
  1.1 21.3 %collective-permute-start.1 = (bf16[16,9216]{1,0:T(8,128)(2,1)S(1)}, bf16[16,9216]{1,0:T(8,128)(2,1)S(1)}, u32[]{:S(2)}, u32[]{:S(2)}) collective-permute-start(bf16[16,9216]{1,0:T(8,128)(2,1)S(1)} %get-tuple-element.76), channel_id=1, source_target_pairs={{0,128},{64,192},{128,0},{192,64},{1,129},{65,193},{129,1},{193,65... | collective-permute-start | bytes 884744 | tf_op jit(solution)/shard_map/z_shifts/ppermute | solution.py:26
  4.2 25.6 %collective-permute-start.2 = (bf16[16,9216]{1,0:T(8,128)(2,1)S(1)}, bf16[16,9216]{1,0:T(8,128)(2,1)S(1)}, u32[]{:S(2)}, u32[]{:S(2)}) collective-permute-start(bf16[16,9216]{1,0:T(8,128)(2,1)S(1)} %get-tuple-element.76), channel_id=1, source_target_pairs={{0,192},{64,128},{128,64},{192,0},{1,193},{65,129},{129,65},{193,1... | collective-permute-start | bytes 884744 | tf_op jit(solution)/shard_map/z_shifts/ppermute | solution.py:26
  29.8 33.7 %slice-start = ((s8[7340032]{0:T(1024)(128)(4,1)}), s8[3145728]{0:T(1024)(128)(4,1)S(1)}, s32[]{:S(2)}) async-start(s8[7340032]{0:T(1024)(128)(4,1)} %bitcast.34), calls=%async_computation | async-start | bytes 6291456
  31.1 15.0 %collective-permute-start.7 = (bf16[32,9216]{1,0:T(8,128)(2,1)}, bf16[32,9216]{1,0:T(8,128)(2,1)}, u32[]{:S(2)}, u32[]{:S(2)}) collective-permute-start(bf16[32,9216]{1,0:T(8,128)(2,1)} %get-tuple-element.74), channel_id=1, source_target_pairs={{0,16},{16,32},{32,48},{48,0},{1,17},{17,33},{33,49},{49,1},{2,18}... | collective-permute-start | bytes 1769480 | tf_op jit(solution)/shard_map/first_axis/ppermute | solution.py:21
  32.5 16.5 %copy-start.1 = (bf16[32,9216]{1,0:T(8,128)(2,1)S(1)}, bf16[32,9216]{1,0:T(8,128)(2,1)}, u32[]{:S(2)}) copy-start(bf16[32,9216]{1,0:T(8,128)(2,1)} %get-tuple-element.73) | copy-start | bytes 1769476
  32.5 31.1 %slice-start.1 = ((s8[7340032]{0:T(1024)(128)(4,1)}), s8[4194304]{0:T(1024)(128)(4,1)S(1)}, s32[]{:S(2)}) async-start(s8[7340032]{0:T(1024)(128)(4,1)} %bitcast.34), calls=%async_computation.1 | async-start | bytes 8388608
  32.5 16.5 %collective-permute-start.8 = (bf16[32,9216]{1,0:T(8,128)(2,1)}, bf16[32,9216]{1,0:T(8,128)(2,1)S(1)}, u32[]{:S(2)}, u32[]{:S(2)}) collective-permute-start(bf16[32,9216]{1,0:T(8,128)(2,1)} %get-tuple-element.73), channel_id=1, source_target_pairs={{0,4},{4,8},{8,12},{12,0},{1,5},{5,9},{9,13},{13,1},{2,6},{6,10},{... | collective-permute-start | bytes 1769480 | tf_op jit(solution)/shard_map/first_axis/ppermute | solution.py:21
  33.7 16.6 %collective-permute-start.5 = (bf16[32,9216]{1,0:T(8,128)(2,1)}, bf16[32,9216]{1,0:T(8,128)(2,1)S(1)}, u32[]{:S(2)}, u32[]{:S(2)}) collective-permute-start(bf16[32,9216]{1,0:T(8,128)(2,1)} %get-tuple-element.73), channel_id=1, source_target_pairs={{0,12},{4,0},{8,4},{12,8},{1,13},{5,1},{9,5},{13,9},{2,14},{6,2},{... | collective-permute-start | bytes 1769480 | tf_op jit(solution)/shard_map/first_axis/ppermute | solution.py:21
  35.2 25.4 %collective-permute-start.6 = (bf16[32,9216]{1,0:T(8,128)(2,1)}, bf16[32,9216]{1,0:T(8,128)(2,1)S(1)}, u32[]{:S(2)}, u32[]{:S(2)}) collective-permute-start(bf16[32,9216]{1,0:T(8,128)(2,1)} %get-tuple-element.73), channel_id=1, source_target_pairs={{0,8},{4,12},{8,0},{12,4},{1,9},{5,13},{9,1},{13,5},{2,10},{6,14},... | collective-permute-start | bytes 1769480 | tf_op jit(solution)/shard_map/first_axis/ppermute | solution.py:21
  36.7 25.3 %collective-permute-start.3 = (bf16[32,9216]{1,0:T(8,128)(2,1)}, bf16[32,9216]{1,0:T(8,128)(2,1)S(1)}, u32[]{:S(2)}, u32[]{:S(2)}) collective-permute-start(bf16[32,9216]{1,0:T(8,128)(2,1)} %get-tuple-element.74), channel_id=1, source_target_pairs={{0,48},{16,0},{32,16},{48,32},{1,49},{17,1},{33,17},{49,33},{2,50}... | collective-permute-start | bytes 1769480 | tf_op jit(solution)/shard_map/first_axis/ppermute | solution.py:21
  46.1 17.4 %collective-permute-start.4 = (bf16[32,9216]{1,0:T(8,128)(2,1)}, bf16[32,9216]{1,0:T(8,128)(2,1)S(1)}, u32[]{:S(2)}, u32[]{:S(2)}) collective-permute-start(bf16[32,9216]{1,0:T(8,128)(2,1)} %get-tuple-element.74), channel_id=1, source_target_pairs={{0,32},{16,48},{32,0},{48,16},{1,33},{17,49},{33,1},{49,17},{2,34}... | collective-permute-start | bytes 1769480 | tf_op jit(solution)/shard_map/first_axis/ppermute | solution.py:21
  49.1 39.0 %collective-permute-start.13 = (bf16[64,9216]{1,0:T(8,128)(2,1)S(1)}, bf16[64,9216]{1,0:T(8,128)(2,1)S(1)}, u32[]{:S(2)}, u32[]{:S(2)}) collective-permute-start(bf16[64,9216]{1,0:T(8,128)(2,1)S(1)} %pad_maximum_fusion.3.refs_0_), channel_id=1, source_target_pairs={{0,4},{4,8},{8,12},{12,0},{1,5},{5,9},{9,13},{13,1},{2,6},{6,10},{... | collective-permute-start | bytes 3538952 | tf_op jit(solution)/shard_map/second_axis/ppermute | solution.py:21
  50.4 38.6 %collective-permute-start.14 = (bf16[64,9216]{1,0:T(8,128)(2,1)S(1)}, bf16[64,9216]{1,0:T(8,128)(2,1)S(1)}, u32[]{:S(2)}, u32[]{:S(2)}) collective-permute-start(bf16[64,9216]{1,0:T(8,128)(2,1)S(1)} %pad_maximum_fusion.3.refs_0_), channel_id=1, source_target_pairs={{0,12},{4,0},{8,4},{12,8},{1,13},{5,1},{9,5},{13,9},{2,14},{6,2},{... | collective-permute-start | bytes 3538952 | tf_op jit(solution)/shard_map/second_axis/ppermute | solution.py:21
  60.6 30.1 %collective-permute-start.15 = (bf16[64,9216]{1,0:T(8,128)(2,1)S(1)}, bf16[64,9216]{1,0:T(8,128)(2,1)S(1)}, u32[]{:S(2)}, u32[]{:S(2)}) collective-permute-start(bf16[64,9216]{1,0:T(8,128)(2,1)S(1)} %pad_maximum_fusion.4.refs_2_), channel_id=1, source_target_pairs={{0,16},{16,32},{32,48},{48,0},{1,17},{17,33},{33,49},{49,1},{2,18}... | collective-permute-start | bytes 3538952 | tf_op jit(solution)/shard_map/second_axis/ppermute | solution.py:21
  62.0 1.6 copy-start
  62.0 28.8 %collective-permute-start.16 = (bf16[64,9216]{1,0:T(8,128)(2,1)S(1)}, bf16[64,9216]{1,0:T(8,128)(2,1)S(1)}, u32[]{:S(2)}, u32[]{:S(2)}) collective-permute-start(bf16[64,9216]{1,0:T(8,128)(2,1)S(1)} %pad_maximum_fusion.4.refs_2_), channel_id=1, source_target_pairs={{0,48},{16,0},{32,16},{48,32},{1,49},{17,1},{33,17},{49,33},{2,50}... | collective-permute-start | bytes 3538952 | tf_op jit(solution)/shard_map/second_axis/ppermute | solution.py:21
  66.9 7.4 %collective-permute-start.17 = (f32[2,2,8,8,512]{4,3,2,1,0:T(8,128)S(1)}, f32[2,2,8,8,512]{4,3,2,1,0:T(8,128)S(1)}, u32[]{:S(2)}, u32[]{:S(2)}) collective-permute-start(f32[2,2,8,8,512]{4,3,2,1,0:T(8,128)S(1)} %get-tuple-element.52), channel_id=1, source_target_pairs={{0,1},{1,0},{2,3},{3,2},{4,5},{5,4},{6,7},{7,6},{8,9},{9,8},{10,11... | collective-permute-start | bytes 1572872 | tf_op jit(solution)/shard_map/reduce/ppermute | solution.py:144
  74.2 35.7 %collective-permute-start.10 = (bf16[64,9216]{1,0:T(8,128)(2,1)S(1)}, bf16[64,9216]{1,0:T(8,128)(2,1)S(1)}, u32[]{:S(2)}, u32[]{:S(2)}) collective-permute-start(bf16[64,9216]{1,0:T(8,128)(2,1)S(1)} %pad_maximum_fusion.1.refs_1_), channel_id=1, source_target_pairs={{0,12},{4,0},{8,4},{12,8},{1,13},{5,1},{9,5},{13,9},{2,14},{6,2},{... | collective-permute-start | bytes 3538952 | tf_op jit(solution)/shard_map/second_axis/ppermute | solution.py:21
  88.1 28.3 %collective-permute-start.11 = (bf16[64,9216]{1,0:T(8,128)(2,1)S(1)}, bf16[64,9216]{1,0:T(8,128)(2,1)S(1)}, u32[]{:S(2)}, u32[]{:S(2)}) collective-permute-start(bf16[64,9216]{1,0:T(8,128)(2,1)S(1)} %pad_maximum_fusion.2.refs_3_), channel_id=1, source_target_pairs={{0,16},{16,32},{32,48},{48,0},{1,17},{17,33},{33,49},{49,1},{2,18}... | collective-permute-start | bytes 3538952 | tf_op jit(solution)/shard_map/second_axis/ppermute | solution.py:21
  89.0 27.4 %collective-permute-start.12 = (bf16[64,9216]{1,0:T(8,128)(2,1)S(1)}, bf16[64,9216]{1,0:T(8,128)(2,1)S(1)}, u32[]{:S(2)}, u32[]{:S(2)}) collective-permute-start(bf16[64,9216]{1,0:T(8,128)(2,1)S(1)} %pad_maximum_fusion.2.refs_3_), channel_id=1, source_target_pairs={{0,48},{16,0},{32,16},{48,32},{1,49},{17,1},{33,17},{49,33},{2,50}... | collective-permute-start | bytes 3538952 | tf_op jit(solution)/shard_map/second_axis/ppermute | solution.py:21
  90.8 27.5 %collective-permute-start.9 = (bf16[64,9216]{1,0:T(8,128)(2,1)S(1)}, bf16[64,9216]{1,0:T(8,128)(2,1)S(1)}, u32[]{:S(2)}, u32[]{:S(2)}) collective-permute-start(bf16[64,9216]{1,0:T(8,128)(2,1)S(1)} %pad_maximum_fusion.1.refs_1_), channel_id=1, source_target_pairs={{0,4},{4,8},{8,12},{12,0},{1,5},{5,9},{9,13},{13,1},{2,6},{6,10},{... | collective-permute-start | bytes 3538952 | tf_op jit(solution)/shard_map/second_axis/ppermute | solution.py:21
  90.8 14.3 %collective-permute-start.18 = (f32[2,8,8,512]{3,2,1,0:T(8,128)S(1)}, f32[2,8,8,512]{3,2,1,0:T(8,128)S(1)}, u32[]{:S(2)}, u32[]{:S(2)}) collective-permute-start(f32[2,8,8,512]{3,2,1,0:T(8,128)S(1)} %fusion.7), channel_id=1, source_target_pairs={{0,2},{2,0},{1,3},{3,1},{4,6},{6,4},{5,7},{7,5},{8,10},{10,8},{9,1... | collective-permute-start | bytes 786440 | tf_op jit(solution)/shard_map/reduce/ppermute | solution.py:141
  105.1 21.8 %collective-permute-start.23 = (f32[2,2,8,8,512]{4,3,2,1,0:T(8,128)S(1)}, f32[2,2,8,8,512]{4,3,2,1,0:T(8,128)S(1)}, u32[]{:S(2)}, u32[]{:S(2)}) collective-permute-start(f32[2,2,8,8,512]{4,3,2,1,0:T(8,128)S(1)} %get-tuple-element.61), channel_id=1, source_target_pairs={{0,1},{1,0},{2,3},{3,2},{4,5},{5,4},{6,7},{7,6},{8,9},{9,8},{10,11... | collective-permute-start | bytes 1572872 | tf_op jit(solution)/shard_map/reduce/ppermute | solution.py:144
  118.3 26.6 %collective-permute-start.19 = (bf16[64,9216]{1,0:T(8,128)(2,1)S(1)}, bf16[64,9216]{1,0:T(8,128)(2,1)S(1)}, u32[]{:S(2)}, u32[]{:S(2)}) collective-permute-start(bf16[64,9216]{1,0:T(8,128)(2,1)S(1)} %collective-permute-done.13.refs_0_), channel_id=1, source_target_pairs={{0,4},{4,8},{8,12},{12,0},{1,5},{5,9},{9,13},{13,1},{2,6},{6,10},{... | collective-permute-start | bytes 3538952 | tf_op jit(solution)/shard_map/second_axis/ppermute | solution.py:21
  118.3 26.6 %collective-permute-start.20 = (bf16[64,9216]{1,0:T(8,128)(2,1)S(1)}, bf16[64,9216]{1,0:T(8,128)(2,1)S(1)}, u32[]{:S(2)}, u32[]{:S(2)}) collective-permute-start(bf16[64,9216]{1,0:T(8,128)(2,1)S(1)} %collective-permute-done.10.refs_1_), channel_id=1, source_target_pairs={{0,12},{4,0},{8,4},{12,8},{1,13},{5,1},{9,5},{13,9},{2,14},{6,2},{... | collective-permute-start | bytes 3538952 | tf_op jit(solution)/shard_map/second_axis/ppermute | solution.py:21
  121.0 26.1 %collective-permute-start.21 = (bf16[64,9216]{1,0:T(8,128)(2,1)S(1)}, bf16[64,9216]{1,0:T(8,128)(2,1)S(1)}, u32[]{:S(2)}, u32[]{:S(2)}) collective-permute-start(bf16[64,9216]{1,0:T(8,128)(2,1)S(1)} %collective-permute-done.15.refs_2_), channel_id=1, source_target_pairs={{0,16},{16,32},{32,48},{48,0},{1,17},{17,33},{33,49},{49,1},{2,18}... | collective-permute-start | bytes 3538952 | tf_op jit(solution)/shard_map/second_axis/ppermute | solution.py:21
  121.0 26.1 %collective-permute-start.22 = (bf16[64,9216]{1,0:T(8,128)(2,1)S(1)}, bf16[64,9216]{1,0:T(8,128)(2,1)S(1)}, u32[]{:S(2)}, u32[]{:S(2)}) collective-permute-start(bf16[64,9216]{1,0:T(8,128)(2,1)S(1)} %collective-permute-done.12.refs_3_), channel_id=1, source_target_pairs={{0,48},{16,0},{32,16},{48,32},{1,49},{17,1},{33,17},{49,33},{2,50}... | collective-permute-start | bytes 3538952 | tf_op jit(solution)/shard_map/second_axis/ppermute | solution.py:21
  126.9 4.8 %collective-permute-start.25 = (f32[2,2,8,8,512]{4,3,2,1,0:T(8,128)S(1)}, f32[2,2,8,8,512]{4,3,2,1,0:T(8,128)S(1)}, u32[]{:S(2)}, u32[]{:S(2)}) collective-permute-start(f32[2,2,8,8,512]{4,3,2,1,0:T(8,128)S(1)} %get-tuple-element.65), channel_id=1, source_target_pairs={{0,1},{1,0},{2,3},{3,2},{4,5},{5,4},{6,7},{7,6},{8,9},{9,8},{10,11... | collective-permute-start | bytes 1572872 | tf_op jit(solution)/shard_map/reduce/ppermute | solution.py:144
  131.7 11.4 %collective-permute-start.24 = (f32[2,8,8,512]{3,2,1,0:T(8,128)S(1)}, f32[2,8,8,512]{3,2,1,0:T(8,128)S(1)}, u32[]{:S(2)}, u32[]{:S(2)}) collective-permute-start(f32[2,8,8,512]{3,2,1,0:T(8,128)S(1)} %fusion.4), channel_id=1, source_target_pairs={{0,2},{2,0},{1,3},{3,1},{4,6},{6,4},{5,7},{7,5},{8,10},{10,8},{9,1... | collective-permute-start | bytes 786440 | tf_op jit(solution)/shard_map/reduce/ppermute | solution.py:141
  150.3 8.1 %collective-permute-start.27 = (f32[2,2,8,8,512]{4,3,2,1,0:T(8,128)S(1)}, f32[2,2,8,8,512]{4,3,2,1,0:T(8,128)S(1)}, u32[]{:S(2)}, u32[]{:S(2)}) collective-permute-start(f32[2,2,8,8,512]{4,3,2,1,0:T(8,128)S(1)} %get-tuple-element.72), channel_id=1, source_target_pairs={{0,1},{1,0},{2,3},{3,2},{4,5},{5,4},{6,7},{7,6},{8,9},{9,8},{10,11... | collective-permute-start | bytes 1572872 | tf_op jit(solution)/shard_map/reduce/ppermute | solution.py:144
  153.9 14.3 %collective-permute-start.26 = (f32[2,8,8,512]{3,2,1,0:T(8,128)S(1)}, f32[2,8,8,512]{3,2,1,0:T(8,128)S(1)}, u32[]{:S(2)}, u32[]{:S(2)}) collective-permute-start(f32[2,8,8,512]{3,2,1,0:T(8,128)S(1)} %fusion.3), channel_id=1, source_target_pairs={{0,2},{2,0},{1,3},{3,1},{4,6},{6,4},{5,7},{7,5},{8,10},{10,8},{9,1... | collective-permute-start | bytes 786440 | tf_op jit(solution)/shard_map/reduce/ppermute | solution.py:141
  158.5 15.4 %collective-permute-start.28 = (f32[2,8,8,512]{3,2,1,0:T(8,128)S(1)}, f32[2,8,8,512]{3,2,1,0:T(8,128)S(1)}, u32[]{:S(2)}, u32[]{:S(2)}) collective-permute-start(f32[2,8,8,512]{3,2,1,0:T(8,128)S(1)} %fusion), channel_id=1, source_target_pairs={{0,2},{2,0},{1,3},{3,1},{4,6},{6,4},{5,7},{7,5},{8,10},{10,8},{9,1... | collective-permute-start | bytes 786440 | tf_op jit(solution)/shard_map/reduce/ppermute | solution.py:141

commit v7 on v4

--- a/solution.py
+++ b/solution.py
@@ -185,7 +185,8 @@
         far, sums2, sent3 = lax.optimization_barrier((far, sums2, sent3))
         keep4, got4 = work(far)
         sums3 = sums(keep3, got3, back3)
-        back4 = exchange(keep4[1] + got4[1])
+        sent4, sums3 = lax.optimization_barrier((keep4[1] + got4[1], sums3))
+        back4 = exchange(sent4)
         return finish(place, (sums1, sums2, sums3), keep4, got4, back4)
 
 

time: 174 us -> 168 us (0.966)
  waiting for transfers between devices: 77 us -> 73.2 us
  starting transfers between devices: 74 us -> 71.8 us
    ppermute x4, starting transfers between devices: 30.1 us -> 27.2 us  [over(): return lax.ppermute(send, 'core', [(0, 1), (1, 0)])]
    ppermute x4, waiting for transfers between devices: 22.3 us -> 20 us  [exchange(): return lax.ppermute(sent, 'zh', [(0, 1), (1, 0)])]
  transfers between devices with their start and end apart: 31 -> 31, of which waited for: 16 -> 15; matrix products, arithmetic and copies ran while one was open for 3% -> 3% of each run, Pallas kernels for 6% -> 8%
where the time goes in v7:
time: 168 us; the launch traced here: 167 us
  waiting for transfers between devices  73.2 us (44%)
  starting transfers between devices  71.8 us (43%)
  Pallas kernels  14.5 us (9%)
  other arithmetic  4.39 us (3%)
  local copies, waits for them, and re-layouts  3.14 us (2%)
    ppermute x4, starting transfers between devices, over(): return lax.ppermute(send, 'core', [(0, 1), (1, 0)])  27.2 us
    ppermute x3, waiting for transfers between devices, flip(): return lax.ppermute(x, axis, [(i, i ^ mask) for i in range(n)])  25.5 us
    ppermute x20, starting transfers between devices, ring(): return lax.ppermute(x, axis, [(i, (i + step) % n) for i in range(n)])  24.9 us
    ppermute x20, waiting for transfers between devices, ring(): return lax.ppermute(x, axis, [(i, (i + step) % n) for i in range(n)])  24.7 us
    ppermute x4, waiting for transfers between devices, exchange(): return lax.ppermute(sent, 'zh', [(0, 1), (1, 0)])  20 us
    ppermute x4, starting transfers between devices, exchange(): return lax.ppermute(sent, 'zh', [(0, 1), (1, 0)])  16.4 us
    pallas_call x4, Pallas kernels, project(): pl.pallas_call(functools.partial(project_kernel, len(blocks)), out_shape=...  12.9 us
  transfers between devices with their start and end apart: 31, of which 15 were waited for; matrix products, arithmetic and copies ran while one was open for 3% of the time, Pallas kernels for 8%

profile of v7, /device:TPU:33, one launch (start us, length us, event | category | flops | bytes accessed | tf_op | source)
XLA Modules:
  0.0 167.3 jit_solution(11960428911443916453)
XLA Ops:
  0.0 1.0 fusion.13
  1.0 0.1 collective-permute-start
  1.1 3.1 %collective-permute-start.1 = (bf16[16,9216]{1,0:T(8,128)(2,1)S(1)}, bf16[16,9216]{1,0:T(8,128)(2,1)S(1)}, u32[]{:S(2)}, u32[]{:S(2)}) collective-permute-start(bf16[16,9216]{1,0:T(8,128)(2,1)S(1)} %get-tuple-element.80), channel_id=1, source_target_pairs={{0,128},{64,192},{128,0},{192,64},{1,129},{65,193},{129,1},{193,65... | collective-permute-start | bytes 884744 | tf_op jit(solution)/shard_map/z_shifts/ppermute | solution.py:26
  4.2 0.2 collective-permute-start.2
  4.4 5.9 %collective-permute-done = bf16[16,9216]{1,0:T(8,128)(2,1)S(1)} collective-permute-done((bf16[16,9216]{1,0:T(8,128)(2,1)S(1)}, bf16[16,9216]{1,0:T(8,128)(2,1)S(1)}, u32[]{:S(2)}, u32[]{:S(2)}) %collective-permute-start) | collective-permute-done | bytes 294944 | tf_op jit(solution)/shard_map/z_shifts/ppermute | solution.py:26
  10.2 12.2 %collective-permute-done.1 = bf16[16,9216]{1,0:T(8,128)(2,1)S(1)} collective-permute-done((bf16[16,9216]{1,0:T(8,128)(2,1)S(1)}, bf16[16,9216]{1,0:T(8,128)(2,1)S(1)}, u32[]{:S(2)}, u32[]{:S(2)}) %collective-permute-start.1) | collective-permute-done | bytes 294944 | tf_op jit(solution)/shard_map/z_shifts/ppermute | solution.py:26
  22.5 7.4 %collective-permute-done.2 = bf16[16,9216]{1,0:T(8,128)(2,1)S(1)} collective-permute-done((bf16[16,9216]{1,0:T(8,128)(2,1)S(1)}, bf16[16,9216]{1,0:T(8,128)(2,1)S(1)}, u32[]{:S(2)}, u32[]{:S(2)}) %collective-permute-start.2) | collective-permute-done | bytes 294944 | tf_op jit(solution)/shard_map/z_shifts/ppermute | solution.py:26
  29.8 0.1 pad_maximum_fusion
  30.0 0.0 slice-start
  30.0 1.1 slice_bitcast_fusion
  31.1 2.5 %collective-permute-start.7 = (bf16[32,9216]{1,0:T(8,128)(2,1)}, bf16[32,9216]{1,0:T(8,128)(2,1)}, u32[]{:S(2)}, u32[]{:S(2)}) collective-permute-start(bf16[32,9216]{1,0:T(8,128)(2,1)} %get-tuple-element.77), channel_id=1, source_target_pairs={{0,12},{4,0},{8,4},{12,8},{1,13},{5,1},{9,5},{13,9},{2,14},{6,2},{... | collective-permute-start | bytes 1769480 | tf_op jit(solution)/shard_map/first_axis/ppermute | solution.py:21
  33.6 0.0 collective-permute-start.8
  33.6 0.1 pad_add_fusion.place_ref
  33.7 1.3 collective-permute-start.4
  35.0 1.5 collective-permute-start.3
  36.5 8.5 %collective-permute-done.7 = bf16[32,9216]{1,0:T(8,128)(2,1)} collective-permute-done((bf16[32,9216]{1,0:T(8,128)(2,1)}, bf16[32,9216]{1,0:T(8,128)(2,1)}, u32[]{:S(2)}, u32[]{:S(2)}) %collective-permute-start.7) | collective-permute-done | bytes 589856 | tf_op jit(solution)/shard_map/first_axis/ppermute | solution.py:21
  45.0 1.0 slice.109
  46.0 3.5 %collective-permute-start.10 = (bf16[16,9216]{1,0:T(8,128)(2,1)S(1)}, bf16[16,9216]{1,0:T(8,128)(2,1)S(1)}, u32[]{:S(2)}, u32[]{:S(2)}) collective-permute-start(bf16[16,9216]{1,0:T(8,128)(2,1)S(1)} %slice.109), channel_id=1, source_target_pairs={{0,12},{4,0},{8,4},{12,8},{1,13},{5,1},{9,5},{13,9},{2,14},{6,2},{... | collective-permute-start | bytes 884744 | tf_op jit(solution)/shard_map/first_axis/ppermute | solution.py:21
  49.5 1.0 slice.108
  50.5 0.1 collective-permute-start.9
  50.6 1.4 pad_maximum_fusion.4.refs_2_
  52.0 0.0 slice-start.1
  52.0 0.1 pad_maximum_fusion.3.refs_0_
  52.1 0.1 collective-permute-start.15
  52.2 2.7 %collective-permute-start.16 = (bf16[64,9216]{1,0:T(8,128)(2,1)S(1)}, bf16[64,9216]{1,0:T(8,128)(2,1)S(1)}, u32[]{:S(2)}, u32[]{:S(2)}) collective-permute-start(bf16[64,9216]{1,0:T(8,128)(2,1)S(1)} %pad_maximum_fusion.3.refs_0_), channel_id=1, source_target_pairs={{0,12},{4,0},{8,4},{12,8},{1,13},{5,1},{9,5},{13,9},{2,14},{6,2},{... | collective-permute-start | bytes 3538952 | tf_op jit(solution)/shard_map/second_axis/ppermute | solution.py:21
  54.9 1.4 collective-permute-start.5
  56.3 1.5 collective-permute-start.6
  57.9 0.8 collective-permute-start.17
  58.7 1.1 pad_maximum_fusion.2.refs_3_
  59.8 0.0 copy-start
  59.8 2.3 %collective-permute-done.5 = bf16[16,9216]{1,0:T(8,128)(2,1)S(1)} collective-permute-done((bf16[16,9216]{1,0:T(8,128)(2,1)S(1)}, bf16[16,9216]{1,0:T(8,128)(2,1)S(1)}, u32[]{:S(2)}, u32[]{:S(2)}) %collective-permute-start.5) | collective-permute-done | bytes 294944 | tf_op jit(solution)/shard_map/first_axis/ppermute | solution.py:21
  62.1 1.5 collective-permute-start.18
  63.6 0.1 pad_maximum_fusion.1.refs_1_
  63.7 3.2 %reduce.8 = (f32[2,2,8,8,512]{4,3,2,1,0:T(8,128)S(1)}, f32[2,2,8,8,512]{4,3,2,1,0:T(8,128)S(1)}) custom-call(s32[3]{0:T(128)S(1)} %pad_add_fusion.place_ref, bf16[64,9216]{1,0:T(8,128)(2,1)S(1)} %pad_maximum_fusion.3.refs_0_, bf16[64,9216]{1,0:T(8,128)(2,1)S(1)} %pad_maximum_fusion.1.refs_1_, bf16[64,9216]{1,0:T(8,128)(2,1)S(1)} %pad_maximum_fusion.4.refs_2_, ...), custom_call_target="tpu_custom_call" | custom-call | flops 1048576 | bytes 65536 | tf_op jit(solution)/shard_map/reduce/pallas_call | solution.py:59
  67.0 7.7 %collective-permute-start.19 = (f32[2,2,8,8,512]{4,3,2,1,0:T(8,128)S(1)}, f32[2,2,8,8,512]{4,3,2,1,0:T(8,128)S(1)}, u32[]{:S(2)}, u32[]{:S(2)}) collective-permute-start(f32[2,2,8,8,512]{4,3,2,1,0:T(8,128)S(1)} %get-tuple-element.54), channel_id=1, source_target_pairs={{0,1},{1,0},{2,3},{3,2},{4,5},{5,4},{6,7},{7,6},{8,9},{9,8},{10,11... | collective-permute-start | bytes 1572872 | tf_op jit(solution)/shard_map/reduce/ppermute | solution.py:146
  74.7 1.5 collective-permute-done.19
  76.2 6.7 %collective-permute-done.15.refs_0_ = bf16[64,9216]{1,0:T(8,128)(2,1)S(1)} collective-permute-done((bf16[64,9216]{1,0:T(8,128)(2,1)S(1)}, bf16[64,9216]{1,0:T(8,128)(2,1)S(1)}, u32[]{:S(2)}, u32[]{:S(2)}) %collective-permute-start.15) | collective-permute-done | bytes 1179680 | tf_op jit(solution)/shard_map/second_axis/ppermute | solution.py:21
  82.9 1.3 collective-permute-start.13
  84.2 2.7 %collective-permute-done.17.refs_2_ = bf16[64,9216]{1,0:T(8,128)(2,1)S(1)} collective-permute-done((bf16[64,9216]{1,0:T(8,128)(2,1)S(1)}, bf16[64,9216]{1,0:T(8,128)(2,1)S(1)}, u32[]{:S(2)}, u32[]{:S(2)}) %collective-permute-start.17) | collective-permute-done | bytes 1179680 | tf_op jit(solution)/shard_map/second_axis/ppermute | solution.py:21
  86.8 1.4 collective-permute-start.14
  88.3 4.5 %collective-permute-start.20 = (f32[2,8,8,512]{3,2,1,0:T(8,128)S(1)}, f32[2,8,8,512]{3,2,1,0:T(8,128)S(1)}, u32[]{:S(2)}, u32[]{:S(2)}) collective-permute-start(f32[2,8,8,512]{3,2,1,0:T(8,128)S(1)} %fusion.7), channel_id=1, source_target_pairs={{0,2},{2,0},{1,3},{3,1},{4,6},{6,4},{5,7},{7,5},{8,10},{10,8},{9,1... | collective-permute-start | bytes 786440 | tf_op jit(solution)/shard_map/reduce/ppermute | solution.py:143
  92.8 3.2 %reduce.9 = (f32[2,2,8,8,512]{4,3,2,1,0:T(8,128)S(1)}, f32[2,2,8,8,512]{4,3,2,1,0:T(8,128)S(1)}) custom-call(s32[3]{0:T(128)S(1)} %pad_add_fusion.place_ref, bf16[64,9216]{1,0:T(8,128)(2,1)S(1)} %collective-permute-done.15.refs_0_, bf16[64,9216]{1,0:T(8,128)(2,1)S(1)} %collective-permute-done.16.refs_1_, ...), custom_call_target="tpu_custom_call" | custom-call | flops 1048576 | bytes 65536 | tf_op jit(solution)/shard_map/reduce/pallas_call | solution.py:59
  96.0 1.5 collective-permute-done.20
  97.5 10.1 %collective-permute-start.25 = (f32[2,2,8,8,512]{4,3,2,1,0:T(8,128)S(1)}, f32[2,2,8,8,512]{4,3,2,1,0:T(8,128)S(1)}, u32[]{:S(2)}, u32[]{:S(2)}) collective-permute-start(f32[2,2,8,8,512]{4,3,2,1,0:T(8,128)S(1)} %get-tuple-element.63), channel_id=1, source_target_pairs={{0,1},{1,0},{2,3},{3,2},{4,5},{5,4},{6,7},{7,6},{8,9},{9,8},{10,11... | collective-permute-start | bytes 1572872 | tf_op jit(solution)/shard_map/reduce/ppermute | solution.py:146
  107.6 0.1 fusion.9
  107.7 0.5 collective-permute-done.11.refs_0_
  108.2 4.0 %collective-permute-done.13.refs_2_ = bf16[64,9216]{1,0:T(8,128)(2,1)S(1)} collective-permute-done((bf16[64,9216]{1,0:T(8,128)(2,1)S(1)}, bf16[64,9216]{1,0:T(8,128)(2,1)S(1)}, u32[]{:S(2)}, u32[]{:S(2)}) %collective-permute-start.13) | collective-permute-done | bytes 1179680 | tf_op jit(solution)/shard_map/second_axis/ppermute | solution.py:21
  112.2 2.7 %collective-permute-start.22 = (bf16[64,9216]{1,0:T(8,128)(2,1)S(1)}, bf16[64,9216]{1,0:T(8,128)(2,1)S(1)}, u32[]{:S(2)}, u32[]{:S(2)}) collective-permute-start(bf16[64,9216]{1,0:T(8,128)(2,1)S(1)} %collective-permute-done.12.refs_1_), channel_id=1, source_target_pairs={{0,12},{4,0},{8,4},{12,8},{1,13},{5,1},{9,5},{13,9},{2,14},{6,2},{... | collective-permute-start | bytes 3538952 | tf_op jit(solution)/shard_map/second_axis/ppermute | solution.py:21
  114.9 0.9 collective-permute-start.23
  115.8 1.8 %collective-permute-start.24 = (bf16[64,9216]{1,0:T(8,128)(2,1)S(1)}, bf16[64,9216]{1,0:T(8,128)(2,1)S(1)}, u32[]{:S(2)}, u32[]{:S(2)}) collective-permute-start(bf16[64,9216]{1,0:T(8,128)(2,1)S(1)} %collective-permute-done.14.refs_3_), channel_id=1, source_target_pairs={{0,48},{16,0},{32,16},{48,32},{1,49},{17,1},{33,17},{49,33},{2,50}... | collective-permute-start | bytes 3538952 | tf_op jit(solution)/shard_map/second_axis/ppermute | solution.py:21
  117.6 4.6 %collective-permute-start.26 = (f32[2,8,8,512]{3,2,1,0:T(8,128)S(1)}, f32[2,8,8,512]{3,2,1,0:T(8,128)S(1)}, u32[]{:S(2)}, u32[]{:S(2)}) collective-permute-start(f32[2,8,8,512]{3,2,1,0:T(8,128)S(1)} %fusion.4), channel_id=1, source_target_pairs={{0,2},{2,0},{1,3},{3,1},{4,6},{6,4},{5,7},{7,5},{8,10},{10,8},{9,1... | collective-permute-start | bytes 786440 | tf_op jit(solution)/shard_map/reduce/ppermute | solution.py:143
  122.2 3.2 %reduce.10 = (f32[2,2,8,8,512]{4,3,2,1,0:T(8,128)S(1)}, f32[2,2,8,8,512]{4,3,2,1,0:T(8,128)S(1)}) custom-call(s32[3]{0:T(128)S(1)} %pad_add_fusion.place_ref, bf16[64,9216]{1,0:T(8,128)(2,1)S(1)} %collective-permute-done.11.refs_0_, bf16[64,9216]{1,0:T(8,128)(2,1)S(1)} %collective-permute-done.12.refs_1_, ...), custom_call_target="tpu_custom_call" | custom-call | flops 1048576 | bytes 65536 | tf_op jit(solution)/shard_map/reduce/pallas_call | solution.py:59
  125.4 3.6 %collective-permute-done.26 = f32[2,8,8,512]{3,2,1,0:T(8,128)S(1)} collective-permute-done((f32[2,8,8,512]{3,2,1,0:T(8,128)S(1)}, f32[2,8,8,512]{3,2,1,0:T(8,128)S(1)}, u32[]{:S(2)}, u32[]{:S(2)}) %collective-permute-start.26) | collective-permute-done | bytes 262176 | tf_op jit(solution)/shard_map/reduce/ppermute | solution.py:143
  129.0 5.8 %collective-permute-start.27 = (f32[2,2,8,8,512]{4,3,2,1,0:T(8,128)S(1)}, f32[2,2,8,8,512]{4,3,2,1,0:T(8,128)S(1)}, u32[]{:S(2)}, u32[]{:S(2)}) collective-permute-start(f32[2,2,8,8,512]{4,3,2,1,0:T(8,128)S(1)} %get-tuple-element.67), channel_id=1, source_target_pairs={{0,1},{1,0},{2,3},{3,2},{4,5},{5,4},{6,7},{7,6},{8,9},{9,8},{10,11... | collective-permute-start | bytes 1572872 | tf_op jit(solution)/shard_map/reduce/ppermute | solution.py:146
  134.8 0.1 fusion.6
  134.9 1.5 collective-permute-done.27
  136.4 4.5 %collective-permute-start.29 = (f32[2,8,8,512]{3,2,1,0:T(8,128)S(1)}, f32[2,8,8,512]{3,2,1,0:T(8,128)S(1)}, u32[]{:S(2)}, u32[]{:S(2)}) collective-permute-start(f32[2,8,8,512]{3,2,1,0:T(8,128)S(1)} %fusion.3), channel_id=1, source_target_pairs={{0,2},{2,0},{1,3},{3,1},{4,6},{6,4},{5,7},{7,5},{8,10},{10,8},{9,1... | collective-permute-start | bytes 786440 | tf_op jit(solution)/shard_map/reduce/ppermute | solution.py:143
  140.9 3.2 %reduce.11 = (f32[2,2,8,8,512]{4,3,2,1,0:T(8,128)S(1)}, f32[2,2,8,8,512]{4,3,2,1,0:T(8,128)S(1)}) custom-call(s32[3]{0:T(128)S(1)} %pad_add_fusion.place_ref, bf16[64,9216]{1,0:T(8,128)(2,1)S(1)} %collective-permute-done.21.refs_0_, bf16[64,9216]{1,0:T(8,128)(2,1)S(1)} %collective-permute-done.22.refs_1_, ...), custom_call_target="tpu_custom_call" | custom-call | flops 1048576 | bytes 65536 | tf_op jit(solution)/shard_map/reduce/pallas_call | solution.py:59
  144.2 3.6 %collective-permute-start.28 = (f32[2,2,8,8,512]{4,3,2,1,0:T(8,128)S(1)}, f32[2,2,8,8,512]{4,3,2,1,0:T(8,128)S(1)}, u32[]{:S(2)}, u32[]{:S(2)}) collective-permute-start(f32[2,2,8,8,512]{4,3,2,1,0:T(8,128)S(1)} %get-tuple-element.74), channel_id=1, source_target_pairs={{0,1},{1,0},{2,3},{3,2},{4,5},{5,4},{6,7},{7,6},{8,9},{9,8},{10,11... | collective-permute-start | bytes 1572872 | tf_op jit(solution)/shard_map/reduce/ppermute | solution.py:146
  147.8 4.2 %collective-permute-done.29 = f32[2,8,8,512]{3,2,1,0:T(8,128)S(1)} collective-permute-done((f32[2,8,8,512]{3,2,1,0:T(8,128)S(1)}, f32[2,8,8,512]{3,2,1,0:T(8,128)S(1)}, u32[]{:S(2)}, u32[]{:S(2)}) %collective-permute-start.29) | collective-permute-done | bytes 262176 | tf_op jit(solution)/shard_map/reduce/ppermute | solution.py:143
  152.1 0.1 fusion.1
  152.2 2.9 %collective-permute-start.30 = (f32[2,8,8,512]{3,2,1,0:T(8,128)S(1)}, f32[2,8,8,512]{3,2,1,0:T(8,128)S(1)}, u32[]{:S(2)}, u32[]{:S(2)}) collective-permute-start(f32[2,8,8,512]{3,2,1,0:T(8,128)S(1)} %fusion.2), channel_id=1, source_target_pairs={{0,2},{2,0},{1,3},{3,1},{4,6},{6,4},{5,7},{7,5},{8,10},{10,8},{9,1... | collective-permute-start | bytes 786440 | tf_op jit(solution)/shard_map/reduce/ppermute | solution.py:143
  155.1 10.7 %collective-permute-done.30.back_ref = f32[2,8,8,512]{3,2,1,0:T(8,128)S(1)} collective-permute-done((f32[2,8,8,512]{3,2,1,0:T(8,128)S(1)}, f32[2,8,8,512]{3,2,1,0:T(8,128)S(1)}, u32[]{:S(2)}, u32[]{:S(2)}) %collective-permute-start.30) | collective-permute-done | bytes 262176 | tf_op jit(solution)/shard_map/reduce/ppermute | solution.py:143
  165.8 1.6 reduce.12
  (34 shorter events, 0.4 us)
Async XLA Ops:
  1.0 9.2 %collective-permute-start = (bf16[16,9216]{1,0:T(8,128)(2,1)S(1)}, bf16[16,9216]{1,0:T(8,128)(2,1)S(1)}, u32[]{:S(2)}, u32[]{:S(2)}) collective-permute-start(bf16[16,9216]{1,0:T(8,128)(2,1)S(1)} %get-tuple-element.80), channel_id=1, source_target_pairs={{0,64},{64,0},{128,192},{192,128},{1,65},{65,1},{129,193},{193,129... | collective-permute-start | bytes 884744 | tf_op jit(solution)/shard_map/z_shifts/ppermute | solution.py:26
  1.1 21.3 %collective-permute-start.1 = (bf16[16,9216]{1,0:T(8,128)(2,1)S(1)}, bf16[16,9216]{1,0:T(8,128)(2,1)S(1)}, u32[]{:S(2)}, u32[]{:S(2)}) collective-permute-start(bf16[16,9216]{1,0:T(8,128)(2,1)S(1)} %get-tuple-element.80), channel_id=1, source_target_pairs={{0,128},{64,192},{128,0},{192,64},{1,129},{65,193},{129,1},{193,65... | collective-permute-start | bytes 884744 | tf_op jit(solution)/shard_map/z_shifts/ppermute | solution.py:26
  4.2 25.6 %collective-permute-start.2 = (bf16[16,9216]{1,0:T(8,128)(2,1)S(1)}, bf16[16,9216]{1,0:T(8,128)(2,1)S(1)}, u32[]{:S(2)}, u32[]{:S(2)}) collective-permute-start(bf16[16,9216]{1,0:T(8,128)(2,1)S(1)} %get-tuple-element.80), channel_id=1, source_target_pairs={{0,192},{64,128},{128,64},{192,0},{1,193},{65,129},{129,65},{193,1... | collective-permute-start | bytes 884744 | tf_op jit(solution)/shard_map/z_shifts/ppermute | solution.py:26
  30.0 33.7 %slice-start = ((s8[7340032]{0:T(1024)(128)(4,1)}), s8[3145728]{0:T(1024)(128)(4,1)S(1)}, s32[]{:S(2)}) async-start(s8[7340032]{0:T(1024)(128)(4,1)} %bitcast.34), calls=%async_computation | async-start | bytes 6291456
  31.1 13.9 %collective-permute-start.7 = (bf16[32,9216]{1,0:T(8,128)(2,1)}, bf16[32,9216]{1,0:T(8,128)(2,1)}, u32[]{:S(2)}, u32[]{:S(2)}) collective-permute-start(bf16[32,9216]{1,0:T(8,128)(2,1)} %get-tuple-element.77), channel_id=1, source_target_pairs={{0,12},{4,0},{8,4},{12,8},{1,13},{5,1},{9,5},{13,9},{2,14},{6,2},{... | collective-permute-start | bytes 1769480 | tf_op jit(solution)/shard_map/first_axis/ppermute | solution.py:21
  33.6 15.9 %collective-permute-start.8 = (bf16[32,9216]{1,0:T(8,128)(2,1)}, bf16[32,9216]{1,0:T(8,128)(2,1)}, u32[]{:S(2)}, u32[]{:S(2)}) collective-permute-start(bf16[32,9216]{1,0:T(8,128)(2,1)} %get-tuple-element.77), channel_id=1, source_target_pairs={{0,4},{4,8},{8,12},{12,0},{1,5},{5,9},{9,13},{13,1},{2,6},{6,10},{... | collective-permute-start | bytes 1769480 | tf_op jit(solution)/shard_map/first_axis/ppermute | solution.py:21
  33.7 18.3 %collective-permute-start.4 = (bf16[32,9216]{1,0:T(8,128)(2,1)}, bf16[32,9216]{1,0:T(8,128)(2,1)S(1)}, u32[]{:S(2)}, u32[]{:S(2)}) collective-permute-start(bf16[32,9216]{1,0:T(8,128)(2,1)} %get-tuple-element.78), channel_id=1, source_target_pairs={{0,16},{16,32},{32,48},{48,0},{1,17},{17,33},{33,49},{49,1},{2,18}... | collective-permute-start | bytes 1769480 | tf_op jit(solution)/shard_map/first_axis/ppermute | solution.py:21
  35.0 19.9 %collective-permute-start.3 = (bf16[32,9216]{1,0:T(8,128)(2,1)}, bf16[32,9216]{1,0:T(8,128)(2,1)S(1)}, u32[]{:S(2)}, u32[]{:S(2)}) collective-permute-start(bf16[32,9216]{1,0:T(8,128)(2,1)} %get-tuple-element.78), channel_id=1, source_target_pairs={{0,48},{16,0},{32,16},{48,32},{1,49},{17,1},{33,17},{49,33},{2,50}... | collective-permute-start | bytes 1769480 | tf_op jit(solution)/shard_map/first_axis/ppermute | solution.py:21
  46.0 10.3 %collective-permute-start.10 = (bf16[16,9216]{1,0:T(8,128)(2,1)S(1)}, bf16[16,9216]{1,0:T(8,128)(2,1)S(1)}, u32[]{:S(2)}, u32[]{:S(2)}) collective-permute-start(bf16[16,9216]{1,0:T(8,128)(2,1)S(1)} %slice.109), channel_id=1, source_target_pairs={{0,12},{4,0},{8,4},{12,8},{1,13},{5,1},{9,5},{13,9},{2,14},{6,2},{... | collective-permute-start | bytes 884744 | tf_op jit(solution)/shard_map/first_axis/ppermute | solution.py:21
  50.5 1.5 copy-start.1
  50.5 7.4 %collective-permute-start.9 = (bf16[16,9216]{1,0:T(8,128)(2,1)S(1)}, bf16[16,9216]{1,0:T(8,128)(2,1)S(1)}, u32[]{:S(2)}, u32[]{:S(2)}) collective-permute-start(bf16[16,9216]{1,0:T(8,128)(2,1)S(1)} %slice.108), channel_id=1, source_target_pairs={{0,4},{4,8},{8,12},{12,0},{1,5},{5,9},{9,13},{13,1},{2,6},{6,10},{... | collective-permute-start | bytes 884744 | tf_op jit(solution)/shard_map/first_axis/ppermute | solution.py:21
  52.0 11.7 %slice-start.1 = ((s8[7340032]{0:T(1024)(128)(4,1)}), s8[4194304]{0:T(1024)(128)(4,1)S(1)}, s32[]{:S(2)}) async-start(s8[7340032]{0:T(1024)(128)(4,1)} %bitcast.34), calls=%async_computation.1 | async-start | bytes 8388608
  52.1 30.8 %collective-permute-start.15 = (bf16[64,9216]{1,0:T(8,128)(2,1)S(1)}, bf16[64,9216]{1,0:T(8,128)(2,1)S(1)}, u32[]{:S(2)}, u32[]{:S(2)}) collective-permute-start(bf16[64,9216]{1,0:T(8,128)(2,1)S(1)} %pad_maximum_fusion.3.refs_0_), channel_id=1, source_target_pairs={{0,4},{4,8},{8,12},{12,0},{1,5},{5,9},{9,13},{13,1},{2,6},{6,10},{... | collective-permute-start | bytes 3538952 | tf_op jit(solution)/shard_map/second_axis/ppermute | solution.py:21
  52.2 30.7 %collective-permute-start.16 = (bf16[64,9216]{1,0:T(8,128)(2,1)S(1)}, bf16[64,9216]{1,0:T(8,128)(2,1)S(1)}, u32[]{:S(2)}, u32[]{:S(2)}) collective-permute-start(bf16[64,9216]{1,0:T(8,128)(2,1)S(1)} %pad_maximum_fusion.3.refs_0_), channel_id=1, source_target_pairs={{0,12},{4,0},{8,4},{12,8},{1,13},{5,1},{9,5},{13,9},{2,14},{6,2},{... | collective-permute-start | bytes 3538952 | tf_op jit(solution)/shard_map/second_axis/ppermute | solution.py:21
  54.9 7.2 %collective-permute-start.5 = (bf16[16,9216]{1,0:T(8,128)(2,1)S(1)}, bf16[16,9216]{1,0:T(8,128)(2,1)S(1)}, u32[]{:S(2)}, u32[]{:S(2)}) collective-permute-start(bf16[16,9216]{1,0:T(8,128)(2,1)S(1)} %slice.105), channel_id=1, source_target_pairs={{0,16},{16,32},{32,48},{48,0},{1,17},{17,33},{33,49},{49,1},{2,18}... | collective-permute-start | bytes 884744 | tf_op jit(solution)/shard_map/first_axis/ppermute | solution.py:21
  56.3 7.3 %collective-permute-start.6 = (bf16[16,9216]{1,0:T(8,128)(2,1)S(1)}, bf16[16,9216]{1,0:T(8,128)(2,1)S(1)}, u32[]{:S(2)}, u32[]{:S(2)}) collective-permute-start(bf16[16,9216]{1,0:T(8,128)(2,1)S(1)} %slice.106), channel_id=1, source_target_pairs={{0,48},{16,0},{32,16},{48,32},{1,49},{17,1},{33,17},{49,33},{2,50}... | collective-permute-start | bytes 884744 | tf_op jit(solution)/shard_map/first_axis/ppermute | solution.py:21
  57.9 29.0 %collective-permute-start.17 = (bf16[64,9216]{1,0:T(8,128)(2,1)S(1)}, bf16[64,9216]{1,0:T(8,128)(2,1)S(1)}, u32[]{:S(2)}, u32[]{:S(2)}) collective-permute-start(bf16[64,9216]{1,0:T(8,128)(2,1)S(1)} %pad_maximum_fusion.4.refs_2_), channel_id=1, source_target_pairs={{0,16},{16,32},{32,48},{48,0},{1,17},{17,33},{33,49},{49,1},{2,18}... | collective-permute-start | bytes 3538952 | tf_op jit(solution)/shard_map/second_axis/ppermute | solution.py:21
  59.8 3.9 %copy-start = (bf16[512,2048]{1,0:T(8,128)(2,1)S(1)}, bf16[512,2048]{1,0:T(8,128)(2,1)}, u32[]{:S(2)}) copy-start(bf16[512,2048]{1,0:T(8,128)(2,1)} %refs_5_.7) | copy-start | bytes 6291460
  62.1 26.2 %collective-permute-start.18 = (bf16[64,9216]{1,0:T(8,128)(2,1)S(1)}, bf16[64,9216]{1,0:T(8,128)(2,1)S(1)}, u32[]{:S(2)}, u32[]{:S(2)}) collective-permute-start(bf16[64,9216]{1,0:T(8,128)(2,1)S(1)} %pad_maximum_fusion.4.refs_2_), channel_id=1, source_target_pairs={{0,48},{16,0},{32,16},{48,32},{1,49},{17,1},{33,17},{49,33},{2,50}... | collective-permute-start | bytes 3538952 | tf_op jit(solution)/shard_map/second_axis/ppermute | solution.py:21
  67.0 9.2 %collective-permute-start.19 = (f32[2,2,8,8,512]{4,3,2,1,0:T(8,128)S(1)}, f32[2,2,8,8,512]{4,3,2,1,0:T(8,128)S(1)}, u32[]{:S(2)}, u32[]{:S(2)}) collective-permute-start(f32[2,2,8,8,512]{4,3,2,1,0:T(8,128)S(1)} %get-tuple-element.54), channel_id=1, source_target_pairs={{0,1},{1,0},{2,3},{3,2},{4,5},{5,4},{6,7},{7,6},{8,9},{9,8},{10,11... | collective-permute-start | bytes 1572872 | tf_op jit(solution)/shard_map/reduce/ppermute | solution.py:146
  76.2 31.9 %collective-permute-start.11 = (bf16[64,9216]{1,0:T(8,128)(2,1)S(1)}, bf16[64,9216]{1,0:T(8,128)(2,1)S(1)}, u32[]{:S(2)}, u32[]{:S(2)}) collective-permute-start(bf16[64,9216]{1,0:T(8,128)(2,1)S(1)} %pad_maximum_fusion.1.refs_1_), channel_id=1, source_target_pairs={{0,4},{4,8},{8,12},{12,0},{1,5},{5,9},{9,13},{13,1},{2,6},{6,10},{... | collective-permute-start | bytes 3538952 | tf_op jit(solution)/shard_map/second_axis/ppermute | solution.py:21
  82.9 25.3 %collective-permute-start.12 = (bf16[64,9216]{1,0:T(8,128)(2,1)S(1)}, bf16[64,9216]{1,0:T(8,128)(2,1)S(1)}, u32[]{:S(2)}, u32[]{:S(2)}) collective-permute-start(bf16[64,9216]{1,0:T(8,128)(2,1)S(1)} %pad_maximum_fusion.1.refs_1_), channel_id=1, source_target_pairs={{0,12},{4,0},{8,4},{12,8},{1,13},{5,1},{9,5},{13,9},{2,14},{6,2},{... | collective-permute-start | bytes 3538952 | tf_op jit(solution)/shard_map/second_axis/ppermute | solution.py:21
  82.9 29.3 %collective-permute-start.13 = (bf16[64,9216]{1,0:T(8,128)(2,1)S(1)}, bf16[64,9216]{1,0:T(8,128)(2,1)S(1)}, u32[]{:S(2)}, u32[]{:S(2)}) collective-permute-start(bf16[64,9216]{1,0:T(8,128)(2,1)S(1)} %pad_maximum_fusion.2.refs_3_), channel_id=1, source_target_pairs={{0,16},{16,32},{32,48},{48,0},{1,17},{17,33},{33,49},{49,1},{2,18}... | collective-permute-start | bytes 3538952 | tf_op jit(solution)/shard_map/second_axis/ppermute | solution.py:21
  86.8 25.4 %collective-permute-start.14 = (bf16[64,9216]{1,0:T(8,128)(2,1)S(1)}, bf16[64,9216]{1,0:T(8,128)(2,1)S(1)}, u32[]{:S(2)}, u32[]{:S(2)}) collective-permute-start(bf16[64,9216]{1,0:T(8,128)(2,1)S(1)} %pad_maximum_fusion.2.refs_3_), channel_id=1, source_target_pairs={{0,48},{16,0},{32,16},{48,32},{1,49},{17,1},{33,17},{49,33},{2,50}... | collective-permute-start | bytes 3538952 | tf_op jit(solution)/shard_map/second_axis/ppermute | solution.py:21
  88.3 9.2 %collective-permute-start.20 = (f32[2,8,8,512]{3,2,1,0:T(8,128)S(1)}, f32[2,8,8,512]{3,2,1,0:T(8,128)S(1)}, u32[]{:S(2)}, u32[]{:S(2)}) collective-permute-start(f32[2,8,8,512]{3,2,1,0:T(8,128)S(1)} %fusion.7), channel_id=1, source_target_pairs={{0,2},{2,0},{1,3},{3,1},{4,6},{6,4},{5,7},{7,5},{8,10},{10,8},{9,1... | collective-permute-start | bytes 786440 | tf_op jit(solution)/shard_map/reduce/ppermute | solution.py:143
  97.5 20.1 %collective-permute-start.25 = (f32[2,2,8,8,512]{4,3,2,1,0:T(8,128)S(1)}, f32[2,2,8,8,512]{4,3,2,1,0:T(8,128)S(1)}, u32[]{:S(2)}, u32[]{:S(2)}) collective-permute-start(f32[2,2,8,8,512]{4,3,2,1,0:T(8,128)S(1)} %get-tuple-element.63), channel_id=1, source_target_pairs={{0,1},{1,0},{2,3},{3,2},{4,5},{5,4},{6,7},{7,6},{8,9},{9,8},{10,11... | collective-permute-start | bytes 1572872 | tf_op jit(solution)/shard_map/reduce/ppermute | solution.py:146
  112.2 28.7 %collective-permute-start.21 = (bf16[64,9216]{1,0:T(8,128)(2,1)S(1)}, bf16[64,9216]{1,0:T(8,128)(2,1)S(1)}, u32[]{:S(2)}, u32[]{:S(2)}) collective-permute-start(bf16[64,9216]{1,0:T(8,128)(2,1)S(1)} %collective-permute-done.15.refs_0_), channel_id=1, source_target_pairs={{0,4},{4,8},{8,12},{12,0},{1,5},{5,9},{9,13},{13,1},{2,6},{6,10},{... | collective-permute-start | bytes 3538952 | tf_op jit(solution)/shard_map/second_axis/ppermute | solution.py:21
  112.2 28.7 %collective-permute-start.22 = (bf16[64,9216]{1,0:T(8,128)(2,1)S(1)}, bf16[64,9216]{1,0:T(8,128)(2,1)S(1)}, u32[]{:S(2)}, u32[]{:S(2)}) collective-permute-start(bf16[64,9216]{1,0:T(8,128)(2,1)S(1)} %collective-permute-done.12.refs_1_), channel_id=1, source_target_pairs={{0,12},{4,0},{8,4},{12,8},{1,13},{5,1},{9,5},{13,9},{2,14},{6,2},{... | collective-permute-start | bytes 3538952 | tf_op jit(solution)/shard_map/second_axis/ppermute | solution.py:21
  114.9 26.0 %collective-permute-start.23 = (bf16[64,9216]{1,0:T(8,128)(2,1)S(1)}, bf16[64,9216]{1,0:T(8,128)(2,1)S(1)}, u32[]{:S(2)}, u32[]{:S(2)}) collective-permute-start(bf16[64,9216]{1,0:T(8,128)(2,1)S(1)} %collective-permute-done.17.refs_2_), channel_id=1, source_target_pairs={{0,16},{16,32},{32,48},{48,0},{1,17},{17,33},{33,49},{49,1},{2,18}... | collective-permute-start | bytes 3538952 | tf_op jit(solution)/shard_map/second_axis/ppermute | solution.py:21
  115.8 25.1 %collective-permute-start.24 = (bf16[64,9216]{1,0:T(8,128)(2,1)S(1)}, bf16[64,9216]{1,0:T(8,128)(2,1)S(1)}, u32[]{:S(2)}, u32[]{:S(2)}) collective-permute-start(bf16[64,9216]{1,0:T(8,128)(2,1)S(1)} %collective-permute-done.14.refs_3_), channel_id=1, source_target_pairs={{0,48},{16,0},{32,16},{48,32},{1,49},{17,1},{33,17},{49,33},{2,50}... | collective-permute-start | bytes 3538952 | tf_op jit(solution)/shard_map/second_axis/ppermute | solution.py:21
  117.6 11.4 %collective-permute-start.26 = (f32[2,8,8,512]{3,2,1,0:T(8,128)S(1)}, f32[2,8,8,512]{3,2,1,0:T(8,128)S(1)}, u32[]{:S(2)}, u32[]{:S(2)}) collective-permute-start(f32[2,8,8,512]{3,2,1,0:T(8,128)S(1)} %fusion.4), channel_id=1, source_target_pairs={{0,2},{2,0},{1,3},{3,1},{4,6},{6,4},{5,7},{7,5},{8,10},{10,8},{9,1... | collective-permute-start | bytes 786440 | tf_op jit(solution)/shard_map/reduce/ppermute | solution.py:143
  129.0 7.3 %collective-permute-start.27 = (f32[2,2,8,8,512]{4,3,2,1,0:T(8,128)S(1)}, f32[2,2,8,8,512]{4,3,2,1,0:T(8,128)S(1)}, u32[]{:S(2)}, u32[]{:S(2)}) collective-permute-start(f32[2,2,8,8,512]{4,3,2,1,0:T(8,128)S(1)} %get-tuple-element.67), channel_id=1, source_target_pairs={{0,1},{1,0},{2,3},{3,2},{4,5},{5,4},{6,7},{7,6},{8,9},{9,8},{10,11... | collective-permute-start | bytes 1572872 | tf_op jit(solution)/shard_map/reduce/ppermute | solution.py:146
  136.4 15.7 %collective-permute-start.29 = (f32[2,8,8,512]{3,2,1,0:T(8,128)S(1)}, f32[2,8,8,512]{3,2,1,0:T(8,128)S(1)}, u32[]{:S(2)}, u32[]{:S(2)}) collective-permute-start(f32[2,8,8,512]{3,2,1,0:T(8,128)S(1)} %fusion.3), channel_id=1, source_target_pairs={{0,2},{2,0},{1,3},{3,1},{4,6},{6,4},{5,7},{7,5},{8,10},{10,8},{9,1... | collective-permute-start | bytes 786440 | tf_op jit(solution)/shard_map/reduce/ppermute | solution.py:143
  144.2 8.0 %collective-permute-start.28 = (f32[2,2,8,8,512]{4,3,2,1,0:T(8,128)S(1)}, f32[2,2,8,8,512]{4,3,2,1,0:T(8,128)S(1)}, u32[]{:S(2)}, u32[]{:S(2)}) collective-permute-start(f32[2,2,8,8,512]{4,3,2,1,0:T(8,128)S(1)} %get-tuple-element.74), channel_id=1, source_target_pairs={{0,1},{1,0},{2,3},{3,2},{4,5},{5,4},{6,7},{7,6},{8,9},{9,8},{10,11... | collective-permute-start | bytes 1572872 | tf_op jit(solution)/shard_map/reduce/ppermute | solution.py:146
  152.2 13.5 %collective-permute-start.30 = (f32[2,8,8,512]{3,2,1,0:T(8,128)S(1)}, f32[2,8,8,512]{3,2,1,0:T(8,128)S(1)}, u32[]{:S(2)}, u32[]{:S(2)}) collective-permute-start(f32[2,8,8,512]{3,2,1,0:T(8,128)S(1)} %fusion.2), channel_id=1, source_target_pairs={{0,2},{2,0},{1,3},{3,1},{4,6},{6,4},{5,7},{7,5},{8,10},{10,8},{9,1... | collective-permute-start | bytes 786440 | tf_op jit(solution)/shard_map/reduce/ppermute | solution.py:143

commit v8 on v7

--- a/solution.py
+++ b/solution.py
@@ -129,11 +129,14 @@
     with jax.named_scope("z_shifts"):
         stacked = jnp.stack([own] + [flip(own, "zl", k) for k in (1, 2, 3)])
 
-    def first(rows, axis):
+    def first(rows, axis, direct):
         block = rows.reshape(GROUPS * RANK, features)
         half = block.shape[0] // 2
         before, after = ring(block, axis, 1), ring(block, axis, -1)
-        far = ring(before[:half], axis, 1), ring(after[half:], axis, -1)
+        if direct:
+            far = (ring(block, axis, 2),)
+        else:
+            far = ring(before[:half], axis, 1), ring(after[half:], axis, -1)
         return jnp.concatenate([block, before]), jnp.concatenate([after, *far])
 
     def both(block, axis):
@@ -153,9 +156,8 @@
         keep, send = project(blocks, train_grads, train_acts, place)
         return keep, over(send)
     with jax.named_scope("first_axis"):
-        lo_a, hi_a = first(stacked[:, :RANK], "y")
-        lo_b, hi_b = first(stacked[:, RANK:], "x")
-        lo_a, lo_b = lax.optimization_barrier((lo_a, lo_b))
+        lo_a, hi_a = first(stacked[:, :RANK], "y", True)
+        lo_b, hi_b = first(stacked[:, RANK:], "x", False)
         hi_a, hi_b = lax.optimization_barrier((hi_a, hi_b))
     with jax.named_scope("second_axis"):
         lo = both(lo_a, "x") + both(lo_b, "y")

time: 168 us -> 181 us (1.077)
  waiting for transfers between devices: 73.2 us -> 91.4 us
  local copies, waits for them, and re-layouts: 3.14 us -> 1.17 us
    ppermute x20 -> x19, waiting for transfers between devices: 24.7 us -> 43.4 us  [ring(): return lax.ppermute(x, axis, [(i, (i + step) % n) for i in range(n)])]
    slice x4 -> x2, local copies, waits for them, and re-layouts: 2 us -> 0.04 us  [first(): far = (ring(before[:half], axis, 1), ring(after[half:], axis, -1))]
    ppermute x4, starting transfers between devices: 27.2 us -> 25.3 us  [over(): return lax.ppermute(send, 'core', [(0, 1), (1, 0)])]
    ppermute x20 -> x19, starting transfers between devices: 24.9 us -> 26.3 us  [ring(): return lax.ppermute(x, axis, [(i, (i + step) % n) for i in range(n)])]
  transfers between devices with their start and end apart: 31 -> 30, of which waited for: 15 -> 15; matrix products, arithmetic and copies ran while one was open for 3% -> 1% of each run, Pallas kernels for 8% -> 7%
where the time goes in v8:
time: 181 us
  waiting for transfers between devices  91.4 us (50%)
  starting transfers between devices  70.5 us (39%)
  Pallas kernels  14.5 us (8%)
  other arithmetic  3.31 us (2%)
    ppermute x19, waiting for transfers between devices, ring(): return lax.ppermute(x, axis, [(i, (i + step) % n) for i in range(n)])  43.4 us
    ppermute x19, starting transfers between devices, ring(): return lax.ppermute(x, axis, [(i, (i + step) % n) for i in range(n)])  26.3 us
    ppermute x3, waiting for transfers between devices, flip(): return lax.ppermute(x, axis, [(i, i ^ mask) for i in range(n)])  25.5 us
    ppermute x4, starting transfers between devices, over(): return lax.ppermute(send, 'core', [(0, 1), (1, 0)])  25.3 us
    ppermute x4, waiting for transfers between devices, exchange(): return lax.ppermute(sent, 'zh', [(0, 1), (1, 0)])  19.2 us
    ppermute x4, starting transfers between devices, exchange(): return lax.ppermute(sent, 'zh', [(0, 1), (1, 0)])  15.5 us
    pallas_call x4, Pallas kernels, project(): pl.pallas_call(functools.partial(project_kernel, len(blocks)), out_shape=...  13 us
  transfers between devices with their start and end apart: 30, of which 15 were waited for; matrix products, arithmetic and copies ran while one was open for 1% of the time, Pallas kernels for 7%

profile of v8, /device:TPU:33, one launch (start us, length us, event | category | flops | bytes accessed | tf_op | source)
XLA Modules:
  0.0 181.1 jit_solution(11226026700780230030)
XLA Ops:
  0.0 1.0 fusion.13
  1.0 0.1 collective-permute-start
  1.1 3.1 %collective-permute-start.1 = (bf16[16,9216]{1,0:T(8,128)(2,1)S(1)}, bf16[16,9216]{1,0:T(8,128)(2,1)S(1)}, u32[]{:S(2)}, u32[]{:S(2)}) collective-permute-start(bf16[16,9216]{1,0:T(8,128)(2,1)S(1)} %get-tuple-element.76), channel_id=1, source_target_pairs={{0,128},{64,192},{128,0},{192,64},{1,129},{65,193},{129,1},{193,65... | collective-permute-start | bytes 884744 | tf_op jit(solution)/shard_map/z_shifts/ppermute | solution.py:26
  4.2 0.2 collective-permute-start.2
  4.4 5.9 %collective-permute-done = bf16[16,9216]{1,0:T(8,128)(2,1)S(1)} collective-permute-done((bf16[16,9216]{1,0:T(8,128)(2,1)S(1)}, bf16[16,9216]{1,0:T(8,128)(2,1)S(1)}, u32[]{:S(2)}, u32[]{:S(2)}) %collective-permute-start) | collective-permute-done | bytes 294944 | tf_op jit(solution)/shard_map/z_shifts/ppermute | solution.py:26
  10.2 12.2 %collective-permute-done.1 = bf16[16,9216]{1,0:T(8,128)(2,1)S(1)} collective-permute-done((bf16[16,9216]{1,0:T(8,128)(2,1)S(1)}, bf16[16,9216]{1,0:T(8,128)(2,1)S(1)}, u32[]{:S(2)}, u32[]{:S(2)}) %collective-permute-start.1) | collective-permute-done | bytes 294944 | tf_op jit(solution)/shard_map/z_shifts/ppermute | solution.py:26
  22.5 7.4 %collective-permute-done.2 = bf16[16,9216]{1,0:T(8,128)(2,1)S(1)} collective-permute-done((bf16[16,9216]{1,0:T(8,128)(2,1)S(1)}, bf16[16,9216]{1,0:T(8,128)(2,1)S(1)}, u32[]{:S(2)}, u32[]{:S(2)}) %collective-permute-start.2) | collective-permute-done | bytes 294944 | tf_op jit(solution)/shard_map/z_shifts/ppermute | solution.py:26
  29.8 0.1 pad_maximum_fusion
  30.0 1.1 slice_bitcast_fusion
  31.1 1.3 collective-permute-start.9
  32.4 0.1 pad_add_fusion.place_ref
  32.5 1.2 collective-permute-start.6
  33.7 1.5 collective-permute-start.5
  35.2 1.4 collective-permute-start.3
  36.6 1.6 collective-permute-start.4
  38.3 7.8 %collective-permute-done.9 = bf16[32,9216]{1,0:T(8,128)(2,1)} collective-permute-done((bf16[32,9216]{1,0:T(8,128)(2,1)}, bf16[32,9216]{1,0:T(8,128)(2,1)}, u32[]{:S(2)}, u32[]{:S(2)}) %collective-permute-start.9) | collective-permute-done | bytes 589856 | tf_op jit(solution)/shard_map/first_axis/ppermute | solution.py:21
  46.1 1.4 pad_maximum_fusion.3.refs_0_
  47.5 0.0 slice-start.1
  47.5 1.3 collective-permute-start.14
  48.8 0.0 collective-permute-done.6
  48.8 1.5 collective-permute-start.15
  50.3 0.1 collective-permute-start.7
  50.4 0.1 pad_maximum_fusion.4.refs_2_
  50.5 2.7 %collective-permute-start.8 = (bf16[16,9216]{1,0:T(8,128)(2,1)S(1)}, bf16[16,9216]{1,0:T(8,128)(2,1)S(1)}, u32[]{:S(2)}, u32[]{:S(2)}) collective-permute-start(bf16[16,9216]{1,0:T(8,128)(2,1)S(1)} %slice.99), channel_id=1, source_target_pairs={{0,12},{4,0},{8,4},{12,8},{1,13},{5,1},{9,5},{13,9},{2,14},{6,2},{... | collective-permute-start | bytes 884744 | tf_op jit(solution)/shard_map/first_axis/ppermute | solution.py:21
  53.2 6.5 %collective-permute-done.4 = bf16[32,9216]{1,0:T(8,128)(2,1)S(1)} collective-permute-done((bf16[32,9216]{1,0:T(8,128)(2,1)}, bf16[32,9216]{1,0:T(8,128)(2,1)S(1)}, u32[]{:S(2)}, u32[]{:S(2)}) %collective-permute-start.4) | collective-permute-done | bytes 589856 | tf_op jit(solution)/shard_map/first_axis/ppermute | solution.py:21
  59.7 2.8 %collective-permute-start.16 = (bf16[64,9216]{1,0:T(8,128)(2,1)S(1)}, bf16[64,9216]{1,0:T(8,128)(2,1)S(1)}, u32[]{:S(2)}, u32[]{:S(2)}) collective-permute-start(bf16[64,9216]{1,0:T(8,128)(2,1)S(1)} %pad_maximum_fusion.4.refs_2_), channel_id=1, source_target_pairs={{0,16},{16,32},{32,48},{48,0},{1,17},{17,33},{33,49},{49,1},{2,18}... | collective-permute-start | bytes 3538952 | tf_op jit(solution)/shard_map/second_axis/ppermute | solution.py:21
  62.5 0.1 pad_maximum_fusion.1.refs_1_
  62.6 0.0 copy-start
  62.6 16.7 %collective-permute-done.7 = bf16[16,9216]{1,0:T(8,128)(2,1)S(1)} collective-permute-done((bf16[16,9216]{1,0:T(8,128)(2,1)S(1)}, bf16[16,9216]{1,0:T(8,128)(2,1)S(1)}, u32[]{:S(2)}, u32[]{:S(2)}) %collective-permute-start.7) | collective-permute-done | bytes 294944 | tf_op jit(solution)/shard_map/first_axis/ppermute | solution.py:21
  79.3 0.2 collective-permute-start.17
  79.5 0.0 collective-permute-done.8
  79.5 0.1 pad_maximum_fusion.2.refs_3_
  79.6 3.2 %reduce.8 = (f32[2,2,8,8,512]{4,3,2,1,0:T(8,128)S(1)}, f32[2,2,8,8,512]{4,3,2,1,0:T(8,128)S(1)}) custom-call(s32[3]{0:T(128)S(1)} %pad_add_fusion.place_ref, bf16[64,9216]{1,0:T(8,128)(2,1)S(1)} %pad_maximum_fusion.3.refs_0_, bf16[64,9216]{1,0:T(8,128)(2,1)S(1)} %pad_maximum_fusion.1.refs_1_, bf16[64,9216]{1,0:T(8,128)(2,1)S(1)} %pad_maximum_fusion.4.refs_2_, ...), custom_call_target="tpu_custom_call" | custom-call | flops 1048576 | bytes 65536 | tf_op jit(solution)/shard_map/reduce/pallas_call | solution.py:59
  82.9 5.7 %collective-permute-start.18 = (f32[2,2,8,8,512]{4,3,2,1,0:T(8,128)S(1)}, f32[2,2,8,8,512]{4,3,2,1,0:T(8,128)S(1)}, u32[]{:S(2)}, u32[]{:S(2)}) collective-permute-start(f32[2,2,8,8,512]{4,3,2,1,0:T(8,128)S(1)} %get-tuple-element.50), channel_id=1, source_target_pairs={{0,1},{1,0},{2,3},{3,2},{4,5},{5,4},{6,7},{7,6},{8,9},{9,8},{10,11... | collective-permute-start | bytes 1572872 | tf_op jit(solution)/shard_map/reduce/ppermute | solution.py:149
  88.6 1.5 collective-permute-done.18
  90.1 0.0 collective-permute-start.10
  90.1 0.0 collective-permute-done.14.refs_0_
  90.1 2.7 %collective-permute-start.11 = (bf16[64,9216]{1,0:T(8,128)(2,1)S(1)}, bf16[64,9216]{1,0:T(8,128)(2,1)S(1)}, u32[]{:S(2)}, u32[]{:S(2)}) collective-permute-start(bf16[64,9216]{1,0:T(8,128)(2,1)S(1)} %pad_maximum_fusion.1.refs_1_), channel_id=1, source_target_pairs={{0,12},{4,0},{8,4},{12,8},{1,13},{5,1},{9,5},{13,9},{2,14},{6,2},{... | collective-permute-start | bytes 3538952 | tf_op jit(solution)/shard_map/second_axis/ppermute | solution.py:21
  92.8 0.1 collective-permute-start.12
  92.9 2.6 %collective-permute-start.13 = (bf16[64,9216]{1,0:T(8,128)(2,1)S(1)}, bf16[64,9216]{1,0:T(8,128)(2,1)S(1)}, u32[]{:S(2)}, u32[]{:S(2)}) collective-permute-start(bf16[64,9216]{1,0:T(8,128)(2,1)S(1)} %pad_maximum_fusion.2.refs_3_), channel_id=1, source_target_pairs={{0,48},{16,0},{32,16},{48,32},{1,49},{17,1},{33,17},{49,33},{2,50}... | collective-permute-start | bytes 3538952 | tf_op jit(solution)/shard_map/second_axis/ppermute | solution.py:21
  95.5 7.1 %collective-permute-done.17.refs_3_ = bf16[64,9216]{1,0:T(8,128)(2,1)S(1)} collective-permute-done((bf16[64,9216]{1,0:T(8,128)(2,1)S(1)}, bf16[64,9216]{1,0:T(8,128)(2,1)S(1)}, u32[]{:S(2)}, u32[]{:S(2)}) %collective-permute-start.17) | collective-permute-done | bytes 1179680 | tf_op jit(solution)/shard_map/second_axis/ppermute | solution.py:21
  102.7 3.5 %collective-permute-start.19 = (f32[2,8,8,512]{3,2,1,0:T(8,128)S(1)}, f32[2,8,8,512]{3,2,1,0:T(8,128)S(1)}, u32[]{:S(2)}, u32[]{:S(2)}) collective-permute-start(f32[2,8,8,512]{3,2,1,0:T(8,128)S(1)} %fusion.7), channel_id=1, source_target_pairs={{0,2},{2,0},{1,3},{3,1},{4,6},{6,4},{5,7},{7,5},{8,10},{10,8},{9,1... | collective-permute-start | bytes 786440 | tf_op jit(solution)/shard_map/reduce/ppermute | solution.py:146
  106.1 3.2 %reduce.9 = (f32[2,2,8,8,512]{4,3,2,1,0:T(8,128)S(1)}, f32[2,2,8,8,512]{4,3,2,1,0:T(8,128)S(1)}) custom-call(s32[3]{0:T(128)S(1)} %pad_add_fusion.place_ref, bf16[64,9216]{1,0:T(8,128)(2,1)S(1)} %collective-permute-done.14.refs_0_, bf16[64,9216]{1,0:T(8,128)(2,1)S(1)} %collective-permute-done.15.refs_1_, ...), custom_call_target="tpu_custom_call" | custom-call | flops 1048576 | bytes 65536 | tf_op jit(solution)/shard_map/reduce/pallas_call | solution.py:59
  109.4 2.5 %collective-permute-done.19 = f32[2,8,8,512]{3,2,1,0:T(8,128)S(1)} collective-permute-done((f32[2,8,8,512]{3,2,1,0:T(8,128)S(1)}, f32[2,8,8,512]{3,2,1,0:T(8,128)S(1)}, u32[]{:S(2)}, u32[]{:S(2)}) %collective-permute-start.19) | collective-permute-done | bytes 262176 | tf_op jit(solution)/shard_map/reduce/ppermute | solution.py:146
  111.9 10.7 %collective-permute-start.24 = (f32[2,2,8,8,512]{4,3,2,1,0:T(8,128)S(1)}, f32[2,2,8,8,512]{4,3,2,1,0:T(8,128)S(1)}, u32[]{:S(2)}, u32[]{:S(2)}) collective-permute-start(f32[2,2,8,8,512]{4,3,2,1,0:T(8,128)S(1)} %get-tuple-element.59), channel_id=1, source_target_pairs={{0,1},{1,0},{2,3},{3,2},{4,5},{5,4},{6,7},{7,6},{8,9},{9,8},{10,11... | collective-permute-start | bytes 1572872 | tf_op jit(solution)/shard_map/reduce/ppermute | solution.py:149
  122.6 0.1 fusion.9
  122.8 5.2 %collective-permute-done.13.refs_3_ = bf16[64,9216]{1,0:T(8,128)(2,1)S(1)} collective-permute-done((bf16[64,9216]{1,0:T(8,128)(2,1)S(1)}, bf16[64,9216]{1,0:T(8,128)(2,1)S(1)}, u32[]{:S(2)}, u32[]{:S(2)}) %collective-permute-start.13) | collective-permute-done | bytes 1179680 | tf_op jit(solution)/shard_map/second_axis/ppermute | solution.py:21
  128.0 2.7 %collective-permute-start.21 = (bf16[64,9216]{1,0:T(8,128)(2,1)S(1)}, bf16[64,9216]{1,0:T(8,128)(2,1)S(1)}, u32[]{:S(2)}, u32[]{:S(2)}) collective-permute-start(bf16[64,9216]{1,0:T(8,128)(2,1)S(1)} %collective-permute-done.11.refs_1_), channel_id=1, source_target_pairs={{0,12},{4,0},{8,4},{12,8},{1,13},{5,1},{9,5},{13,9},{2,14},{6,2},{... | collective-permute-start | bytes 3538952 | tf_op jit(solution)/shard_map/second_axis/ppermute | solution.py:21
  130.6 2.7 %collective-permute-start.23 = (bf16[64,9216]{1,0:T(8,128)(2,1)S(1)}, bf16[64,9216]{1,0:T(8,128)(2,1)S(1)}, u32[]{:S(2)}, u32[]{:S(2)}) collective-permute-start(bf16[64,9216]{1,0:T(8,128)(2,1)S(1)} %collective-permute-done.13.refs_3_), channel_id=1, source_target_pairs={{0,48},{16,0},{32,16},{48,32},{1,49},{17,1},{33,17},{49,33},{2,50}... | collective-permute-start | bytes 3538952 | tf_op jit(solution)/shard_map/second_axis/ppermute | solution.py:21
  133.3 3.6 %collective-permute-start.25 = (f32[2,8,8,512]{3,2,1,0:T(8,128)S(1)}, f32[2,8,8,512]{3,2,1,0:T(8,128)S(1)}, u32[]{:S(2)}, u32[]{:S(2)}) collective-permute-start(f32[2,8,8,512]{3,2,1,0:T(8,128)S(1)} %fusion.4), channel_id=1, source_target_pairs={{0,2},{2,0},{1,3},{3,1},{4,6},{6,4},{5,7},{7,5},{8,10},{10,8},{9,1... | collective-permute-start | bytes 786440 | tf_op jit(solution)/shard_map/reduce/ppermute | solution.py:146
  136.9 3.2 %reduce.10 = (f32[2,2,8,8,512]{4,3,2,1,0:T(8,128)S(1)}, f32[2,2,8,8,512]{4,3,2,1,0:T(8,128)S(1)}) custom-call(s32[3]{0:T(128)S(1)} %pad_add_fusion.place_ref, bf16[64,9216]{1,0:T(8,128)(2,1)S(1)} %collective-permute-done.10.refs_0_, bf16[64,9216]{1,0:T(8,128)(2,1)S(1)} %collective-permute-done.11.refs_1_, ...), custom_call_target="tpu_custom_call" | custom-call | flops 1048576 | bytes 65536 | tf_op jit(solution)/shard_map/reduce/pallas_call | solution.py:59
  140.2 4.7 %collective-permute-done.25 = f32[2,8,8,512]{3,2,1,0:T(8,128)S(1)} collective-permute-done((f32[2,8,8,512]{3,2,1,0:T(8,128)S(1)}, f32[2,8,8,512]{3,2,1,0:T(8,128)S(1)}, u32[]{:S(2)}, u32[]{:S(2)}) %collective-permute-start.25) | collective-permute-done | bytes 262176 | tf_op jit(solution)/shard_map/reduce/ppermute | solution.py:146
  144.9 5.1 %collective-permute-start.26 = (f32[2,2,8,8,512]{4,3,2,1,0:T(8,128)S(1)}, f32[2,2,8,8,512]{4,3,2,1,0:T(8,128)S(1)}, u32[]{:S(2)}, u32[]{:S(2)}) collective-permute-start(f32[2,2,8,8,512]{4,3,2,1,0:T(8,128)S(1)} %get-tuple-element.63), channel_id=1, source_target_pairs={{0,1},{1,0},{2,3},{3,2},{4,5},{5,4},{6,7},{7,6},{8,9},{9,8},{10,11... | collective-permute-start | bytes 1572872 | tf_op jit(solution)/shard_map/reduce/ppermute | solution.py:149
  150.0 0.1 fusion.6
  150.1 1.5 collective-permute-done.26
  151.6 4.9 %collective-permute-start.28 = (f32[2,8,8,512]{3,2,1,0:T(8,128)S(1)}, f32[2,8,8,512]{3,2,1,0:T(8,128)S(1)}, u32[]{:S(2)}, u32[]{:S(2)}) collective-permute-start(f32[2,8,8,512]{3,2,1,0:T(8,128)S(1)} %fusion.3), channel_id=1, source_target_pairs={{0,2},{2,0},{1,3},{3,1},{4,6},{6,4},{5,7},{7,5},{8,10},{10,8},{9,1... | collective-permute-start | bytes 786440 | tf_op jit(solution)/shard_map/reduce/ppermute | solution.py:146
  156.5 3.2 %reduce.11 = (f32[2,2,8,8,512]{4,3,2,1,0:T(8,128)S(1)}, f32[2,2,8,8,512]{4,3,2,1,0:T(8,128)S(1)}) custom-call(s32[3]{0:T(128)S(1)} %pad_add_fusion.place_ref, bf16[64,9216]{1,0:T(8,128)(2,1)S(1)} %collective-permute-done.20.refs_0_, bf16[64,9216]{1,0:T(8,128)(2,1)S(1)} %collective-permute-done.21.refs_1_, ...), custom_call_target="tpu_custom_call" | custom-call | flops 1048576 | bytes 65536 | tf_op jit(solution)/shard_map/reduce/pallas_call | solution.py:59
  159.8 3.8 %collective-permute-start.27 = (f32[2,2,8,8,512]{4,3,2,1,0:T(8,128)S(1)}, f32[2,2,8,8,512]{4,3,2,1,0:T(8,128)S(1)}, u32[]{:S(2)}, u32[]{:S(2)}) collective-permute-start(f32[2,2,8,8,512]{4,3,2,1,0:T(8,128)S(1)} %get-tuple-element.70), channel_id=1, source_target_pairs={{0,1},{1,0},{2,3},{3,2},{4,5},{5,4},{6,7},{7,6},{8,9},{9,8},{10,11... | collective-permute-start | bytes 1572872 | tf_op jit(solution)/shard_map/reduce/ppermute | solution.py:149
  163.6 1.1 collective-permute-done.28
  164.6 0.1 fusion.1
  164.7 0.4 collective-permute-done.27.got_ref
  165.1 3.6 %collective-permute-start.29 = (f32[2,8,8,512]{3,2,1,0:T(8,128)S(1)}, f32[2,8,8,512]{3,2,1,0:T(8,128)S(1)}, u32[]{:S(2)}, u32[]{:S(2)}) collective-permute-start(f32[2,8,8,512]{3,2,1,0:T(8,128)S(1)} %fusion.2), channel_id=1, source_target_pairs={{0,2},{2,0},{1,3},{3,1},{4,6},{6,4},{5,7},{7,5},{8,10},{10,8},{9,1... | collective-permute-start | bytes 786440 | tf_op jit(solution)/shard_map/reduce/ppermute | solution.py:146
  168.7 10.9 %collective-permute-done.29.back_ref = f32[2,8,8,512]{3,2,1,0:T(8,128)S(1)} collective-permute-done((f32[2,8,8,512]{3,2,1,0:T(8,128)S(1)}, f32[2,8,8,512]{3,2,1,0:T(8,128)S(1)}, u32[]{:S(2)}, u32[]{:S(2)}) %collective-permute-start.29) | collective-permute-done | bytes 262176 | tf_op jit(solution)/shard_map/reduce/ppermute | solution.py:146
  179.6 1.6 reduce.12
  (30 shorter events, 0.4 us)
Async XLA Ops:
  1.0 9.2 %collective-permute-start = (bf16[16,9216]{1,0:T(8,128)(2,1)S(1)}, bf16[16,9216]{1,0:T(8,128)(2,1)S(1)}, u32[]{:S(2)}, u32[]{:S(2)}) collective-permute-start(bf16[16,9216]{1,0:T(8,128)(2,1)S(1)} %get-tuple-element.76), channel_id=1, source_target_pairs={{0,64},{64,0},{128,192},{192,128},{1,65},{65,1},{129,193},{193,129... | collective-permute-start | bytes 884744 | tf_op jit(solution)/shard_map/z_shifts/ppermute | solution.py:26
  1.1 21.3 %collective-permute-start.1 = (bf16[16,9216]{1,0:T(8,128)(2,1)S(1)}, bf16[16,9216]{1,0:T(8,128)(2,1)S(1)}, u32[]{:S(2)}, u32[]{:S(2)}) collective-permute-start(bf16[16,9216]{1,0:T(8,128)(2,1)S(1)} %get-tuple-element.76), channel_id=1, source_target_pairs={{0,128},{64,192},{128,0},{192,64},{1,129},{65,193},{129,1},{193,65... | collective-permute-start | bytes 884744 | tf_op jit(solution)/shard_map/z_shifts/ppermute | solution.py:26
  4.2 25.6 %collective-permute-start.2 = (bf16[16,9216]{1,0:T(8,128)(2,1)S(1)}, bf16[16,9216]{1,0:T(8,128)(2,1)S(1)}, u32[]{:S(2)}, u32[]{:S(2)}) collective-permute-start(bf16[16,9216]{1,0:T(8,128)(2,1)S(1)} %get-tuple-element.76), channel_id=1, source_target_pairs={{0,192},{64,128},{128,64},{192,0},{1,193},{65,129},{129,65},{193,1... | collective-permute-start | bytes 884744 | tf_op jit(solution)/shard_map/z_shifts/ppermute | solution.py:26
  29.8 49.7 %slice-start = ((s8[7340032]{0:T(1024)(128)(4,1)}), s8[3145728]{0:T(1024)(128)(4,1)S(1)}, s32[]{:S(2)}) async-start(s8[7340032]{0:T(1024)(128)(4,1)} %bitcast.34), calls=%async_computation | async-start | bytes 6291456
  31.1 15.0 %collective-permute-start.9 = (bf16[32,9216]{1,0:T(8,128)(2,1)}, bf16[32,9216]{1,0:T(8,128)(2,1)}, u32[]{:S(2)}, u32[]{:S(2)}) collective-permute-start(bf16[32,9216]{1,0:T(8,128)(2,1)} %get-tuple-element.74), channel_id=1, source_target_pairs={{0,16},{16,32},{32,48},{48,0},{1,17},{17,33},{33,49},{49,1},{2,18}... | collective-permute-start | bytes 1769480 | tf_op jit(solution)/shard_map/first_axis/ppermute | solution.py:21
  32.5 16.3 %collective-permute-start.6 = (bf16[32,9216]{1,0:T(8,128)(2,1)}, bf16[32,9216]{1,0:T(8,128)(2,1)S(1)}, u32[]{:S(2)}, u32[]{:S(2)}) collective-permute-start(bf16[32,9216]{1,0:T(8,128)(2,1)} %get-tuple-element.73), channel_id=1, source_target_pairs={{0,4},{4,8},{8,12},{12,0},{1,5},{5,9},{9,13},{13,1},{2,6},{6,10},{... | collective-permute-start | bytes 1769480 | tf_op jit(solution)/shard_map/first_axis/ppermute | solution.py:21
  33.7 16.6 %collective-permute-start.5 = (bf16[32,9216]{1,0:T(8,128)(2,1)}, bf16[32,9216]{1,0:T(8,128)(2,1)S(1)}, u32[]{:S(2)}, u32[]{:S(2)}) collective-permute-start(bf16[32,9216]{1,0:T(8,128)(2,1)} %get-tuple-element.73), channel_id=1, source_target_pairs={{0,12},{4,0},{8,4},{12,8},{1,13},{5,1},{9,5},{13,9},{2,14},{6,2},{... | collective-permute-start | bytes 1769480 | tf_op jit(solution)/shard_map/first_axis/ppermute | solution.py:21
  35.2 15.3 %collective-permute-start.3 = (bf16[32,9216]{1,0:T(8,128)(2,1)}, bf16[32,9216]{1,0:T(8,128)(2,1)S(1)}, u32[]{:S(2)}, u32[]{:S(2)}) collective-permute-start(bf16[32,9216]{1,0:T(8,128)(2,1)} %get-tuple-element.74), channel_id=1, source_target_pairs={{0,48},{16,0},{32,16},{48,32},{1,49},{17,1},{33,17},{49,33},{2,50}... | collective-permute-start | bytes 1769480 | tf_op jit(solution)/shard_map/first_axis/ppermute | solution.py:21
  36.6 23.1 %collective-permute-start.4 = (bf16[32,9216]{1,0:T(8,128)(2,1)}, bf16[32,9216]{1,0:T(8,128)(2,1)S(1)}, u32[]{:S(2)}, u32[]{:S(2)}) collective-permute-start(bf16[32,9216]{1,0:T(8,128)(2,1)} %get-tuple-element.74), channel_id=1, source_target_pairs={{0,32},{16,48},{32,0},{48,16},{1,33},{17,49},{33,1},{49,17},{2,34}... | collective-permute-start | bytes 1769480 | tf_op jit(solution)/shard_map/first_axis/ppermute | solution.py:21
  46.1 4.3 %copy-start.1 = (bf16[32,9216]{1,0:T(8,128)(2,1)S(1)}, bf16[32,9216]{1,0:T(8,128)(2,1)}, u32[]{:S(2)}) copy-start(bf16[32,9216]{1,0:T(8,128)(2,1)} %get-tuple-element.73) | copy-start | bytes 1769476
  47.5 32.1 %slice-start.1 = ((s8[7340032]{0:T(1024)(128)(4,1)}), s8[4194304]{0:T(1024)(128)(4,1)S(1)}, s32[]{:S(2)}) async-start(s8[7340032]{0:T(1024)(128)(4,1)} %bitcast.34), calls=%async_computation.1 | async-start | bytes 8388608
  47.5 42.7 %collective-permute-start.14 = (bf16[64,9216]{1,0:T(8,128)(2,1)S(1)}, bf16[64,9216]{1,0:T(8,128)(2,1)S(1)}, u32[]{:S(2)}, u32[]{:S(2)}) collective-permute-start(bf16[64,9216]{1,0:T(8,128)(2,1)S(1)} %pad_maximum_fusion.3.refs_0_), channel_id=1, source_target_pairs={{0,4},{4,8},{8,12},{12,0},{1,5},{5,9},{9,13},{13,1},{2,6},{6,10},{... | collective-permute-start | bytes 3538952 | tf_op jit(solution)/shard_map/second_axis/ppermute | solution.py:21
  48.8 44.1 %collective-permute-start.15 = (bf16[64,9216]{1,0:T(8,128)(2,1)S(1)}, bf16[64,9216]{1,0:T(8,128)(2,1)S(1)}, u32[]{:S(2)}, u32[]{:S(2)}) collective-permute-start(bf16[64,9216]{1,0:T(8,128)(2,1)S(1)} %pad_maximum_fusion.3.refs_0_), channel_id=1, source_target_pairs={{0,12},{4,0},{8,4},{12,8},{1,13},{5,1},{9,5},{13,9},{2,14},{6,2},{... | collective-permute-start | bytes 3538952 | tf_op jit(solution)/shard_map/second_axis/ppermute | solution.py:21
  50.3 29.1 %collective-permute-start.7 = (bf16[16,9216]{1,0:T(8,128)(2,1)S(1)}, bf16[16,9216]{1,0:T(8,128)(2,1)S(1)}, u32[]{:S(2)}, u32[]{:S(2)}) collective-permute-start(bf16[16,9216]{1,0:T(8,128)(2,1)S(1)} %slice.98), channel_id=1, source_target_pairs={{0,4},{4,8},{8,12},{12,0},{1,5},{5,9},{9,13},{13,1},{2,6},{6,10},{... | collective-permute-start | bytes 884744 | tf_op jit(solution)/shard_map/first_axis/ppermute | solution.py:21
  50.5 29.0 %collective-permute-start.8 = (bf16[16,9216]{1,0:T(8,128)(2,1)S(1)}, bf16[16,9216]{1,0:T(8,128)(2,1)S(1)}, u32[]{:S(2)}, u32[]{:S(2)}) collective-permute-start(bf16[16,9216]{1,0:T(8,128)(2,1)S(1)} %slice.99), channel_id=1, source_target_pairs={{0,12},{4,0},{8,4},{12,8},{1,13},{5,1},{9,5},{13,9},{2,14},{6,2},{... | collective-permute-start | bytes 884744 | tf_op jit(solution)/shard_map/first_axis/ppermute | solution.py:21
  59.7 33.2 %collective-permute-start.16 = (bf16[64,9216]{1,0:T(8,128)(2,1)S(1)}, bf16[64,9216]{1,0:T(8,128)(2,1)S(1)}, u32[]{:S(2)}, u32[]{:S(2)}) collective-permute-start(bf16[64,9216]{1,0:T(8,128)(2,1)S(1)} %pad_maximum_fusion.4.refs_2_), channel_id=1, source_target_pairs={{0,16},{16,32},{32,48},{48,0},{1,17},{17,33},{33,49},{49,1},{2,18}... | collective-permute-start | bytes 3538952 | tf_op jit(solution)/shard_map/second_axis/ppermute | solution.py:21
  62.6 17.0 %copy-start = (bf16[512,2048]{1,0:T(8,128)(2,1)S(1)}, bf16[512,2048]{1,0:T(8,128)(2,1)}, u32[]{:S(2)}) copy-start(bf16[512,2048]{1,0:T(8,128)(2,1)} %refs_5_.7) | copy-start | bytes 6291460
  79.3 23.3 %collective-permute-start.17 = (bf16[64,9216]{1,0:T(8,128)(2,1)S(1)}, bf16[64,9216]{1,0:T(8,128)(2,1)S(1)}, u32[]{:S(2)}, u32[]{:S(2)}) collective-permute-start(bf16[64,9216]{1,0:T(8,128)(2,1)S(1)} %pad_maximum_fusion.4.refs_2_), channel_id=1, source_target_pairs={{0,48},{16,0},{32,16},{48,32},{1,49},{17,1},{33,17},{49,33},{2,50}... | collective-permute-start | bytes 3538952 | tf_op jit(solution)/shard_map/second_axis/ppermute | solution.py:21
  82.9 7.3 %collective-permute-start.18 = (f32[2,2,8,8,512]{4,3,2,1,0:T(8,128)S(1)}, f32[2,2,8,8,512]{4,3,2,1,0:T(8,128)S(1)}, u32[]{:S(2)}, u32[]{:S(2)}) collective-permute-start(f32[2,2,8,8,512]{4,3,2,1,0:T(8,128)S(1)} %get-tuple-element.50), channel_id=1, source_target_pairs={{0,1},{1,0},{2,3},{3,2},{4,5},{5,4},{6,7},{7,6},{8,9},{9,8},{10,11... | collective-permute-start | bytes 1572872 | tf_op jit(solution)/shard_map/reduce/ppermute | solution.py:149
  90.1 32.6 %collective-permute-start.10 = (bf16[64,9216]{1,0:T(8,128)(2,1)S(1)}, bf16[64,9216]{1,0:T(8,128)(2,1)S(1)}, u32[]{:S(2)}, u32[]{:S(2)}) collective-permute-start(bf16[64,9216]{1,0:T(8,128)(2,1)S(1)} %pad_maximum_fusion.1.refs_1_), channel_id=1, source_target_pairs={{0,4},{4,8},{8,12},{12,0},{1,5},{5,9},{9,13},{13,1},{2,6},{6,10},{... | collective-permute-start | bytes 3538952 | tf_op jit(solution)/shard_map/second_axis/ppermute | solution.py:21
  90.1 32.6 %collective-permute-start.11 = (bf16[64,9216]{1,0:T(8,128)(2,1)S(1)}, bf16[64,9216]{1,0:T(8,128)(2,1)S(1)}, u32[]{:S(2)}, u32[]{:S(2)}) collective-permute-start(bf16[64,9216]{1,0:T(8,128)(2,1)S(1)} %pad_maximum_fusion.1.refs_1_), channel_id=1, source_target_pairs={{0,12},{4,0},{8,4},{12,8},{1,13},{5,1},{9,5},{13,9},{2,14},{6,2},{... | collective-permute-start | bytes 3538952 | tf_op jit(solution)/shard_map/second_axis/ppermute | solution.py:21
  92.8 30.0 %collective-permute-start.12 = (bf16[64,9216]{1,0:T(8,128)(2,1)S(1)}, bf16[64,9216]{1,0:T(8,128)(2,1)S(1)}, u32[]{:S(2)}, u32[]{:S(2)}) collective-permute-start(bf16[64,9216]{1,0:T(8,128)(2,1)S(1)} %pad_maximum_fusion.2.refs_3_), channel_id=1, source_target_pairs={{0,16},{16,32},{32,48},{48,0},{1,17},{17,33},{33,49},{49,1},{2,18}... | collective-permute-start | bytes 3538952 | tf_op jit(solution)/shard_map/second_axis/ppermute | solution.py:21
  92.9 35.1 %collective-permute-start.13 = (bf16[64,9216]{1,0:T(8,128)(2,1)S(1)}, bf16[64,9216]{1,0:T(8,128)(2,1)S(1)}, u32[]{:S(2)}, u32[]{:S(2)}) collective-permute-start(bf16[64,9216]{1,0:T(8,128)(2,1)S(1)} %pad_maximum_fusion.2.refs_3_), channel_id=1, source_target_pairs={{0,48},{16,0},{32,16},{48,32},{1,49},{17,1},{33,17},{49,33},{2,50}... | collective-permute-start | bytes 3538952 | tf_op jit(solution)/shard_map/second_axis/ppermute | solution.py:21
  102.7 9.2 %collective-permute-start.19 = (f32[2,8,8,512]{3,2,1,0:T(8,128)S(1)}, f32[2,8,8,512]{3,2,1,0:T(8,128)S(1)}, u32[]{:S(2)}, u32[]{:S(2)}) collective-permute-start(f32[2,8,8,512]{3,2,1,0:T(8,128)S(1)} %fusion.7), channel_id=1, source_target_pairs={{0,2},{2,0},{1,3},{3,1},{4,6},{6,4},{5,7},{7,5},{8,10},{10,8},{9,1... | collective-permute-start | bytes 786440 | tf_op jit(solution)/shard_map/reduce/ppermute | solution.py:146
  111.9 21.4 %collective-permute-start.24 = (f32[2,2,8,8,512]{4,3,2,1,0:T(8,128)S(1)}, f32[2,2,8,8,512]{4,3,2,1,0:T(8,128)S(1)}, u32[]{:S(2)}, u32[]{:S(2)}) collective-permute-start(f32[2,2,8,8,512]{4,3,2,1,0:T(8,128)S(1)} %get-tuple-element.59), channel_id=1, source_target_pairs={{0,1},{1,0},{2,3},{3,2},{4,5},{5,4},{6,7},{7,6},{8,9},{9,8},{10,11... | collective-permute-start | bytes 1572872 | tf_op jit(solution)/shard_map/reduce/ppermute | solution.py:149
  128.0 28.5 %collective-permute-start.20 = (bf16[64,9216]{1,0:T(8,128)(2,1)S(1)}, bf16[64,9216]{1,0:T(8,128)(2,1)S(1)}, u32[]{:S(2)}, u32[]{:S(2)}) collective-permute-start(bf16[64,9216]{1,0:T(8,128)(2,1)S(1)} %collective-permute-done.14.refs_0_), channel_id=1, source_target_pairs={{0,4},{4,8},{8,12},{12,0},{1,5},{5,9},{9,13},{13,1},{2,6},{6,10},{... | collective-permute-start | bytes 3538952 | tf_op jit(solution)/shard_map/second_axis/ppermute | solution.py:21
  128.0 28.6 %collective-permute-start.21 = (bf16[64,9216]{1,0:T(8,128)(2,1)S(1)}, bf16[64,9216]{1,0:T(8,128)(2,1)S(1)}, u32[]{:S(2)}, u32[]{:S(2)}) collective-permute-start(bf16[64,9216]{1,0:T(8,128)(2,1)S(1)} %collective-permute-done.11.refs_1_), channel_id=1, source_target_pairs={{0,12},{4,0},{8,4},{12,8},{1,13},{5,1},{9,5},{13,9},{2,14},{6,2},{... | collective-permute-start | bytes 3538952 | tf_op jit(solution)/shard_map/second_axis/ppermute | solution.py:21
  130.6 25.9 %collective-permute-start.22 = (bf16[64,9216]{1,0:T(8,128)(2,1)S(1)}, bf16[64,9216]{1,0:T(8,128)(2,1)S(1)}, u32[]{:S(2)}, u32[]{:S(2)}) collective-permute-start(bf16[64,9216]{1,0:T(8,128)(2,1)S(1)} %collective-permute-done.16.refs_2_), channel_id=1, source_target_pairs={{0,16},{16,32},{32,48},{48,0},{1,17},{17,33},{33,49},{49,1},{2,18}... | collective-permute-start | bytes 3538952 | tf_op jit(solution)/shard_map/second_axis/ppermute | solution.py:21
  130.6 25.9 %collective-permute-start.23 = (bf16[64,9216]{1,0:T(8,128)(2,1)S(1)}, bf16[64,9216]{1,0:T(8,128)(2,1)S(1)}, u32[]{:S(2)}, u32[]{:S(2)}) collective-permute-start(bf16[64,9216]{1,0:T(8,128)(2,1)S(1)} %collective-permute-done.13.refs_3_), channel_id=1, source_target_pairs={{0,48},{16,0},{32,16},{48,32},{1,49},{17,1},{33,17},{49,33},{2,50}... | collective-permute-start | bytes 3538952 | tf_op jit(solution)/shard_map/second_axis/ppermute | solution.py:21
  133.3 11.5 %collective-permute-start.25 = (f32[2,8,8,512]{3,2,1,0:T(8,128)S(1)}, f32[2,8,8,512]{3,2,1,0:T(8,128)S(1)}, u32[]{:S(2)}, u32[]{:S(2)}) collective-permute-start(f32[2,8,8,512]{3,2,1,0:T(8,128)S(1)} %fusion.4), channel_id=1, source_target_pairs={{0,2},{2,0},{1,3},{3,1},{4,6},{6,4},{5,7},{7,5},{8,10},{10,8},{9,1... | collective-permute-start | bytes 786440 | tf_op jit(solution)/shard_map/reduce/ppermute | solution.py:146
  144.9 6.6 %collective-permute-start.26 = (f32[2,2,8,8,512]{4,3,2,1,0:T(8,128)S(1)}, f32[2,2,8,8,512]{4,3,2,1,0:T(8,128)S(1)}, u32[]{:S(2)}, u32[]{:S(2)}) collective-permute-start(f32[2,2,8,8,512]{4,3,2,1,0:T(8,128)S(1)} %get-tuple-element.63), channel_id=1, source_target_pairs={{0,1},{1,0},{2,3},{3,2},{4,5},{5,4},{6,7},{7,6},{8,9},{9,8},{10,11... | collective-permute-start | bytes 1572872 | tf_op jit(solution)/shard_map/reduce/ppermute | solution.py:149
  151.6 13.1 %collective-permute-start.28 = (f32[2,8,8,512]{3,2,1,0:T(8,128)S(1)}, f32[2,8,8,512]{3,2,1,0:T(8,128)S(1)}, u32[]{:S(2)}, u32[]{:S(2)}) collective-permute-start(f32[2,8,8,512]{3,2,1,0:T(8,128)S(1)} %fusion.3), channel_id=1, source_target_pairs={{0,2},{2,0},{1,3},{3,1},{4,6},{6,4},{5,7},{7,5},{8,10},{10,8},{9,1... | collective-permute-start | bytes 786440 | tf_op jit(solution)/shard_map/reduce/ppermute | solution.py:146
  159.8 5.3 %collective-permute-start.27 = (f32[2,2,8,8,512]{4,3,2,1,0:T(8,128)S(1)}, f32[2,2,8,8,512]{4,3,2,1,0:T(8,128)S(1)}, u32[]{:S(2)}, u32[]{:S(2)}) collective-permute-start(f32[2,2,8,8,512]{4,3,2,1,0:T(8,128)S(1)} %get-tuple-element.70), channel_id=1, source_target_pairs={{0,1},{1,0},{2,3},{3,2},{4,5},{5,4},{6,7},{7,6},{8,9},{9,8},{10,11... | collective-permute-start | bytes 1572872 | tf_op jit(solution)/shard_map/reduce/ppermute | solution.py:149
  165.1 14.4 %collective-permute-start.29 = (f32[2,8,8,512]{3,2,1,0:T(8,128)S(1)}, f32[2,8,8,512]{3,2,1,0:T(8,128)S(1)}, u32[]{:S(2)}, u32[]{:S(2)}) collective-permute-start(f32[2,8,8,512]{3,2,1,0:T(8,128)S(1)} %fusion.2), channel_id=1, source_target_pairs={{0,2},{2,0},{1,3},{3,1},{4,6},{6,4},{5,7},{7,5},{8,10},{10,8},{9,1... | collective-permute-start | bytes 786440 | tf_op jit(solution)/shard_map/reduce/ppermute | solution.py:146

commit v9 on v7

--- a/solution.py
+++ b/solution.py
@@ -155,7 +155,7 @@
     with jax.named_scope("first_axis"):
         lo_a, hi_a = first(stacked[:, :RANK], "y")
         lo_b, hi_b = first(stacked[:, RANK:], "x")
-        lo_a, lo_b = lax.optimization_barrier((lo_a, lo_b))
+        lo_a, lo_b, hi_b = lax.optimization_barrier((lo_a, lo_b, hi_b))
         hi_a, hi_b = lax.optimization_barrier((hi_a, hi_b))
     with jax.named_scope("second_axis"):
         lo = both(lo_a, "x") + both(lo_b, "y")

time: 168 us -> 170 us (1.012)
  starting transfers between devices: 71.8 us -> 67.3 us
  other arithmetic: 4.39 us -> 6.64 us
  waiting for transfers between devices: 73.2 us -> 75.4 us
  local copies, waits for them, and re-layouts: 3.14 us -> 5.08 us
    ppermute x4, waiting for transfers between devices: 20 us -> 26 us  [exchange(): return lax.ppermute(sent, 'zh', [(0, 1), (1, 0)])]
    ppermute x20, waiting for transfers between devices: 24.7 us -> 20.9 us  [ring(): return lax.ppermute(x, axis, [(i, (i + step) % n) for i in range(n)])]
    ppermute x4, starting transfers between devices: 27.2 us -> 24.5 us  [over(): return lax.ppermute(send, 'core', [(0, 1), (1, 0)])]
    ppermute x4, starting transfers between devices: 16.4 us -> 14 us  [exchange(): return lax.ppermute(sent, 'zh', [(0, 1), (1, 0)])]
    concatenate x4, other arithmetic: 2.69 us -> 4.92 us  [first(): return (jnp.concatenate([block, before]), jnp.concatenate([after, *far]))]
    slice x4, local copies, waits for them, and re-layouts: 2 us -> 3.93 us  [first(): far = (ring(before[:half], axis, 1), ring(after[half:], axis, -1))]
  transfers between devices with their start and end apart: 31 -> 31, of which waited for: 15 -> 13; matrix products, arithmetic and copies ran while one was open for 3% -> 6% of each run, Pallas kernels for 8% -> 8%
where the time goes in v9:
time: 170 us; the launch traced here: 169 us
  waiting for transfers between devices  75.4 us (44%)
  starting transfers between devices  67.3 us (40%)
  Pallas kernels  14.5 us (9%)
  other arithmetic  6.64 us (4%)
  local copies, waits for them, and re-layouts  5.08 us (3%)
    ppermute x4, waiting for transfers between devices, exchange(): return lax.ppermute(sent, 'zh', [(0, 1), (1, 0)])  26 us
    ppermute x3, waiting for transfers between devices, flip(): return lax.ppermute(x, axis, [(i, i ^ mask) for i in range(n)])  25.5 us
    ppermute x20, starting transfers between devices, ring(): return lax.ppermute(x, axis, [(i, (i + step) % n) for i in range(n)])  25.4 us
    ppermute x4, starting transfers between devices, over(): return lax.ppermute(send, 'core', [(0, 1), (1, 0)])  24.5 us
    ppermute x20, waiting for transfers between devices, ring(): return lax.ppermute(x, axis, [(i, (i + step) % n) for i in range(n)])  20.9 us
    ppermute x4, starting transfers between devices, exchange(): return lax.ppermute(sent, 'zh', [(0, 1), (1, 0)])  14 us
    pallas_call x4, Pallas kernels, project(): pl.pallas_call(functools.partial(project_kernel, len(blocks)), out_shape=...  13 us
    concatenate x4, other arithmetic, first(): return (jnp.concatenate([block, before]), jnp.concatenate([after, *far]))  4.92 us
  transfers between devices with their start and end apart: 31, of which 13 were waited for; matrix products, arithmetic and copies ran while one was open for 6% of the time, Pallas kernels for 8%

profile of v9, /device:TPU:33, one launch (start us, length us, event | category | flops | bytes accessed | tf_op | source)
XLA Modules:
  0.0 169.3 jit_solution(18015404285217440889)
XLA Ops:
  0.0 1.0 fusion.13
  1.0 0.1 collective-permute-start
  1.1 3.1 %collective-permute-start.1 = (bf16[16,9216]{1,0:T(8,128)(2,1)S(1)}, bf16[16,9216]{1,0:T(8,128)(2,1)S(1)}, u32[]{:S(2)}, u32[]{:S(2)}) collective-permute-start(bf16[16,9216]{1,0:T(8,128)(2,1)S(1)} %get-tuple-element.82), channel_id=1, source_target_pairs={{0,128},{64,192},{128,0},{192,64},{1,129},{65,193},{129,1},{193,65... | collective-permute-start | bytes 884744 | tf_op jit(solution)/shard_map/z_shifts/ppermute | solution.py:26
  4.2 0.2 collective-permute-start.2
  4.4 5.9 %collective-permute-done = bf16[16,9216]{1,0:T(8,128)(2,1)S(1)} collective-permute-done((bf16[16,9216]{1,0:T(8,128)(2,1)S(1)}, bf16[16,9216]{1,0:T(8,128)(2,1)S(1)}, u32[]{:S(2)}, u32[]{:S(2)}) %collective-permute-start) | collective-permute-done | bytes 294944 | tf_op jit(solution)/shard_map/z_shifts/ppermute | solution.py:26
  10.2 12.2 %collective-permute-done.1 = bf16[16,9216]{1,0:T(8,128)(2,1)S(1)} collective-permute-done((bf16[16,9216]{1,0:T(8,128)(2,1)S(1)}, bf16[16,9216]{1,0:T(8,128)(2,1)S(1)}, u32[]{:S(2)}, u32[]{:S(2)}) %collective-permute-start.1) | collective-permute-done | bytes 294944 | tf_op jit(solution)/shard_map/z_shifts/ppermute | solution.py:26
  22.5 7.4 %collective-permute-done.2 = bf16[16,9216]{1,0:T(8,128)(2,1)S(1)} collective-permute-done((bf16[16,9216]{1,0:T(8,128)(2,1)S(1)}, bf16[16,9216]{1,0:T(8,128)(2,1)S(1)}, u32[]{:S(2)}, u32[]{:S(2)}) %collective-permute-start.2) | collective-permute-done | bytes 294944 | tf_op jit(solution)/shard_map/z_shifts/ppermute | solution.py:26
  29.8 0.1 pad_maximum_fusion
  30.0 0.0 slice-start
  30.0 1.1 slice_bitcast_fusion
  31.1 2.5 %collective-permute-start.8 = (bf16[32,9216]{1,0:T(8,128)(2,1)}, bf16[32,9216]{1,0:T(8,128)(2,1)}, u32[]{:S(2)}, u32[]{:S(2)}) collective-permute-start(bf16[32,9216]{1,0:T(8,128)(2,1)} %get-tuple-element.79), channel_id=1, source_target_pairs={{0,12},{4,0},{8,4},{12,8},{1,13},{5,1},{9,5},{13,9},{2,14},{6,2},{... | collective-permute-start | bytes 1769480 | tf_op jit(solution)/shard_map/first_axis/ppermute | solution.py:21
  33.6 0.0 collective-permute-start.7
  33.6 1.3 collective-permute-start.4
  34.9 1.4 collective-permute-start.3
  36.4 0.1 pad_add_fusion.place_ref
  36.4 8.6 %collective-permute-done.8 = bf16[32,9216]{1,0:T(8,128)(2,1)} collective-permute-done((bf16[32,9216]{1,0:T(8,128)(2,1)}, bf16[32,9216]{1,0:T(8,128)(2,1)}, u32[]{:S(2)}, u32[]{:S(2)}) %collective-permute-start.8) | collective-permute-done | bytes 589856 | tf_op jit(solution)/shard_map/first_axis/ppermute | solution.py:21
  45.1 1.0 slice.109
  46.0 3.5 %collective-permute-start.10 = (bf16[16,9216]{1,0:T(8,128)(2,1)S(1)}, bf16[16,9216]{1,0:T(8,128)(2,1)S(1)}, u32[]{:S(2)}, u32[]{:S(2)}) collective-permute-start(bf16[16,9216]{1,0:T(8,128)(2,1)S(1)} %slice.109), channel_id=1, source_target_pairs={{0,12},{4,0},{8,4},{12,8},{1,13},{5,1},{9,5},{13,9},{2,14},{6,2},{... | collective-permute-start | bytes 884744 | tf_op jit(solution)/shard_map/first_axis/ppermute | solution.py:21
  49.5 1.0 slice.108
  50.5 0.1 collective-permute-start.9
  50.6 1.0 slice.105
  51.6 1.4 collective-permute-start.5
  53.0 1.0 slice.106
  54.0 0.0 slice-start.1
  54.0 1.5 collective-permute-start.6
  55.5 1.3 pad_maximum_fusion.3.refs_2_
  56.8 1.3 pad_maximum_fusion.2.refs_0_
  58.2 1.1 pad_maximum_fusion.4.refs_3_
  59.3 0.0 copy-start
  59.3 0.1 collective-permute-start.15
  59.4 2.7 %collective-permute-start.16 = (bf16[64,9216]{1,0:T(8,128)(2,1)S(1)}, bf16[64,9216]{1,0:T(8,128)(2,1)S(1)}, u32[]{:S(2)}, u32[]{:S(2)}) collective-permute-start(bf16[64,9216]{1,0:T(8,128)(2,1)S(1)} %pad_maximum_fusion.2.refs_0_), channel_id=1, source_target_pairs={{0,12},{4,0},{8,4},{12,8},{1,13},{5,1},{9,5},{13,9},{2,14},{6,2},{... | collective-permute-start | bytes 3538952 | tf_op jit(solution)/shard_map/second_axis/ppermute | solution.py:21
  62.2 0.4 collective-permute-start.17
  62.6 2.3 %collective-permute-start.18 = (bf16[64,9216]{1,0:T(8,128)(2,1)S(1)}, bf16[64,9216]{1,0:T(8,128)(2,1)S(1)}, u32[]{:S(2)}, u32[]{:S(2)}) collective-permute-start(bf16[64,9216]{1,0:T(8,128)(2,1)S(1)} %pad_maximum_fusion.3.refs_2_), channel_id=1, source_target_pairs={{0,48},{16,0},{32,16},{48,32},{1,49},{17,1},{33,17},{49,33},{2,50}... | collective-permute-start | bytes 3538952 | tf_op jit(solution)/shard_map/second_axis/ppermute | solution.py:21
  64.8 1.1 pad_maximum_fusion.1.refs_1_
  66.0 3.2 %reduce.8 = (f32[2,2,8,8,512]{4,3,2,1,0:T(8,128)S(1)}, f32[2,2,8,8,512]{4,3,2,1,0:T(8,128)S(1)}) custom-call(s32[3]{0:T(128)S(1)} %pad_add_fusion.place_ref, bf16[64,9216]{1,0:T(8,128)(2,1)S(1)} %pad_maximum_fusion.2.refs_0_, bf16[64,9216]{1,0:T(8,128)(2,1)S(1)} %pad_maximum_fusion.1.refs_1_, bf16[64,9216]{1,0:T(8,128)(2,1)S(1)} %pad_maximum_fusion.3.refs_2_, ...), custom_call_target="tpu_custom_call" | custom-call | flops 1048576 | bytes 65536 | tf_op jit(solution)/shard_map/reduce/pallas_call | solution.py:59
  69.3 4.4 %collective-permute-start.19 = (f32[2,2,8,8,512]{4,3,2,1,0:T(8,128)S(1)}, f32[2,2,8,8,512]{4,3,2,1,0:T(8,128)S(1)}, u32[]{:S(2)}, u32[]{:S(2)}) collective-permute-start(f32[2,2,8,8,512]{4,3,2,1,0:T(8,128)S(1)} %get-tuple-element.56), channel_id=1, source_target_pairs={{0,1},{1,0},{2,3},{3,2},{4,5},{5,4},{6,7},{7,6},{8,9},{9,8},{10,11... | collective-permute-start | bytes 1572872 | tf_op jit(solution)/shard_map/reduce/ppermute | solution.py:146
  73.7 1.5 collective-permute-done.19
  75.2 9.7 %collective-permute-done.15.refs_0_ = bf16[64,9216]{1,0:T(8,128)(2,1)S(1)} collective-permute-done((bf16[64,9216]{1,0:T(8,128)(2,1)S(1)}, bf16[64,9216]{1,0:T(8,128)(2,1)S(1)}, u32[]{:S(2)}, u32[]{:S(2)}) %collective-permute-start.15) | collective-permute-done | bytes 1179680 | tf_op jit(solution)/shard_map/second_axis/ppermute | solution.py:21
  84.9 1.2 collective-permute-start.12
  86.1 1.0 collective-permute-done.17.refs_2_
  87.1 1.7 collective-permute-start.14
  88.8 4.5 %collective-permute-start.20 = (f32[2,8,8,512]{3,2,1,0:T(8,128)S(1)}, f32[2,8,8,512]{3,2,1,0:T(8,128)S(1)}, u32[]{:S(2)}, u32[]{:S(2)}) collective-permute-start(f32[2,8,8,512]{3,2,1,0:T(8,128)S(1)} %fusion.7), channel_id=1, source_target_pairs={{0,2},{2,0},{1,3},{3,1},{4,6},{6,4},{5,7},{7,5},{8,10},{10,8},{9,1... | collective-permute-start | bytes 786440 | tf_op jit(solution)/shard_map/reduce/ppermute | solution.py:143
  93.3 3.2 %reduce.9 = (f32[2,2,8,8,512]{4,3,2,1,0:T(8,128)S(1)}, f32[2,2,8,8,512]{4,3,2,1,0:T(8,128)S(1)}) custom-call(s32[3]{0:T(128)S(1)} %pad_add_fusion.place_ref, bf16[64,9216]{1,0:T(8,128)(2,1)S(1)} %collective-permute-done.15.refs_0_, bf16[64,9216]{1,0:T(8,128)(2,1)S(1)} %collective-permute-done.16.refs_1_, ...), custom_call_target="tpu_custom_call" | custom-call | flops 1048576 | bytes 65536 | tf_op jit(solution)/shard_map/reduce/pallas_call | solution.py:59
  96.6 1.5 collective-permute-done.20
  98.0 10.5 %collective-permute-start.25 = (f32[2,2,8,8,512]{4,3,2,1,0:T(8,128)S(1)}, f32[2,2,8,8,512]{4,3,2,1,0:T(8,128)S(1)}, u32[]{:S(2)}, u32[]{:S(2)}) collective-permute-start(f32[2,2,8,8,512]{4,3,2,1,0:T(8,128)S(1)} %get-tuple-element.65), channel_id=1, source_target_pairs={{0,1},{1,0},{2,3},{3,2},{4,5},{5,4},{6,7},{7,6},{8,9},{9,8},{10,11... | collective-permute-start | bytes 1572872 | tf_op jit(solution)/shard_map/reduce/ppermute | solution.py:146
  108.5 0.1 fusion.9
  108.6 1.6 collective-permute-done.11.refs_0_
  110.2 0.1 collective-permute-start.21
  110.3 2.7 %collective-permute-start.22 = (bf16[64,9216]{1,0:T(8,128)(2,1)S(1)}, bf16[64,9216]{1,0:T(8,128)(2,1)S(1)}, u32[]{:S(2)}, u32[]{:S(2)}) collective-permute-start(bf16[64,9216]{1,0:T(8,128)(2,1)S(1)} %collective-permute-done.12.refs_1_), channel_id=1, source_target_pairs={{0,12},{4,0},{8,4},{12,8},{1,13},{5,1},{9,5},{13,9},{2,14},{6,2},{... | collective-permute-start | bytes 3538952 | tf_op jit(solution)/shard_map/second_axis/ppermute | solution.py:21
  113.0 2.7 %collective-permute-start.24 = (bf16[64,9216]{1,0:T(8,128)(2,1)S(1)}, bf16[64,9216]{1,0:T(8,128)(2,1)S(1)}, u32[]{:S(2)}, u32[]{:S(2)}) collective-permute-start(bf16[64,9216]{1,0:T(8,128)(2,1)S(1)} %collective-permute-done.14.refs_3_), channel_id=1, source_target_pairs={{0,48},{16,0},{32,16},{48,32},{1,49},{17,1},{33,17},{49,33},{2,50}... | collective-permute-start | bytes 3538952 | tf_op jit(solution)/shard_map/second_axis/ppermute | solution.py:21
  115.6 3.2 %reduce.10 = (f32[2,2,8,8,512]{4,3,2,1,0:T(8,128)S(1)}, f32[2,2,8,8,512]{4,3,2,1,0:T(8,128)S(1)}) custom-call(s32[3]{0:T(128)S(1)} %pad_add_fusion.place_ref, bf16[64,9216]{1,0:T(8,128)(2,1)S(1)} %collective-permute-done.11.refs_0_, bf16[64,9216]{1,0:T(8,128)(2,1)S(1)} %collective-permute-done.12.refs_1_, ...), custom_call_target="tpu_custom_call" | custom-call | flops 1048576 | bytes 65536 | tf_op jit(solution)/shard_map/reduce/pallas_call | solution.py:59
  118.9 8.0 %collective-permute-start.27 = (f32[2,2,8,8,512]{4,3,2,1,0:T(8,128)S(1)}, f32[2,2,8,8,512]{4,3,2,1,0:T(8,128)S(1)}, u32[]{:S(2)}, u32[]{:S(2)}) collective-permute-start(f32[2,2,8,8,512]{4,3,2,1,0:T(8,128)S(1)} %get-tuple-element.69), channel_id=1, source_target_pairs={{0,1},{1,0},{2,3},{3,2},{4,5},{5,4},{6,7},{7,6},{8,9},{9,8},{10,11... | collective-permute-start | bytes 1572872 | tf_op jit(solution)/shard_map/reduce/ppermute | solution.py:146
  126.9 1.5 collective-permute-done.27
  128.4 4.8 %collective-permute-start.26 = (f32[2,8,8,512]{3,2,1,0:T(8,128)S(1)}, f32[2,8,8,512]{3,2,1,0:T(8,128)S(1)}, u32[]{:S(2)}, u32[]{:S(2)}) collective-permute-start(f32[2,8,8,512]{3,2,1,0:T(8,128)S(1)} %fusion.4), channel_id=1, source_target_pairs={{0,2},{2,0},{1,3},{3,1},{4,6},{6,4},{5,7},{7,5},{8,10},{10,8},{9,1... | collective-permute-start | bytes 786440 | tf_op jit(solution)/shard_map/reduce/ppermute | solution.py:143
  133.2 6.8 %collective-permute-done.26 = f32[2,8,8,512]{3,2,1,0:T(8,128)S(1)} collective-permute-done((f32[2,8,8,512]{3,2,1,0:T(8,128)S(1)}, f32[2,8,8,512]{3,2,1,0:T(8,128)S(1)}, u32[]{:S(2)}, u32[]{:S(2)}) %collective-permute-start.26) | collective-permute-done | bytes 262176 | tf_op jit(solution)/shard_map/reduce/ppermute | solution.py:143
  140.0 4.6 %collective-permute-start.29 = (f32[2,8,8,512]{3,2,1,0:T(8,128)S(1)}, f32[2,8,8,512]{3,2,1,0:T(8,128)S(1)}, u32[]{:S(2)}, u32[]{:S(2)}) collective-permute-start(f32[2,8,8,512]{3,2,1,0:T(8,128)S(1)} %fusion.3), channel_id=1, source_target_pairs={{0,2},{2,0},{1,3},{3,1},{4,6},{6,4},{5,7},{7,5},{8,10},{10,8},{9,1... | collective-permute-start | bytes 786440 | tf_op jit(solution)/shard_map/reduce/ppermute | solution.py:143
  144.6 0.1 fusion.6
  144.8 3.2 %reduce.11 = (f32[2,2,8,8,512]{4,3,2,1,0:T(8,128)S(1)}, f32[2,2,8,8,512]{4,3,2,1,0:T(8,128)S(1)}) custom-call(s32[3]{0:T(128)S(1)} %pad_add_fusion.place_ref, bf16[64,9216]{1,0:T(8,128)(2,1)S(1)} %collective-permute-done.21.refs_0_, bf16[64,9216]{1,0:T(8,128)(2,1)S(1)} %collective-permute-done.22.refs_1_, ...), custom_call_target="tpu_custom_call" | custom-call | flops 1048576 | bytes 65536 | tf_op jit(solution)/shard_map/reduce/pallas_call | solution.py:59
  148.0 1.7 collective-permute-start.28
  149.7 6.6 %collective-permute-done.29 = f32[2,8,8,512]{3,2,1,0:T(8,128)S(1)} collective-permute-done((f32[2,8,8,512]{3,2,1,0:T(8,128)S(1)}, f32[2,8,8,512]{3,2,1,0:T(8,128)S(1)}, u32[]{:S(2)}, u32[]{:S(2)}) %collective-permute-start.29) | collective-permute-done | bytes 262176 | tf_op jit(solution)/shard_map/reduce/ppermute | solution.py:143
  156.3 0.1 fusion.1
  156.4 0.1 collective-permute-start.30
  156.5 11.2 %collective-permute-done.30.back_ref = f32[2,8,8,512]{3,2,1,0:T(8,128)S(1)} collective-permute-done((f32[2,8,8,512]{3,2,1,0:T(8,128)S(1)}, f32[2,8,8,512]{3,2,1,0:T(8,128)S(1)}, u32[]{:S(2)}, u32[]{:S(2)}) %collective-permute-start.30) | collective-permute-done | bytes 262176 | tf_op jit(solution)/shard_map/reduce/ppermute | solution.py:143
  167.7 1.6 reduce.12
  (32 shorter events, 0.4 us)
Async XLA Ops:
  1.0 9.2 %collective-permute-start = (bf16[16,9216]{1,0:T(8,128)(2,1)S(1)}, bf16[16,9216]{1,0:T(8,128)(2,1)S(1)}, u32[]{:S(2)}, u32[]{:S(2)}) collective-permute-start(bf16[16,9216]{1,0:T(8,128)(2,1)S(1)} %get-tuple-element.82), channel_id=1, source_target_pairs={{0,64},{64,0},{128,192},{192,128},{1,65},{65,1},{129,193},{193,129... | collective-permute-start | bytes 884744 | tf_op jit(solution)/shard_map/z_shifts/ppermute | solution.py:26
  1.1 21.3 %collective-permute-start.1 = (bf16[16,9216]{1,0:T(8,128)(2,1)S(1)}, bf16[16,9216]{1,0:T(8,128)(2,1)S(1)}, u32[]{:S(2)}, u32[]{:S(2)}) collective-permute-start(bf16[16,9216]{1,0:T(8,128)(2,1)S(1)} %get-tuple-element.82), channel_id=1, source_target_pairs={{0,128},{64,192},{128,0},{192,64},{1,129},{65,193},{129,1},{193,65... | collective-permute-start | bytes 884744 | tf_op jit(solution)/shard_map/z_shifts/ppermute | solution.py:26
  4.2 25.6 %collective-permute-start.2 = (bf16[16,9216]{1,0:T(8,128)(2,1)S(1)}, bf16[16,9216]{1,0:T(8,128)(2,1)S(1)}, u32[]{:S(2)}, u32[]{:S(2)}) collective-permute-start(bf16[16,9216]{1,0:T(8,128)(2,1)S(1)} %get-tuple-element.82), channel_id=1, source_target_pairs={{0,192},{64,128},{128,64},{192,0},{1,193},{65,129},{129,65},{193,1... | collective-permute-start | bytes 884744 | tf_op jit(solution)/shard_map/z_shifts/ppermute | solution.py:26
  30.0 36.0 %slice-start = ((s8[7340032]{0:T(1024)(128)(4,1)}), s8[3145728]{0:T(1024)(128)(4,1)S(1)}, s32[]{:S(2)}) async-start(s8[7340032]{0:T(1024)(128)(4,1)} %bitcast.34), calls=%async_computation | async-start | bytes 6291456
  31.1 13.9 %collective-permute-start.8 = (bf16[32,9216]{1,0:T(8,128)(2,1)}, bf16[32,9216]{1,0:T(8,128)(2,1)}, u32[]{:S(2)}, u32[]{:S(2)}) collective-permute-start(bf16[32,9216]{1,0:T(8,128)(2,1)} %get-tuple-element.79), channel_id=1, source_target_pairs={{0,12},{4,0},{8,4},{12,8},{1,13},{5,1},{9,5},{13,9},{2,14},{6,2},{... | collective-permute-start | bytes 1769480 | tf_op jit(solution)/shard_map/first_axis/ppermute | solution.py:21
  33.6 15.9 %collective-permute-start.7 = (bf16[32,9216]{1,0:T(8,128)(2,1)}, bf16[32,9216]{1,0:T(8,128)(2,1)}, u32[]{:S(2)}, u32[]{:S(2)}) collective-permute-start(bf16[32,9216]{1,0:T(8,128)(2,1)} %get-tuple-element.79), channel_id=1, source_target_pairs={{0,4},{4,8},{8,12},{12,0},{1,5},{5,9},{9,13},{13,1},{2,6},{6,10},{... | collective-permute-start | bytes 1769480 | tf_op jit(solution)/shard_map/first_axis/ppermute | solution.py:21
  33.6 17.0 %collective-permute-start.4 = (bf16[32,9216]{1,0:T(8,128)(2,1)}, bf16[32,9216]{1,0:T(8,128)(2,1)}, u32[]{:S(2)}, u32[]{:S(2)}) collective-permute-start(bf16[32,9216]{1,0:T(8,128)(2,1)} %get-tuple-element.80), channel_id=1, source_target_pairs={{0,16},{16,32},{32,48},{48,0},{1,17},{17,33},{33,49},{49,1},{2,18}... | collective-permute-start | bytes 1769480 | tf_op jit(solution)/shard_map/first_axis/ppermute | solution.py:21
  34.9 18.1 %collective-permute-start.3 = (bf16[32,9216]{1,0:T(8,128)(2,1)}, bf16[32,9216]{1,0:T(8,128)(2,1)}, u32[]{:S(2)}, u32[]{:S(2)}) collective-permute-start(bf16[32,9216]{1,0:T(8,128)(2,1)} %get-tuple-element.80), channel_id=1, source_target_pairs={{0,48},{16,0},{32,16},{48,32},{1,49},{17,1},{33,17},{49,33},{2,50}... | collective-permute-start | bytes 1769480 | tf_op jit(solution)/shard_map/first_axis/ppermute | solution.py:21
  46.0 12.1 %collective-permute-start.10 = (bf16[16,9216]{1,0:T(8,128)(2,1)S(1)}, bf16[16,9216]{1,0:T(8,128)(2,1)S(1)}, u32[]{:S(2)}, u32[]{:S(2)}) collective-permute-start(bf16[16,9216]{1,0:T(8,128)(2,1)S(1)} %slice.109), channel_id=1, source_target_pairs={{0,12},{4,0},{8,4},{12,8},{1,13},{5,1},{9,5},{13,9},{2,14},{6,2},{... | collective-permute-start | bytes 884744 | tf_op jit(solution)/shard_map/first_axis/ppermute | solution.py:21
  50.5 7.7 %collective-permute-start.9 = (bf16[16,9216]{1,0:T(8,128)(2,1)S(1)}, bf16[16,9216]{1,0:T(8,128)(2,1)S(1)}, u32[]{:S(2)}, u32[]{:S(2)}) collective-permute-start(bf16[16,9216]{1,0:T(8,128)(2,1)S(1)} %slice.108), channel_id=1, source_target_pairs={{0,4},{4,8},{8,12},{12,0},{1,5},{5,9},{9,13},{13,1},{2,6},{6,10},{... | collective-permute-start | bytes 884744 | tf_op jit(solution)/shard_map/first_axis/ppermute | solution.py:21
  51.6 11.0 %collective-permute-start.5 = (bf16[16,9216]{1,0:T(8,128)(2,1)S(1)}, bf16[16,9216]{1,0:T(8,128)(2,1)S(1)}, u32[]{:S(2)}, u32[]{:S(2)}) collective-permute-start(bf16[16,9216]{1,0:T(8,128)(2,1)S(1)} %slice.105), channel_id=1, source_target_pairs={{0,16},{16,32},{32,48},{48,0},{1,17},{17,33},{33,49},{49,1},{2,18}... | collective-permute-start | bytes 884744 | tf_op jit(solution)/shard_map/first_axis/ppermute | solution.py:21
  54.0 12.0 %slice-start.1 = ((s8[7340032]{0:T(1024)(128)(4,1)}), s8[4194304]{0:T(1024)(128)(4,1)S(1)}, s32[]{:S(2)}) async-start(s8[7340032]{0:T(1024)(128)(4,1)} %bitcast.34), calls=%async_computation.1 | async-start | bytes 8388608
  54.0 10.9 %collective-permute-start.6 = (bf16[16,9216]{1,0:T(8,128)(2,1)S(1)}, bf16[16,9216]{1,0:T(8,128)(2,1)S(1)}, u32[]{:S(2)}, u32[]{:S(2)}) collective-permute-start(bf16[16,9216]{1,0:T(8,128)(2,1)S(1)} %slice.106), channel_id=1, source_target_pairs={{0,48},{16,0},{32,16},{48,32},{1,49},{17,1},{33,17},{49,33},{2,50}... | collective-permute-start | bytes 884744 | tf_op jit(solution)/shard_map/first_axis/ppermute | solution.py:21
  59.3 6.7 %copy-start = (bf16[512,2048]{1,0:T(8,128)(2,1)S(1)}, bf16[512,2048]{1,0:T(8,128)(2,1)}, u32[]{:S(2)}) copy-start(bf16[512,2048]{1,0:T(8,128)(2,1)} %refs_5_.7) | copy-start | bytes 6291460
  59.3 25.6 %collective-permute-start.15 = (bf16[64,9216]{1,0:T(8,128)(2,1)S(1)}, bf16[64,9216]{1,0:T(8,128)(2,1)S(1)}, u32[]{:S(2)}, u32[]{:S(2)}) collective-permute-start(bf16[64,9216]{1,0:T(8,128)(2,1)S(1)} %pad_maximum_fusion.2.refs_0_), channel_id=1, source_target_pairs={{0,4},{4,8},{8,12},{12,0},{1,5},{5,9},{9,13},{13,1},{2,6},{6,10},{... | collective-permute-start | bytes 3538952 | tf_op jit(solution)/shard_map/second_axis/ppermute | solution.py:21
  59.4 26.6 %collective-permute-start.16 = (bf16[64,9216]{1,0:T(8,128)(2,1)S(1)}, bf16[64,9216]{1,0:T(8,128)(2,1)S(1)}, u32[]{:S(2)}, u32[]{:S(2)}) collective-permute-start(bf16[64,9216]{1,0:T(8,128)(2,1)S(1)} %pad_maximum_fusion.2.refs_0_), channel_id=1, source_target_pairs={{0,12},{4,0},{8,4},{12,8},{1,13},{5,1},{9,5},{13,9},{2,14},{6,2},{... | collective-permute-start | bytes 3538952 | tf_op jit(solution)/shard_map/second_axis/ppermute | solution.py:21
  62.2 24.9 %collective-permute-start.17 = (bf16[64,9216]{1,0:T(8,128)(2,1)S(1)}, bf16[64,9216]{1,0:T(8,128)(2,1)S(1)}, u32[]{:S(2)}, u32[]{:S(2)}) collective-permute-start(bf16[64,9216]{1,0:T(8,128)(2,1)S(1)} %pad_maximum_fusion.3.refs_2_), channel_id=1, source_target_pairs={{0,16},{16,32},{32,48},{48,0},{1,17},{17,33},{33,49},{49,1},{2,18}... | collective-permute-start | bytes 3538952 | tf_op jit(solution)/shard_map/second_axis/ppermute | solution.py:21
  62.6 26.2 %collective-permute-start.18 = (bf16[64,9216]{1,0:T(8,128)(2,1)S(1)}, bf16[64,9216]{1,0:T(8,128)(2,1)S(1)}, u32[]{:S(2)}, u32[]{:S(2)}) collective-permute-start(bf16[64,9216]{1,0:T(8,128)(2,1)S(1)} %pad_maximum_fusion.3.refs_2_), channel_id=1, source_target_pairs={{0,48},{16,0},{32,16},{48,32},{1,49},{17,1},{33,17},{49,33},{2,50}... | collective-permute-start | bytes 3538952 | tf_op jit(solution)/shard_map/second_axis/ppermute | solution.py:21
  69.3 5.9 %collective-permute-start.19 = (f32[2,2,8,8,512]{4,3,2,1,0:T(8,128)S(1)}, f32[2,2,8,8,512]{4,3,2,1,0:T(8,128)S(1)}, u32[]{:S(2)}, u32[]{:S(2)}) collective-permute-start(f32[2,2,8,8,512]{4,3,2,1,0:T(8,128)S(1)} %get-tuple-element.56), channel_id=1, source_target_pairs={{0,1},{1,0},{2,3},{3,2},{4,5},{5,4},{6,7},{7,6},{8,9},{9,8},{10,11... | collective-permute-start | bytes 1572872 | tf_op jit(solution)/shard_map/reduce/ppermute | solution.py:146
  75.2 35.0 %collective-permute-start.11 = (bf16[64,9216]{1,0:T(8,128)(2,1)S(1)}, bf16[64,9216]{1,0:T(8,128)(2,1)S(1)}, u32[]{:S(2)}, u32[]{:S(2)}) collective-permute-start(bf16[64,9216]{1,0:T(8,128)(2,1)S(1)} %pad_maximum_fusion.1.refs_1_), channel_id=1, source_target_pairs={{0,4},{4,8},{8,12},{12,0},{1,5},{5,9},{9,13},{13,1},{2,6},{6,10},{... | collective-permute-start | bytes 3538952 | tf_op jit(solution)/shard_map/second_axis/ppermute | solution.py:21
  84.9 25.3 %collective-permute-start.12 = (bf16[64,9216]{1,0:T(8,128)(2,1)S(1)}, bf16[64,9216]{1,0:T(8,128)(2,1)S(1)}, u32[]{:S(2)}, u32[]{:S(2)}) collective-permute-start(bf16[64,9216]{1,0:T(8,128)(2,1)S(1)} %pad_maximum_fusion.1.refs_1_), channel_id=1, source_target_pairs={{0,12},{4,0},{8,4},{12,8},{1,13},{5,1},{9,5},{13,9},{2,14},{6,2},{... | collective-permute-start | bytes 3538952 | tf_op jit(solution)/shard_map/second_axis/ppermute | solution.py:21
  86.1 24.1 %collective-permute-start.13 = (bf16[64,9216]{1,0:T(8,128)(2,1)S(1)}, bf16[64,9216]{1,0:T(8,128)(2,1)S(1)}, u32[]{:S(2)}, u32[]{:S(2)}) collective-permute-start(bf16[64,9216]{1,0:T(8,128)(2,1)S(1)} %pad_maximum_fusion.4.refs_3_), channel_id=1, source_target_pairs={{0,16},{16,32},{32,48},{48,0},{1,17},{17,33},{33,49},{49,1},{2,18}... | collective-permute-start | bytes 3538952 | tf_op jit(solution)/shard_map/second_axis/ppermute | solution.py:21
  87.1 23.1 %collective-permute-start.14 = (bf16[64,9216]{1,0:T(8,128)(2,1)S(1)}, bf16[64,9216]{1,0:T(8,128)(2,1)S(1)}, u32[]{:S(2)}, u32[]{:S(2)}) collective-permute-start(bf16[64,9216]{1,0:T(8,128)(2,1)S(1)} %pad_maximum_fusion.4.refs_3_), channel_id=1, source_target_pairs={{0,48},{16,0},{32,16},{48,32},{1,49},{17,1},{33,17},{49,33},{2,50}... | collective-permute-start | bytes 3538952 | tf_op jit(solution)/shard_map/second_axis/ppermute | solution.py:21
  88.8 9.2 %collective-permute-start.20 = (f32[2,8,8,512]{3,2,1,0:T(8,128)S(1)}, f32[2,8,8,512]{3,2,1,0:T(8,128)S(1)}, u32[]{:S(2)}, u32[]{:S(2)}) collective-permute-start(f32[2,8,8,512]{3,2,1,0:T(8,128)S(1)} %fusion.7), channel_id=1, source_target_pairs={{0,2},{2,0},{1,3},{3,1},{4,6},{6,4},{5,7},{7,5},{8,10},{10,8},{9,1... | collective-permute-start | bytes 786440 | tf_op jit(solution)/shard_map/reduce/ppermute | solution.py:143
  98.0 20.8 %collective-permute-start.25 = (f32[2,2,8,8,512]{4,3,2,1,0:T(8,128)S(1)}, f32[2,2,8,8,512]{4,3,2,1,0:T(8,128)S(1)}, u32[]{:S(2)}, u32[]{:S(2)}) collective-permute-start(f32[2,2,8,8,512]{4,3,2,1,0:T(8,128)S(1)} %get-tuple-element.65), channel_id=1, source_target_pairs={{0,1},{1,0},{2,3},{3,2},{4,5},{5,4},{6,7},{7,6},{8,9},{9,8},{10,11... | collective-permute-start | bytes 1572872 | tf_op jit(solution)/shard_map/reduce/ppermute | solution.py:146
  110.2 34.5 %collective-permute-start.21 = (bf16[64,9216]{1,0:T(8,128)(2,1)S(1)}, bf16[64,9216]{1,0:T(8,128)(2,1)S(1)}, u32[]{:S(2)}, u32[]{:S(2)}) collective-permute-start(bf16[64,9216]{1,0:T(8,128)(2,1)S(1)} %collective-permute-done.15.refs_0_), channel_id=1, source_target_pairs={{0,4},{4,8},{8,12},{12,0},{1,5},{5,9},{9,13},{13,1},{2,6},{6,10},{... | collective-permute-start | bytes 3538952 | tf_op jit(solution)/shard_map/second_axis/ppermute | solution.py:21
  110.3 34.4 %collective-permute-start.22 = (bf16[64,9216]{1,0:T(8,128)(2,1)S(1)}, bf16[64,9216]{1,0:T(8,128)(2,1)S(1)}, u32[]{:S(2)}, u32[]{:S(2)}) collective-permute-start(bf16[64,9216]{1,0:T(8,128)(2,1)S(1)} %collective-permute-done.12.refs_1_), channel_id=1, source_target_pairs={{0,12},{4,0},{8,4},{12,8},{1,13},{5,1},{9,5},{13,9},{2,14},{6,2},{... | collective-permute-start | bytes 3538952 | tf_op jit(solution)/shard_map/second_axis/ppermute | solution.py:21
  112.9 31.8 %collective-permute-start.23 = (bf16[64,9216]{1,0:T(8,128)(2,1)S(1)}, bf16[64,9216]{1,0:T(8,128)(2,1)S(1)}, u32[]{:S(2)}, u32[]{:S(2)}) collective-permute-start(bf16[64,9216]{1,0:T(8,128)(2,1)S(1)} %collective-permute-done.17.refs_2_), channel_id=1, source_target_pairs={{0,16},{16,32},{32,48},{48,0},{1,17},{17,33},{33,49},{49,1},{2,18}... | collective-permute-start | bytes 3538952 | tf_op jit(solution)/shard_map/second_axis/ppermute | solution.py:21
  113.0 31.8 %collective-permute-start.24 = (bf16[64,9216]{1,0:T(8,128)(2,1)S(1)}, bf16[64,9216]{1,0:T(8,128)(2,1)S(1)}, u32[]{:S(2)}, u32[]{:S(2)}) collective-permute-start(bf16[64,9216]{1,0:T(8,128)(2,1)S(1)} %collective-permute-done.14.refs_3_), channel_id=1, source_target_pairs={{0,48},{16,0},{32,16},{48,32},{1,49},{17,1},{33,17},{49,33},{2,50}... | collective-permute-start | bytes 3538952 | tf_op jit(solution)/shard_map/second_axis/ppermute | solution.py:21
  118.9 9.5 %collective-permute-start.27 = (f32[2,2,8,8,512]{4,3,2,1,0:T(8,128)S(1)}, f32[2,2,8,8,512]{4,3,2,1,0:T(8,128)S(1)}, u32[]{:S(2)}, u32[]{:S(2)}) collective-permute-start(f32[2,2,8,8,512]{4,3,2,1,0:T(8,128)S(1)} %get-tuple-element.69), channel_id=1, source_target_pairs={{0,1},{1,0},{2,3},{3,2},{4,5},{5,4},{6,7},{7,6},{8,9},{9,8},{10,11... | collective-permute-start | bytes 1572872 | tf_op jit(solution)/shard_map/reduce/ppermute | solution.py:146
  128.4 11.6 %collective-permute-start.26 = (f32[2,8,8,512]{3,2,1,0:T(8,128)S(1)}, f32[2,8,8,512]{3,2,1,0:T(8,128)S(1)}, u32[]{:S(2)}, u32[]{:S(2)}) collective-permute-start(f32[2,8,8,512]{3,2,1,0:T(8,128)S(1)} %fusion.4), channel_id=1, source_target_pairs={{0,2},{2,0},{1,3},{3,1},{4,6},{6,4},{5,7},{7,5},{8,10},{10,8},{9,1... | collective-permute-start | bytes 786440 | tf_op jit(solution)/shard_map/reduce/ppermute | solution.py:143
  140.0 16.3 %collective-permute-start.29 = (f32[2,8,8,512]{3,2,1,0:T(8,128)S(1)}, f32[2,8,8,512]{3,2,1,0:T(8,128)S(1)}, u32[]{:S(2)}, u32[]{:S(2)}) collective-permute-start(f32[2,8,8,512]{3,2,1,0:T(8,128)S(1)} %fusion.3), channel_id=1, source_target_pairs={{0,2},{2,0},{1,3},{3,1},{4,6},{6,4},{5,7},{7,5},{8,10},{10,8},{9,1... | collective-permute-start | bytes 786440 | tf_op jit(solution)/shard_map/reduce/ppermute | solution.py:143
  148.0 8.4 %collective-permute-start.28 = (f32[2,2,8,8,512]{4,3,2,1,0:T(8,128)S(1)}, f32[2,2,8,8,512]{4,3,2,1,0:T(8,128)S(1)}, u32[]{:S(2)}, u32[]{:S(2)}) collective-permute-start(f32[2,2,8,8,512]{4,3,2,1,0:T(8,128)S(1)} %get-tuple-element.76), channel_id=1, source_target_pairs={{0,1},{1,0},{2,3},{3,2},{4,5},{5,4},{6,7},{7,6},{8,9},{9,8},{10,11... | collective-permute-start | bytes 1572872 | tf_op jit(solution)/shard_map/reduce/ppermute | solution.py:146
  156.4 11.3 %collective-permute-start.30 = (f32[2,8,8,512]{3,2,1,0:T(8,128)S(1)}, f32[2,8,8,512]{3,2,1,0:T(8,128)S(1)}, u32[]{:S(2)}, u32[]{:S(2)}) collective-permute-start(f32[2,8,8,512]{3,2,1,0:T(8,128)S(1)} %fusion.2), channel_id=1, source_target_pairs={{0,2},{2,0},{1,3},{3,1},{4,6},{6,4},{5,7},{7,5},{8,10},{10,8},{9,1... | collective-permute-start | bytes 786440 | tf_op jit(solution)/shard_map/reduce/ppermute | solution.py:143

commit v10 on v9

--- a/solution.py
+++ b/solution.py
@@ -133,8 +133,7 @@
         block = rows.reshape(GROUPS * RANK, features)
         half = block.shape[0] // 2
         before, after = ring(block, axis, 1), ring(block, axis, -1)
-        far = ring(before[:half], axis, 1), ring(after[half:], axis, -1)
-        return jnp.concatenate([block, before]), jnp.concatenate([after, *far])
+        return jnp.concatenate([block, before]), after, before[:half], after[half:]
 
     def both(block, axis):
         return ring(block, axis, 1), ring(block, axis, -1)
@@ -153,9 +152,11 @@
         keep, send = project(blocks, train_grads, train_acts, place)
         return keep, over(send)
     with jax.named_scope("first_axis"):
-        lo_a, hi_a = first(stacked[:, :RANK], "y")
-        lo_b, hi_b = first(stacked[:, RANK:], "x")
-        lo_a, lo_b, hi_b = lax.optimization_barrier((lo_a, lo_b, hi_b))
+        (lo_a, after_a, up_a, down_a), (lo_b, after_b, up_b, down_b) = lax.optimization_barrier(
+            (first(stacked[:, :RANK], "y"), first(stacked[:, RANK:], "x"))
+        )
+        hi_a = jnp.concatenate([after_a, ring(up_a, "y", 1), ring(down_a, "y", -1)])
+        hi_b = jnp.concatenate([after_b, ring(up_b, "x", 1), ring(down_b, "x", -1)])
         hi_a, hi_b = lax.optimization_barrier((hi_a, hi_b))
     with jax.named_scope("second_axis"):
         lo = both(lo_a, "x") + both(lo_b, "y")

time: 170 us -> 168 us (0.988)
  waiting for transfers between devices: 75.4 us -> 68 us
  starting transfers between devices: 67.3 us -> 72.4 us
    ppermute x4, waiting for transfers between devices: 26 us -> 15.4 us  [exchange(): return lax.ppermute(sent, 'zh', [(0, 1), (1, 0)])]
    ppermute x4, starting transfers between devices: 14 us -> 19.1 us  [exchange(): return lax.ppermute(sent, 'zh', [(0, 1), (1, 0)])]
    unnamed x6 -> x16, local copies, waits for them, and re-layouts: 0.02 us -> 3.28 us
    ppermute x4, starting transfers between devices: 24.5 us -> 27.3 us  [over(): return lax.ppermute(send, 'core', [(0, 1), (1, 0)])]
    ppermute x20, starting transfers between devices: 25.4 us -> 22.7 us  [ring(): return lax.ppermute(x, axis, [(i, (i + step) % n) for i in range(n)])]
    ppermute x20, waiting for transfers between devices: 20.9 us -> 23.7 us  [ring(): return lax.ppermute(x, axis, [(i, (i + step) % n) for i in range(n)])]
  transfers between devices with their start and end apart: 31 -> 31, of which waited for: 13 -> 21; matrix products, arithmetic and copies ran while one was open for 6% -> 4% of each run, Pallas kernels for 8% -> 8%
where the time goes in v10:
time: 168 us
  starting transfers between devices  72.4 us (43%)
  waiting for transfers between devices  68 us (40%)
  Pallas kernels  14.5 us (9%)
  other arithmetic  6.4 us (4%)
  local copies, waits for them, and re-layouts  6.37 us (4%)
    ppermute x4, starting transfers between devices, over(): return lax.ppermute(send, 'core', [(0, 1), (1, 0)])  27.3 us
    ppermute x3, waiting for transfers between devices, flip(): return lax.ppermute(x, axis, [(i, i ^ mask) for i in range(n)])  25.5 us
    ppermute x20, waiting for transfers between devices, ring(): return lax.ppermute(x, axis, [(i, (i + step) % n) for i in range(n)])  23.7 us
    ppermute x20, starting transfers between devices, ring(): return lax.ppermute(x, axis, [(i, (i + step) % n) for i in range(n)])  22.7 us
    ppermute x4, starting transfers between devices, exchange(): return lax.ppermute(sent, 'zh', [(0, 1), (1, 0)])  19.1 us
    ppermute x4, waiting for transfers between devices, exchange(): return lax.ppermute(sent, 'zh', [(0, 1), (1, 0)])  15.4 us
    pallas_call x4, Pallas kernels, project(): pl.pallas_call(functools.partial(project_kernel, len(blocks)), out_shape=...  12.9 us
    ppermute x4, waiting for transfers between devices, over(): return lax.ppermute(send, 'core', [(0, 1), (1, 0)])  3.43 us
  transfers between devices with their start and end apart: 31, of which 21 were waited for; matrix products, arithmetic and copies ran while one was open for 4% of the time, Pallas kernels for 8%

profile of v10, /device:TPU:33, one launch (start us, length us, event | category | flops | bytes accessed | tf_op | source)
XLA Modules:
  0.0 167.9 jit_solution(14670817968334383464)
XLA Ops:
  0.0 1.0 fusion.13
  1.1 3.1 %collective-permute-start.1 = (bf16[16,9216]{1,0:T(8,128)(2,1)S(1)}, bf16[16,9216]{1,0:T(8,128)(2,1)S(1)}, u32[]{:S(2)}, u32[]{:S(2)}) collective-permute-start(bf16[16,9216]{1,0:T(8,128)(2,1)S(1)} %get-tuple-element.92), channel_id=1, source_target_pairs={{0,128},{64,192},{128,0},{192,64},{1,129},{65,193},{129,1},{193,65... | collective-permute-start | bytes 884744 | tf_op jit(solution)/shard_map/z_shifts/ppermute | solution.py:26
  4.2 0.2 collective-permute-start.2
  4.4 5.9 %collective-permute-done = bf16[16,9216]{1,0:T(8,128)(2,1)S(1)} collective-permute-done((bf16[16,9216]{1,0:T(8,128)(2,1)S(1)}, bf16[16,9216]{1,0:T(8,128)(2,1)S(1)}, u32[]{:S(2)}, u32[]{:S(2)}) %collective-permute-start) | collective-permute-done | bytes 294944 | tf_op jit(solution)/shard_map/z_shifts/ppermute | solution.py:26
  10.2 12.2 %collective-permute-done.1 = bf16[16,9216]{1,0:T(8,128)(2,1)S(1)} collective-permute-done((bf16[16,9216]{1,0:T(8,128)(2,1)S(1)}, bf16[16,9216]{1,0:T(8,128)(2,1)S(1)}, u32[]{:S(2)}, u32[]{:S(2)}) %collective-permute-start.1) | collective-permute-done | bytes 294944 | tf_op jit(solution)/shard_map/z_shifts/ppermute | solution.py:26
  22.5 7.4 %collective-permute-done.2 = bf16[16,9216]{1,0:T(8,128)(2,1)S(1)} collective-permute-done((bf16[16,9216]{1,0:T(8,128)(2,1)S(1)}, bf16[16,9216]{1,0:T(8,128)(2,1)S(1)}, u32[]{:S(2)}, u32[]{:S(2)}) %collective-permute-start.2) | collective-permute-done | bytes 294944 | tf_op jit(solution)/shard_map/z_shifts/ppermute | solution.py:26
  30.1 1.4 collective-permute-start.3
  31.5 1.2 collective-permute-start.5
  32.7 1.5 collective-permute-start.4
  34.2 1.5 collective-permute-start.6
  35.7 9.2 %collective-permute-done.3 = bf16[32,9216]{1,0:T(8,128)(2,1)S(1)} collective-permute-done((bf16[32,9216]{1,0:T(8,128)(2,1)S(1)}, bf16[32,9216]{1,0:T(8,128)(2,1)S(1)}, u32[]{:S(2)}, u32[]{:S(2)}) %collective-permute-start.3) | collective-permute-done | bytes 589856 | tf_op jit(solution)/shard_map/first_axis/ppermute | solution.py:21
  44.8 0.7 slice.105
  45.7 0.7 slice.108
  46.5 1.1 pad_maximum_fusion.2.refs_2_
  47.6 0.8 slice.106
  48.4 1.1 pad_maximum_fusion.1.refs_0_
  49.5 0.8 slice.109
  50.2 0.2 copy-done.5
  50.4 2.3 %collective-permute-start.10 = (bf16[16,9216]{1,0:T(8,128)(2,1)}, bf16[16,9216]{1,0:T(8,128)(2,1)S(1)}, u32[]{:S(2)}, u32[]{:S(2)}) collective-permute-start(bf16[16,9216]{1,0:T(8,128)(2,1)} %slice.109), channel_id=1, source_target_pairs={{0,12},{4,0},{8,4},{12,8},{1,13},{5,1},{9,5},{13,9},{2,14},{6,2},{... | collective-permute-start | bytes 884744 | tf_op jit(solution)/shard_map/first_axis/ppermute | solution.py:21
  52.8 0.2 collective-permute-start.15
  53.0 2.6 %collective-permute-start.16 = (bf16[64,9216]{1,0:T(8,128)(2,1)}, bf16[64,9216]{1,0:T(8,128)(2,1)S(1)}, u32[]{:S(2)}, u32[]{:S(2)}) collective-permute-start(bf16[64,9216]{1,0:T(8,128)(2,1)} %pad_maximum_fusion.1.refs_0_), channel_id=1, source_target_pairs={{0,12},{4,0},{8,4},{12,8},{1,13},{5,1},{9,5},{13,9},{2,14},{6,2},{... | collective-permute-start | bytes 3538952 | tf_op jit(solution)/shard_map/second_axis/ppermute | solution.py:21
  55.6 0.4 collective-permute-start.7
  55.9 1.0 collective-permute-done.10
  57.0 1.3 collective-permute-start.8
  58.3 1.5 collective-permute-done.9
  59.8 0.2 collective-permute-start.17
  60.1 1.3 pad_maximum_fusion.4.refs_3_
  61.4 1.6 collective-permute-done.7
  63.0 1.1 collective-permute-start.18
  64.1 1.1 pad_maximum_fusion.3.refs_1_
  65.3 3.1 %copy-done = bf16[512,7168]{1,0:T(8,128)(2,1)S(1)} copy-done((bf16[512,7168]{1,0:T(8,128)(2,1)S(1)}, bf16[512,7168]{1,0:T(8,128)(2,1)}, u32[]{:S(2)}) %copy-start) | copy-done | bytes 7340056
  68.4 3.2 %reduce.8 = (f32[2,2,8,8,512]{4,3,2,1,0:T(8,128)S(1)}, f32[2,2,8,8,512]{4,3,2,1,0:T(8,128)S(1)}) custom-call(s32[3]{0:T(128)S(1)} %pad_add_fusion.place_ref, bf16[64,9216]{1,0:T(8,128)(2,1)S(1)} %copy-done.3, bf16[64,9216]{1,0:T(8,128)(2,1)S(1)} %pad_maximum_fusion.3.refs_1_, bf16[64,9216]{1,0:T(8,128)(2,1)S(1)} %copy-done.2, ...), custom_call_target="tpu_custom_call" | custom-call | flops 1048576 | bytes 65536 | tf_op jit(solution)/shard_map/reduce/pallas_call | solution.py:59
  71.6 9.3 %collective-permute-start.19 = (f32[2,2,8,8,512]{4,3,2,1,0:T(8,128)S(1)}, f32[2,2,8,8,512]{4,3,2,1,0:T(8,128)S(1)}, u32[]{:S(2)}, u32[]{:S(2)}) collective-permute-start(f32[2,2,8,8,512]{4,3,2,1,0:T(8,128)S(1)} %get-tuple-element.66), channel_id=1, source_target_pairs={{0,1},{1,0},{2,3},{3,2},{4,5},{5,4},{6,7},{7,6},{8,9},{9,8},{10,11... | collective-permute-start | bytes 1572872 | tf_op jit(solution)/shard_map/reduce/ppermute | solution.py:145
  80.9 1.5 collective-permute-done.19
  82.5 0.7 collective-permute-start.11
  83.2 2.1 %collective-permute-done.15.refs_0_ = bf16[64,9216]{1,0:T(8,128)(2,1)S(1)} collective-permute-done((bf16[64,9216]{1,0:T(8,128)(2,1)}, bf16[64,9216]{1,0:T(8,128)(2,1)S(1)}, u32[]{:S(2)}, u32[]{:S(2)}) %collective-permute-start.15) | collective-permute-done | bytes 1179680 | tf_op jit(solution)/shard_map/second_axis/ppermute | solution.py:21
  85.3 0.4 collective-permute-start.12
  85.7 0.8 collective-permute-start.13
  86.5 0.4 collective-permute-done.17.refs_2_
  86.9 1.6 collective-permute-start.14
  88.5 1.5 collective-permute-done.18.refs_3_
  90.0 4.3 %collective-permute-start.20 = (f32[2,8,8,512]{3,2,1,0:T(8,128)S(1)}, f32[2,8,8,512]{3,2,1,0:T(8,128)S(1)}, u32[]{:S(2)}, u32[]{:S(2)}) collective-permute-start(f32[2,8,8,512]{3,2,1,0:T(8,128)S(1)} %fusion.7), channel_id=1, source_target_pairs={{0,2},{2,0},{1,3},{3,1},{4,6},{6,4},{5,7},{7,5},{8,10},{10,8},{9,1... | collective-permute-start | bytes 786440 | tf_op jit(solution)/shard_map/reduce/ppermute | solution.py:142
  94.3 3.2 %reduce.9 = (f32[2,2,8,8,512]{4,3,2,1,0:T(8,128)S(1)}, f32[2,2,8,8,512]{4,3,2,1,0:T(8,128)S(1)}) custom-call(s32[3]{0:T(128)S(1)} %pad_add_fusion.place_ref, bf16[64,9216]{1,0:T(8,128)(2,1)S(1)} %collective-permute-done.15.refs_0_, bf16[64,9216]{1,0:T(8,128)(2,1)S(1)} %collective-permute-done.16.refs_1_, ...), custom_call_target="tpu_custom_call" | custom-call | flops 1048576 | bytes 65536 | tf_op jit(solution)/shard_map/reduce/pallas_call | solution.py:59
  97.6 1.7 %collective-permute-done.20 = f32[2,8,8,512]{3,2,1,0:T(8,128)S(1)} collective-permute-done((f32[2,8,8,512]{3,2,1,0:T(8,128)S(1)}, f32[2,8,8,512]{3,2,1,0:T(8,128)S(1)}, u32[]{:S(2)}, u32[]{:S(2)}) %collective-permute-start.20) | collective-permute-done | bytes 262176 | tf_op jit(solution)/shard_map/reduce/ppermute | solution.py:142
  99.3 9.6 %collective-permute-start.25 = (f32[2,2,8,8,512]{4,3,2,1,0:T(8,128)S(1)}, f32[2,2,8,8,512]{4,3,2,1,0:T(8,128)S(1)}, u32[]{:S(2)}, u32[]{:S(2)}) collective-permute-start(f32[2,2,8,8,512]{4,3,2,1,0:T(8,128)S(1)} %get-tuple-element.75), channel_id=1, source_target_pairs={{0,1},{1,0},{2,3},{3,2},{4,5},{5,4},{6,7},{7,6},{8,9},{9,8},{10,11... | collective-permute-start | bytes 1572872 | tf_op jit(solution)/shard_map/reduce/ppermute | solution.py:145
  109.0 3.3 %collective-permute-done.11.refs_0_ = bf16[64,9216]{1,0:T(8,128)(2,1)S(1)} collective-permute-done((bf16[64,9216]{1,0:T(8,128)(2,1)S(1)}, bf16[64,9216]{1,0:T(8,128)(2,1)S(1)}, u32[]{:S(2)}, u32[]{:S(2)}) %collective-permute-start.11) | collective-permute-done | bytes 1179680 | tf_op jit(solution)/shard_map/second_axis/ppermute | solution.py:21
  112.3 1.9 %collective-permute-done.13.refs_2_ = bf16[64,9216]{1,0:T(8,128)(2,1)S(1)} collective-permute-done((bf16[64,9216]{1,0:T(8,128)(2,1)S(1)}, bf16[64,9216]{1,0:T(8,128)(2,1)S(1)}, u32[]{:S(2)}, u32[]{:S(2)}) %collective-permute-start.13) | collective-permute-done | bytes 1179680 | tf_op jit(solution)/shard_map/second_axis/ppermute | solution.py:21
  114.2 1.1 collective-permute-done.14.refs_3_
  115.3 2.7 %collective-permute-start.22 = (bf16[64,9216]{1,0:T(8,128)(2,1)S(1)}, bf16[64,9216]{1,0:T(8,128)(2,1)S(1)}, u32[]{:S(2)}, u32[]{:S(2)}) collective-permute-start(bf16[64,9216]{1,0:T(8,128)(2,1)S(1)} %collective-permute-done.12.refs_1_), channel_id=1, source_target_pairs={{0,12},{4,0},{8,4},{12,8},{1,13},{5,1},{9,5},{13,9},{2,14},{6,2},{... | collective-permute-start | bytes 3538952 | tf_op jit(solution)/shard_map/second_axis/ppermute | solution.py:21
  118.0 0.5 collective-permute-start.23
  118.5 2.2 %collective-permute-start.24 = (bf16[64,9216]{1,0:T(8,128)(2,1)S(1)}, bf16[64,9216]{1,0:T(8,128)(2,1)S(1)}, u32[]{:S(2)}, u32[]{:S(2)}) collective-permute-start(bf16[64,9216]{1,0:T(8,128)(2,1)S(1)} %collective-permute-done.14.refs_3_), channel_id=1, source_target_pairs={{0,48},{16,0},{32,16},{48,32},{1,49},{17,1},{33,17},{49,33},{2,50}... | collective-permute-start | bytes 3538952 | tf_op jit(solution)/shard_map/second_axis/ppermute | solution.py:21
  120.7 4.9 %collective-permute-start.26 = (f32[2,8,8,512]{3,2,1,0:T(8,128)S(1)}, f32[2,8,8,512]{3,2,1,0:T(8,128)S(1)}, u32[]{:S(2)}, u32[]{:S(2)}) collective-permute-start(f32[2,8,8,512]{3,2,1,0:T(8,128)S(1)} %fusion.4), channel_id=1, source_target_pairs={{0,2},{2,0},{1,3},{3,1},{4,6},{6,4},{5,7},{7,5},{8,10},{10,8},{9,1... | collective-permute-start | bytes 786440 | tf_op jit(solution)/shard_map/reduce/ppermute | solution.py:142
  125.6 3.2 %reduce.10 = (f32[2,2,8,8,512]{4,3,2,1,0:T(8,128)S(1)}, f32[2,2,8,8,512]{4,3,2,1,0:T(8,128)S(1)}) custom-call(s32[3]{0:T(128)S(1)} %pad_add_fusion.place_ref, bf16[64,9216]{1,0:T(8,128)(2,1)S(1)} %collective-permute-done.11.refs_0_, bf16[64,9216]{1,0:T(8,128)(2,1)S(1)} %collective-permute-done.12.refs_1_, ...), custom_call_target="tpu_custom_call" | custom-call | flops 1048576 | bytes 65536 | tf_op jit(solution)/shard_map/reduce/pallas_call | solution.py:59
  128.9 3.9 %collective-permute-done.26 = f32[2,8,8,512]{3,2,1,0:T(8,128)S(1)} collective-permute-done((f32[2,8,8,512]{3,2,1,0:T(8,128)S(1)}, f32[2,8,8,512]{3,2,1,0:T(8,128)S(1)}, u32[]{:S(2)}, u32[]{:S(2)}) %collective-permute-start.26) | collective-permute-done | bytes 262176 | tf_op jit(solution)/shard_map/reduce/ppermute | solution.py:142
  132.7 4.0 %collective-permute-start.27 = (f32[2,2,8,8,512]{4,3,2,1,0:T(8,128)S(1)}, f32[2,2,8,8,512]{4,3,2,1,0:T(8,128)S(1)}, u32[]{:S(2)}, u32[]{:S(2)}) collective-permute-start(f32[2,2,8,8,512]{4,3,2,1,0:T(8,128)S(1)} %get-tuple-element.79), channel_id=1, source_target_pairs={{0,1},{1,0},{2,3},{3,2},{4,5},{5,4},{6,7},{7,6},{8,9},{9,8},{10,11... | collective-permute-start | bytes 1572872 | tf_op jit(solution)/shard_map/reduce/ppermute | solution.py:145
  136.8 1.5 collective-permute-done.27
  138.3 4.9 %collective-permute-start.29 = (f32[2,8,8,512]{3,2,1,0:T(8,128)S(1)}, f32[2,8,8,512]{3,2,1,0:T(8,128)S(1)}, u32[]{:S(2)}, u32[]{:S(2)}) collective-permute-start(f32[2,8,8,512]{3,2,1,0:T(8,128)S(1)} %fusion.3), channel_id=1, source_target_pairs={{0,2},{2,0},{1,3},{3,1},{4,6},{6,4},{5,7},{7,5},{8,10},{10,8},{9,1... | collective-permute-start | bytes 786440 | tf_op jit(solution)/shard_map/reduce/ppermute | solution.py:142
  143.3 3.2 %reduce.11 = (f32[2,2,8,8,512]{4,3,2,1,0:T(8,128)S(1)}, f32[2,2,8,8,512]{4,3,2,1,0:T(8,128)S(1)}) custom-call(s32[3]{0:T(128)S(1)} %pad_add_fusion.place_ref, bf16[64,9216]{1,0:T(8,128)(2,1)S(1)} %collective-permute-done.21.refs_0_, bf16[64,9216]{1,0:T(8,128)(2,1)S(1)} %collective-permute-done.22.refs_1_, ...), custom_call_target="tpu_custom_call" | custom-call | flops 1048576 | bytes 65536 | tf_op jit(solution)/shard_map/reduce/pallas_call | solution.py:59
  146.5 4.4 %collective-permute-start.28 = (f32[2,2,8,8,512]{4,3,2,1,0:T(8,128)S(1)}, f32[2,2,8,8,512]{4,3,2,1,0:T(8,128)S(1)}, u32[]{:S(2)}, u32[]{:S(2)}) collective-permute-start(f32[2,2,8,8,512]{4,3,2,1,0:T(8,128)S(1)} %get-tuple-element.86), channel_id=1, source_target_pairs={{0,1},{1,0},{2,3},{3,2},{4,5},{5,4},{6,7},{7,6},{8,9},{9,8},{10,11... | collective-permute-start | bytes 1572872 | tf_op jit(solution)/shard_map/reduce/ppermute | solution.py:145
  150.9 1.0 collective-permute-done.29
  152.0 0.4 collective-permute-done.28.got_ref
  152.5 4.9 %collective-permute-start.30 = (f32[2,8,8,512]{3,2,1,0:T(8,128)S(1)}, f32[2,8,8,512]{3,2,1,0:T(8,128)S(1)}, u32[]{:S(2)}, u32[]{:S(2)}) collective-permute-start(f32[2,8,8,512]{3,2,1,0:T(8,128)S(1)} %fusion.2), channel_id=1, source_target_pairs={{0,2},{2,0},{1,3},{3,1},{4,6},{6,4},{5,7},{7,5},{8,10},{10,8},{9,1... | collective-permute-start | bytes 786440 | tf_op jit(solution)/shard_map/reduce/ppermute | solution.py:142
  157.4 8.9 %collective-permute-done.30.back_ref = f32[2,8,8,512]{3,2,1,0:T(8,128)S(1)} collective-permute-done((f32[2,8,8,512]{3,2,1,0:T(8,128)S(1)}, f32[2,8,8,512]{3,2,1,0:T(8,128)S(1)}, u32[]{:S(2)}, u32[]{:S(2)}) %collective-permute-start.30) | collective-permute-done | bytes 262176 | tf_op jit(solution)/shard_map/reduce/ppermute | solution.py:142
  166.3 1.6 reduce.12
  (42 shorter events, 1.1 us)
Async XLA Ops:
  1.0 9.2 %collective-permute-start = (bf16[16,9216]{1,0:T(8,128)(2,1)S(1)}, bf16[16,9216]{1,0:T(8,128)(2,1)S(1)}, u32[]{:S(2)}, u32[]{:S(2)}) collective-permute-start(bf16[16,9216]{1,0:T(8,128)(2,1)S(1)} %get-tuple-element.92), channel_id=1, source_target_pairs={{0,64},{64,0},{128,192},{192,128},{1,65},{65,1},{129,193},{193,129... | collective-permute-start | bytes 884744 | tf_op jit(solution)/shard_map/z_shifts/ppermute | solution.py:26
  1.1 21.3 %collective-permute-start.1 = (bf16[16,9216]{1,0:T(8,128)(2,1)S(1)}, bf16[16,9216]{1,0:T(8,128)(2,1)S(1)}, u32[]{:S(2)}, u32[]{:S(2)}) collective-permute-start(bf16[16,9216]{1,0:T(8,128)(2,1)S(1)} %get-tuple-element.92), channel_id=1, source_target_pairs={{0,128},{64,192},{128,0},{192,64},{1,129},{65,193},{129,1},{193,65... | collective-permute-start | bytes 884744 | tf_op jit(solution)/shard_map/z_shifts/ppermute | solution.py:26
  4.2 25.6 %collective-permute-start.2 = (bf16[16,9216]{1,0:T(8,128)(2,1)S(1)}, bf16[16,9216]{1,0:T(8,128)(2,1)S(1)}, u32[]{:S(2)}, u32[]{:S(2)}) collective-permute-start(bf16[16,9216]{1,0:T(8,128)(2,1)S(1)} %get-tuple-element.92), channel_id=1, source_target_pairs={{0,192},{64,128},{128,64},{192,0},{1,193},{65,129},{129,65},{193,1... | collective-permute-start | bytes 884744 | tf_op jit(solution)/shard_map/z_shifts/ppermute | solution.py:26
  30.1 14.7 %collective-permute-start.3 = (bf16[32,9216]{1,0:T(8,128)(2,1)S(1)}, bf16[32,9216]{1,0:T(8,128)(2,1)S(1)}, u32[]{:S(2)}, u32[]{:S(2)}) collective-permute-start(bf16[32,9216]{1,0:T(8,128)(2,1)S(1)} %get-tuple-element.90), channel_id=1, source_target_pairs={{0,16},{16,32},{32,48},{48,0},{1,17},{17,33},{33,49},{49,1},{2,18}... | collective-permute-start | bytes 1769480 | tf_op jit(solution)/shard_map/first_axis/ppermute | solution.py:21
  31.5 14.2 %collective-permute-start.5 = (bf16[32,9216]{1,0:T(8,128)(2,1)S(1)}, bf16[32,9216]{1,0:T(8,128)(2,1)S(1)}, u32[]{:S(2)}, u32[]{:S(2)}) collective-permute-start(bf16[32,9216]{1,0:T(8,128)(2,1)S(1)} %get-tuple-element.89), channel_id=1, source_target_pairs={{0,4},{4,8},{8,12},{12,0},{1,5},{5,9},{9,13},{13,1},{2,6},{6,10},{... | collective-permute-start | bytes 1769480 | tf_op jit(solution)/shard_map/first_axis/ppermute | solution.py:21
  32.7 14.9 %collective-permute-start.4 = (bf16[32,9216]{1,0:T(8,128)(2,1)S(1)}, bf16[32,9216]{1,0:T(8,128)(2,1)S(1)}, u32[]{:S(2)}, u32[]{:S(2)}) collective-permute-start(bf16[32,9216]{1,0:T(8,128)(2,1)S(1)} %get-tuple-element.90), channel_id=1, source_target_pairs={{0,48},{16,0},{32,16},{48,32},{1,49},{17,1},{33,17},{49,33},{2,50}... | collective-permute-start | bytes 1769480 | tf_op jit(solution)/shard_map/first_axis/ppermute | solution.py:21
  34.2 15.3 %collective-permute-start.6 = (bf16[32,9216]{1,0:T(8,128)(2,1)S(1)}, bf16[32,9216]{1,0:T(8,128)(2,1)S(1)}, u32[]{:S(2)}, u32[]{:S(2)}) collective-permute-start(bf16[32,9216]{1,0:T(8,128)(2,1)S(1)} %get-tuple-element.89), channel_id=1, source_target_pairs={{0,12},{4,0},{8,4},{12,8},{1,13},{5,1},{9,5},{13,9},{2,14},{6,2},{... | collective-permute-start | bytes 1769480 | tf_op jit(solution)/shard_map/first_axis/ppermute | solution.py:21
  47.6 1.9 %copy-start.4 = (bf16[32,9216]{1,0:T(8,128)(2,1)}, bf16[32,9216]{1,0:T(8,128)(2,1)S(1)}, u32[]{:S(2)}) copy-start(bf16[32,9216]{1,0:T(8,128)(2,1)S(1)} %collective-permute-done.4) | copy-start | bytes 1769476
  48.4 46.0 %slice-start = ((s8[7340032]{0:T(1024)(128)(4,1)}), s8[3145728]{0:T(1024)(128)(4,1)S(1)}, s32[]{:S(2)}) async-start(s8[7340032]{0:T(1024)(128)(4,1)} %bitcast.34), calls=%async_computation | async-start | bytes 6291456
  49.5 0.9 copy-start.5
  50.4 6.6 %collective-permute-start.10 = (bf16[16,9216]{1,0:T(8,128)(2,1)}, bf16[16,9216]{1,0:T(8,128)(2,1)S(1)}, u32[]{:S(2)}, u32[]{:S(2)}) collective-permute-start(bf16[16,9216]{1,0:T(8,128)(2,1)} %slice.109), channel_id=1, source_target_pairs={{0,12},{4,0},{8,4},{12,8},{1,13},{5,1},{9,5},{13,9},{2,14},{6,2},{... | collective-permute-start | bytes 884744 | tf_op jit(solution)/shard_map/first_axis/ppermute | solution.py:21
  52.7 7.1 %collective-permute-start.9 = (bf16[16,9216]{1,0:T(8,128)(2,1)}, bf16[16,9216]{1,0:T(8,128)(2,1)}, u32[]{:S(2)}, u32[]{:S(2)}) collective-permute-start(bf16[16,9216]{1,0:T(8,128)(2,1)} %slice.108), channel_id=1, source_target_pairs={{0,4},{4,8},{8,12},{12,0},{1,5},{5,9},{9,13},{13,1},{2,6},{6,10},{... | collective-permute-start | bytes 884744 | tf_op jit(solution)/shard_map/first_axis/ppermute | solution.py:21
  52.8 10.2 %copy-start.2 = (bf16[64,9216]{1,0:T(8,128)(2,1)S(1)}, bf16[64,9216]{1,0:T(8,128)(2,1)}, u32[]{:S(2)}) copy-start(bf16[64,9216]{1,0:T(8,128)(2,1)} %pad_maximum_fusion.2.refs_2_) | copy-start | bytes 3538948
  52.8 32.5 %collective-permute-start.15 = (bf16[64,9216]{1,0:T(8,128)(2,1)}, bf16[64,9216]{1,0:T(8,128)(2,1)S(1)}, u32[]{:S(2)}, u32[]{:S(2)}) collective-permute-start(bf16[64,9216]{1,0:T(8,128)(2,1)} %pad_maximum_fusion.1.refs_0_), channel_id=1, source_target_pairs={{0,4},{4,8},{8,12},{12,0},{1,5},{5,9},{9,13},{13,1},{2,6},{6,10},{... | collective-permute-start | bytes 3538952 | tf_op jit(solution)/shard_map/second_axis/ppermute | solution.py:21
  53.0 32.7 %collective-permute-start.16 = (bf16[64,9216]{1,0:T(8,128)(2,1)}, bf16[64,9216]{1,0:T(8,128)(2,1)S(1)}, u32[]{:S(2)}, u32[]{:S(2)}) collective-permute-start(bf16[64,9216]{1,0:T(8,128)(2,1)} %pad_maximum_fusion.1.refs_0_), channel_id=1, source_target_pairs={{0,12},{4,0},{8,4},{12,8},{1,13},{5,1},{9,5},{13,9},{2,14},{6,2},{... | collective-permute-start | bytes 3538952 | tf_op jit(solution)/shard_map/second_axis/ppermute | solution.py:21
  55.6 7.4 %collective-permute-start.7 = (bf16[16,9216]{1,0:T(8,128)(2,1)}, bf16[16,9216]{1,0:T(8,128)(2,1)S(1)}, u32[]{:S(2)}, u32[]{:S(2)}) collective-permute-start(bf16[16,9216]{1,0:T(8,128)(2,1)} %slice.105), channel_id=1, source_target_pairs={{0,16},{16,32},{32,48},{48,0},{1,17},{17,33},{33,49},{49,1},{2,18}... | collective-permute-start | bytes 884744 | tf_op jit(solution)/shard_map/first_axis/ppermute | solution.py:21
  57.0 7.1 %collective-permute-start.8 = (bf16[16,9216]{1,0:T(8,128)(2,1)}, bf16[16,9216]{1,0:T(8,128)(2,1)S(1)}, u32[]{:S(2)}, u32[]{:S(2)}) collective-permute-start(bf16[16,9216]{1,0:T(8,128)(2,1)} %slice.106), channel_id=1, source_target_pairs={{0,48},{16,0},{32,16},{48,32},{1,49},{17,1},{33,17},{49,33},{2,50}... | collective-permute-start | bytes 884744 | tf_op jit(solution)/shard_map/first_axis/ppermute | solution.py:21
  59.8 27.0 %collective-permute-start.17 = (bf16[64,9216]{1,0:T(8,128)(2,1)}, bf16[64,9216]{1,0:T(8,128)(2,1)S(1)}, u32[]{:S(2)}, u32[]{:S(2)}) collective-permute-start(bf16[64,9216]{1,0:T(8,128)(2,1)} %pad_maximum_fusion.2.refs_2_), channel_id=1, source_target_pairs={{0,16},{16,32},{32,48},{48,0},{1,17},{17,33},{33,49},{49,1},{2,18}... | collective-permute-start | bytes 3538952 | tf_op jit(solution)/shard_map/second_axis/ppermute | solution.py:21
  60.1 5.2 %copy-start.3 = (bf16[64,9216]{1,0:T(8,128)(2,1)S(1)}, bf16[64,9216]{1,0:T(8,128)(2,1)}, u32[]{:S(2)}) copy-start(bf16[64,9216]{1,0:T(8,128)(2,1)} %pad_maximum_fusion.1.refs_0_) | copy-start | bytes 3538948
  61.4 3.9 %copy-start.1 = (bf16[512,2048]{1,0:T(8,128)(2,1)S(1)}, bf16[512,2048]{1,0:T(8,128)(2,1)}, u32[]{:S(2)}) copy-start(bf16[512,2048]{1,0:T(8,128)(2,1)} %refs_5_.7) | copy-start | bytes 6291460
  63.0 27.1 %collective-permute-start.18 = (bf16[64,9216]{1,0:T(8,128)(2,1)S(1)}, bf16[64,9216]{1,0:T(8,128)(2,1)S(1)}, u32[]{:S(2)}, u32[]{:S(2)}) collective-permute-start(bf16[64,9216]{1,0:T(8,128)(2,1)S(1)} %copy-done.2), channel_id=1, source_target_pairs={{0,48},{16,0},{32,16},{48,32},{1,49},{17,1},{33,17},{49,33},{2,50}... | collective-permute-start | bytes 3538952 | tf_op jit(solution)/shard_map/second_axis/ppermute | solution.py:21
  65.3 3.1 %copy-start = (bf16[512,7168]{1,0:T(8,128)(2,1)S(1)}, bf16[512,7168]{1,0:T(8,128)(2,1)}, u32[]{:S(2)}) copy-start(bf16[512,7168]{1,0:T(8,128)(2,1)} %refs_4_.7) | copy-start | bytes 22020100
  68.4 26.0 %slice-start.1 = ((s8[7340032]{0:T(1024)(128)(4,1)}), s8[4194304]{0:T(1024)(128)(4,1)S(1)}, s32[]{:S(2)}) async-start(s8[7340032]{0:T(1024)(128)(4,1)} %bitcast.34), calls=%async_computation.1 | async-start | bytes 8388608
  71.6 10.8 %collective-permute-start.19 = (f32[2,2,8,8,512]{4,3,2,1,0:T(8,128)S(1)}, f32[2,2,8,8,512]{4,3,2,1,0:T(8,128)S(1)}, u32[]{:S(2)}, u32[]{:S(2)}) collective-permute-start(f32[2,2,8,8,512]{4,3,2,1,0:T(8,128)S(1)} %get-tuple-element.66), channel_id=1, source_target_pairs={{0,1},{1,0},{2,3},{3,2},{4,5},{5,4},{6,7},{7,6},{8,9},{9,8},{10,11... | collective-permute-start | bytes 1572872 | tf_op jit(solution)/shard_map/reduce/ppermute | solution.py:145
  82.5 29.9 %collective-permute-start.11 = (bf16[64,9216]{1,0:T(8,128)(2,1)S(1)}, bf16[64,9216]{1,0:T(8,128)(2,1)S(1)}, u32[]{:S(2)}, u32[]{:S(2)}) collective-permute-start(bf16[64,9216]{1,0:T(8,128)(2,1)S(1)} %pad_maximum_fusion.3.refs_1_), channel_id=1, source_target_pairs={{0,4},{4,8},{8,12},{12,0},{1,5},{5,9},{9,13},{13,1},{2,6},{6,10},{... | collective-permute-start | bytes 3538952 | tf_op jit(solution)/shard_map/second_axis/ppermute | solution.py:21
  85.3 27.0 %collective-permute-start.12 = (bf16[64,9216]{1,0:T(8,128)(2,1)S(1)}, bf16[64,9216]{1,0:T(8,128)(2,1)S(1)}, u32[]{:S(2)}, u32[]{:S(2)}) collective-permute-start(bf16[64,9216]{1,0:T(8,128)(2,1)S(1)} %pad_maximum_fusion.3.refs_1_), channel_id=1, source_target_pairs={{0,12},{4,0},{8,4},{12,8},{1,13},{5,1},{9,5},{13,9},{2,14},{6,2},{... | collective-permute-start | bytes 3538952 | tf_op jit(solution)/shard_map/second_axis/ppermute | solution.py:21
  85.7 28.5 %collective-permute-start.13 = (bf16[64,9216]{1,0:T(8,128)(2,1)S(1)}, bf16[64,9216]{1,0:T(8,128)(2,1)S(1)}, u32[]{:S(2)}, u32[]{:S(2)}) collective-permute-start(bf16[64,9216]{1,0:T(8,128)(2,1)S(1)} %pad_maximum_fusion.4.refs_3_), channel_id=1, source_target_pairs={{0,16},{16,32},{32,48},{48,0},{1,17},{17,33},{33,49},{49,1},{2,18}... | collective-permute-start | bytes 3538952 | tf_op jit(solution)/shard_map/second_axis/ppermute | solution.py:21
  86.9 28.4 %collective-permute-start.14 = (bf16[64,9216]{1,0:T(8,128)(2,1)S(1)}, bf16[64,9216]{1,0:T(8,128)(2,1)S(1)}, u32[]{:S(2)}, u32[]{:S(2)}) collective-permute-start(bf16[64,9216]{1,0:T(8,128)(2,1)S(1)} %pad_maximum_fusion.4.refs_3_), channel_id=1, source_target_pairs={{0,48},{16,0},{32,16},{48,32},{1,49},{17,1},{33,17},{49,33},{2,50}... | collective-permute-start | bytes 3538952 | tf_op jit(solution)/shard_map/second_axis/ppermute | solution.py:21
  90.0 9.2 %collective-permute-start.20 = (f32[2,8,8,512]{3,2,1,0:T(8,128)S(1)}, f32[2,8,8,512]{3,2,1,0:T(8,128)S(1)}, u32[]{:S(2)}, u32[]{:S(2)}) collective-permute-start(f32[2,8,8,512]{3,2,1,0:T(8,128)S(1)} %fusion.7), channel_id=1, source_target_pairs={{0,2},{2,0},{1,3},{3,1},{4,6},{6,4},{5,7},{7,5},{8,10},{10,8},{9,1... | collective-permute-start | bytes 786440 | tf_op jit(solution)/shard_map/reduce/ppermute | solution.py:142
  99.3 21.4 %collective-permute-start.25 = (f32[2,2,8,8,512]{4,3,2,1,0:T(8,128)S(1)}, f32[2,2,8,8,512]{4,3,2,1,0:T(8,128)S(1)}, u32[]{:S(2)}, u32[]{:S(2)}) collective-permute-start(f32[2,2,8,8,512]{4,3,2,1,0:T(8,128)S(1)} %get-tuple-element.75), channel_id=1, source_target_pairs={{0,1},{1,0},{2,3},{3,2},{4,5},{5,4},{6,7},{7,6},{8,9},{9,8},{10,11... | collective-permute-start | bytes 1572872 | tf_op jit(solution)/shard_map/reduce/ppermute | solution.py:145
  115.3 27.9 %collective-permute-start.21 = (bf16[64,9216]{1,0:T(8,128)(2,1)S(1)}, bf16[64,9216]{1,0:T(8,128)(2,1)S(1)}, u32[]{:S(2)}, u32[]{:S(2)}) collective-permute-start(bf16[64,9216]{1,0:T(8,128)(2,1)S(1)} %collective-permute-done.15.refs_0_), channel_id=1, source_target_pairs={{0,4},{4,8},{8,12},{12,0},{1,5},{5,9},{9,13},{13,1},{2,6},{6,10},{... | collective-permute-start | bytes 3538952 | tf_op jit(solution)/shard_map/second_axis/ppermute | solution.py:21
  115.3 28.0 %collective-permute-start.22 = (bf16[64,9216]{1,0:T(8,128)(2,1)S(1)}, bf16[64,9216]{1,0:T(8,128)(2,1)S(1)}, u32[]{:S(2)}, u32[]{:S(2)}) collective-permute-start(bf16[64,9216]{1,0:T(8,128)(2,1)S(1)} %collective-permute-done.12.refs_1_), channel_id=1, source_target_pairs={{0,12},{4,0},{8,4},{12,8},{1,13},{5,1},{9,5},{13,9},{2,14},{6,2},{... | collective-permute-start | bytes 3538952 | tf_op jit(solution)/shard_map/second_axis/ppermute | solution.py:21
  118.0 25.3 %collective-permute-start.23 = (bf16[64,9216]{1,0:T(8,128)(2,1)S(1)}, bf16[64,9216]{1,0:T(8,128)(2,1)S(1)}, u32[]{:S(2)}, u32[]{:S(2)}) collective-permute-start(bf16[64,9216]{1,0:T(8,128)(2,1)S(1)} %collective-permute-done.17.refs_2_), channel_id=1, source_target_pairs={{0,16},{16,32},{32,48},{48,0},{1,17},{17,33},{33,49},{49,1},{2,18}... | collective-permute-start | bytes 3538952 | tf_op jit(solution)/shard_map/second_axis/ppermute | solution.py:21
  118.5 24.8 %collective-permute-start.24 = (bf16[64,9216]{1,0:T(8,128)(2,1)S(1)}, bf16[64,9216]{1,0:T(8,128)(2,1)S(1)}, u32[]{:S(2)}, u32[]{:S(2)}) collective-permute-start(bf16[64,9216]{1,0:T(8,128)(2,1)S(1)} %collective-permute-done.14.refs_3_), channel_id=1, source_target_pairs={{0,48},{16,0},{32,16},{48,32},{1,49},{17,1},{33,17},{49,33},{2,50}... | collective-permute-start | bytes 3538952 | tf_op jit(solution)/shard_map/second_axis/ppermute | solution.py:21
  120.7 12.0 %collective-permute-start.26 = (f32[2,8,8,512]{3,2,1,0:T(8,128)S(1)}, f32[2,8,8,512]{3,2,1,0:T(8,128)S(1)}, u32[]{:S(2)}, u32[]{:S(2)}) collective-permute-start(f32[2,8,8,512]{3,2,1,0:T(8,128)S(1)} %fusion.4), channel_id=1, source_target_pairs={{0,2},{2,0},{1,3},{3,1},{4,6},{6,4},{5,7},{7,5},{8,10},{10,8},{9,1... | collective-permute-start | bytes 786440 | tf_op jit(solution)/shard_map/reduce/ppermute | solution.py:142
  132.7 5.5 %collective-permute-start.27 = (f32[2,2,8,8,512]{4,3,2,1,0:T(8,128)S(1)}, f32[2,2,8,8,512]{4,3,2,1,0:T(8,128)S(1)}, u32[]{:S(2)}, u32[]{:S(2)}) collective-permute-start(f32[2,2,8,8,512]{4,3,2,1,0:T(8,128)S(1)} %get-tuple-element.79), channel_id=1, source_target_pairs={{0,1},{1,0},{2,3},{3,2},{4,5},{5,4},{6,7},{7,6},{8,9},{9,8},{10,11... | collective-permute-start | bytes 1572872 | tf_op jit(solution)/shard_map/reduce/ppermute | solution.py:145
  138.3 13.6 %collective-permute-start.29 = (f32[2,8,8,512]{3,2,1,0:T(8,128)S(1)}, f32[2,8,8,512]{3,2,1,0:T(8,128)S(1)}, u32[]{:S(2)}, u32[]{:S(2)}) collective-permute-start(f32[2,8,8,512]{3,2,1,0:T(8,128)S(1)} %fusion.3), channel_id=1, source_target_pairs={{0,2},{2,0},{1,3},{3,1},{4,6},{6,4},{5,7},{7,5},{8,10},{10,8},{9,1... | collective-permute-start | bytes 786440 | tf_op jit(solution)/shard_map/reduce/ppermute | solution.py:142
  146.5 5.9 %collective-permute-start.28 = (f32[2,2,8,8,512]{4,3,2,1,0:T(8,128)S(1)}, f32[2,2,8,8,512]{4,3,2,1,0:T(8,128)S(1)}, u32[]{:S(2)}, u32[]{:S(2)}) collective-permute-start(f32[2,2,8,8,512]{4,3,2,1,0:T(8,128)S(1)} %get-tuple-element.86), channel_id=1, source_target_pairs={{0,1},{1,0},{2,3},{3,2},{4,5},{5,4},{6,7},{7,6},{8,9},{9,8},{10,11... | collective-permute-start | bytes 1572872 | tf_op jit(solution)/shard_map/reduce/ppermute | solution.py:145
  152.5 13.8 %collective-permute-start.30 = (f32[2,8,8,512]{3,2,1,0:T(8,128)S(1)}, f32[2,8,8,512]{3,2,1,0:T(8,128)S(1)}, u32[]{:S(2)}, u32[]{:S(2)}) collective-permute-start(f32[2,8,8,512]{3,2,1,0:T(8,128)S(1)} %fusion.2), channel_id=1, source_target_pairs={{0,2},{2,0},{1,3},{3,1},{4,6},{6,4},{5,7},{7,5},{8,10},{10,8},{9,1... | collective-permute-start | bytes 786440 | tf_op jit(solution)/shard_map/reduce/ppermute | solution.py:142
